TPU v7x, 128 devices: a whole 4x4x4 slice. The times are simulated.
128 devices in a mesh: ctx: 16 (over x_hi, y, core), fsdp: 8 (over x_lo, z).
Axes of the slice: x: 4 (x_hi: 2, x_lo: 2; x = x_hi * 2 + x_lo), y: 4, z: 4, core: 2. Of those that a mesh axis runs over, the one named last changes fastest.
Arguments:
- query_rows: bfloat16 [8, 2048, 1024], P('fsdp', 'ctx'), may hold values from -12 to 12
- key_rows: bfloat16 [8, 2048, 1024], P('fsdp', 'ctx'), may hold values from -12 to 12
- value_rows: bfloat16 [8, 2048, 1024], P('fsdp', 'ctx'), may hold values from -6 to 6
- session: int32 [8, 2048], P('fsdp'), may hold values from 0 to 127, never falling along the last dimension, each value on 1 to 64 neighbouring positions
- lengths: int32 [8], P('fsdp'), may hold values from 256 to 2048, as said below
- out_weight: bfloat16 [1024, 2048], P('fsdp'), may hold values from -0.1875 to 0.1875
- upstream: bfloat16 [8, 2048, 2048], P('fsdp', 'ctx'), may hold values from -6 to 6
Outputs:
- attended: bfloat16 [8, 2048, 2048], P('fsdp', 'ctx')
- query_grad: bfloat16 [8, 2048, 1024], P('fsdp', 'ctx')
- key_grad: bfloat16 [8, 2048, 1024], P('fsdp', 'ctx')
- value_grad: bfloat16 [8, 2048, 1024], P('fsdp', 'ctx')
- weight_grad: float32 [1024, 2048], P('fsdp')
Inputs may be any that keep to these rules, and one draw needn't show every extreme that they name: `lengths`: some history has all 2048 events valid and some history only one eighth of 2048. session numbers never fall along a history; a session spans 1 to 64 events.
All inputs are finite; a program needn't handle non-finite values.
Results may differ from a plain program's by a relative error of at most 0.022.
Values may be sent and summed in bfloat16 or wider, within the bound.
No kernel may reach another device: no remote copies, remote signals or barrier semaphores. Data moves between devices by JAX's collectives and lax.ppermute only.
A program may use at most 128 MiB of HBM per device.

v0:
```python
import math

import jax
import jax.numpy as jnp
from jax import lax
from jax.sharding import PartitionSpec as P

HEADS = 8
HS = 128


NEG = -1e30


def head_split(matrix):
    return matrix.reshape(matrix.shape[0], HEADS, HS)


def keep_same(current):
    return current


def shards(query_rows, key_rows, value_rows, session, lengths, out_weight, upstream):
    token_count = query_rows.shape[1]
    half_rows = token_count // 2
    cycle_index = lax.axis_index("ctx")
    history_len = session.shape[1]
    session_ids = session[0]
    valid_len = lengths[0]
    score_scale = 1.0 / math.sqrt(HS)
    width = HEADS * HS
    own_query = query_rows[0]
    own_key = key_rows[0]
    own_value = value_rows[0]
    own_upstream = upstream[0]
    own_start = cycle_index * token_count
    own_positions = own_start + jnp.arange(token_count, dtype=jnp.int32)
    whole_weight = lax.all_gather(out_weight, "fsdp", axis=0, tiled=True)
    own_valid = own_positions < valid_len
    back_proj = lax.dot_general(
        own_upstream, whole_weight, (((1,), (1,)), ((), ())), preferred_element_type=jnp.float32
    )
    context_grad = (back_proj * own_valid[:, None].astype(jnp.float32)).astype(jnp.bfloat16)
    query_heads = []
    grad_heads = []
    query_sess = []
    query_ok = []
    sess_limit = []
    for portion in range(2):
        positions = own_positions[portion * half_rows : (portion + 1) * half_rows]
        sessions = jnp.take(session_ids, positions)
        valid_here = positions < valid_len
        query_heads.append(head_split(own_query[portion * half_rows : (portion + 1) * half_rows]))
        grad_heads.append(head_split(context_grad[portion * half_rows : (portion + 1) * half_rows]))
        query_sess.append(sessions)
        query_ok.append(valid_here)
        sess_limit.append(jnp.max(jnp.where(valid_here, sessions, -1)))

    def allowed_for(portion, key_pos, key_sess):
        allowed = (key_sess[None, :] <= query_sess[portion][:, None]) & (
            key_pos[None, :] < valid_len
        )
        return (allowed & query_ok[portion][:, None])[None]

    def needed(portion, first_row):
        return (first_row < valid_len) & (session_ids[first_row] <= sess_limit[portion])

    start_max = jnp.full((2, HEADS, half_rows), NEG, jnp.float32)
    start_sum = jnp.zeros((2, HEADS, half_rows), jnp.float32)
    first_row = jnp.int32(0)
    run_max = start_max
    run_sum = start_sum
    piece_key = lax.all_gather(own_key, "ctx", axis=0, tiled=True)
    piece_value = lax.all_gather(own_value, "ctx", axis=0, tiled=True)
    row_count = piece_key.shape[0]
    key_pos = jnp.arange(row_count, dtype=jnp.int32)
    key_sess = session_ids
    key_heads = head_split(piece_key)
    new_max = []
    new_sum = []
    for absorb_portion in range(2):

        def update(current):
            old_max, old_sum = current
            scores = (
                jnp.einsum(
                    "qhd,khd->hqk",
                    query_heads[absorb_portion],
                    key_heads,
                    preferred_element_type=jnp.float32,
                )
                * score_scale
            )
            allowed = allowed_for(absorb_portion, key_pos, key_sess)
            masked = jnp.where(allowed, scores, NEG)
            next_max = jnp.maximum(old_max, jnp.max(masked, axis=2))
            terms = jnp.where(allowed, jnp.exp(masked - next_max[:, :, None]), 0.0)
            next_sum = jnp.sum(terms, axis=2)
            return (next_max, next_sum)

        result = lax.cond(
            needed(absorb_portion, first_row),
            update,
            keep_same,
            (run_max[absorb_portion], run_sum[absorb_portion]),
        )
        new_max.append(result[0])
        new_sum.append(result[1])
    run_max = jnp.stack(new_max)
    run_sum = jnp.stack(new_sum)
    log_total = [
        jnp.where(query_ok[portion][None, :], run_max[portion] + jnp.log(run_sum[portion]), 0.0)
        for portion in range(2)
    ]
    key_block = math.gcd(history_len, 512)
    block_count = history_len // key_block

    def slice_keys(block_index):
        first_row = block_index * key_block
        key_slice = head_split(lax.dynamic_slice_in_dim(piece_key, first_row, key_block))
        value_slice = head_split(lax.dynamic_slice_in_dim(piece_value, first_row, key_block))
        key_pos = first_row + jnp.arange(key_block, dtype=jnp.int32)
        key_sess = lax.dynamic_slice_in_dim(session_ids, first_row, key_block)
        return (first_row, key_slice, value_slice, key_pos, key_sess)

    def probability_of(portion, key_slice, key_pos, key_sess):
        scores = (
            jnp.einsum(
                "qhd,khd->hqk", query_heads[portion], key_slice, preferred_element_type=jnp.float32
            )
            * score_scale
        )
        allowed = allowed_for(portion, key_pos, key_sess)
        masked = jnp.where(allowed, scores, NEG)
        return jnp.where(allowed, jnp.exp(masked - log_total[portion][:, :, None]), 0.0)

    def context_step(block_index, sums):
        first_row, key_slice, value_slice, key_pos, key_sess = slice_keys(block_index)
        out_sums = []
        for portion in range(2):

            def accumulate(current):
                probability = probability_of(portion, key_slice, key_pos, key_sess)
                return current + jnp.einsum(
                    "hqk,khd->qhd",
                    probability.astype(jnp.bfloat16),
                    value_slice,
                    preferred_element_type=jnp.float32,
                )

            out_sums.append(
                lax.cond(needed(portion, first_row), accumulate, keep_same, sums[portion])
            )
        return tuple(out_sums)

    zero_part = jnp.zeros((half_rows, HEADS, HS), jnp.float32)
    context_parts = lax.fori_loop(0, block_count, context_step, (zero_part, zero_part))
    context_local = jnp.concatenate(
        [context_parts[0].reshape(half_rows, width), context_parts[1].reshape(half_rows, width)],
        axis=0,
    ).astype(jnp.bfloat16)
    deltas = []
    for portion in range(2):
        context_here = head_split(
            context_local[portion * half_rows : (portion + 1) * half_rows]
        ).astype(jnp.float32)
        deltas.append(jnp.sum(grad_heads[portion].astype(jnp.float32) * context_here, axis=2).T)

    def backward_step(block_index, running):
        first_row, key_slice, value_slice, key_pos, key_sess = slice_keys(block_index)
        grad_parts = [running[0], running[1]]
        term_arrays = tuple(running[2:])
        for portion in range(2):

            def backprop(current):
                probability = probability_of(portion, key_slice, key_pos, key_sess)
                dprob = jnp.einsum(
                    "qhd,khd->hqk",
                    grad_heads[portion],
                    value_slice,
                    preferred_element_type=jnp.float32,
                )
                dscore = (probability * (dprob - deltas[portion][:, :, None]) * score_scale).astype(
                    jnp.bfloat16
                )
                new_grad = current[0] + jnp.einsum(
                    "hqk,khd->qhd", dscore, key_slice, preferred_element_type=jnp.float32
                )
                add_key = jnp.einsum(
                    "hqk,qhd->khd", dscore, query_heads[portion], preferred_element_type=jnp.float32
                )
                add_value = jnp.einsum(
                    "hqk,qhd->khd",
                    probability.astype(jnp.bfloat16),
                    grad_heads[portion],
                    preferred_element_type=jnp.float32,
                )
                key_part = lax.dynamic_slice_in_dim(current[1], first_row, key_block) + add_key
                value_part = lax.dynamic_slice_in_dim(current[2], first_row, key_block) + add_value
                return (
                    new_grad,
                    lax.dynamic_update_slice_in_dim(current[1], key_part, first_row, 0),
                    lax.dynamic_update_slice_in_dim(current[2], value_part, first_row, 0),
                )

            result = lax.cond(
                needed(portion, first_row),
                backprop,
                keep_same,
                (grad_parts[portion],) + term_arrays,
            )
            grad_parts[portion] = result[0]
            term_arrays = tuple(result[1:])
        return (grad_parts[0], grad_parts[1]) + term_arrays

    zero_terms = jnp.zeros((history_len, HEADS, HS), jnp.float32)
    backward_init = (zero_part, zero_part, zero_terms, zero_terms)
    back_result = lax.fori_loop(0, block_count, backward_step, backward_init)
    query_grad_local = jnp.concatenate(
        [back_result[0].reshape(half_rows, width), back_result[1].reshape(half_rows, width)], axis=0
    ).astype(jnp.bfloat16)
    summed_key, summed_value = (
        lax.psum_scatter(
            back_result[2].reshape(history_len, width), "ctx", scatter_dimension=0, tiled=True
        ),
        lax.psum_scatter(
            back_result[3].reshape(history_len, width), "ctx", scatter_dimension=0, tiled=True
        ),
    )
    key_grad = summed_key.astype(jnp.bfloat16)
    value_grad = summed_value.astype(jnp.bfloat16)
    attended = jnp.dot(context_local, whole_weight, preferred_element_type=jnp.float32).astype(
        jnp.bfloat16
    )
    weight_grad = lax.psum_scatter(
        lax.dot_general(
            context_local,
            own_upstream,
            (((0,), (0,)), ((), ())),
            preferred_element_type=jnp.float32,
        ),
        "fsdp",
        scatter_dimension=0,
        tiled=True,
    )
    weight_grad = lax.psum(weight_grad, "ctx")
    return (attended[None], query_grad_local[None], key_grad[None], value_grad[None], weight_grad)


def solution(mesh):
    placed = (
        P("fsdp", "ctx", None),
        P("fsdp", "ctx", None),
        P("fsdp", "ctx", None),
        P("fsdp", None),
        P("fsdp"),
        P("fsdp", None),
        P("fsdp", "ctx", None),
    )
    return jax.shard_map(
        shards,
        mesh=mesh,
        in_specs=placed,
        out_specs=(
            P("fsdp", "ctx", None),
            P("fsdp", "ctx", None),
            P("fsdp", "ctx", None),
            P("fsdp", "ctx", None),
            P("fsdp", None),
        ),
        check_vma=False,
    )
```

profile of v0, /device:TPU:1, one launch (start us, length us, event | category | flops | bytes accessed | tf_op | source)
XLA Modules:
  0.0 739.7 jit_solution(12379975720167414522)
XLA Ops:
  22.4 43.3 %all-gather.6.cloned.1.call-done = bf16[1024,2048]{1,0:T(8,128)(2,1)} async-done(((bf16[128,2048]{1,0:T(8,128)(2,1)}), bf16[1024,2048]{1,0:T(8,128)(2,1)}) %all-gather.6.cloned.1.call-update) | async-done | bytes 4194320 | tf_op jit(solution)/shard_map/all_gather | solution.py:38
  65.7 3.7 fusion.69
  69.4 54.8 %all-gather.8.cloned.1.call-done = bf16[1,2048,1024]{1,2,0:T(8,128)(2,1)} async-done(((bf16[1,128,1024]{1,2,0:T(8,128)(2,1)}), bf16[1,2048,1024]{1,2,0:T(8,128)(2,1)}) %all-gather.8.cloned.1.call-update) | async-done | bytes 4194320 | tf_op jit(solution)/shard_map/all_gather | solution.py:73
  124.2 6.9 conditional.7
  125.1 3.5 fusion.3
  131.2 7.7 %conditional.6 = (f32[8,64]{1,0:T(8,128)}, f32[8,64]{1,0:T(8,128)S(1)}) conditional(s32[]{:T(128)} %convert_element_type.99, () %tuple.91, (s32[1,2048]{1,0:T(1,128)S(1)}, s32[64]{0:T(128)}, s32[]{:T(128)}, s32[2048]{0:T(1024)S(1)}, pred[64]{0:T(512)(128)(4,1)}, /*index=5*/bf16[64,8,128]{2,1,0:T(8,128)(2,1)S(1)}, ...), branch_computations={%region_1.3_spmd, %region_2.0_spmd} | conditional | flops 277218816 | bytes 13142356 | solution.py:101
  132.6 3.6 fusion
  140.2 41.3 %all-gather.10.cloned.1.call-done = bf16[1,2048,1024]{1,2,0:T(8,128)(2,1)} async-done(((bf16[1,128,1024]{1,2,0:T(8,128)(2,1)}), bf16[1,2048,1024]{1,2,0:T(8,128)(2,1)}) %all-gather.10.cloned.1.call-update) | async-done | bytes 4194320 | tf_op jit(solution)/shard_map/all_gather | solution.py:74
  182.2 38.2 %while.40 = (s32[]{:T(128)}, f32[64,8,128]{2,0,1:T(8,128)S(1)}, f32[64,8,128]{2,0,1:T(8,128)}, s32[]{:T(128)}, s32[2048]{0:T(1024)S(1)}, /*index=5*/s32[]{:T(128...) while((s32[]{:T(128)}, f32[64,8,128]{2,0,1:T(8,128)S(1)}, ...), condition=%wide.region_15.17_spmd, body=%wide.region_10.16_spmd.sunk | while | flops 271386112 | bytes 14046374 | solution.py:157
  188.1 3.6 conditional.12
  223.7 4.6 fusion.70
  229.3 3.9 broadcast_in_dim.182
  233.3 3.9 broadcast_in_dim.182.clone
  237.2 47.7 %while.41 = (s32[]{:T(128)}, f32[64,8,128]{2,0,1:T(8,128)S(1)}, f32[64,8,128]{2,0,1:T(8,128)S(1)}, f32[2048,8,128]{2,0,1:T(8,128)}, f32[2048,8,128]{2,0,1:T(8,12...) while((s32[]{:T(128)}, f32[64,8,128]{2,0,1:T(8,128)S(1)}, ...), condition=%wide.region_23.25_spmd, body=%wide.region_18.24_spmd.sunk | while | flops 678233600 | bytes 55731728 | solution.py:218
  241.6 11.9 %conditional.14 = ((f32[64,8,128]{2,0,1:T(8,128)S(1)}, f32[2048,8,128]{2,0,1:T(8,128)}, f32[2048,8,128]{2,0,1:T(8,128)})) conditional(s32[]{:T(128)} %convert_element_type.153, (f32[64,8,128]{2,0,1:T(8,128)S(1)}, f32[2048,8,128]{2,0,1:T(8,128)}, f32[2048,8,128]{2,0,1:T(8,128)}) %tuple.153, (s32[512]{0:T(512)S(1)}, s32[64]{0:T(128)}, s32[]{:T(128)}, ...), branch_computations={%region_19.20_spmd, %region_20.21_spmd} | conditional | flops 339116544 | bytes 25765318 | solution.py:206
  254.9 12.3 %conditional.15 = ((f32[64,8,128]{2,0,1:T(8,128)S(1)}, f32[2048,8,128]{2,0,1:T(8,128)}, f32[2048,8,128]{2,0,1:T(8,128)})) conditional(s32[]{:T(128)} %convert_element_type.154, (f32[64,8,128]{2,0,1:T(8,128)S(1)}, f32[2048,8,128]{2,0,1:T(8,128)}, f32[2048,8,128]{2,0,1:T(8,128)}) %tuple.155, (s32[512]{0:T(512)S(1)}, s32[64]{0:T(128)}, s32[]{:T(128)}, ...), branch_computations={%region_21.22_spmd, %region_22.23_spmd} | conditional | flops 339116544 | bytes 25765318 | solution.py:206
  260.2 3.5 fusion.58
  284.8 7.9 %copy_bitcast_fusion.1 = f32[2048,1024]{1,0:T(8,128)} fusion(f32[2048,8,128]{2,0,1:T(8,128)} %get-tuple-element.896), kind=kLoop, calls=%fused_computation.103 | loop fusion | bytes 16777216 | tf_op jit(solution)/shard_map/reshape | solution.py:224
  292.8 7.9 %copy_bitcast_fusion = f32[2048,1024]{1,0:T(8,128)} fusion(f32[2048,8,128]{2,0,1:T(8,128)} %get-tuple-element.897), kind=kLoop, calls=%fused_computation.102 | loop fusion | bytes 16777216 | tf_op jit(solution)/shard_map/reshape | solution.py:227
  300.8 36.6 %reduce-scatter.8.cloned.1.call-done = f32[128,2048]{1,0:T(8,128)} async-done(((f32[1024,2048]{1,0:T(8,128)}), f32[128,2048]{1,0:T(8,128)}) %reduce-scatter.8.cloned.1.call-update) | async-done | bytes 1048592 | tf_op jit(solution)/shard_map/reduce_scatter | solution.py:235
  338.5 3.7 fusion.68
  342.3 140.4 %reduce-scatter.4.cloned.1.call-done = f32[128,1024]{1,0:T(8,128)} async-done(((f32[2048,1024]{1,0:T(8,128)}), f32[128,1024]{1,0:T(8,128)}) %reduce-scatter.4.cloned.1.call-update) | async-done | bytes 524304 | tf_op jit(solution)/shard_map/reduce_scatter | solution.py:223
  484.5 103.4 %reduce-scatter.6.cloned.1.call-done = f32[128,1024]{1,0:T(8,128)} async-done(((f32[2048,1024]{1,0:T(8,128)}), f32[128,1024]{1,0:T(8,128)}) %reduce-scatter.6.cloned.1.call-update) | async-done | bytes 524304 | tf_op jit(solution)/shard_map/reduce_scatter | solution.py:226
  589.7 140.9 %all-reduce.2.cloned.1.call-done = f32[128,2048]{1,0:T(8,128)} async-done(((f32[128,2048]{1,0:T(8,128)}), f32[128,2048]{1,0:T(8,128)}) %all-reduce.2.cloned.1.call-update) | async-done | bytes 1048592 | tf_op jit(solution)/shard_map/psum | solution.py:246
  (172 shorter events, 90.3 us)
Async XLA Ops:
  7.2 58.5 %copy-start = (bf16[1,128,2048]{2,1,0:T(8,128)(2,1)S(1)}, bf16[1,128,2048]{2,1,0:T(8,128)(2,1)}, u32[]{:S(2)}) copy-start(bf16[1,128,2048]{2,1,0:T(8,128)(2,1)} %param.31) | copy-start | bytes 1572868
  7.2 58.5 %all-gather.6.cloned.1.call-start = ((), (), s32[]{:S(2)}) async-start(), calls=%async_computation.3 | async-start | bytes 4718592 | tf_op jit(solution)/shard_map/all_gather | solution.py:38
  7.9 116.3 %all-gather.8.cloned.1.call-start = ((), (), s32[]{:S(2)}) async-start(), calls=%async_computation.8 | async-start | bytes 4456448 | tf_op jit(solution)/shard_map/all_gather | solution.py:73
  9.8 114.5 %copy-start.2 = (s32[1,2048]{1,0:T(1,128)S(1)}, s32[1,2048]{1,0:T(1,128)}, u32[]{:S(2)}) copy-start(s32[1,2048]{1,0:T(1,128)} %param.28) | copy-start | bytes 24580
  9.8 171.7 %all-gather.10.cloned.1.call-start = ((), (), s32[]{:S(2)}) async-start(), calls=%async_computation.9 | async-start | bytes 4456448 | tf_op jit(solution)/shard_map/all_gather | solution.py:74
  11.7 325.7 %reduce-scatter.8.cloned.1.call-start = ((), (), s32[]{:S(2)}) async-start(), calls=%async_computation.6 | async-start | bytes 9437184 | tf_op jit(solution)/shard_map/reduce_scatter | solution.py:235
  188.1 4.9 copy-start.9
  195.9 0.7 copy-start.10
  202.5 1.4 copy-start.9
  203.9 0.7 copy-start.10
  210.4 1.4 copy-start.9
  218.4 1.4 copy-start.9
  220.5 7.7 %copy-start.11 = (pred[64]{0:T(512)(128)(4,1)}, pred[64]{0:T(512)(128)(4,1)S(1)}, u32[]{:S(2)}) copy-start(pred[64]{0:T(512)(128)(4,1)S(1)} %get-tuple-element.1637) | copy-start | bytes 196
  220.5 7.7 %copy-start.12 = (s32[64]{0:T(128)}, s32[64]{0:T(128)S(1)}, u32[]{:S(2)}) copy-start(s32[64]{0:T(128)S(1)} %get-tuple-element.1638) | copy-start | bytes 772
  220.5 7.7 %copy-start.13 = (f32[8,64]{1,0:T(8,128)}, f32[8,64]{1,0:T(8,128)S(1)}, u32[]{:S(2)}) copy-start(f32[8,64]{1,0:T(8,128)S(1)} %get-tuple-element.1639) | copy-start | bytes 6148
  228.3 254.5 %reduce-scatter.4.cloned.1.call-start = ((), (), s32[]{:S(2)}) async-start(), calls=%async_computation.4 | async-start | bytes 8912896 | tf_op jit(solution)/shard_map/reduce_scatter | solution.py:223
  244.2 1.0 copy-start.3
  246.6 3.5 copy-start.4
  257.7 1.0 copy-start.5
  259.7 4.0 copy-start.6
  292.7 295.2 %reduce-scatter.6.cloned.1.call-start = ((), (), s32[]{:S(2)}) async-start(), calls=%async_computation.5 | async-start | bytes 8912896 | tf_op jit(solution)/shard_map/reduce_scatter | solution.py:226
  300.7 37.8 %copy-start.8 = (bf16[128,1024]{1,0:T(8,128)(2,1)S(1)}, bf16[128,1024]{1,0:T(8,128)(2,1)}, u32[]{:S(2)}) copy-start(bf16[128,1024]{1,0:T(8,128)(2,1)} %copy-done.7) | copy-start | bytes 786436
  300.8 429.8 %all-reduce.2.cloned.1.call-start = ((), (), s32[]{:S(2)}) async-start(), calls=%async_computation.7 | async-start | bytes 2097152 | tf_op jit(solution)/shard_map/psum | solution.py:246
  337.8 395.1 %copy-start.1 = (bf16[1,128,2048]{2,1,0:T(8,128)(2,1)S(1)}, bf16[1,128,2048]{2,1,0:T(8,128)(2,1)}, u32[]{:S(2)}) copy-start(bf16[1,128,2048]{2,1,0:T(8,128)(2,1)} %param.31) | copy-start | bytes 1572868
  (3 other events, 2.1 us)
Sparse Core Ops, SparseCore 0:
  9.7 55.9 all-gather.5
  68.5 55.6 all-gather.7
  127.1 54.3 all-gather.9
  228.4 108.9 reduce-scatter.7
  341.5 141.1 reduce-scatter.3
  486.8 101.0 reduce-scatter.5
  590.4 140.1 all-reduce.1
where the time goes:
time: 742 us; the launch traced here: 740 us
  waiting for transfers between devices  562 us (76%)
  local copies, waits for them, and re-layouts  67 us (9%)
  matrix products  42.7 us (6%)
  loops' own time  27.7 us (4%)
  other arithmetic  22.6 us (3%)
  between operations  17.7 us (2%)
    psum x1, waiting for transfers between devices, shards(): weight_grad = lax.psum(weight_grad, 'ctx')  141 us
    reduce_scatter x1, waiting for transfers between devices, shards(): lax.psum_scatter(back_result[2].reshape(history_len, width), 'ctx', scatt...  140 us
    reduce_scatter x1, waiting for transfers between devices, shards(): lax.psum_scatter(back_result[3].reshape(history_len, width), 'ctx', scatt...  103 us
    all_gather x1, waiting for transfers between devices, shards(): piece_key = lax.all_gather(own_key, 'ctx', axis=0, tiled=True)  54.8 us
    all_gather x1, waiting for transfers between devices, shards(): whole_weight = lax.all_gather(out_weight, 'fsdp', axis=0, tiled=True)  43.3 us
    all_gather x1, waiting for transfers between devices, shards(): piece_value = lax.all_gather(own_value, 'ctx', axis=0, tiled=True)  41.3 us
    reduce_scatter x1, waiting for transfers between devices, shards(): lax.psum_scatter(lax.dot_general(context_local, own_upstream, (((0,), (0,...  36.6 us
  transfers between devices with their start and end apart: 7, of which 7 were waited for; matrix products, arithmetic and copies ran while one was open for 13% of the time, Pallas kernels for 0%

commit v1 on v0

v1 whole, which is shorter than its diff:
```python
import functools
import math

import jax
import jax.numpy as jnp
from jax import lax
from jax.experimental import pallas as pl
from jax.experimental.pallas import tpu as pltpu
from jax.sharding import PartitionSpec as P

HEADS = 8
HS = 128
BLOCK = 128
TILE = 256
SPAN = 512
REACH = 128
CHIPS = 8
LEN = 2048
NEG = -1e30
SCALE = 1.0 / math.sqrt(HS)
SCALE2 = SCALE * math.log2(math.e)
F32 = jnp.float32
BF16 = jnp.bfloat16

CORE_SWAP = [(i, i ^ 1) for i in range(16)]
PAIR_SWAP = [(i, i ^ 8) for i in range(16)]
SAME_CORE = [[2 * j + c for j in range(CHIPS)] for c in range(2)]
REDUCE = [
    [(8 * h + 2 * y + c) * 8 + f for f in range(8) for y in range(4)]
    for h in range(2)
    for c in range(2)
]


def dot_nt(a, b):
    return lax.dot_general(a, b, (((1,), (1,)), ((), ())), preferred_element_type=F32)


def dot_tn(a, b):
    return lax.dot_general(a, b, (((0,), (0,)), ((), ())), preferred_element_type=F32)


def dot_nn(a, b):
    return lax.dot_general(a, b, (((1,), (0,)), ((), ())), preferred_element_type=F32)


def params():
    return pltpu.CompilerParams(vmem_limit_bytes=56 * 1024 * 1024)


def call(kernel, out_shape, smem=0, scratch=(), flops=0, inputs=()):
    specs = [
        pl.BlockSpec(memory_space=pltpu.SMEM if i < smem else pltpu.VMEM)
        for i in range(len(inputs))
    ]
    outs = jax.tree.map(lambda _: pl.BlockSpec(memory_space=pltpu.VMEM), out_shape)
    return pl.pallas_call(
        kernel,
        out_shape=out_shape,
        in_specs=specs,
        out_specs=outs,
        scratch_shapes=list(scratch),
        compiler_params=params(),
        cost_estimate=pl.CostEstimate(flops=flops, bytes_accessed=2_000_000, transcendentals=0),
    )(*inputs)


def pack_kernel(q_ref, k_ref, v_ref, out_ref):
    for a in range(HEADS):
        cols = slice(a * HS, (a + 1) * HS)
        out_ref[a, 0] = q_ref[0, :, cols]
        out_ref[a, 1] = k_ref[0, :, cols]
        out_ref[a, 2] = v_ref[0, :, cols]


def in_order(core, own_ref, other_ref, slot, dst_ref):
    for j in range(CHIPS):
        own = pl.multiple_of(2 * BLOCK * j + BLOCK * core, BLOCK)
        other = pl.multiple_of(2 * BLOCK * j + BLOCK * (1 - core), BLOCK)
        dst_ref[pl.ds(own, BLOCK)] = own_ref[j, slot]
        dst_ref[pl.ds(other, BLOCK)] = other_ref[j, slot]


def chunks_of(m):
    stop = min(SPAN * (m + 1) + REACH, LEN)
    return [(start, min(start + SPAN, stop)) for start in range(0, stop, SPAN)]


def masked_scores(k_s, q, end, m, start, stop):
    scores = dot_nt(k_s[start:stop], q)
    if stop > SPAN * m:
        at = lax.broadcasted_iota(jnp.int32, scores.shape, 0) + start
        scores = jnp.where(at < end, scores, NEG)
    return scores


def forward_kernel(core_ref, own_ref, other_ref, end_ref, valid_ref, ctx_ref, lse_ref, k_s, v_s, s_s):
    core = core_ref[0]
    in_order(core, own_ref, other_ref, 1, k_s)
    in_order(core, own_ref, other_ref, 2, v_s)
    for m in range(4):
        q = own_ref[2 * m : 2 * m + 2, 0].reshape(TILE, HS)
        end = end_ref[m]
        top = jnp.full((1, TILE), NEG, F32)
        for start, stop in chunks_of(m):
            scores = masked_scores(k_s, q, end, m, start, stop)
            s_s[start:stop] = scores
            top = jnp.maximum(top, jnp.max(scores, axis=0, keepdims=True))
        top2 = top * SCALE2
        total = jnp.zeros((1, TILE), F32)
        acc = jnp.zeros((HS, TILE), F32)
        for start, stop in chunks_of(m):
            p = jnp.exp2(s_s[start:stop] * SCALE2 - top2)
            total = total + jnp.sum(p, axis=0, keepdims=True)
            acc = acc + dot_tn(v_s[start:stop], p.astype(BF16))
        lse_ref[m] = top2 + jnp.log2(total)
        ctx = (acc * (valid_ref[m] / total)).T.astype(BF16)
        for t in range(2):
            j = 2 * m + t
            block = ctx[t * BLOCK : (t + 1) * BLOCK]
            ctx_ref[j, 0] = block
            ctx_ref[j ^ 4, 1] = block


def backward_kernel(
    core_ref, own_ref, other_ref, end_ref, lse_ref, ctx_ref, grad_ref,
    dq_ref, keep_ref, send_ref, k_s, v_s, dk_s, dv_s,
):
    core = core_ref[0]
    in_order(core, own_ref, other_ref, 1, k_s)
    in_order(core, own_ref, other_ref, 2, v_s)
    dk_s[...] = jnp.zeros(dk_s.shape, F32)
    dv_s[...] = jnp.zeros(dv_s.shape, F32)
    for m in range(4):
        rows = slice(2 * m, 2 * m + 2)
        q = own_ref[rows, 0].reshape(TILE, HS)
        do = grad_ref[rows].reshape(TILE, HS)
        ctx = ctx_ref[rows, 0].reshape(TILE, HS)
        delta = jnp.sum((do.astype(F32) * ctx.astype(F32)).T, axis=0, keepdims=True)
        end = end_ref[m]
        lse = lse_ref[m]
        dq = jnp.zeros((HS, TILE), F32)
        for start, stop in chunks_of(m):
            scores = masked_scores(k_s, q, end, m, start, stop)
            p = jnp.exp2(scores * SCALE2 - lse)
            dp = dot_nt(v_s[start:stop], do)
            ds = (p * (dp - delta) * SCALE).astype(BF16)
            dv_s[start:stop] += dot_nn(p.astype(BF16), do)
            dk_s[start:stop] += dot_nn(ds, q)
            dq = dq + dot_tn(k_s[start:stop], ds)
        dq_rows = dq.T.astype(BF16)
        dq_ref[2 * m] = dq_rows[:BLOCK]
        dq_ref[2 * m + 1] = dq_rows[BLOCK:]
    for j in range(CHIPS):
        own = pl.multiple_of(2 * BLOCK * j + BLOCK * core, BLOCK)
        other = pl.multiple_of(2 * BLOCK * j + BLOCK * (1 - core), BLOCK)
        keep_ref[j, 0] = dk_s[pl.ds(own, BLOCK)]
        keep_ref[j, 1] = dv_s[pl.ds(own, BLOCK)]
        send_ref[j, 0] = dk_s[pl.ds(other, BLOCK)].astype(BF16)
        send_ref[j, 1] = dv_s[pl.ds(other, BLOCK)].astype(BF16)


def project_kernel(core_ref, up_ref, mine_ref, other_ref, valid_ref, out_ref):
    half = mine_ref.shape[1]
    core = core_ref[0]
    up_mine = up_ref[0, :, pl.ds(pl.multiple_of(core * half, half), half)]
    up_other = up_ref[0, :, pl.ds(pl.multiple_of((1 - core) * half, half), half)]
    for a in range(HEADS):
        rows = slice(a * HS, (a + 1) * HS)
        total = dot_nt(up_mine, mine_ref[rows]) + dot_nt(up_other, other_ref[rows])
        out_ref[a] = (total * valid_ref[...]).astype(BF16)


def attend_kernel(core_ref, ctx_ref, mine_ref, other_ref, out_ref):
    half = mine_ref.shape[1]
    core = core_ref[0]
    ctx = jnp.concatenate([ctx_ref[a, 0] for a in range(HEADS)], axis=1)
    for n in range(4):
        cols = slice(n * half // 4, (n + 1) * half // 4)
        at = pl.multiple_of(core * half + n * half // 4, half // 4)
        out_ref[0, :, pl.ds(at, half // 4)] = dot_nn(ctx, mine_ref[:, cols]).astype(BF16)
        at = pl.multiple_of((1 - core) * half + n * half // 4, half // 4)
        out_ref[0, :, pl.ds(at, half // 4)] = dot_nn(ctx, other_ref[:, cols]).astype(BF16)


def weight_kernel(ctx_ref, ctx_other_ref, up_ref, up_other_ref, out_ref):
    quarter = up_ref.shape[2]
    up = up_ref[...].reshape(TILE, quarter)
    up_other = up_other_ref[...].reshape(TILE, quarter)
    for a in range(HEADS):
        total = dot_tn(ctx_ref[a].reshape(TILE, HS), up)
        total = total + dot_tn(ctx_other_ref[a].reshape(TILE, HS), up_other)
        out_ref[4 * a : 4 * a + 4] = total.reshape(4, HS // 4, quarter).astype(BF16)


def join_kernel(dq_ref, keep_ref, came_ref, terms_ref, out_ref):
    total = terms_ref[0].astype(F32)
    for s in range(1, terms_ref.shape[0]):
        total = total + terms_ref[s].astype(F32)
    weight = total.astype(BF16)
    rows = weight.shape[0]
    for j in range(CHIPS):
        out_ref[j, 0] = dq_ref[j]
        out_ref[j, 1] = (keep_ref[j, 0] + came_ref[j, 0].astype(F32)).astype(BF16)
        out_ref[j, 2] = (keep_ref[j, 1] + came_ref[j, 1].astype(F32)).astype(BF16)
        for t in range(4):
            out_ref[j, 3, t * rows : (t + 1) * rows] = weight[:, t * HS : (t + 1) * HS]


def unpack_kernel(core_ref, mine_ref, other_ref, dq_ref, dk_ref, dv_ref, dw_ref):
    core = core_ref[0]
    for a in range(HEADS):
        cols = slice(a * HS, (a + 1) * HS)
        dq_ref[0, :, cols] = mine_ref[a, 0]
        dk_ref[0, :, cols] = mine_ref[a, 1]
        dv_ref[0, :, cols] = mine_ref[a, 2]
        x, y = a // 4, a % 4
        for t in range(4):
            rows = slice(32 * y, 32 * y + 32)
            part = slice(32 * t, 32 * t + 32)
            at = pl.multiple_of(1024 * x + 512 * core + HS * t, HS)
            dw_ref[rows, pl.ds(at, HS)] = mine_ref[a, 3, part].astype(F32)
            at = pl.multiple_of(1024 * x + 512 * (1 - core) + HS * t, HS)
            dw_ref[rows, pl.ds(at, HS)] = other_ref[a, part].astype(F32)


def shape(dims, dtype):
    return jax.ShapeDtypeStruct(dims, dtype)


def exchange(operand):
    return lax.all_to_all(
        operand, "ctx", split_axis=0, concat_axis=0, tiled=True, axis_index_groups=SAME_CORE
    )


def shards(query_rows, key_rows, value_rows, session, lengths, out_weight, upstream):
    index = lax.axis_index("ctx")
    core = index % 2
    high = index // 8
    core_ref = core.reshape(1).astype(jnp.int32)
    valid_len = lengths[0]
    half = out_weight.shape[1] // 2
    quarter = half // 2

    own_half = lax.dynamic_slice_in_dim(out_weight, core * half, half, 1)
    weight_mine = lax.all_gather(own_half, "fsdp", axis=0, tiled=True)
    weight_other = lax.ppermute(weight_mine, "ctx", CORE_SWAP)

    up = upstream[0]
    up_pair = lax.ppermute(
        lax.dynamic_slice_in_dim(up, (1 - high) * half, half, 1), "ctx", PAIR_SWAP
    )
    up_both = jnp.stack([lax.dynamic_slice_in_dim(up, high * half, half, 1), up_pair])
    up_mine = lax.dynamic_slice_in_dim(up_both, core * quarter, quarter, 2)
    up_other = lax.ppermute(
        lax.dynamic_slice_in_dim(up_both, (1 - core) * quarter, quarter, 2), "ctx", CORE_SWAP
    )

    session_ids = session[0]
    positions = jnp.arange(LEN, dtype=jnp.int32).reshape(CHIPS, 2, BLOCK)
    own_sessions = lax.dynamic_index_in_dim(session_ids.reshape(CHIPS, 2, BLOCK), core, 1, False)
    own_positions = lax.dynamic_index_in_dim(positions, core, 1, False)
    end = jnp.sum(
        (session_ids[:, None] <= own_sessions.reshape(1, -1)).astype(jnp.int32), axis=0
    )
    end = jnp.minimum(end, valid_len).reshape(4, 1, TILE)
    valid = (own_positions < valid_len).astype(F32).reshape(4, 1, TILE)
    rows_here = index * BLOCK + jnp.arange(BLOCK, dtype=jnp.int32)
    valid_here = (rows_here < valid_len).astype(F32)[:, None]

    packed = call(
        pack_kernel,
        shape((HEADS, 3, BLOCK, HS), BF16),
        inputs=(query_rows, key_rows, value_rows),
    )
    own = exchange(packed)
    other = lax.ppermute(own, "ctx", CORE_SWAP)
    pairs = 4 * TILE * SPAN * 5 // 2
    context, lse = call(
        forward_kernel,
        (shape((CHIPS, 2, BLOCK, HS), BF16), shape((4, 1, TILE), F32)),
        smem=1,
        scratch=(
            pltpu.VMEM((LEN, HS), BF16),
            pltpu.VMEM((LEN, HS), BF16),
            pltpu.VMEM((LEN, TILE), F32),
        ),
        flops=4 * pairs * HS,
        inputs=(core_ref, own, other, end, valid),
    )
    context_mine = exchange(context)
    context_other = lax.ppermute(context_mine, "ctx", CORE_SWAP)
    terms = call(
        weight_kernel,
        shape((32, 32, quarter), BF16),
        flops=2 * 512 * 1024 * 512,
        inputs=(context_mine, context_other, up_mine, up_other),
    )
    terms = lax.all_to_all(
        terms, ("ctx", "fsdp"), split_axis=0, concat_axis=0, tiled=True, axis_index_groups=REDUCE
    )

    grads = call(
        project_kernel,
        shape((HEADS, BLOCK, HS), BF16),
        smem=1,
        flops=2 * 128 * 1024 * 2048,
        inputs=(core_ref, upstream, weight_mine, weight_other, valid_here),
    )
    grads = exchange(grads)
    dq, keep, send = call(
        backward_kernel,
        (
            shape((CHIPS, BLOCK, HS), BF16),
            shape((CHIPS, 2, BLOCK, HS), F32),
            shape((CHIPS, 2, BLOCK, HS), BF16),
        ),
        smem=1,
        scratch=(
            pltpu.VMEM((LEN, HS), BF16),
            pltpu.VMEM((LEN, HS), BF16),
            pltpu.VMEM((LEN, HS), F32),
            pltpu.VMEM((LEN, HS), F32),
        ),
        flops=10 * pairs * HS,
        inputs=(core_ref, own, other, end, lse, context, grads),
    )
    came = lax.ppermute(send, "ctx", CORE_SWAP)
    attended = call(
        attend_kernel,
        shape((1, BLOCK, 2 * half), BF16),
        smem=1,
        flops=2 * 128 * 1024 * 2048,
        inputs=(core_ref, context_mine, weight_mine, weight_other),
    )
    joined = call(
        join_kernel,
        shape((CHIPS, 4, BLOCK, HS), BF16),
        inputs=(dq, keep, came, terms),
    )
    result = exchange(joined)
    weight_part = lax.ppermute(result[:, 3], "ctx", CORE_SWAP)
    query_grad, key_grad, value_grad, weight_grad = call(
        unpack_kernel,
        (
            shape((1, BLOCK, HEADS * HS), BF16),
            shape((1, BLOCK, HEADS * HS), BF16),
            shape((1, BLOCK, HEADS * HS), BF16),
            shape((HS, 2 * half), F32),
        ),
        smem=1,
        inputs=(core_ref, result, weight_part),
    )
    return (attended, query_grad, key_grad, value_grad, weight_grad)


def solution(mesh):
    rows = P("fsdp", "ctx", None)
    return jax.shard_map(
        shards,
        mesh=mesh,
        in_specs=(rows, rows, rows, P("fsdp", None), P("fsdp"), P("fsdp", None), rows),
        out_specs=(rows, rows, rows, rows, P("fsdp", None)),
        check_vma=False,
    )
```

time: 742 us -> 173 us (0.23)
  waiting for transfers between devices: 562 us -> 56.1 us
  local copies, waits for them, and re-layouts: 67 us -> 7.33 us
  matrix products: 42.7 us -> 0 us
  starting transfers between devices: 0.47 us -> 37.7 us
  Pallas kernels: 0 us -> 31.2 us
  loops' own time: 27.7 us -> 0 us
  blocking collectives: 0 us -> 20.5 us
  other arithmetic: 22.6 us -> 4.61 us
    reduce_scatter x3 -> x0, waiting for transfers between devices: 280 us -> none  [the longest x1 140 us: shards(): lax.psum_scatter(back_result[2].reshape(history_len, width), 'ctx', scatt...]
    psum x1 -> x0, waiting for transfers between devices: 141 us -> none  [shards(): weight_grad = lax.psum(weight_grad, 'ctx')]
    all_gather x3 -> x1, waiting for transfers between devices: 139 us -> 36.2 us  [shards(): weight_mine = lax.all_gather(own_half, 'fsdp', axis=0, tiled=True)]
    dot_general x17 -> x0, matrix products: 42.7 us -> none  [the longest x2 7.15 us: update(): jnp.einsum('qhd,khd->hqk', query_heads[absorb_portion], key_heads, prefer...]
    pallas_call x0 -> x8, Pallas kernels: none -> 31.2 us  [call(): pl.pallas_call(kernel, out_shape=out_shape, in_specs=specs, out_specs=out...]
    another operation x20 -> x0, loops' own time: 27.7 us -> none  [the longest x1 13.7 us: shards(): back_result = lax.fori_loop(0, block_count, backward_step, backward_init)]
    all_to_all x0 -> x4, starting transfers between devices: none -> 21.9 us  [the longest x3 17.2 us: exchange(): lax.all_to_all(operand, 'ctx', split_axis=0, concat_axis=0, tiled=True, a...]
    reshape x6 -> x0, local copies, waits for them, and re-layouts: 21.7 us -> none  [the longest x1 7.93 us: shards(): back_result[3].reshape(history_len, width)]
  transfers between devices with their start and end apart: 7 -> 12, of which waited for: 7 -> 6; matrix products, arithmetic and copies ran while one was open for 13% -> 4% of each run, Pallas kernels for 0% -> 15%
where the time goes in v1:
time: 173 us; the launch traced here: 172 us
  waiting for transfers between devices  56.1 us (32%)
  starting transfers between devices  37.7 us (22%)
  Pallas kernels  31.2 us (18%)
  blocking collectives  20.5 us (12%)
  between operations  14.8 us (9%)
  local copies, waits for them, and re-layouts  7.33 us (4%)
  other arithmetic  4.61 us (3%)
    all_gather x1, waiting for transfers between devices, shards(): weight_mine = lax.all_gather(own_half, 'fsdp', axis=0, tiled=True)  36.2 us
    pallas_call x8, Pallas kernels, call(): pl.pallas_call(kernel, out_shape=out_shape, in_specs=specs, out_specs=out...  31.2 us
    all_to_all x1, blocking collectives, exchange(): lax.all_to_all(operand, 'ctx', split_axis=0, concat_axis=0, tiled=True, a...  20.5 us
    all_to_all x3, starting transfers between devices, exchange(): lax.all_to_all(operand, 'ctx', split_axis=0, concat_axis=0, tiled=True, a...  17.2 us
    all_to_all x3, waiting for transfers between devices, exchange(): lax.all_to_all(operand, 'ctx', split_axis=0, concat_axis=0, tiled=True, a...  8.94 us
    all_to_all x1, waiting for transfers between devices, shards(): lax.all_to_all(terms, ('ctx', 'fsdp'), split_axis=0, concat_axis=0, tiled...  6.13 us
    unnamed x22, local copies, waits for them, and re-layouts  4.82 us
    all_to_all x1, starting transfers between devices, shards(): lax.all_to_all(terms, ('ctx', 'fsdp'), split_axis=0, concat_axis=0, tiled...  4.64 us
  transfers between devices with their start and end apart: 12, of which 6 were waited for; matrix products, arithmetic and copies ran while one was open for 4% of the time, Pallas kernels for 15%

profile of v1, /device:TPU:1, one launch (start us, length us, event | category | flops | bytes accessed | tf_op | source)
XLA Modules:
  0.0 172.2 jit_solution(9155385014637996171)
XLA Ops:
  9.0 2.1 %shard_map.110 = bf16[8,3,128,128]{3,2,1,0:T(8,128)(2,1)} custom-call(bf16[1,128,1024]{2,1,0:T(8,128)(2,1)} %q_ref.1, bf16[1,128,1024]{2,1,0:T(8,128)(2,1)} %k_ref.1, bf16[1,128,1024]{2,1,0:T(8,128)(2,1)} %v_ref.1), custom_call_target="tpu_custom_call" | custom-call | bytes 2000000 | tf_op jit(solution)/shard_map/pallas_call | solution.py:57
  11.1 7.5 %all-to-all-start = ((bf16[8,3,128,128]{3,2,1,0:T(8,128)(2,1)}), bf16[8,3,128,128]{3,2,1,0:T(8,128)(2,1)S(1)}, u32[]{:S(2)}, u32[]{:S(2)}) async-start(bf16[8,3,128,128]{3,2,1,0:T(8,128)(2,1)} %shard_map.110), calls=%async_computation | async-start | bytes 1572864 | tf_op jit(solution)/shard_map/all_to_all | solution.py:232
  18.6 36.2 %all-gather.2.cloned.1.call-done.mine_ref = bf16[1024,1024]{1,0:T(8,128)(2,1)} async-done(((bf16[128,1024]{1,0:T(8,128)(2,1)}), bf16[1024,1024]{1,0:T(8,128)(2,1)}) %all-gather.2.cloned.1.call-update) | async-done | bytes 2097168 | tf_op jit(solution)/shard_map/all_gather | solution.py:247
  54.7 3.9 %collective-permute-start.1 = (bf16[1024,1024]{1,0:T(8,128)(2,1)}, bf16[1024,1024]{1,0:T(8,128)(2,1)S(1)}, u32[]{:S(2)}, u32[]{:S(2)}) collective-permute-start(bf16[1024,1024]{1,0:T(8,128)(2,1)} %all-gather.2.cloned.1.call-done.mine_ref), channel_id=1, source_target_pairs={{0,8},{8,0},{16,24},{24,16},{32,40},{40,32},{48,56},{56,48},{64,72... | collective-permute-start | bytes 6291464 | tf_op jit(solution)/shard_map/ppermute | solution.py:248
  61.7 1.9 %collective-permute-done.other_ref = bf16[8,3,128,128]{3,2,1,0:T(8,128)(2,1)} collective-permute-done((bf16[8,3,128,128]{3,2,1,0:T(8,128)(2,1)S(1)}, bf16[8,3,128,128]{3,2,1,0:T(8,128)(2,1)}, u32[]{:S(2)}, u32[]{:S(2)}) %collective-permute-start) | collective-permute-done | bytes 786464 | tf_op jit(solution)/shard_map/ppermute | solution.py:278
  63.6 5.0 %shard_map.111 = (bf16[8,2,128,128]{3,2,1,0:T(8,128)(2,1)}, f32[4,1,256]{2,1,0:T(1,128)}) custom-call(s32[1]{0:T(128)} %bitcast.core_ref, bf16[8,3,128,128]{3,2,1,0:T(8,128)(2,1)} %copy-done.5, bf16[8,3,128,128]{3,2,1,0:T(8,128)(2,1)} %collective-permute-done.other_ref, s32[4,1,256]{2,1,0:T(1,128)} %bitcast.18, f32[4,1,256]{2,1,0:T(1,128)} %bitcast.17), custom_call_target="tpu_custom_call" | custom-call | flops 671088640 | bytes 2000000 | tf_op jit(solution)/shard_map/pallas_call | solution.py:57
  68.6 5.8 %all-to-all-start.1 = ((bf16[8,2,128,128]{3,2,1,0:T(8,128)(2,1)}), bf16[8,2,128,128]{3,2,1,0:T(8,128)(2,1)S(1)}, u32[]{:S(2)}, u32[]{:S(2)}) async-start(bf16[8,2,128,128]{3,2,1,0:T(8,128)(2,1)} %get-tuple-element.14.ctx_ref), calls=%async_computation.1 | async-start | bytes 1048576 | tf_op jit(solution)/shard_map/all_to_all | solution.py:232
  76.2 3.0 %collective-permute-start.4 = (bf16[128,1024]{1,0:T(8,128)(2,1)}, bf16[128,1024]{1,0:T(8,128)(2,1)}, u32[]{:S(2)}, u32[]{:S(2)}) collective-permute-start(bf16[128,1024]{1,0:T(8,128)(2,1)} %get-tuple-element.25), channel_id=1, source_target_pairs={{0,64},{8,72},{16,80},{24,88},{32,96},{40,104},{48,112},{56,120},{... | collective-permute-start | bytes 786440 | tf_op jit(solution)/shard_map/ppermute | solution.py:251
  79.1 5.1 %all-to-all-done.1.ctx_ref = bf16[8,2,128,128]{3,2,1,0:T(8,128)(2,1)S(1)} async-done(((bf16[8,2,128,128]{3,2,1,0:T(8,128)(2,1)}), bf16[8,2,128,128]{3,2,1,0:T(8,128)(2,1)S(1)}, u32[]{:S(2)}, u32[]{:S(2)}) %all-to-all-start.1) | async-done | bytes 524320 | tf_op jit(solution)/shard_map/all_to_all | solution.py:232
  84.3 2.2 %collective-permute-start.3 = (bf16[8,2,128,128]{3,2,1,0:T(8,128)(2,1)S(1)}, bf16[8,2,128,128]{3,2,1,0:T(8,128)(2,1)}, u32[]{:S(2)}, u32[]{:S(2)}) collective-permute-start(bf16[8,2,128,128]{3,2,1,0:T(8,128)(2,1)S(1)} %all-to-all-done.1.ctx_ref), channel_id=1, source_target_pairs={{0,8},{8,0},{16,24},{24,16},{32,40},{40,32},{48,56},{56,48},{64,72... | collective-permute-start | bytes 1572872 | tf_op jit(solution)/shard_map/ppermute | solution.py:293
  86.4 2.9 %collective-permute-done.4 = bf16[128,1024]{1,0:T(8,128)(2,1)} collective-permute-done((bf16[128,1024]{1,0:T(8,128)(2,1)}, bf16[128,1024]{1,0:T(8,128)(2,1)}, u32[]{:S(2)}, u32[]{:S(2)}) %collective-permute-start.4) | collective-permute-done | bytes 262176 | tf_op jit(solution)/shard_map/ppermute | solution.py:251
  89.3 1.8 %fusion = (bf16[2,128,512]{2,1,0:T(8,128)(2,1)}, bf16[2,128,512]{2,1,0:T(8,128)(2,1)}) fusion(s32[]{:T(128)S(6)} %select_n.38, bf16[1,128,1024]{2,1,0:T(8,128)(2,1)S(1)} %get-tuple-element.26, bf16[1,128,1024]{2,1,0:T(8,128)(2,1)} %bitcast.8, s32[]{:T(128)S(6)} %select_n.37), kind=kLoop, calls=%fused_computation.5 | loop fusion | flops 1048576 | bytes 1048584 | tf_op jit(solution)/shard_map/stack | solution.py:254
  94.3 4.3 %shard_map.113 = bf16[8,128,128]{2,1,0:T(8,128)(2,1)} custom-call(s32[1]{0:T(128)} %bitcast.core_ref, bf16[1,128,2048]{2,1,0:T(8,128)(2,1)} %up_ref.1, bf16[1024,1024]{1,0:T(8,128)(2,1)} %all-gather.2.cloned.1.call-done.mine_ref, bf16[1024,1024]{1,0:T(8,128)(2,1)} %copy-done.1, f32[128,1]{1,0:T(8,128)} %fusion.2.valid_ref), custom_call_target="tpu_custom_call" | custom-call | flops 536870912 | bytes 2000000 | tf_op jit(solution)/shard_map/pallas_call | solution.py:57
  98.6 4.0 %all-to-all-start.2 = ((bf16[8,128,128]{2,1,0:T(8,128)(2,1)}), bf16[8,128,128]{2,1,0:T(8,128)(2,1)S(1)}, u32[]{:S(2)}, u32[]{:S(2)}) async-start(bf16[8,128,128]{2,1,0:T(8,128)(2,1)} %shard_map.113), calls=%async_computation.2 | async-start | bytes 524288 | tf_op jit(solution)/shard_map/all_to_all | solution.py:232
  103.3 3.1 %shard_map.115 = bf16[32,32,512]{2,1,0:T(8,128)(2,1)} custom-call(bf16[8,2,128,128]{3,2,1,0:T(8,128)(2,1)} %copy-done.3, bf16[8,2,128,128]{3,2,1,0:T(8,128)(2,1)} %collective-permute-done.3.ctx_other_ref, bf16[2,128,512]{2,1,0:T(8,128)(2,1)} %get-tuple-element.24.up_ref, bf16[2,128,512]{2,1,0:T(8,128)(2,1)} %copy-done.7), custom_call_target="tpu_custom_call" | custom-call | flops 536870912 | bytes 2000000 | tf_op jit(solution)/shard_map/pallas_call | solution.py:57
  106.4 3.8 %all-to-all-done.2.grad_ref = bf16[8,128,128]{2,1,0:T(8,128)(2,1)S(1)} async-done(((bf16[8,128,128]{2,1,0:T(8,128)(2,1)}), bf16[8,128,128]{2,1,0:T(8,128)(2,1)S(1)}, u32[]{:S(2)}, u32[]{:S(2)}) %all-to-all-start.2) | async-done | bytes 262176 | tf_op jit(solution)/shard_map/all_to_all | solution.py:232
  110.2 4.6 %all-to-all-start.3 = ((bf16[32,32,512]{2,1,0:T(8,128)(2,1)}), bf16[32,32,512]{2,1,0:T(8,128)(2,1)S(1)}, u32[]{:S(2)}, u32[]{:S(2)}) async-start(bf16[32,32,512]{2,1,0:T(8,128)(2,1)} %shard_map.115), calls=%async_computation.3 | async-start | bytes 2097152 | tf_op jit(solution)/shard_map/all_to_all | solution.py:300
  114.9 6.9 %shard_map.114 = (bf16[8,128,128]{2,1,0:T(8,128)(2,1)}, f32[8,2,128,128]{3,2,1,0:T(8,128)}, bf16[8,2,128,128]{3,2,1,0:T(8,128)(2,1)}) custom-call(s32[1]{0:T(128)} %bitcast.core_ref, bf16[8,3,128,128]{3,2,1,0:T(8,128)(2,1)} %copy-done.5, bf16[8,3,128,128]{3,2,1,0:T(8,128)(2,1)} %collective-permute-done.other_ref, s32[4,1,256]{2,1,0:T(1,128)} %bitcast.19, ...), custom_call_target="tpu_custom_call" | custom-call | flops 1677721600 | bytes 2000000 | tf_op jit(solution)/shard_map/pallas_call | solution.py:57
  123.2 6.1 %all-to-all-done.3.terms_ref = bf16[32,32,512]{2,1,0:T(8,128)(2,1)S(1)} async-done(((bf16[32,32,512]{2,1,0:T(8,128)(2,1)}), bf16[32,32,512]{2,1,0:T(8,128)(2,1)S(1)}, u32[]{:S(2)}, u32[]{:S(2)}) %all-to-all-start.3) | async-done | bytes 1048608 | tf_op jit(solution)/shard_map/all_to_all | solution.py:300
  130.4 3.0 %shard_map.116 = bf16[8,4,128,128]{3,2,1,0:T(8,128)(2,1)} custom-call(bf16[8,128,128]{2,1,0:T(8,128)(2,1)} %get-tuple-element.16.dq_ref, f32[8,2,128,128]{3,2,1,0:T(8,128)} %get-tuple-element.17.keep_ref, bf16[8,2,128,128]{3,2,1,0:T(8,128)(2,1)} %copy-done.6, bf16[32,32,512]{2,1,0:T(8,128)(2,1)} %copy-done.4), custom_call_target="tpu_custom_call" | custom-call | bytes 2000000 | tf_op jit(solution)/shard_map/pallas_call | solution.py:57
  133.5 20.5 %all_to_all.25.mine_ref = bf16[8,4,128,128]{3,2,1,0:T(8,128)(2,1)S(1)} all-to-all(bf16[8,4,128,128]{3,2,1,0:T(8,128)(2,1)} %shard_map.116), channel_id=1, replica_groups={{0,16,32,48,64,80,96,112},{8,24,40,56,72,88,104,120},{1,17,33,49,65,81,..., dimensions={0} | all-to-all | bytes 2097152 | tf_op jit(solution)/shard_map/all_to_all | solution.py:232
  154.0 4.0 %collective-permute-start.6 = (bf16[8,128,128]{2,1,0:T(8,128)(2,1)S(1)}, bf16[8,128,128]{2,1,0:T(8,128)(2,1)S(1)}, u32[]{:S(2)}, u32[]{:S(2)}) collective-permute-start(bf16[8,128,128]{2,1,0:T(8,128)(2,1)S(1)} %slice_bitcast_fusion), channel_id=1, source_target_pairs={{0,8},{8,0},{16,24},{24,16},{32,40},{40,32},{48,56},{56,48},{64,72... | collective-permute-start | bytes 786440 | tf_op jit(solution)/shard_map/ppermute | solution.py:343
  158.0 3.9 %shard_map.112 = bf16[1,128,2048]{2,1,0:T(8,128)(2,1)} custom-call(s32[1]{0:T(128)} %bitcast.core_ref, bf16[8,2,128,128]{3,2,1,0:T(8,128)(2,1)} %copy-done.3, bf16[1024,1024]{1,0:T(8,128)(2,1)} %all-gather.2.cloned.1.call-done.mine_ref, bf16[1024,1024]{1,0:T(8,128)(2,1)} %copy-done.1), custom_call_target="tpu_custom_call" | custom-call | flops 536870912 | bytes 2000000 | tf_op jit(solution)/shard_map/pallas_call | solution.py:57
  162.6 2.8 %shard_map.117 = (bf16[1,128,1024]{2,1,0:T(8,128)(2,1)}, bf16[1,128,1024]{2,1,0:T(8,128)(2,1)}, bf16[1,128,1024]{2,1,0:T(8,128)(2,1)}, f32[128,2048]{1,0:T(8,128)}) custom-call(s32[1]{0:T(128)} %bitcast.core_ref, bf16[8,4,128,128]{3,2,1,0:T(8,128)(2,1)} %copy-done.2, bf16[8,128,128]{2,1,0:T(8,128)(2,1)} %copy-done.8), custom_call_target="tpu_custom_call" | custom-call | bytes 2000000 | tf_op jit(solution)/shard_map/pallas_call | solution.py:57
  (41 shorter events, 12.9 us)
Async XLA Ops:
  7.2 1.0 copy-start
  7.2 52.3 %copy-start.10 = (s32[1,2048]{1,0:T(1,128)S(1)}, s32[1,2048]{1,0:T(1,128)}, u32[]{:S(2)}) copy-start(s32[1,2048]{1,0:T(1,128)} %param.10) | copy-start | bytes 24580
  7.2 47.5 %all-gather.2.cloned.1.call-start = ((), (), s32[]{:S(2)}) async-start(), calls=%async_computation.5 | async-start | bytes 2359296 | tf_op jit(solution)/shard_map/all_gather | solution.py:247
  11.1 47.6 %all-to-all-start = ((bf16[8,3,128,128]{3,2,1,0:T(8,128)(2,1)}), bf16[8,3,128,128]{3,2,1,0:T(8,128)(2,1)S(1)}, u32[]{:S(2)}, u32[]{:S(2)}) async-start(bf16[8,3,128,128]{3,2,1,0:T(8,128)(2,1)} %shard_map.110), calls=%async_computation | async-start | bytes 1572864 | tf_op jit(solution)/shard_map/all_to_all | solution.py:232
  54.7 38.3 %collective-permute-start.1 = (bf16[1024,1024]{1,0:T(8,128)(2,1)}, bf16[1024,1024]{1,0:T(8,128)(2,1)S(1)}, u32[]{:S(2)}, u32[]{:S(2)}) collective-permute-start(bf16[1024,1024]{1,0:T(8,128)(2,1)} %all-gather.2.cloned.1.call-done.mine_ref), channel_id=1, source_target_pairs={{0,8},{8,0},{16,24},{24,16},{32,40},{40,32},{48,56},{56,48},{64,72... | collective-permute-start | bytes 6291464 | tf_op jit(solution)/shard_map/ppermute | solution.py:248
  58.7 4.9 %copy-start.5 = (bf16[8,3,128,128]{3,2,1,0:T(8,128)(2,1)}, bf16[8,3,128,128]{3,2,1,0:T(8,128)(2,1)S(1)}, u32[]{:S(2)}) copy-start(bf16[8,3,128,128]{3,2,1,0:T(8,128)(2,1)S(1)} %all-to-all-done.own_ref) | copy-start | bytes 2359300
  58.7 4.9 %collective-permute-start = (bf16[8,3,128,128]{3,2,1,0:T(8,128)(2,1)S(1)}, bf16[8,3,128,128]{3,2,1,0:T(8,128)(2,1)}, u32[]{:S(2)}, u32[]{:S(2)}) collective-permute-start(bf16[8,3,128,128]{3,2,1,0:T(8,128)(2,1)S(1)} %all-to-all-done.own_ref), channel_id=1, source_target_pairs={{0,8},{8,0},{16,24},{24,16},{32,40},{40,32},{48,56},{56,48},{64,72... | collective-permute-start | bytes 2359304 | tf_op jit(solution)/shard_map/ppermute | solution.py:278
  68.6 15.6 %all-to-all-start.1 = ((bf16[8,2,128,128]{3,2,1,0:T(8,128)(2,1)}), bf16[8,2,128,128]{3,2,1,0:T(8,128)(2,1)S(1)}, u32[]{:S(2)}, u32[]{:S(2)}) async-start(bf16[8,2,128,128]{3,2,1,0:T(8,128)(2,1)} %get-tuple-element.14.ctx_ref), calls=%async_computation.1 | async-start | bytes 1048576 | tf_op jit(solution)/shard_map/all_to_all | solution.py:232
  76.2 13.1 %collective-permute-start.4 = (bf16[128,1024]{1,0:T(8,128)(2,1)}, bf16[128,1024]{1,0:T(8,128)(2,1)}, u32[]{:S(2)}, u32[]{:S(2)}) collective-permute-start(bf16[128,1024]{1,0:T(8,128)(2,1)} %get-tuple-element.25), channel_id=1, source_target_pairs={{0,64},{8,72},{16,80},{24,88},{32,96},{40,104},{48,112},{56,120},{... | collective-permute-start | bytes 786440 | tf_op jit(solution)/shard_map/ppermute | solution.py:251
  84.3 14.4 %copy-start.3 = (bf16[8,2,128,128]{3,2,1,0:T(8,128)(2,1)}, bf16[8,2,128,128]{3,2,1,0:T(8,128)(2,1)S(1)}, u32[]{:S(2)}) copy-start(bf16[8,2,128,128]{3,2,1,0:T(8,128)(2,1)S(1)} %all-to-all-done.1.ctx_ref) | copy-start | bytes 1572868
  84.3 18.4 %collective-permute-start.3 = (bf16[8,2,128,128]{3,2,1,0:T(8,128)(2,1)S(1)}, bf16[8,2,128,128]{3,2,1,0:T(8,128)(2,1)}, u32[]{:S(2)}, u32[]{:S(2)}) collective-permute-start(bf16[8,2,128,128]{3,2,1,0:T(8,128)(2,1)S(1)} %all-to-all-done.1.ctx_ref), channel_id=1, source_target_pairs={{0,8},{8,0},{16,24},{24,16},{32,40},{40,32},{48,56},{56,48},{64,72... | collective-permute-start | bytes 1572872 | tf_op jit(solution)/shard_map/ppermute | solution.py:293
  91.1 11.5 %collective-permute-start.5 = (bf16[2,128,512]{2,1,0:T(8,128)(2,1)}, bf16[2,128,512]{2,1,0:T(8,128)(2,1)S(1)}, u32[]{:S(2)}, u32[]{:S(2)}) collective-permute-start(bf16[2,128,512]{2,1,0:T(8,128)(2,1)} %get-tuple-element.23), channel_id=1, source_target_pairs={{0,8},{8,0},{16,24},{24,16},{32,40},{40,32},{48,56},{56,48},{64,72... | collective-permute-start | bytes 786440 | tf_op jit(solution)/shard_map/ppermute | solution.py:256
  93.0 1.3 copy-start.1
  98.6 11.6 %all-to-all-start.2 = ((bf16[8,128,128]{2,1,0:T(8,128)(2,1)}), bf16[8,128,128]{2,1,0:T(8,128)(2,1)S(1)}, u32[]{:S(2)}, u32[]{:S(2)}) async-start(bf16[8,128,128]{2,1,0:T(8,128)(2,1)} %shard_map.113), calls=%async_computation.2 | async-start | bytes 524288 | tf_op jit(solution)/shard_map/all_to_all | solution.py:232
  102.6 0.7 copy-start.7
  110.2 4.7 %copy-start.9 = (bf16[8,128,128]{2,1,0:T(8,128)(2,1)}, bf16[8,128,128]{2,1,0:T(8,128)(2,1)S(1)}, u32[]{:S(2)}) copy-start(bf16[8,128,128]{2,1,0:T(8,128)(2,1)S(1)} %all-to-all-done.2.grad_ref) | copy-start | bytes 786436
  110.2 19.0 %all-to-all-start.3 = ((bf16[32,32,512]{2,1,0:T(8,128)(2,1)}), bf16[32,32,512]{2,1,0:T(8,128)(2,1)S(1)}, u32[]{:S(2)}, u32[]{:S(2)}) async-start(bf16[32,32,512]{2,1,0:T(8,128)(2,1)} %shard_map.115), calls=%async_computation.3 | async-start | bytes 2097152 | tf_op jit(solution)/shard_map/all_to_all | solution.py:300
  121.8 7.5 %collective-permute-start.2 = (bf16[8,2,128,128]{3,2,1,0:T(8,128)(2,1)}, bf16[8,2,128,128]{3,2,1,0:T(8,128)(2,1)S(1)}, u32[]{:S(2)}, u32[]{:S(2)}) collective-permute-start(bf16[8,2,128,128]{3,2,1,0:T(8,128)(2,1)} %get-tuple-element.18), channel_id=1, source_target_pairs={{0,8},{8,0},{16,24},{24,16},{32,40},{40,32},{48,56},{56,48},{64,72... | collective-permute-start | bytes 1572872 | tf_op jit(solution)/shard_map/ppermute | solution.py:329
  129.3 1.0 copy-start.4
  129.3 1.1 copy-start.6
  154.0 7.9 %copy-start.2 = (bf16[8,4,128,128]{3,2,1,0:T(8,128)(2,1)}, bf16[8,4,128,128]{3,2,1,0:T(8,128)(2,1)S(1)}, u32[]{:S(2)}) copy-start(bf16[8,4,128,128]{3,2,1,0:T(8,128)(2,1)S(1)} %all_to_all.25.mine_ref) | copy-start | bytes 3145732
  154.0 7.9 %collective-permute-start.6 = (bf16[8,128,128]{2,1,0:T(8,128)(2,1)S(1)}, bf16[8,128,128]{2,1,0:T(8,128)(2,1)S(1)}, u32[]{:S(2)}, u32[]{:S(2)}) collective-permute-start(bf16[8,128,128]{2,1,0:T(8,128)(2,1)S(1)} %slice_bitcast_fusion), channel_id=1, source_target_pairs={{0,8},{8,0},{16,24},{24,16},{32,40},{40,32},{48,56},{56,48},{64,72... | collective-permute-start | bytes 786440 | tf_op jit(solution)/shard_map/ppermute | solution.py:343
  161.9 0.7 copy-start.8
Sparse Core Ops, SparseCore 0:
  10.2 44.4 all-gather.1

commit v2 on v1

--- a/solution.py
+++ b/solution.py
@@ -24,6 +24,7 @@
 
 CORE_SWAP = [(i, i ^ 1) for i in range(16)]
 PAIR_SWAP = [(i, i ^ 8) for i in range(16)]
+DIAG_SWAP = [(i, i ^ 9) for i in range(16)]
 SAME_CORE = [[2 * j + c for j in range(CHIPS)] for c in range(2)]
 REDUCE = [
     [(8 * h + 2 * y + c) * 8 + f for f in range(8) for y in range(4)]
@@ -45,7 +46,7 @@
 
 
 def params():
-    return pltpu.CompilerParams(vmem_limit_bytes=56 * 1024 * 1024)
+    return pltpu.CompilerParams(vmem_limit_bytes=14 * 1024 * 1024)
 
 
 def call(kernel, out_shape, smem=0, scratch=(), flops=0, inputs=()):
@@ -65,12 +66,27 @@
     )(*inputs)
 
 
-def pack_kernel(q_ref, k_ref, v_ref, out_ref):
+def pack_kernel(
+    core_ref, high_ref, q_ref, k_ref, v_ref, w_ref, up_ref,
+    out_ref, half_ref, keep_ref, core_out_ref, pair_ref, diag_ref,
+):
+    core, high = core_ref[0], high_ref[0]
     for a in range(HEADS):
         cols = slice(a * HS, (a + 1) * HS)
         out_ref[a, 0] = q_ref[0, :, cols]
         out_ref[a, 1] = k_ref[0, :, cols]
         out_ref[a, 2] = v_ref[0, :, cols]
+    half = half_ref.shape[1]
+    quarter = half // 2
+    half_ref[...] = w_ref[:, pl.ds(pl.multiple_of(core * half, half), half)]
+    for ref, x, c in (
+        (keep_ref, high, core),
+        (core_out_ref, high, 1 - core),
+        (pair_ref, 1 - high, core),
+        (diag_ref, 1 - high, 1 - core),
+    ):
+        at = pl.multiple_of(x * half + c * quarter, quarter)
+        ref[...] = up_ref[0, :, pl.ds(at, quarter)]
 
 
 def in_order(core, own_ref, other_ref, slot, dst_ref):
@@ -160,33 +176,39 @@
         send_ref[j, 1] = dv_s[pl.ds(other, BLOCK)].astype(BF16)
 
 
-def project_kernel(core_ref, up_ref, mine_ref, other_ref, valid_ref, out_ref):
-    half = mine_ref.shape[1]
-    core = core_ref[0]
+def project_kernel(core_ref, row_ref, up_ref, own_ref, valid_ref, *refs):
+    mine, other, out_ref = refs[:7], refs[7:14], refs[14]
+    half = mine[0].shape[1]
+    core, row = core_ref[0], row_ref[0]
+    valid = valid_ref[...]
+    out_ref[row] = (dot_nt(up_ref[0], own_ref[...]) * valid).astype(BF16)
     up_mine = up_ref[0, :, pl.ds(pl.multiple_of(core * half, half), half)]
     up_other = up_ref[0, :, pl.ds(pl.multiple_of((1 - core) * half, half), half)]
-    for a in range(HEADS):
-        rows = slice(a * HS, (a + 1) * HS)
-        total = dot_nt(up_mine, mine_ref[rows]) + dot_nt(up_other, other_ref[rows])
-        out_ref[a] = (total * valid_ref[...]).astype(BF16)
-
-
-def attend_kernel(core_ref, ctx_ref, mine_ref, other_ref, out_ref):
-    half = mine_ref.shape[1]
-    core = core_ref[0]
-    ctx = jnp.concatenate([ctx_ref[a, 0] for a in range(HEADS)], axis=1)
-    for n in range(4):
-        cols = slice(n * half // 4, (n + 1) * half // 4)
-        at = pl.multiple_of(core * half + n * half // 4, half // 4)
-        out_ref[0, :, pl.ds(at, half // 4)] = dot_nn(ctx, mine_ref[:, cols]).astype(BF16)
-        at = pl.multiple_of((1 - core) * half + n * half // 4, half // 4)
-        out_ref[0, :, pl.ds(at, half // 4)] = dot_nn(ctx, other_ref[:, cols]).astype(BF16)
-
-
-def weight_kernel(ctx_ref, ctx_other_ref, up_ref, up_other_ref, out_ref):
-    quarter = up_ref.shape[2]
-    up = up_ref[...].reshape(TILE, quarter)
-    up_other = up_other_ref[...].reshape(TILE, quarter)
+    for s in range(1, HEADS):
+        total = dot_nt(up_mine, mine[s - 1][...]) + dot_nt(up_other, other[s - 1][...])
+        out_ref[jnp.bitwise_xor(row, s)] = (total * valid).astype(BF16)
+
+
+def attend_kernel(core_ref, row_ref, ctx_ref, own_ref, *refs):
+    mine, other, out_ref = refs[:7], refs[7:14], refs[14]
+    half = mine[0].shape[1]
+    core, row = core_ref[0], row_ref[0]
+    ctx = jnp.concatenate([ctx_ref[jnp.bitwise_xor(row, s), 0] for s in range(HEADS)], axis=1)
+    step = half // 4
+    for side, parts in ((core, mine), (1 - core, other)):
+        for n in range(4):
+            at = pl.multiple_of(side * half + n * step, step)
+            cols = slice(n * step, (n + 1) * step)
+            weight = jnp.concatenate(
+                [own_ref[:, pl.ds(at, step)]] + [part[:, cols] for part in parts], axis=0
+            )
+            out_ref[0, :, pl.ds(at, step)] = dot_nn(ctx, weight).astype(BF16)
+
+
+def weight_kernel(ctx_ref, ctx_other_ref, keep_ref, pair_ref, core_ref, diag_ref, out_ref):
+    quarter = keep_ref.shape[1]
+    up = jnp.concatenate([keep_ref[...], pair_ref[...]], axis=0)
+    up_other = jnp.concatenate([core_ref[...], diag_ref[...]], axis=0)
     for a in range(HEADS):
         total = dot_tn(ctx_ref[a].reshape(TILE, HS), up)
         total = total + dot_tn(ctx_other_ref[a].reshape(TILE, HS), up_other)
@@ -234,28 +256,38 @@
     )
 
 
+def after(value, *others):
+    return lax.optimization_barrier((value, *others))[0]
+
+
 def shards(query_rows, key_rows, value_rows, session, lengths, out_weight, upstream):
-    index = lax.axis_index("ctx")
-    core = index % 2
-    high = index // 8
-    core_ref = core.reshape(1).astype(jnp.int32)
+    index = lax.axis_index("ctx").astype(jnp.int32)
+    core = index & 1
+    core_ref = core.reshape(1)
+    high_ref = (index >> 3).reshape(1)
+    row_ref = lax.axis_index("fsdp").astype(jnp.int32).reshape(1)
     valid_len = lengths[0]
-    half = out_weight.shape[1] // 2
+    width = out_weight.shape[1]
+    half = width // 2
     quarter = half // 2
 
-    own_half = lax.dynamic_slice_in_dim(out_weight, core * half, half, 1)
-    weight_mine = lax.all_gather(own_half, "fsdp", axis=0, tiled=True)
-    weight_other = lax.ppermute(weight_mine, "ctx", CORE_SWAP)
-
-    up = upstream[0]
-    up_pair = lax.ppermute(
-        lax.dynamic_slice_in_dim(up, (1 - high) * half, half, 1), "ctx", PAIR_SWAP
-    )
-    up_both = jnp.stack([lax.dynamic_slice_in_dim(up, high * half, half, 1), up_pair])
-    up_mine = lax.dynamic_slice_in_dim(up_both, core * quarter, quarter, 2)
-    up_other = lax.ppermute(
-        lax.dynamic_slice_in_dim(up_both, (1 - core) * quarter, quarter, 2), "ctx", CORE_SWAP
-    )
+    part = shape((BLOCK, quarter), BF16)
+    packed, own_half, up_keep, up_core, up_pair, up_diag = call(
+        pack_kernel,
+        (shape((HEADS, 3, BLOCK, HS), BF16), shape((HS, half), BF16), part, part, part, part),
+        smem=2,
+        inputs=(core_ref, high_ref, query_rows, key_rows, value_rows, out_weight, upstream),
+    )
+    own = exchange(packed)
+
+    mine, other_half = [], []
+    for s in range(1, HEADS):
+        piece = lax.ppermute(own_half, "fsdp", [(i, i ^ s) for i in range(8)])
+        mine.append(piece)
+        other_half.append(lax.ppermute(piece, "ctx", CORE_SWAP))
+    up_core = lax.ppermute(up_core, "ctx", CORE_SWAP)
+    up_pair = lax.ppermute(up_pair, "ctx", PAIR_SWAP)
+    up_diag = lax.ppermute(up_diag, "ctx", DIAG_SWAP)
 
     session_ids = session[0]
     positions = jnp.arange(LEN, dtype=jnp.int32).reshape(CHIPS, 2, BLOCK)
@@ -269,12 +301,7 @@
     rows_here = index * BLOCK + jnp.arange(BLOCK, dtype=jnp.int32)
     valid_here = (rows_here < valid_len).astype(F32)[:, None]
 
-    packed = call(
-        pack_kernel,
-        shape((HEADS, 3, BLOCK, HS), BF16),
-        inputs=(query_rows, key_rows, value_rows),
-    )
-    own = exchange(packed)
+    own = after(own, end, valid, valid_here, up_core, up_pair, up_diag, *mine[:3])
     other = lax.ppermute(own, "ctx", CORE_SWAP)
     pairs = 4 * TILE * SPAN * 5 // 2
     context, lse = call(
@@ -290,25 +317,29 @@
         inputs=(core_ref, own, other, end, valid),
     )
     context_mine = exchange(context)
+    grads = call(
+        project_kernel,
+        shape((HEADS, BLOCK, HS), BF16),
+        smem=2,
+        flops=2 * 128 * 1024 * 2048,
+        inputs=(core_ref, row_ref, upstream, out_weight, valid_here, *mine, *other_half),
+    )
+    grads = exchange(after(grads, context_mine))
     context_other = lax.ppermute(context_mine, "ctx", CORE_SWAP)
     terms = call(
         weight_kernel,
         shape((32, 32, quarter), BF16),
         flops=2 * 512 * 1024 * 512,
-        inputs=(context_mine, context_other, up_mine, up_other),
+        inputs=(context_mine, context_other, up_keep, up_pair, up_core, up_diag),
     )
     terms = lax.all_to_all(
-        terms, ("ctx", "fsdp"), split_axis=0, concat_axis=0, tiled=True, axis_index_groups=REDUCE
-    )
-
-    grads = call(
-        project_kernel,
-        shape((HEADS, BLOCK, HS), BF16),
-        smem=1,
-        flops=2 * 128 * 1024 * 2048,
-        inputs=(core_ref, upstream, weight_mine, weight_other, valid_here),
-    )
-    grads = exchange(grads)
+        after(terms, grads),
+        ("ctx", "fsdp"),
+        split_axis=0,
+        concat_axis=0,
+        tiled=True,
+        axis_index_groups=REDUCE,
+    )
     dq, keep, send = call(
         backward_kernel,
         (
@@ -329,15 +360,15 @@
     came = lax.ppermute(send, "ctx", CORE_SWAP)
     attended = call(
         attend_kernel,
-        shape((1, BLOCK, 2 * half), BF16),
-        smem=1,
+        shape((1, BLOCK, width), BF16),
+        smem=2,
         flops=2 * 128 * 1024 * 2048,
-        inputs=(core_ref, context_mine, weight_mine, weight_other),
+        inputs=(core_ref, row_ref, context_mine, out_weight, *mine, *other_half),
     )
     joined = call(
         join_kernel,
         shape((CHIPS, 4, BLOCK, HS), BF16),
-        inputs=(dq, keep, came, terms),
+        inputs=(after(dq, attended), keep, came, terms),
     )
     result = exchange(joined)
     weight_part = lax.ppermute(result[:, 3], "ctx", CORE_SWAP)
@@ -347,7 +378,7 @@
             shape((1, BLOCK, HEADS * HS), BF16),
             shape((1, BLOCK, HEADS * HS), BF16),
             shape((1, BLOCK, HEADS * HS), BF16),
-            shape((HS, 2 * half), F32),
+            shape((HS, width), F32),
         ),
         smem=1,
         inputs=(core_ref, result, weight_part),

time: 173 us -> 141 us (0.82)
  waiting for transfers between devices: 56.1 us -> 25.4 us
  local copies, waits for them, and re-layouts: 7.33 us -> 24.4 us
  between operations: 14.8 us -> 1.52 us
  Pallas kernels: 31.2 us -> 18.4 us
  starting transfers between devices: 37.7 us -> 49.1 us
  other arithmetic: 4.61 us -> 1.01 us
    all_gather x1 -> x0, waiting for transfers between devices: 36.2 us -> none  [shards(): weight_mine = lax.all_gather(own_half, 'fsdp', axis=0, tiled=True)]
    unnamed x22 -> x70, local copies, waits for them, and re-layouts: 4.82 us -> 24.4 us
    ppermute x3 -> x17, waiting for transfers between devices: 2.86 us -> 19 us  [the longest x7 6.78 us: shards(): piece = lax.ppermute(own_half, 'fsdp', [(i, i ^ s) for i in range(8)])]
    ppermute x3 -> x17, starting transfers between devices: 8.19 us -> 21.5 us  [the longest x7 10.2 us: shards(): piece = lax.ppermute(own_half, 'fsdp', [(i, i ^ s) for i in range(8)])]
    pallas_call x8, Pallas kernels: 31.2 us -> 18.4 us  [call(): pl.pallas_call(kernel, out_shape=out_shape, in_specs=specs, out_specs=out...]
    all_to_all x1, waiting for transfers between devices: 6.13 us -> 0.01 us  [shards(): lax.all_to_all(after(terms, grads), ('ctx', 'fsdp'), split_axis=0, concat...]
    all_to_all x3, waiting for transfers between devices: 8.94 us -> 5.21 us  [exchange(): lax.all_to_all(operand, 'ctx', split_axis=0, concat_axis=0, tiled=True, a...]
    dynamic_slice x2 -> x0, local copies, waits for them, and re-layouts: 2.49 us -> none  [the longest x1 1.76 us: shards(): lax.dynamic_slice_in_dim(up, (1 - high) * half, half, 1)]
  transfers between devices with their start and end apart: 12 -> 25, of which waited for: 6 -> 10; matrix products, arithmetic and copies ran while one was open for 4% -> 1% of each run, Pallas kernels for 15% -> 11%
where the time goes in v2:
time: 141 us; the launch traced here: 140 us
  starting transfers between devices  49.1 us (35%)
  waiting for transfers between devices  25.4 us (18%)
  local copies, waits for them, and re-layouts  24.4 us (17%)
  blocking collectives  19.8 us (14%)
  Pallas kernels  18.4 us (13%)
  between operations  1.52 us (1%)
    unnamed x70, local copies, waits for them, and re-layouts  24.4 us
    all_to_all x1, blocking collectives, exchange(): lax.all_to_all(operand, 'ctx', split_axis=0, concat_axis=0, tiled=True, a...  19.8 us
    pallas_call x8, Pallas kernels, call(): pl.pallas_call(kernel, out_shape=out_shape, in_specs=specs, out_specs=out...  18.4 us
    all_to_all x3, starting transfers between devices, exchange(): lax.all_to_all(operand, 'ctx', split_axis=0, concat_axis=0, tiled=True, a...  15.2 us
    ppermute x7, starting transfers between devices, shards(): piece = lax.ppermute(own_half, 'fsdp', [(i, i ^ s) for i in range(8)])  10.2 us
    ppermute x7, waiting for transfers between devices, shards(): piece = lax.ppermute(own_half, 'fsdp', [(i, i ^ s) for i in range(8)])  6.78 us
    ppermute x7, starting transfers between devices, shards(): other_half.append(lax.ppermute(piece, 'ctx', CORE_SWAP))  6.54 us
    ppermute x1, waiting for transfers between devices, shards(): up_pair = lax.ppermute(up_pair, 'ctx', PAIR_SWAP)  6.48 us
  transfers between devices with their start and end apart: 25, of which 10 were waited for; matrix products, arithmetic and copies ran while one was open for 1% of the time, Pallas kernels for 11%

profile of v2, /device:TPU:1, one launch (start us, length us, event | category | flops | bytes accessed | tf_op | source)
XLA Modules:
  0.0 139.6 jit_solution(9212071611695019082)
XLA Ops:
  7.4 4.6 %collective-permute-start.5 = (bf16[128,1024]{1,0:T(8,128)(2,1)}, bf16[128,1024]{1,0:T(8,128)(2,1)S(1)}, u32[]{:S(2)}, u32[]{:S(2)}) collective-permute-start(bf16[128,1024]{1,0:T(8,128)(2,1)} %get-tuple-element.28), channel_id=1, source_target_pairs={{0,3},{1,2},{2,1},{3,0},{4,7},{5,6},{6,5},{7,4},{8,11},{9,10},{10,... | collective-permute-start | bytes 786440 | tf_op jit(solution)/shard_map/ppermute | solution.py:285
  12.6 6.7 %all-to-all-start = ((bf16[8,3,128,128]{3,2,1,0:T(8,128)(2,1)}), bf16[8,3,128,128]{3,2,1,0:T(8,128)(2,1)S(1)}, u32[]{:S(2)}, u32[]{:S(2)}) async-start(bf16[8,3,128,128]{3,2,1,0:T(8,128)(2,1)} %get-tuple-element.24), calls=%async_computation | async-start | bytes 1572864 | tf_op jit(solution)/shard_map/all_to_all | solution.py:254
  19.2 1.5 %collective-permute-start = (bf16[128,512]{1,0:T(8,128)(2,1)S(1)}, bf16[128,512]{1,0:T(8,128)(2,1)S(1)}, u32[]{:S(2)}, u32[]{:S(2)}) collective-permute-start(bf16[128,512]{1,0:T(8,128)(2,1)S(1)} %get-tuple-element.25), channel_id=1, source_target_pairs={{0,8},{8,0},{16,24},{24,16},{32,40},{40,32},{48,56},{56,48},{64,72... | collective-permute-start | bytes 393224 | tf_op jit(solution)/shard_map/ppermute | solution.py:288
  20.7 3.2 %collective-permute-start.1 = (bf16[128,512]{1,0:T(8,128)(2,1)S(1)}, bf16[128,512]{1,0:T(8,128)(2,1)S(1)}, u32[]{:S(2)}, u32[]{:S(2)}) collective-permute-start(bf16[128,512]{1,0:T(8,128)(2,1)S(1)} %get-tuple-element.26), channel_id=1, source_target_pairs={{0,64},{8,72},{16,80},{24,88},{32,96},{40,104},{48,112},{56,120},{... | collective-permute-start | bytes 393224 | tf_op jit(solution)/shard_map/ppermute | solution.py:289
  26.3 6.5 %collective-permute-done.1.pair_ref = bf16[128,512]{1,0:T(8,128)(2,1)S(1)} collective-permute-done((bf16[128,512]{1,0:T(8,128)(2,1)S(1)}, bf16[128,512]{1,0:T(8,128)(2,1)S(1)}, u32[]{:S(2)}, u32[]{:S(2)}) %collective-permute-start.1) | collective-permute-done | bytes 131104 | tf_op jit(solution)/shard_map/ppermute | solution.py:289
  33.5 3.9 %collective-permute-done.2.diag_ref = bf16[128,512]{1,0:T(8,128)(2,1)S(1)} collective-permute-done((bf16[128,512]{1,0:T(8,128)(2,1)S(1)}, bf16[128,512]{1,0:T(8,128)(2,1)S(1)}, u32[]{:S(2)}, u32[]{:S(2)}) %collective-permute-start.2) | collective-permute-done | bytes 131104 | tf_op jit(solution)/shard_map/ppermute | solution.py:290
  38.1 3.0 %collective-permute-start.10 = (bf16[128,1024]{1,0:T(8,128)(2,1)}, bf16[128,1024]{1,0:T(8,128)(2,1)S(1)}, u32[]{:S(2)}, u32[]{:S(2)}) collective-permute-start(bf16[128,1024]{1,0:T(8,128)(2,1)} %get-tuple-element.28), channel_id=1, source_target_pairs={{0,7},{1,6},{2,5},{3,4},{4,3},{5,2},{6,1},{7,0},{8,15},{9,14},{10,... | collective-permute-start | bytes 786440 | tf_op jit(solution)/shard_map/ppermute | solution.py:285
  42.6 2.9 %shard_map.111 = (bf16[8,2,128,128]{3,2,1,0:T(8,128)(2,1)S(1)}, f32[4,1,256]{2,1,0:T(1,128)S(1)}) custom-call(s32[1]{0:T(128)} %bitcast.core_ref, bf16[8,3,128,128]{3,2,1,0:T(8,128)(2,1)S(1)} %all-to-all-done.own_ref, bf16[8,3,128,128]{3,2,1,0:T(8,128)(2,1)S(1)} %collective-permute-done.6.other_ref, s32[4,1,256]{2,1,0:T(1,128)S(1)} %bitcast.17, ...), custom_call_target="tpu_custom_call" | custom-call | flops 671088640 | bytes 2000000 | tf_op jit(solution)/shard_map/pallas_call | solution.py:58
  48.1 4.5 %all-to-all-start.1 = ((bf16[8,2,128,128]{3,2,1,0:T(8,128)(2,1)}), bf16[8,2,128,128]{3,2,1,0:T(8,128)(2,1)S(1)}, u32[]{:S(2)}, u32[]{:S(2)}) async-start(bf16[8,2,128,128]{3,2,1,0:T(8,128)(2,1)} %copy-done.15), calls=%async_computation.1 | async-start | bytes 1048576 | tf_op jit(solution)/shard_map/all_to_all | solution.py:254
  53.1 1.8 %collective-permute-start.17 = (bf16[128,1024]{1,0:T(8,128)(2,1)S(1)}, bf16[128,1024]{1,0:T(8,128)(2,1)}, u32[]{:S(2)}, u32[]{:S(2)}) collective-permute-start(bf16[128,1024]{1,0:T(8,128)(2,1)S(1)} %collective-permute-done.10.refs_6_), channel_id=1, source_target_pairs={{0,8},{8,0},{16,24},{24,16},{32,40},{40,32},{48,56},{56,48},{64,72... | collective-permute-start | bytes 786440 | tf_op jit(solution)/shard_map/ppermute | solution.py:287
  55.7 3.7 %collective-permute-done.8.refs_4_ = bf16[128,1024]{1,0:T(8,128)(2,1)S(1)} collective-permute-done((bf16[128,1024]{1,0:T(8,128)(2,1)}, bf16[128,1024]{1,0:T(8,128)(2,1)S(1)}, u32[]{:S(2)}, u32[]{:S(2)}) %collective-permute-start.8) | collective-permute-done | bytes 262176 | tf_op jit(solution)/shard_map/ppermute | solution.py:285
  59.4 2.1 %collective-permute-start.15 = (bf16[128,1024]{1,0:T(8,128)(2,1)S(1)}, bf16[128,1024]{1,0:T(8,128)(2,1)}, u32[]{:S(2)}, u32[]{:S(2)}) collective-permute-start(bf16[128,1024]{1,0:T(8,128)(2,1)S(1)} %collective-permute-done.8.refs_4_), channel_id=1, source_target_pairs={{0,8},{8,0},{16,24},{24,16},{32,40},{40,32},{48,56},{56,48},{64,72... | collective-permute-start | bytes 786440 | tf_op jit(solution)/shard_map/ppermute | solution.py:287
  61.5 4.1 %all-to-all-done.1.ctx_ref = bf16[8,2,128,128]{3,2,1,0:T(8,128)(2,1)S(1)} async-done(((bf16[8,2,128,128]{3,2,1,0:T(8,128)(2,1)}), bf16[8,2,128,128]{3,2,1,0:T(8,128)(2,1)S(1)}, u32[]{:S(2)}, u32[]{:S(2)}) %all-to-all-start.1) | async-done | bytes 524320 | tf_op jit(solution)/shard_map/all_to_all | solution.py:254
  65.6 2.1 %collective-permute-start.19 = (bf16[8,2,128,128]{3,2,1,0:T(8,128)(2,1)S(1)}, bf16[8,2,128,128]{3,2,1,0:T(8,128)(2,1)}, u32[]{:S(2)}, u32[]{:S(2)}) collective-permute-start(bf16[8,2,128,128]{3,2,1,0:T(8,128)(2,1)S(1)} %all-to-all-done.1.ctx_ref), channel_id=1, source_target_pairs={{0,8},{8,0},{16,24},{24,16},{32,40},{40,32},{48,56},{56,48},{64,72... | collective-permute-start | bytes 1572872 | tf_op jit(solution)/shard_map/ppermute | solution.py:328
  67.7 3.1 %collective-permute-done.7.refs_3_ = bf16[128,1024]{1,0:T(8,128)(2,1)S(1)} collective-permute-done((bf16[128,1024]{1,0:T(8,128)(2,1)}, bf16[128,1024]{1,0:T(8,128)(2,1)S(1)}, u32[]{:S(2)}, u32[]{:S(2)}) %collective-permute-start.7) | collective-permute-done | bytes 262176 | tf_op jit(solution)/shard_map/ppermute | solution.py:285
  74.4 2.7 %shard_map.113 = bf16[8,128,128]{2,1,0:T(8,128)(2,1)S(1)} custom-call(s32[1]{0:T(128)} %bitcast.core_ref, s32[1]{0:T(128)} %bitcast.1.row_ref, bf16[1,128,2048]{2,1,0:T(8,128)(2,1)S(1)} %copy-done.3, bf16[128,2048]{1,0:T(8,128)(2,1)S(1)} %copy-done.1, f32[128,1]{1,0:T(8,128)S(1)} %fusion.valid_ref, bf16[128,1024]{1,0:T(8,128)(2,1)S(1)} %collective-permute-done.3.refs_0_, ...), custom_call_target="tpu_custom_call" | custom-call | flops 536870912 | bytes 2000000 | tf_op jit(solution)/shard_map/pallas_call | solution.py:58
  77.8 4.0 %all-to-all-start.2 = ((bf16[8,128,128]{2,1,0:T(8,128)(2,1)}), bf16[8,128,128]{2,1,0:T(8,128)(2,1)S(1)}, u32[]{:S(2)}, u32[]{:S(2)}) async-start(bf16[8,128,128]{2,1,0:T(8,128)(2,1)} %copy-done.8), calls=%async_computation.2 | async-start | bytes 524288 | tf_op jit(solution)/shard_map/all_to_all | solution.py:254
  85.5 2.8 %shard_map.115 = bf16[32,32,512]{2,1,0:T(8,128)(2,1)} custom-call(bf16[8,2,128,128]{3,2,1,0:T(8,128)(2,1)S(1)} %all-to-all-done.1.ctx_ref, bf16[8,2,128,128]{3,2,1,0:T(8,128)(2,1)} %collective-permute-done.19.ctx_other_ref, bf16[128,512]{1,0:T(8,128)(2,1)S(1)} %copy-done.25, bf16[128,512]{1,0:T(8,128)(2,1)S(1)} %copy-done.29, ...), custom_call_target="tpu_custom_call" | custom-call | flops 536870912 | bytes 2000000 | tf_op jit(solution)/shard_map/pallas_call | solution.py:58
  90.1 4.1 %all-to-all-start.3 = ((bf16[32,32,512]{2,1,0:T(8,128)(2,1)}), bf16[32,32,512]{2,1,0:T(8,128)(2,1)S(1)}, u32[]{:S(2)}, u32[]{:S(2)}) async-start(bf16[32,32,512]{2,1,0:T(8,128)(2,1)} %shard_map.115), calls=%async_computation.3 | async-start | bytes 2097152 | tf_op jit(solution)/shard_map/all_to_all | solution.py:335
  98.5 4.1 %shard_map.114 = (bf16[8,128,128]{2,1,0:T(8,128)(2,1)S(1)}, f32[8,2,128,128]{3,2,1,0:T(8,128)S(1)}, bf16[8,2,128,128]{3,2,1,0:T(8,128)(2,1)S(1)}) custom-call(s32[1]{0:T(128)} %bitcast.core_ref, bf16[8,3,128,128]{3,2,1,0:T(8,128)(2,1)S(1)} %copy-done.12, bf16[8,3,128,128]{3,2,1,0:T(8,128)(2,1)S(1)} %copy-done.33, s32[4,1,256]{2,1,0:T(1,128)S(1)} %bitcast.18, ...), custom_call_target="tpu_custom_call" | custom-call | flops 1677721600 | bytes 2000000 | tf_op jit(solution)/shard_map/pallas_call | solution.py:58
  103.6 2.1 %collective-permute-start.18 = (bf16[8,2,128,128]{3,2,1,0:T(8,128)(2,1)S(1)}, bf16[8,2,128,128]{3,2,1,0:T(8,128)(2,1)S(1)}, u32[]{:S(2)}, u32[]{:S(2)}) collective-permute-start(bf16[8,2,128,128]{3,2,1,0:T(8,128)(2,1)S(1)} %get-tuple-element.36), channel_id=1, source_target_pairs={{0,8},{8,0},{16,24},{24,16},{32,40},{40,32},{48,56},{56,48},{64,72... | collective-permute-start | bytes 1572872 | tf_op jit(solution)/shard_map/ppermute | solution.py:360
  105.7 3.0 %shard_map.112 = bf16[1,128,2048]{2,1,0:T(8,128)(2,1)} custom-call(s32[1]{0:T(128)} %bitcast.core_ref, s32[1]{0:T(128)} %bitcast.1.row_ref, bf16[8,2,128,128]{3,2,1,0:T(8,128)(2,1)S(1)} %all-to-all-done.1.ctx_ref, bf16[128,2048]{1,0:T(8,128)(2,1)S(1)} %copy-done.1, bf16[128,1024]{1,0:T(8,128)(2,1)S(1)} %collective-permute-done.3.refs_0_, ...), custom_call_target="tpu_custom_call" | custom-call | flops 536870912 | bytes 2000000 | tf_op jit(solution)/shard_map/pallas_call | solution.py:58
  113.0 19.8 %all_to_all.25.mine_ref = bf16[8,4,128,128]{3,2,1,0:T(8,128)(2,1)S(1)} all-to-all(bf16[8,4,128,128]{3,2,1,0:T(8,128)(2,1)S(1)} %shard_map.116), channel_id=1, replica_groups={{0,16,32,48,64,80,96,112},{8,24,40,56,72,88,104,120},{1,17,33,49,65,81,..., dimensions={0} | all-to-all | bytes 2097152 | tf_op jit(solution)/shard_map/all_to_all | solution.py:254
  132.8 4.0 %collective-permute-start.20 = (bf16[8,128,128]{2,1,0:T(8,128)(2,1)S(1)}, bf16[8,128,128]{2,1,0:T(8,128)(2,1)S(1)}, u32[]{:S(2)}, u32[]{:S(2)}) collective-permute-start(bf16[8,128,128]{2,1,0:T(8,128)(2,1)S(1)} %slice_bitcast_fusion), channel_id=1, source_target_pairs={{0,8},{8,0},{16,24},{24,16},{32,40},{40,32},{48,56},{56,48},{64,72... | collective-permute-start | bytes 786440 | tf_op jit(solution)/shard_map/ppermute | solution.py:374
  (111 shorter events, 37.8 us)
Async XLA Ops:
  7.4 30.6 %collective-permute-start.5 = (bf16[128,1024]{1,0:T(8,128)(2,1)}, bf16[128,1024]{1,0:T(8,128)(2,1)S(1)}, u32[]{:S(2)}, u32[]{:S(2)}) collective-permute-start(bf16[128,1024]{1,0:T(8,128)(2,1)} %get-tuple-element.28), channel_id=1, source_target_pairs={{0,3},{1,2},{2,1},{3,0},{4,7},{5,6},{6,5},{7,4},{8,11},{9,10},{10,... | collective-permute-start | bytes 786440 | tf_op jit(solution)/shard_map/ppermute | solution.py:285
  12.0 26.1 %collective-permute-start.4 = (bf16[128,1024]{1,0:T(8,128)(2,1)}, bf16[128,1024]{1,0:T(8,128)(2,1)S(1)}, u32[]{:S(2)}, u32[]{:S(2)}) collective-permute-start(bf16[128,1024]{1,0:T(8,128)(2,1)} %get-tuple-element.28), channel_id=1, source_target_pairs={{0,2},{1,3},{2,0},{3,1},{4,6},{5,7},{6,4},{7,5},{8,10},{9,11},{10,... | collective-permute-start | bytes 786440 | tf_op jit(solution)/shard_map/ppermute | solution.py:285
  12.0 26.1 %collective-permute-start.3 = (bf16[128,1024]{1,0:T(8,128)(2,1)}, bf16[128,1024]{1,0:T(8,128)(2,1)S(1)}, u32[]{:S(2)}, u32[]{:S(2)}) collective-permute-start(bf16[128,1024]{1,0:T(8,128)(2,1)} %get-tuple-element.28), channel_id=1, source_target_pairs={{0,1},{1,0},{2,3},{3,2},{4,5},{5,4},{6,7},{7,6},{8,9},{9,8},{10,11... | collective-permute-start | bytes 786440 | tf_op jit(solution)/shard_map/ppermute | solution.py:285
  12.6 25.5 %all-to-all-start = ((bf16[8,3,128,128]{3,2,1,0:T(8,128)(2,1)}), bf16[8,3,128,128]{3,2,1,0:T(8,128)(2,1)S(1)}, u32[]{:S(2)}, u32[]{:S(2)}) async-start(bf16[8,3,128,128]{3,2,1,0:T(8,128)(2,1)} %get-tuple-element.24), calls=%async_computation | async-start | bytes 1572864 | tf_op jit(solution)/shard_map/all_to_all | solution.py:254
  19.2 6.4 %collective-permute-start = (bf16[128,512]{1,0:T(8,128)(2,1)S(1)}, bf16[128,512]{1,0:T(8,128)(2,1)S(1)}, u32[]{:S(2)}, u32[]{:S(2)}) collective-permute-start(bf16[128,512]{1,0:T(8,128)(2,1)S(1)} %get-tuple-element.25), channel_id=1, source_target_pairs={{0,8},{8,0},{16,24},{24,16},{32,40},{40,32},{48,56},{56,48},{64,72... | collective-permute-start | bytes 393224 | tf_op jit(solution)/shard_map/ppermute | solution.py:288
  20.7 12.1 %collective-permute-start.1 = (bf16[128,512]{1,0:T(8,128)(2,1)S(1)}, bf16[128,512]{1,0:T(8,128)(2,1)S(1)}, u32[]{:S(2)}, u32[]{:S(2)}) collective-permute-start(bf16[128,512]{1,0:T(8,128)(2,1)S(1)} %get-tuple-element.26), channel_id=1, source_target_pairs={{0,64},{8,72},{16,80},{24,88},{32,96},{40,104},{48,112},{56,120},{... | collective-permute-start | bytes 393224 | tf_op jit(solution)/shard_map/ppermute | solution.py:289
  26.3 11.1 %collective-permute-start.2 = (bf16[128,512]{1,0:T(8,128)(2,1)S(1)}, bf16[128,512]{1,0:T(8,128)(2,1)S(1)}, u32[]{:S(2)}, u32[]{:S(2)}) collective-permute-start(bf16[128,512]{1,0:T(8,128)(2,1)S(1)} %get-tuple-element.27), channel_id=1, source_target_pairs={{0,72},{8,64},{16,88},{24,80},{32,104},{40,96},{48,120},{56,112},{... | collective-permute-start | bytes 393224 | tf_op jit(solution)/shard_map/ppermute | solution.py:290
  38.0 4.5 %collective-permute-start.6 = (bf16[8,3,128,128]{3,2,1,0:T(8,128)(2,1)S(1)}, bf16[8,3,128,128]{3,2,1,0:T(8,128)(2,1)S(1)}, u32[]{:S(2)}, u32[]{:S(2)}) collective-permute-start(bf16[8,3,128,128]{3,2,1,0:T(8,128)(2,1)S(1)} %all-to-all-done.own_ref), channel_id=1, source_target_pairs={{0,8},{8,0},{16,24},{24,16},{32,40},{40,32},{48,56},{56,48},{64,72... | collective-permute-start | bytes 2359304 | tf_op jit(solution)/shard_map/ppermute | solution.py:305
  38.1 15.0 %collective-permute-start.10 = (bf16[128,1024]{1,0:T(8,128)(2,1)}, bf16[128,1024]{1,0:T(8,128)(2,1)S(1)}, u32[]{:S(2)}, u32[]{:S(2)}) collective-permute-start(bf16[128,1024]{1,0:T(8,128)(2,1)} %get-tuple-element.28), channel_id=1, source_target_pairs={{0,7},{1,6},{2,5},{3,4},{4,3},{5,2},{6,1},{7,0},{8,15},{9,14},{10,... | collective-permute-start | bytes 786440 | tf_op jit(solution)/shard_map/ppermute | solution.py:285
  41.1 13.9 %collective-permute-start.9 = (bf16[128,1024]{1,0:T(8,128)(2,1)}, bf16[128,1024]{1,0:T(8,128)(2,1)S(1)}, u32[]{:S(2)}, u32[]{:S(2)}) collective-permute-start(bf16[128,1024]{1,0:T(8,128)(2,1)} %get-tuple-element.28), channel_id=1, source_target_pairs={{0,6},{1,7},{2,4},{3,5},{4,2},{5,3},{6,0},{7,1},{8,14},{9,15},{10,... | collective-permute-start | bytes 786440 | tf_op jit(solution)/shard_map/ppermute | solution.py:285
  41.8 17.6 %collective-permute-start.8 = (bf16[128,1024]{1,0:T(8,128)(2,1)}, bf16[128,1024]{1,0:T(8,128)(2,1)S(1)}, u32[]{:S(2)}, u32[]{:S(2)}) collective-permute-start(bf16[128,1024]{1,0:T(8,128)(2,1)} %get-tuple-element.28), channel_id=1, source_target_pairs={{0,5},{1,4},{2,7},{3,6},{4,1},{5,0},{6,3},{7,2},{8,13},{9,12},{10,... | collective-permute-start | bytes 786440 | tf_op jit(solution)/shard_map/ppermute | solution.py:285
  48.1 17.5 %all-to-all-start.1 = ((bf16[8,2,128,128]{3,2,1,0:T(8,128)(2,1)}), bf16[8,2,128,128]{3,2,1,0:T(8,128)(2,1)S(1)}, u32[]{:S(2)}, u32[]{:S(2)}) async-start(bf16[8,2,128,128]{3,2,1,0:T(8,128)(2,1)} %copy-done.15), calls=%async_computation.1 | async-start | bytes 1048576 | tf_op jit(solution)/shard_map/all_to_all | solution.py:254
  52.6 18.2 %collective-permute-start.7 = (bf16[128,1024]{1,0:T(8,128)(2,1)}, bf16[128,1024]{1,0:T(8,128)(2,1)S(1)}, u32[]{:S(2)}, u32[]{:S(2)}) collective-permute-start(bf16[128,1024]{1,0:T(8,128)(2,1)} %get-tuple-element.28), channel_id=1, source_target_pairs={{0,4},{1,5},{2,6},{3,7},{4,0},{5,1},{6,2},{7,3},{8,12},{9,13},{10,... | collective-permute-start | bytes 786440 | tf_op jit(solution)/shard_map/ppermute | solution.py:285
  53.1 18.9 %collective-permute-start.17 = (bf16[128,1024]{1,0:T(8,128)(2,1)S(1)}, bf16[128,1024]{1,0:T(8,128)(2,1)}, u32[]{:S(2)}, u32[]{:S(2)}) collective-permute-start(bf16[128,1024]{1,0:T(8,128)(2,1)S(1)} %collective-permute-done.10.refs_6_), channel_id=1, source_target_pairs={{0,8},{8,0},{16,24},{24,16},{32,40},{40,32},{48,56},{56,48},{64,72... | collective-permute-start | bytes 786440 | tf_op jit(solution)/shard_map/ppermute | solution.py:287
  55.0 17.1 %collective-permute-start.16 = (bf16[128,1024]{1,0:T(8,128)(2,1)S(1)}, bf16[128,1024]{1,0:T(8,128)(2,1)}, u32[]{:S(2)}, u32[]{:S(2)}) collective-permute-start(bf16[128,1024]{1,0:T(8,128)(2,1)S(1)} %collective-permute-done.9.refs_5_), channel_id=1, source_target_pairs={{0,8},{8,0},{16,24},{24,16},{32,40},{40,32},{48,56},{56,48},{64,72... | collective-permute-start | bytes 786440 | tf_op jit(solution)/shard_map/ppermute | solution.py:287
  59.4 13.1 %collective-permute-start.15 = (bf16[128,1024]{1,0:T(8,128)(2,1)S(1)}, bf16[128,1024]{1,0:T(8,128)(2,1)}, u32[]{:S(2)}, u32[]{:S(2)}) collective-permute-start(bf16[128,1024]{1,0:T(8,128)(2,1)S(1)} %collective-permute-done.8.refs_4_), channel_id=1, source_target_pairs={{0,8},{8,0},{16,24},{24,16},{32,40},{40,32},{48,56},{56,48},{64,72... | collective-permute-start | bytes 786440 | tf_op jit(solution)/shard_map/ppermute | solution.py:287
  65.6 16.3 %collective-permute-start.19 = (bf16[8,2,128,128]{3,2,1,0:T(8,128)(2,1)S(1)}, bf16[8,2,128,128]{3,2,1,0:T(8,128)(2,1)}, u32[]{:S(2)}, u32[]{:S(2)}) collective-permute-start(bf16[8,2,128,128]{3,2,1,0:T(8,128)(2,1)S(1)} %all-to-all-done.1.ctx_ref), channel_id=1, source_target_pairs={{0,8},{8,0},{16,24},{24,16},{32,40},{40,32},{48,56},{56,48},{64,72... | collective-permute-start | bytes 1572872 | tf_op jit(solution)/shard_map/ppermute | solution.py:328
  70.8 2.9 %collective-permute-start.13 = (bf16[128,1024]{1,0:T(8,128)(2,1)S(1)}, bf16[128,1024]{1,0:T(8,128)(2,1)}, u32[]{:S(2)}, u32[]{:S(2)}) collective-permute-start(bf16[128,1024]{1,0:T(8,128)(2,1)S(1)} %collective-permute-done.5.refs_2_), channel_id=1, source_target_pairs={{0,8},{8,0},{16,24},{24,16},{32,40},{40,32},{48,56},{56,48},{64,72... | collective-permute-start | bytes 786440 | tf_op jit(solution)/shard_map/ppermute | solution.py:287
  72.1 2.0 %collective-permute-start.12 = (bf16[128,1024]{1,0:T(8,128)(2,1)S(1)}, bf16[128,1024]{1,0:T(8,128)(2,1)}, u32[]{:S(2)}, u32[]{:S(2)}) collective-permute-start(bf16[128,1024]{1,0:T(8,128)(2,1)S(1)} %collective-permute-done.4.refs_1_), channel_id=1, source_target_pairs={{0,8},{8,0},{16,24},{24,16},{32,40},{40,32},{48,56},{56,48},{64,72... | collective-permute-start | bytes 786440 | tf_op jit(solution)/shard_map/ppermute | solution.py:287
  72.5 1.9 %collective-permute-start.11 = (bf16[128,1024]{1,0:T(8,128)(2,1)S(1)}, bf16[128,1024]{1,0:T(8,128)(2,1)}, u32[]{:S(2)}, u32[]{:S(2)}) collective-permute-start(bf16[128,1024]{1,0:T(8,128)(2,1)S(1)} %collective-permute-done.3.refs_0_), channel_id=1, source_target_pairs={{0,8},{8,0},{16,24},{24,16},{32,40},{40,32},{48,56},{56,48},{64,72... | collective-permute-start | bytes 786440 | tf_op jit(solution)/shard_map/ppermute | solution.py:287
  77.8 11.6 %all-to-all-start.2 = ((bf16[8,128,128]{2,1,0:T(8,128)(2,1)}), bf16[8,128,128]{2,1,0:T(8,128)(2,1)S(1)}, u32[]{:S(2)}, u32[]{:S(2)}) async-start(bf16[8,128,128]{2,1,0:T(8,128)(2,1)} %copy-done.8), calls=%async_computation.2 | async-start | bytes 524288 | tf_op jit(solution)/shard_map/all_to_all | solution.py:254
  90.1 19.4 %all-to-all-start.3 = ((bf16[32,32,512]{2,1,0:T(8,128)(2,1)}), bf16[32,32,512]{2,1,0:T(8,128)(2,1)S(1)}, u32[]{:S(2)}, u32[]{:S(2)}) async-start(bf16[32,32,512]{2,1,0:T(8,128)(2,1)} %shard_map.115), calls=%async_computation.3 | async-start | bytes 2097152 | tf_op jit(solution)/shard_map/all_to_all | solution.py:335
  103.6 5.1 %collective-permute-start.18 = (bf16[8,2,128,128]{3,2,1,0:T(8,128)(2,1)S(1)}, bf16[8,2,128,128]{3,2,1,0:T(8,128)(2,1)S(1)}, u32[]{:S(2)}, u32[]{:S(2)}) collective-permute-start(bf16[8,2,128,128]{3,2,1,0:T(8,128)(2,1)S(1)} %get-tuple-element.36), channel_id=1, source_target_pairs={{0,8},{8,0},{16,24},{24,16},{32,40},{40,32},{48,56},{56,48},{64,72... | collective-permute-start | bytes 1572872 | tf_op jit(solution)/shard_map/ppermute | solution.py:360
  132.8 5.2 %collective-permute-start.20 = (bf16[8,128,128]{2,1,0:T(8,128)(2,1)S(1)}, bf16[8,128,128]{2,1,0:T(8,128)(2,1)S(1)}, u32[]{:S(2)}, u32[]{:S(2)}) collective-permute-start(bf16[8,128,128]{2,1,0:T(8,128)(2,1)S(1)} %slice_bitcast_fusion), channel_id=1, source_target_pairs={{0,8},{8,0},{16,24},{24,16},{32,40},{40,32},{48,56},{56,48},{64,72... | collective-permute-start | bytes 786440 | tf_op jit(solution)/shard_map/ppermute | solution.py:374
  (36 other events, 139.0 us)

commit v3 on v2

v3 whole, which is shorter than its diff:
```python
import functools
import math

import jax
import jax.numpy as jnp
from jax import lax
from jax.experimental import pallas as pl
from jax.experimental.pallas import tpu as pltpu
from jax.sharding import PartitionSpec as P

HEADS = 8
HS = 128
BLOCK = 128
TILE = 256
SPAN = 512
REACH = 128
CHIPS = 8
LEN = 2048
NEG = -1e30
SEMS = 48
SCALE = 1.0 / math.sqrt(HS)
SCALE2 = SCALE * math.log2(math.e)
F32 = jnp.float32
BF16 = jnp.bfloat16

CORE_SWAP = [(i, i ^ 1) for i in range(16)]
PAIR_SWAP = [(i, i ^ 8) for i in range(16)]
DIAG_SWAP = [(i, i ^ 9) for i in range(16)]
SAME_CORE = [[2 * j + c for j in range(CHIPS)] for c in range(2)]
REDUCE = [
    [(8 * h + 2 * y + c) * 8 + f for f in range(8) for y in range(4)]
    for h in range(2)
    for c in range(2)
]


def dot_nt(a, b):
    return lax.dot_general(a, b, (((1,), (1,)), ((), ())), preferred_element_type=F32)


def dot_tn(a, b):
    return lax.dot_general(a, b, (((0,), (0,)), ((), ())), preferred_element_type=F32)


def dot_nn(a, b):
    return lax.dot_general(a, b, (((1,), (0,)), ((), ())), preferred_element_type=F32)


class Load:
    def __init__(self, copy, ref):
        self.copy, self.ref, self.done = copy, ref, False

    def get(self):
        if not self.done:
            self.copy.wait()
            self.done = True
        return self.ref


class Store:
    def __init__(self, hbm, ref, sems):
        self.hbm, self.ref, self.sems, self.copies = hbm, ref, sems, []

    def push(self, *index):
        src = self.ref.at[index] if index else self.ref
        dst = self.hbm.at[index] if index else self.hbm
        copy = pltpu.make_async_copy(src, dst, next(self.sems))
        copy.start()
        self.copies.append(copy)


SPACES = {"S": pltpu.SMEM, "V": pltpu.VMEM, "H": pltpu.HBM, "A": pl.ANY, "R": pltpu.HBM}


def call(kernel, ins, outs, scratch=(), flops=0, mib=14):
    copied = [
        pltpu.VMEM(jax.eval_shape(lambda x: x[i[2]] if len(i) > 2 else x, i[1]).shape, i[1].dtype)
        for i in ins
        if i[0] in "HA"
    ] + [pltpu.VMEM(o[1], o[2]) for o in outs if o[0] == "H"]

    def body(*refs):
        refs = list(refs)
        in_refs = [refs.pop(0) for _ in ins]
        out_refs = [refs.pop(0) for _ in outs]
        sem_ref = refs.pop(0)
        buffers = [refs.pop(0) for _ in copied]
        sems = (sem_ref.at[n] for n in range(SEMS))
        given, made = [], []
        for one, ref in zip(ins, in_refs):
            if one[0] in "HA":
                buffer = buffers.pop(0)
                copy = pltpu.make_async_copy(
                    ref.at[one[2]] if len(one) > 2 else ref, buffer, next(sems)
                )
                copy.start()
                ref = Load(copy, buffer)
            given.append(ref)
        for one, ref in zip(outs, out_refs):
            made.append(Store(ref, buffers.pop(0), sems) if one[0] == "H" else ref)
        more = kernel(given, made, refs, sems) or []
        for one in given:
            if isinstance(one, Load):
                one.get()
        for one in made:
            if isinstance(one, Store):
                for copy in one.copies:
                    copy.wait()
        for copy in more:
            copy.wait()

    result = pl.pallas_call(
        body,
        out_shape=[
            SPACES[o[0]](o[1], o[2]) if o[0] in "HR" else jax.ShapeDtypeStruct(o[1], o[2])
            for o in outs
        ],
        in_specs=[pl.BlockSpec(memory_space=SPACES[i[0]]) for i in ins],
        out_specs=[pl.BlockSpec(memory_space=SPACES[o[0]]) for o in outs],
        scratch_shapes=[pltpu.SemaphoreType.DMA((SEMS,)), *copied, *scratch],
        compiler_params=pltpu.CompilerParams(vmem_limit_bytes=mib * 1024 * 1024),
        cost_estimate=pl.CostEstimate(flops=flops, bytes_accessed=2_000_000, transcendentals=0),
    )(*[
        pltpu.with_memory_space_constraint(i[1], pltpu.HBM) if i[0] in "HR" else i[1] for i in ins
    ])
    return result[0] if len(outs) == 1 else result


def pack_kernel(ins, outs, scratch, sems):
    core_ref, high_ref, q_ref, k_ref, v_ref, w_ref, up_ref = ins
    out_ref, half_ref, keep_ref, core_out_ref, pair_ref, diag_ref = outs
    core, high = core_ref[0], high_ref[0]
    half = half_ref.shape[1]
    quarter = half // 2
    copies = []

    def copy(src, dst):
        copies.append(pltpu.make_async_copy(src, dst, next(sems)))
        copies[-1].start()

    for a in range(HEADS):
        cols = pl.ds(a * HS, HS)
        copy(q_ref.at[0, :, cols], out_ref.at[a, 0])
        copy(k_ref.at[0, :, cols], out_ref.at[a, 1])
        copy(v_ref.at[0, :, cols], out_ref.at[a, 2])
    copy(w_ref.at[:, pl.ds(pl.multiple_of(core * half, half), half)], half_ref)
    for ref, x, c in (
        (keep_ref, high, core),
        (core_out_ref, high, 1 - core),
        (pair_ref, 1 - high, core),
        (diag_ref, 1 - high, 1 - core),
    ):
        at = pl.multiple_of(x * half + c * quarter, quarter)
        copy(up_ref.at[0, :, pl.ds(at, quarter)], ref)
    return copies


def in_order(core, own_ref, other_ref, slot, dst_ref):
    for j in range(CHIPS):
        own = pl.multiple_of(2 * BLOCK * j + BLOCK * core, BLOCK)
        other = pl.multiple_of(2 * BLOCK * j + BLOCK * (1 - core), BLOCK)
        dst_ref[pl.ds(own, BLOCK)] = own_ref[j, slot]
        dst_ref[pl.ds(other, BLOCK)] = other_ref[j, slot]


def chunks_of(m):
    stop = min(SPAN * (m + 1) + REACH, LEN)
    return [(start, min(start + SPAN, stop)) for start in range(0, stop, SPAN)]


def masked_scores(k_s, q, end, m, start, stop):
    scores = dot_nt(k_s[start:stop], q)
    if stop > SPAN * m:
        at = lax.broadcasted_iota(jnp.int32, scores.shape, 0) + start
        scores = jnp.where(at < end, scores, NEG)
    return scores


def forward_kernel(ins, outs, scratch, sems):
    core_ref, own_ref, other_ref, end_ref, valid_ref = ins
    ctx_out, lse_out, q_out, k_out, v_out = outs
    (s_s,) = scratch
    core = core_ref[0]
    k_s, v_s = k_out.ref, v_out.ref
    in_order(core, own_ref, other_ref, 1, k_s)
    k_out.push()
    in_order(core, own_ref, other_ref, 2, v_s)
    v_out.push()
    q_out.ref[...] = own_ref[:, 0]
    q_out.push()
    for m in range(4):
        q = own_ref[2 * m : 2 * m + 2, 0].reshape(TILE, HS)
        end = end_ref[m]
        top = jnp.full((1, TILE), NEG, F32)
        for start, stop in chunks_of(m):
            scores = masked_scores(k_s, q, end, m, start, stop)
            s_s[start:stop] = scores
            top = jnp.maximum(top, jnp.max(scores, axis=0, keepdims=True))
        top2 = top * SCALE2
        total = jnp.zeros((1, TILE), F32)
        acc = jnp.zeros((HS, TILE), F32)
        for start, stop in chunks_of(m):
            p = jnp.exp2(s_s[start:stop] * SCALE2 - top2)
            total = total + jnp.sum(p, axis=0, keepdims=True)
            acc = acc + dot_tn(v_s[start:stop], p.astype(BF16))
        lse_out.ref[m] = top2 + jnp.log2(total)
        ctx = (acc * (valid_ref[m] / total)).T.astype(BF16)
        for t in range(2):
            j = 2 * m + t
            block = ctx[t * BLOCK : (t + 1) * BLOCK]
            ctx_out.ref[j, 0] = block
            ctx_out.ref[j ^ 4, 1] = block
            ctx_out.push(j, 0)
            ctx_out.push(j ^ 4, 1)
    lse_out.push()


def backward_kernel(ins, outs, scratch, sems):
    core_ref, q_in, k_in, grad_in, v_in, ctx_in, end_in, lse_in = ins
    dq_out, keep_out, send_out = outs
    dk_s, dv_s = scratch
    core = core_ref[0]
    dk_s[...] = jnp.zeros(dk_s.shape, F32)
    dv_s[...] = jnp.zeros(dv_s.shape, F32)
    end_ref, lse_ref = end_in.get(), lse_in.get()
    q_ref, k_s = q_in.get(), k_in.get()
    grad_ref, v_s, ctx_ref = grad_in.get(), v_in.get(), ctx_in.get()
    for m in range(3, -1, -1):
        rows = slice(2 * m, 2 * m + 2)
        q = q_ref[rows].reshape(TILE, HS)
        do = grad_ref[rows].reshape(TILE, HS)
        ctx = ctx_ref[rows].reshape(TILE, HS)
        delta = jnp.sum((do.astype(F32) * ctx.astype(F32)).T, axis=0, keepdims=True)
        end = end_ref[m]
        lse = lse_ref[m]
        dq = jnp.zeros((HS, TILE), F32)
        for start, stop in chunks_of(m):
            scores = masked_scores(k_s, q, end, m, start, stop)
            p = jnp.exp2(scores * SCALE2 - lse)
            dp = dot_nt(v_s[start:stop], do)
            ds = (p * (dp - delta) * SCALE).astype(BF16)
            dv_s[start:stop] += dot_nn(p.astype(BF16), do)
            dk_s[start:stop] += dot_nn(ds, q)
            dq = dq + dot_tn(k_s[start:stop], ds)
        dq_rows = dq.T.astype(BF16)
        dq_out.ref[2 * m] = dq_rows[:BLOCK]
        dq_out.ref[2 * m + 1] = dq_rows[BLOCK:]
        dq_out.push(pl.ds(2 * m, 2))
        first = 2 * m + 1 if m else 0
        last = 2 * m + 3 if m < 3 else CHIPS
        for j in range(first, last):
            own = pl.multiple_of(2 * BLOCK * j + BLOCK * core, BLOCK)
            other = pl.multiple_of(2 * BLOCK * j + BLOCK * (1 - core), BLOCK)
            send_out.ref[j, 0] = dk_s[pl.ds(other, BLOCK)].astype(BF16)
            send_out.ref[j, 1] = dv_s[pl.ds(other, BLOCK)].astype(BF16)
            send_out.push(j)
            keep_out.ref[j, 0] = dk_s[pl.ds(own, BLOCK)]
            keep_out.ref[j, 1] = dv_s[pl.ds(own, BLOCK)]
            keep_out.push(j)


def project_kernel(ins, outs, scratch, sems):
    core_ref, row_ref, valid_ref, up_in, own_in = ins[:5]
    mine, other = ins[5:12], ins[12:19]
    out = outs[0]
    core, row = core_ref[0], row_ref[0]
    half = up_in.ref.shape[1] // 2
    valid = valid_ref[...]
    up_ref = up_in.get()
    out.ref[row] = (dot_nt(up_ref[...], own_in.get()[...]) * valid).astype(BF16)
    out.push(row)
    up_mine = up_ref[:, pl.ds(pl.multiple_of(core * half, half), half)]
    up_other = up_ref[:, pl.ds(pl.multiple_of((1 - core) * half, half), half)]
    for s in range(1, HEADS):
        total = dot_nt(up_mine, mine[s - 1].get()[...]) + dot_nt(up_other, other[s - 1].get()[...])
        at = jnp.bitwise_xor(row, s)
        out.ref[at] = (total * valid).astype(BF16)
        out.push(at)


def attend_kernel(ins, outs, scratch, sems):
    core_ref, row_ref, ctx_in, own_in = ins[:4]
    mine, other = ins[4:11], ins[11:18]
    out = outs[0]
    core, row = core_ref[0], row_ref[0]
    ctx_ref, own_ref = ctx_in.get(), own_in.get()
    half = own_ref.shape[1] // 2
    ctx = jnp.concatenate([ctx_ref[jnp.bitwise_xor(row, s)] for s in range(HEADS)], axis=1)
    step = half // 4
    for side, parts in ((core, mine), (1 - core, other)):
        parts = [part.get() for part in parts]
        for n in range(4):
            at = pl.ds(pl.multiple_of(side * half + n * step, step), step)
            cols = slice(n * step, (n + 1) * step)
            weight = jnp.concatenate(
                [own_ref[:, at]] + [part[:, cols] for part in parts], axis=0
            )
            out.ref[0, :, at] = dot_nn(ctx, weight).astype(BF16)
            out.push(0, slice(None), at)


def weight_kernel(ins, outs, scratch, sems):
    out = outs[0]
    keep, pair, core, diag, ctx_ref, ctx_other_ref = [one.get() for one in ins]
    quarter = keep.shape[1]
    up = jnp.concatenate([keep[...], pair[...]], axis=0)
    up_other = jnp.concatenate([core[...], diag[...]], axis=0)
    for a in range(HEADS):
        total = dot_tn(ctx_ref[a].reshape(TILE, HS), up)
        total = total + dot_tn(ctx_other_ref[a].reshape(TILE, HS), up_other)
        part = pl.ds(4 * a, 4)
        out.ref[part] = total.reshape(4, HS // 4, quarter).astype(BF16)
        out.push(part)


def join_kernel(ins, outs, scratch, sems):
    dq_in, keep_in, came_in, terms_ref = ins
    out_ref = outs[0]
    total = terms_ref[0].astype(F32)
    for s in range(1, terms_ref.shape[0]):
        total = total + terms_ref[s].astype(F32)
    weight = total.astype(BF16)
    rows = weight.shape[0]
    for j in range(CHIPS):
        for t in range(4):
            out_ref[j, 3, t * rows : (t + 1) * rows] = weight[:, t * HS : (t + 1) * HS]
    dq_ref, keep_ref, came_ref = dq_in.get(), keep_in.get(), came_in.get()
    for j in range(CHIPS):
        out_ref[j, 0] = dq_ref[j]
        out_ref[j, 1] = (keep_ref[j, 0] + came_ref[j, 0].astype(F32)).astype(BF16)
        out_ref[j, 2] = (keep_ref[j, 1] + came_ref[j, 1].astype(F32)).astype(BF16)


def unpack_kernel(ins, outs, scratch, sems):
    core_ref, mine_ref, other_ref = ins
    dw_out = outs[3]
    core = core_ref[0]
    copies = []
    for a in range(HEADS):
        for i in range(3):
            dst = outs[i].at[0, :, pl.ds(a * HS, HS)]
            copies.append(pltpu.make_async_copy(mine_ref.at[a, i], dst, next(sems)))
            copies[-1].start()
    for y in range(4):
        rows = pl.ds(32 * y, 32)
        for x in range(2):
            a = 4 * x + y
            for t in range(4):
                part = slice(32 * t, 32 * t + 32)
                at = pl.multiple_of(1024 * x + 512 * core + HS * t, HS)
                dw_out.ref[rows, pl.ds(at, HS)] = mine_ref[a, 3, part].astype(F32)
                at = pl.multiple_of(1024 * x + 512 * (1 - core) + HS * t, HS)
                dw_out.ref[rows, pl.ds(at, HS)] = other_ref[a, part].astype(F32)
        dw_out.push(rows)
    return copies


def exchange(operand):
    return lax.all_to_all(
        operand, "ctx", split_axis=0, concat_axis=0, tiled=True, axis_index_groups=SAME_CORE
    )


def after(value, *others):
    return lax.optimization_barrier((value, *others))[0]


def shards(query_rows, key_rows, value_rows, session, lengths, out_weight, upstream):
    index = lax.axis_index("ctx").astype(jnp.int32)
    core = index & 1
    core_ref = core.reshape(1)
    high_ref = (index >> 3).reshape(1)
    row_ref = lax.axis_index("fsdp").astype(jnp.int32).reshape(1)
    valid_len = lengths[0]
    width = out_weight.shape[1]
    half = width // 2
    quarter = half // 2

    part = ("R", (BLOCK, quarter), BF16)
    packed, own_half, up_keep, up_core, up_pair, up_diag = call(
        pack_kernel,
        [
            ("S", core_ref), ("S", high_ref), ("R", query_rows), ("R", key_rows),
            ("R", value_rows), ("R", out_weight), ("R", upstream),
        ],
        [("R", (HEADS, 3, BLOCK, HS), BF16), ("R", (HS, half), BF16), part, part, part, part],
    )
    own = exchange(packed)

    session_ids = session[0]
    positions = jnp.arange(LEN, dtype=jnp.int32).reshape(CHIPS, 2, BLOCK)
    own_sessions = lax.dynamic_index_in_dim(session_ids.reshape(CHIPS, 2, BLOCK), core, 1, False)
    own_positions = lax.dynamic_index_in_dim(positions, core, 1, False)
    end = jnp.sum(
        (session_ids[:, None] <= own_sessions.reshape(1, -1)).astype(jnp.int32), axis=0
    )
    end = jnp.minimum(end, valid_len).reshape(4, 1, TILE)
    valid = (own_positions < valid_len).astype(F32).reshape(4, 1, TILE)
    rows_here = index * BLOCK + jnp.arange(BLOCK, dtype=jnp.int32)
    valid_here = (rows_here < valid_len).astype(F32)[:, None]

    def gather(halves, s):
        piece = lax.ppermute(halves, "fsdp", [(i, i ^ s) for i in range(8)])
        return piece, lax.ppermute(piece, "ctx", CORE_SWAP)

    pieces = [gather(own_half, s) for s in (1, 2, 3)]
    own = after(own, end, valid, valid_here, *[one for one, _ in pieces])
    own_half = after(own_half, own)
    pieces += [gather(own_half, s) for s in (4, 5, 6, 7)]
    mine = [("A", one) for one, _ in pieces]
    other_half = [("A", one) for _, one in pieces]

    other = lax.ppermute(own, "ctx", CORE_SWAP)
    pairs = 4 * TILE * SPAN * 5 // 2
    rows = ("H", (LEN, HS), BF16)
    context, lse, query, key, value = call(
        forward_kernel,
        [("S", core_ref), ("V", own), ("V", other), ("V", end), ("V", valid)],
        [
            ("H", (CHIPS, 2, BLOCK, HS), BF16),
            ("H", (4, 1, TILE), F32),
            ("H", (CHIPS, BLOCK, HS), BF16),
            rows,
            rows,
        ],
        scratch=(pltpu.VMEM((LEN, TILE), F32),),
        flops=4 * pairs * HS,
    )
    context_mine = exchange(context)
    up_pair = lax.ppermute(after(up_pair, context), "ctx", PAIR_SWAP)
    up_diag = lax.ppermute(after(up_diag, context), "ctx", DIAG_SWAP)
    up_core = lax.ppermute(after(up_core, context), "ctx", CORE_SWAP)
    grads = call(
        project_kernel,
        [
            ("S", core_ref), ("S", row_ref), ("V", valid_here), ("H", upstream, 0),
            ("H", out_weight), *mine, *other_half,
        ],
        [("H", (HEADS, BLOCK, HS), BF16)],
        flops=2 * 128 * 1024 * 2048,
    )
    grads = exchange(after(grads, context_mine))
    context_other = lax.ppermute(context_mine, "ctx", CORE_SWAP)
    terms = call(
        weight_kernel,
        [
            ("H", up_keep), ("A", up_pair), ("A", up_core), ("A", up_diag),
            ("A", context_mine), ("A", context_other),
        ],
        [("H", (32, 32, quarter), BF16)],
        flops=2 * 512 * 1024 * 512,
    )
    terms = lax.all_to_all(
        after(terms, grads),
        ("ctx", "fsdp"),
        split_axis=0,
        concat_axis=0,
        tiled=True,
        axis_index_groups=REDUCE,
    )
    dq, keep, send = call(
        backward_kernel,
        [
            ("S", core_ref), ("H", query), ("H", key), ("H", grads), ("H", value),
            ("H", context, (slice(None), 0)), ("A", end), ("H", lse),
        ],
        [
            ("H", (CHIPS, BLOCK, HS), BF16),
            ("H", (CHIPS, 2, BLOCK, HS), F32),
            ("H", (CHIPS, 2, BLOCK, HS), BF16),
        ],
        scratch=(pltpu.VMEM((LEN, HS), F32), pltpu.VMEM((LEN, HS), F32)),
        flops=10 * pairs * HS,
    )
    came = lax.ppermute(send, "ctx", CORE_SWAP)
    attended = call(
        attend_kernel,
        [
            ("S", core_ref), ("S", row_ref), ("A", context_mine, (slice(None), 0)),
            ("H", out_weight), *mine, *other_half,
        ],
        [("H", (1, BLOCK, width), BF16)],
        flops=2 * 128 * 1024 * 2048,
    )
    joined = call(
        join_kernel,
        [("H", after(dq, attended)), ("H", keep), ("H", came), ("V", terms)],
        [("V", (CHIPS, 4, BLOCK, HS), BF16)],
    )
    result = exchange(joined)
    weight_part = lax.ppermute(result[:, 3], "ctx", CORE_SWAP)
    grad = ("R", (1, BLOCK, HEADS * HS), BF16)
    query_grad, key_grad, value_grad, weight_grad = call(
        unpack_kernel,
        [("S", core_ref), ("V", result), ("V", weight_part)],
        [grad, grad, grad, ("H", (HS, width), F32)],
    )
    return (attended, query_grad, key_grad, value_grad, weight_grad)


def solution(mesh):
    rows = P("fsdp", "ctx", None)
    return jax.shard_map(
        shards,
        mesh=mesh,
        in_specs=(rows, rows, rows, P("fsdp", None), P("fsdp"), P("fsdp", None), rows),
        out_specs=(rows, rows, rows, rows, P("fsdp", None)),
        check_vma=False,
    )
```

time: 141 us -> 198 us (1.40)
  Pallas kernels: 18.4 us -> 75.9 us
  local copies, waits for them, and re-layouts: 24.4 us -> 0.79 us
  waiting for transfers between devices: 25.4 us -> 45.1 us
  starting transfers between devices: 49.1 us -> 54.3 us
    pallas_call x8, Pallas kernels: 18.4 us -> 75.9 us  [call(): pl.pallas_call(body, out_shape=[SPACES[o[0]](o[1], o[2]) if o[0] in 'HR'...]
    unnamed x70 -> x20, local copies, waits for them, and re-layouts: 24.4 us -> 0.76 us
    ppermute x17, waiting for transfers between devices: 19 us -> 29.8 us  [the longest x7 20.2 us: gather(): piece = lax.ppermute(halves, 'fsdp', [(i, i ^ s) for i in range(8)])]
    all_to_all x1, waiting for transfers between devices: 0.01 us -> 6.04 us  [shards(): lax.all_to_all(after(terms, grads), ('ctx', 'fsdp'), split_axis=0, concat...]
    ppermute x1, starting transfers between devices: 0.09 us -> 3.86 us  [shards(): other = lax.ppermute(own, 'ctx', CORE_SWAP)]
    all_to_all x3, starting transfers between devices: 15.2 us -> 17.4 us  [exchange(): lax.all_to_all(operand, 'ctx', split_axis=0, concat_axis=0, tiled=True, a...]
    ppermute x1, starting transfers between devices: 2.1 us -> 0.09 us  [shards(): came = lax.ppermute(send, 'ctx', CORE_SWAP)]
  transfers between devices with their start and end apart: 25 -> 25, of which waited for: 10 -> 14; matrix products, arithmetic and copies ran while one was open for 1% -> 1% of each run, Pallas kernels for 11% -> 12%
where the time goes in v3:
time: 198 us
  Pallas kernels  75.9 us (38%)
  starting transfers between devices  54.3 us (27%)
  waiting for transfers between devices  45.1 us (23%)
  blocking collectives  18.7 us (9%)
    pallas_call x8, Pallas kernels, call(): pl.pallas_call(body, out_shape=[SPACES[o[0]](o[1], o[2]) if o[0] in 'HR'...  75.9 us
    ppermute x7, waiting for transfers between devices, gather(): piece = lax.ppermute(halves, 'fsdp', [(i, i ^ s) for i in range(8)])  20.2 us
    all_to_all x1, blocking collectives, exchange(): lax.all_to_all(operand, 'ctx', split_axis=0, concat_axis=0, tiled=True, a...  18.7 us
    all_to_all x3, starting transfers between devices, exchange(): lax.all_to_all(operand, 'ctx', split_axis=0, concat_axis=0, tiled=True, a...  17.4 us
    ppermute x7, starting transfers between devices, gather(): piece = lax.ppermute(halves, 'fsdp', [(i, i ^ s) for i in range(8)])  11.8 us
    ppermute x7, starting transfers between devices, gather(): return (piece, lax.ppermute(piece, 'ctx', CORE_SWAP))  6.83 us
    all_to_all x3, waiting for transfers between devices, exchange(): lax.all_to_all(operand, 'ctx', split_axis=0, concat_axis=0, tiled=True, a...  6.65 us
    all_to_all x1, waiting for transfers between devices, shards(): lax.all_to_all(after(terms, grads), ('ctx', 'fsdp'), split_axis=0, concat...  6.04 us
  transfers between devices with their start and end apart: 25, of which 14 were waited for; matrix products, arithmetic and copies ran while one was open for 1% of the time, Pallas kernels for 12%

profile of v3, /device:TPU:1, one launch (start us, length us, event | category | flops | bytes accessed | tf_op | source)
XLA Modules:
  0.0 197.5 jit_solution(5713556477999043984)
XLA Ops:
  0.6 49.2 %shard_map.110 = (bf16[8,3,128,128]{3,2,1,0:T(8,128)(2,1)}, bf16[128,1024]{1,0:T(8,128)(2,1)}, bf16[128,512]{1,0:T(8,128)(2,1)}, bf16[128,512]{1,0:T(8,128)(2,1)...) custom-call(s32[1]{0:T(128)} %bitcast.refs_0_, s32[1]{0:T(128)} %bitcast.2.refs_1_, bf16[1,128,1024]{2,1,0:T(8,128)(2,1)} %refs_2_.1, ...), custom_call_target="tpu_custom_call" | custom-call | bytes 2000000 | tf_op jit(solution)/shard_map/pallas_call | solution.py:112
  52.4 3.3 %collective-permute-start.1 = (bf16[128,1024]{1,0:T(8,128)(2,1)}, bf16[128,1024]{1,0:T(8,128)(2,1)S(1)}, u32[]{:S(2)}, u32[]{:S(2)}) collective-permute-start(bf16[128,1024]{1,0:T(8,128)(2,1)} %get-tuple-element.35), channel_id=1, source_target_pairs={{0,2},{1,3},{2,0},{3,1},{4,6},{5,7},{6,4},{7,5},{8,10},{9,11},{10,... | collective-permute-start | bytes 786440 | tf_op jit(solution)/shard_map/ppermute | solution.py:403
  55.7 6.7 %all-to-all-start = ((bf16[8,3,128,128]{3,2,1,0:T(8,128)(2,1)}), bf16[8,3,128,128]{3,2,1,0:T(8,128)(2,1)S(1)}, u32[]{:S(2)}, u32[]{:S(2)}) async-start(bf16[8,3,128,128]{3,2,1,0:T(8,128)(2,1)} %get-tuple-element.31), calls=%async_computation | async-start | bytes 1572864 | tf_op jit(solution)/shard_map/all_to_all | solution.py:359
  64.1 3.2 %collective-permute-done.1.refs_5_.refs_6_ = bf16[128,1024]{1,0:T(8,128)(2,1)S(1)} collective-permute-done((bf16[128,1024]{1,0:T(8,128)(2,1)}, bf16[128,1024]{1,0:T(8,128)(2,1)S(1)}, u32[]{:S(2)}, u32[]{:S(2)}) %collective-permute-start.1) | collective-permute-done | bytes 262176 | tf_op jit(solution)/shard_map/ppermute | solution.py:403
  69.3 3.6 %all-to-all-done.refs_1_ = bf16[8,3,128,128]{3,2,1,0:T(8,128)(2,1)S(1)} async-done(((bf16[8,3,128,128]{3,2,1,0:T(8,128)(2,1)}), bf16[8,3,128,128]{3,2,1,0:T(8,128)(2,1)S(1)}, u32[]{:S(2)}, u32[]{:S(2)}) %all-to-all-start) | async-done | bytes 786464 | tf_op jit(solution)/shard_map/all_to_all | solution.py:359
  72.9 3.9 %collective-permute-start.3 = (bf16[8,3,128,128]{3,2,1,0:T(8,128)(2,1)S(1)}, bf16[8,3,128,128]{3,2,1,0:T(8,128)(2,1)S(1)}, u32[]{:S(2)}, u32[]{:S(2)}) collective-permute-start(bf16[8,3,128,128]{3,2,1,0:T(8,128)(2,1)S(1)} %all-to-all-done.refs_1_), channel_id=1, source_target_pairs={{0,8},{8,0},{16,24},{24,16},{32,40},{40,32},{48,56},{56,48},{64,72... | collective-permute-start | bytes 2359304 | tf_op jit(solution)/shard_map/ppermute | solution.py:413
  78.7 4.0 %shard_map.111 = (bf16[8,2,128,128]{3,2,1,0:T(8,128)(2,1)}, f32[4,1,256]{2,1,0:T(1,128)}, bf16[8,128,128]{2,1,0:T(8,128)(2,1)}, bf16[2048,128]{1,0:T(8,128)(2,1)}, bf16[2048,128]{1,0:T(8,128)(2,1)}) custom-call(s32[1]{0:T(128)} %bitcast.refs_0_, bf16[8,3,128,128]{3,2,1,0:T(8,128)(2,1)S(1)} %all-to-all-done.refs_1_, ...), custom_call_target="tpu_custom_call" | custom-call | flops 671088640 | bytes 2000000 | tf_op jit(solution)/shard_map/pallas_call | solution.py:112
  82.6 3.5 %all-to-all-start.1 = ((bf16[8,2,128,128]{3,2,1,0:T(8,128)(2,1)}), bf16[8,2,128,128]{3,2,1,0:T(8,128)(2,1)S(1)}, u32[]{:S(2)}, u32[]{:S(2)}) async-start(bf16[8,2,128,128]{3,2,1,0:T(8,128)(2,1)} %get-tuple-element.34.refs_5_), calls=%async_computation.1 | async-start | bytes 1048576 | tf_op jit(solution)/shard_map/all_to_all | solution.py:359
  87.6 4.3 %collective-permute-start.6 = (bf16[128,1024]{1,0:T(8,128)(2,1)}, bf16[128,1024]{1,0:T(8,128)(2,1)S(1)}, u32[]{:S(2)}, u32[]{:S(2)}) collective-permute-start(bf16[128,1024]{1,0:T(8,128)(2,1)} %get-tuple-element.35), channel_id=1, source_target_pairs={{0,6},{1,7},{2,4},{3,5},{4,2},{5,3},{6,0},{7,1},{8,14},{9,15},{10,... | collective-permute-start | bytes 786440 | tf_op jit(solution)/shard_map/ppermute | solution.py:403
  92.7 3.1 %all-to-all-done.1.refs_2_.refs_4_ = bf16[8,2,128,128]{3,2,1,0:T(8,128)(2,1)S(1)} async-done(((bf16[8,2,128,128]{3,2,1,0:T(8,128)(2,1)}), bf16[8,2,128,128]{3,2,1,0:T(8,128)(2,1)S(1)}, u32[]{:S(2)}, u32[]{:S(2)}) %all-to-all-start.1) | async-done | bytes 524320 | tf_op jit(solution)/shard_map/all_to_all | solution.py:359
  100.2 3.3 %collective-permute-done.5.refs_8_.refs_9_ = bf16[128,1024]{1,0:T(8,128)(2,1)S(1)} collective-permute-done((bf16[128,1024]{1,0:T(8,128)(2,1)}, bf16[128,1024]{1,0:T(8,128)(2,1)S(1)}, u32[]{:S(2)}, u32[]{:S(2)}) %collective-permute-start.5) | collective-permute-done | bytes 262176 | tf_op jit(solution)/shard_map/ppermute | solution.py:403
  105.3 5.8 %collective-permute-done.6.refs_9_.refs_10_ = bf16[128,1024]{1,0:T(8,128)(2,1)S(1)} collective-permute-done((bf16[128,1024]{1,0:T(8,128)(2,1)}, bf16[128,1024]{1,0:T(8,128)(2,1)S(1)}, u32[]{:S(2)}, u32[]{:S(2)}) %collective-permute-start.6) | collective-permute-done | bytes 262176 | tf_op jit(solution)/shard_map/ppermute | solution.py:403
  112.5 5.7 %collective-permute-done.7.refs_10_.refs_11_ = bf16[128,1024]{1,0:T(8,128)(2,1)S(1)} collective-permute-done((bf16[128,1024]{1,0:T(8,128)(2,1)}, bf16[128,1024]{1,0:T(8,128)(2,1)S(1)}, u32[]{:S(2)}, u32[]{:S(2)}) %collective-permute-start.7) | collective-permute-done | bytes 262176 | tf_op jit(solution)/shard_map/ppermute | solution.py:403
  120.3 5.8 %shard_map.113 = bf16[8,128,128]{2,1,0:T(8,128)(2,1)} custom-call(s32[1]{0:T(128)} %bitcast.refs_0_, s32[1]{0:T(128)} %bitcast.1.refs_1_, f32[128,1]{1,0:T(8,128)S(1)} %fusion.refs_2_, bf16[1,128,2048]{2,1,0:T(8,128)(2,1)} %refs_3_.5, bf16[128,2048]{1,0:T(8,128)(2,1)} %refs_4_.3, bf16[128,1024]{1,0:T(8,128)(2,1)S(1)} %collective-permute-done.refs_4_.refs_5_, ...), custom_call_target="tpu_custom_call" | custom-call | flops 536870912 | bytes 2000000 | tf_op jit(solution)/shard_map/pallas_call | solution.py:112
  126.2 7.2 %all-to-all-start.2 = ((bf16[8,128,128]{2,1,0:T(8,128)(2,1)}), bf16[8,128,128]{2,1,0:T(8,128)(2,1)S(1)}, u32[]{:S(2)}, u32[]{:S(2)}) async-start(bf16[8,128,128]{2,1,0:T(8,128)(2,1)} %shard_map.113), calls=%async_computation.2 | async-start | bytes 524288 | tf_op jit(solution)/shard_map/all_to_all | solution.py:359
  137.6 4.7 %collective-permute-done.16.refs_1_ = bf16[128,512]{1,0:T(8,128)(2,1)S(1)} collective-permute-done((bf16[128,512]{1,0:T(8,128)(2,1)}, bf16[128,512]{1,0:T(8,128)(2,1)S(1)}, u32[]{:S(2)}, u32[]{:S(2)}) %collective-permute-start.16) | collective-permute-done | bytes 131104 | tf_op jit(solution)/shard_map/ppermute | solution.py:430
  142.3 3.6 %collective-permute-done.18.refs_3_ = bf16[128,512]{1,0:T(8,128)(2,1)S(1)} collective-permute-done((bf16[128,512]{1,0:T(8,128)(2,1)}, bf16[128,512]{1,0:T(8,128)(2,1)S(1)}, u32[]{:S(2)}, u32[]{:S(2)}) %collective-permute-start.18) | collective-permute-done | bytes 131104 | tf_op jit(solution)/shard_map/ppermute | solution.py:431
  146.0 3.4 %shard_map.115 = bf16[32,32,512]{2,1,0:T(8,128)(2,1)} custom-call(bf16[128,512]{1,0:T(8,128)(2,1)} %get-tuple-element.45.refs_0_, bf16[128,512]{1,0:T(8,128)(2,1)S(1)} %collective-permute-done.16.refs_1_, bf16[128,512]{1,0:T(8,128)(2,1)S(1)} %collective-permute-done.17.refs_2_, bf16[128,512]{1,0:T(8,128)(2,1)S(1)} %collective-permute-done.18.refs_3_, ...), custom_call_target="tpu_custom_call" | custom-call | flops 536870912 | bytes 2000000 | tf_op jit(solution)/shard_map/pallas_call | solution.py:112
  150.1 4.6 %all-to-all-start.3 = ((bf16[32,32,512]{2,1,0:T(8,128)(2,1)}), bf16[32,32,512]{2,1,0:T(8,128)(2,1)S(1)}, u32[]{:S(2)}, u32[]{:S(2)}) async-start(bf16[32,32,512]{2,1,0:T(8,128)(2,1)} %shard_map.115), calls=%async_computation.3 | async-start | bytes 2097152 | tf_op jit(solution)/shard_map/all_to_all | solution.py:453
  154.7 6.8 %shard_map.114 = (bf16[8,128,128]{2,1,0:T(8,128)(2,1)}, f32[8,2,128,128]{3,2,1,0:T(8,128)}, bf16[8,2,128,128]{3,2,1,0:T(8,128)(2,1)}) custom-call(s32[1]{0:T(128)} %bitcast.refs_0_, bf16[8,128,128]{2,1,0:T(8,128)(2,1)} %get-tuple-element.36.refs_1_, bf16[2048,128]{1,0:T(8,128)(2,1)} %get-tuple-element.37.refs_2_, bf16[8,128,128]{2,1,0:T(8,128)(2,1)} %copy-done.8, ...), custom_call_target="tpu_custom_call" | custom-call | flops 1677721600 | bytes 2000000 | tf_op jit(solution)/shard_map/pallas_call | solution.py:112
  161.7 3.1 %shard_map.112 = bf16[1,128,2048]{2,1,0:T(8,128)(2,1)} custom-call(s32[1]{0:T(128)} %bitcast.refs_0_, s32[1]{0:T(128)} %bitcast.1.refs_1_, bf16[8,2,128,128]{3,2,1,0:T(8,128)(2,1)S(1)} %all-to-all-done.1.refs_2_.refs_4_, bf16[128,2048]{1,0:T(8,128)(2,1)} %refs_4_.3, bf16[128,1024]{1,0:T(8,128)(2,1)S(1)} %collective-permute-done.refs_4_.refs_5_, ...), custom_call_target="tpu_custom_call" | custom-call | flops 536870912 | bytes 2000000 | tf_op jit(solution)/shard_map/pallas_call | solution.py:112
  164.8 6.0 %all-to-all-done.3.refs_3_ = bf16[32,32,512]{2,1,0:T(8,128)(2,1)S(1)} async-done(((bf16[32,32,512]{2,1,0:T(8,128)(2,1)}), bf16[32,32,512]{2,1,0:T(8,128)(2,1)S(1)}, u32[]{:S(2)}, u32[]{:S(2)}) %all-to-all-start.3) | async-done | bytes 1048608 | tf_op jit(solution)/shard_map/all_to_all | solution.py:453
  172.8 18.7 %all_to_all.25.refs_1_ = bf16[8,4,128,128]{3,2,1,0:T(8,128)(2,1)S(1)} all-to-all(bf16[8,4,128,128]{3,2,1,0:T(8,128)(2,1)S(1)} %shard_map.116), channel_id=1, replica_groups={{0,16,32,48,64,80,96,112},{8,24,40,56,72,88,104,120},{1,17,33,49,65,81,..., dimensions={0} | all-to-all | bytes 2097152 | tf_op jit(solution)/shard_map/all_to_all | solution.py:359
  191.5 3.0 %collective-permute-start.20 = (bf16[8,128,128]{2,1,0:T(8,128)(2,1)S(1)}, bf16[8,128,128]{2,1,0:T(8,128)(2,1)S(1)}, u32[]{:S(2)}, u32[]{:S(2)}) collective-permute-start(bf16[8,128,128]{2,1,0:T(8,128)(2,1)S(1)} %slice_bitcast_fusion), channel_id=1, source_target_pairs={{0,8},{8,0},{16,24},{24,16},{32,40},{40,32},{48,56},{56,48},{64,72... | collective-permute-start | bytes 786440 | tf_op jit(solution)/shard_map/ppermute | solution.py:491
  (61 shorter events, 29.4 us)
Async XLA Ops:
  49.8 14.2 %collective-permute-start = (bf16[128,1024]{1,0:T(8,128)(2,1)}, bf16[128,1024]{1,0:T(8,128)(2,1)S(1)}, u32[]{:S(2)}, u32[]{:S(2)}) collective-permute-start(bf16[128,1024]{1,0:T(8,128)(2,1)} %get-tuple-element.35), channel_id=1, source_target_pairs={{0,1},{1,0},{2,3},{3,2},{4,5},{5,4},{6,7},{7,6},{8,9},{9,8},{10,11... | collective-permute-start | bytes 786440 | tf_op jit(solution)/shard_map/ppermute | solution.py:403
  52.4 14.9 %collective-permute-start.1 = (bf16[128,1024]{1,0:T(8,128)(2,1)}, bf16[128,1024]{1,0:T(8,128)(2,1)S(1)}, u32[]{:S(2)}, u32[]{:S(2)}) collective-permute-start(bf16[128,1024]{1,0:T(8,128)(2,1)} %get-tuple-element.35), channel_id=1, source_target_pairs={{0,2},{1,3},{2,0},{3,1},{4,6},{5,7},{6,4},{7,5},{8,10},{9,11},{10,... | collective-permute-start | bytes 786440 | tf_op jit(solution)/shard_map/ppermute | solution.py:403
  55.7 13.6 %collective-permute-start.2 = (bf16[128,1024]{1,0:T(8,128)(2,1)}, bf16[128,1024]{1,0:T(8,128)(2,1)S(1)}, u32[]{:S(2)}, u32[]{:S(2)}) collective-permute-start(bf16[128,1024]{1,0:T(8,128)(2,1)} %get-tuple-element.35), channel_id=1, source_target_pairs={{0,3},{1,2},{2,1},{3,0},{4,7},{5,6},{6,5},{7,4},{8,11},{9,10},{10,... | collective-permute-start | bytes 786440 | tf_op jit(solution)/shard_map/ppermute | solution.py:403
  55.7 17.2 %all-to-all-start = ((bf16[8,3,128,128]{3,2,1,0:T(8,128)(2,1)}), bf16[8,3,128,128]{3,2,1,0:T(8,128)(2,1)S(1)}, u32[]{:S(2)}, u32[]{:S(2)}) async-start(bf16[8,3,128,128]{3,2,1,0:T(8,128)(2,1)} %get-tuple-element.31), calls=%async_computation | async-start | bytes 1572864 | tf_op jit(solution)/shard_map/all_to_all | solution.py:359
  72.9 5.8 %collective-permute-start.3 = (bf16[8,3,128,128]{3,2,1,0:T(8,128)(2,1)S(1)}, bf16[8,3,128,128]{3,2,1,0:T(8,128)(2,1)S(1)}, u32[]{:S(2)}, u32[]{:S(2)}) collective-permute-start(bf16[8,3,128,128]{3,2,1,0:T(8,128)(2,1)S(1)} %all-to-all-done.refs_1_), channel_id=1, source_target_pairs={{0,8},{8,0},{16,24},{24,16},{32,40},{40,32},{48,56},{56,48},{64,72... | collective-permute-start | bytes 2359304 | tf_op jit(solution)/shard_map/ppermute | solution.py:413
  76.7 10.9 %collective-permute-start.8 = (bf16[128,1024]{1,0:T(8,128)(2,1)S(1)}, bf16[128,1024]{1,0:T(8,128)(2,1)S(1)}, u32[]{:S(2)}, u32[]{:S(2)}) collective-permute-start(bf16[128,1024]{1,0:T(8,128)(2,1)S(1)} %collective-permute-done.refs_4_.refs_5_), channel_id=1, source_target_pairs={{0,8},{8,0},{16,24},{24,16},{32,40},{40,32},{48,56},{56,48},{64,72... | collective-permute-start | bytes 786440 | tf_op jit(solution)/shard_map/ppermute | solution.py:404
  76.7 15.2 %collective-permute-start.9 = (bf16[128,1024]{1,0:T(8,128)(2,1)S(1)}, bf16[128,1024]{1,0:T(8,128)(2,1)S(1)}, u32[]{:S(2)}, u32[]{:S(2)}) collective-permute-start(bf16[128,1024]{1,0:T(8,128)(2,1)S(1)} %collective-permute-done.1.refs_5_.refs_6_), channel_id=1, source_target_pairs={{0,8},{8,0},{16,24},{24,16},{32,40},{40,32},{48,56},{56,48},{64,72... | collective-permute-start | bytes 786440 | tf_op jit(solution)/shard_map/ppermute | solution.py:404
  82.6 13.1 %all-to-all-start.1 = ((bf16[8,2,128,128]{3,2,1,0:T(8,128)(2,1)}), bf16[8,2,128,128]{3,2,1,0:T(8,128)(2,1)S(1)}, u32[]{:S(2)}, u32[]{:S(2)}) async-start(bf16[8,2,128,128]{3,2,1,0:T(8,128)(2,1)} %get-tuple-element.34.refs_5_), calls=%async_computation.1 | async-start | bytes 1048576 | tf_op jit(solution)/shard_map/all_to_all | solution.py:359
  86.2 6.5 %collective-permute-start.10 = (bf16[128,1024]{1,0:T(8,128)(2,1)S(1)}, bf16[128,1024]{1,0:T(8,128)(2,1)S(1)}, u32[]{:S(2)}, u32[]{:S(2)}) collective-permute-start(bf16[128,1024]{1,0:T(8,128)(2,1)S(1)} %collective-permute-done.2.refs_6_.refs_7_), channel_id=1, source_target_pairs={{0,8},{8,0},{16,24},{24,16},{32,40},{40,32},{48,56},{56,48},{64,72... | collective-permute-start | bytes 786440 | tf_op jit(solution)/shard_map/ppermute | solution.py:404
  86.7 11.8 %collective-permute-start.4 = (bf16[128,1024]{1,0:T(8,128)(2,1)}, bf16[128,1024]{1,0:T(8,128)(2,1)S(1)}, u32[]{:S(2)}, u32[]{:S(2)}) collective-permute-start(bf16[128,1024]{1,0:T(8,128)(2,1)} %get-tuple-element.35), channel_id=1, source_target_pairs={{0,4},{1,5},{2,6},{3,7},{4,0},{5,1},{6,2},{7,3},{8,12},{9,13},{10,... | collective-permute-start | bytes 786440 | tf_op jit(solution)/shard_map/ppermute | solution.py:403
  87.1 16.5 %collective-permute-start.5 = (bf16[128,1024]{1,0:T(8,128)(2,1)}, bf16[128,1024]{1,0:T(8,128)(2,1)S(1)}, u32[]{:S(2)}, u32[]{:S(2)}) collective-permute-start(bf16[128,1024]{1,0:T(8,128)(2,1)} %get-tuple-element.35), channel_id=1, source_target_pairs={{0,5},{1,4},{2,7},{3,6},{4,1},{5,0},{6,3},{7,2},{8,13},{9,12},{10,... | collective-permute-start | bytes 786440 | tf_op jit(solution)/shard_map/ppermute | solution.py:403
  87.6 23.5 %collective-permute-start.6 = (bf16[128,1024]{1,0:T(8,128)(2,1)}, bf16[128,1024]{1,0:T(8,128)(2,1)S(1)}, u32[]{:S(2)}, u32[]{:S(2)}) collective-permute-start(bf16[128,1024]{1,0:T(8,128)(2,1)} %get-tuple-element.35), channel_id=1, source_target_pairs={{0,6},{1,7},{2,4},{3,5},{4,2},{5,3},{6,0},{7,1},{8,14},{9,15},{10,... | collective-permute-start | bytes 786440 | tf_op jit(solution)/shard_map/ppermute | solution.py:403
  91.9 26.2 %collective-permute-start.7 = (bf16[128,1024]{1,0:T(8,128)(2,1)}, bf16[128,1024]{1,0:T(8,128)(2,1)S(1)}, u32[]{:S(2)}, u32[]{:S(2)}) collective-permute-start(bf16[128,1024]{1,0:T(8,128)(2,1)} %get-tuple-element.35), channel_id=1, source_target_pairs={{0,7},{1,6},{2,5},{3,4},{4,3},{5,2},{6,1},{7,0},{8,15},{9,14},{10,... | collective-permute-start | bytes 786440 | tf_op jit(solution)/shard_map/ppermute | solution.py:403
  95.7 50.2 %collective-permute-start.19 = (bf16[8,2,128,128]{3,2,1,0:T(8,128)(2,1)S(1)}, bf16[8,2,128,128]{3,2,1,0:T(8,128)(2,1)}, u32[]{:S(2)}, u32[]{:S(2)}) collective-permute-start(bf16[8,2,128,128]{3,2,1,0:T(8,128)(2,1)S(1)} %all-to-all-done.1.refs_2_.refs_4_), channel_id=1, source_target_pairs={{0,8},{8,0},{16,24},{24,16},{32,40},{40,32},{48,56},{56,48},{64,72... | collective-permute-start | bytes 1572872 | tf_op jit(solution)/shard_map/ppermute | solution.py:443
  98.5 20.5 %collective-permute-start.11 = (bf16[128,1024]{1,0:T(8,128)(2,1)S(1)}, bf16[128,1024]{1,0:T(8,128)(2,1)S(1)}, u32[]{:S(2)}, u32[]{:S(2)}) collective-permute-start(bf16[128,1024]{1,0:T(8,128)(2,1)S(1)} %collective-permute-done.4.refs_7_.refs_8_), channel_id=1, source_target_pairs={{0,8},{8,0},{16,24},{24,16},{32,40},{40,32},{48,56},{56,48},{64,72... | collective-permute-start | bytes 786440 | tf_op jit(solution)/shard_map/ppermute | solution.py:404
  103.5 15.5 %collective-permute-start.12 = (bf16[128,1024]{1,0:T(8,128)(2,1)S(1)}, bf16[128,1024]{1,0:T(8,128)(2,1)}, u32[]{:S(2)}, u32[]{:S(2)}) collective-permute-start(bf16[128,1024]{1,0:T(8,128)(2,1)S(1)} %collective-permute-done.5.refs_8_.refs_9_), channel_id=1, source_target_pairs={{0,8},{8,0},{16,24},{24,16},{32,40},{40,32},{48,56},{56,48},{64,72... | collective-permute-start | bytes 786440 | tf_op jit(solution)/shard_map/ppermute | solution.py:404
  111.1 8.0 %collective-permute-start.13 = (bf16[128,1024]{1,0:T(8,128)(2,1)S(1)}, bf16[128,1024]{1,0:T(8,128)(2,1)}, u32[]{:S(2)}, u32[]{:S(2)}) collective-permute-start(bf16[128,1024]{1,0:T(8,128)(2,1)S(1)} %collective-permute-done.6.refs_9_.refs_10_), channel_id=1, source_target_pairs={{0,8},{8,0},{16,24},{24,16},{32,40},{40,32},{48,56},{56,48},{64,72... | collective-permute-start | bytes 786440 | tf_op jit(solution)/shard_map/ppermute | solution.py:404
  126.2 23.2 %all-to-all-start.2 = ((bf16[8,128,128]{2,1,0:T(8,128)(2,1)}), bf16[8,128,128]{2,1,0:T(8,128)(2,1)S(1)}, u32[]{:S(2)}, u32[]{:S(2)}) async-start(bf16[8,128,128]{2,1,0:T(8,128)(2,1)} %shard_map.113), calls=%async_computation.2 | async-start | bytes 524288 | tf_op jit(solution)/shard_map/all_to_all | solution.py:359
  133.4 8.9 %collective-permute-start.16 = (bf16[128,512]{1,0:T(8,128)(2,1)}, bf16[128,512]{1,0:T(8,128)(2,1)S(1)}, u32[]{:S(2)}, u32[]{:S(2)}) collective-permute-start(bf16[128,512]{1,0:T(8,128)(2,1)} %get-tuple-element.47), channel_id=1, source_target_pairs={{0,64},{8,72},{16,80},{24,88},{32,96},{40,104},{48,112},{56,120},{... | collective-permute-start | bytes 393224 | tf_op jit(solution)/shard_map/ppermute | solution.py:430
  136.4 5.9 %collective-permute-start.17 = (bf16[128,512]{1,0:T(8,128)(2,1)}, bf16[128,512]{1,0:T(8,128)(2,1)S(1)}, u32[]{:S(2)}, u32[]{:S(2)}) collective-permute-start(bf16[128,512]{1,0:T(8,128)(2,1)} %get-tuple-element.49), channel_id=1, source_target_pairs={{0,8},{8,0},{16,24},{24,16},{32,40},{40,32},{48,56},{56,48},{64,72... | collective-permute-start | bytes 393224 | tf_op jit(solution)/shard_map/ppermute | solution.py:432
  137.6 8.4 %collective-permute-start.18 = (bf16[128,512]{1,0:T(8,128)(2,1)}, bf16[128,512]{1,0:T(8,128)(2,1)S(1)}, u32[]{:S(2)}, u32[]{:S(2)}) collective-permute-start(bf16[128,512]{1,0:T(8,128)(2,1)} %get-tuple-element.51), channel_id=1, source_target_pairs={{0,72},{8,64},{16,88},{24,80},{32,104},{40,96},{48,120},{56,112},{... | collective-permute-start | bytes 393224 | tf_op jit(solution)/shard_map/ppermute | solution.py:431
  150.1 20.8 %all-to-all-start.3 = ((bf16[32,32,512]{2,1,0:T(8,128)(2,1)}), bf16[32,32,512]{2,1,0:T(8,128)(2,1)S(1)}, u32[]{:S(2)}, u32[]{:S(2)}) async-start(bf16[32,32,512]{2,1,0:T(8,128)(2,1)} %shard_map.115), calls=%async_computation.3 | async-start | bytes 2097152 | tf_op jit(solution)/shard_map/all_to_all | solution.py:453
  161.6 3.2 %collective-permute-start.15 = (bf16[8,2,128,128]{3,2,1,0:T(8,128)(2,1)}, bf16[8,2,128,128]{3,2,1,0:T(8,128)(2,1)}, u32[]{:S(2)}, u32[]{:S(2)}) collective-permute-start(bf16[8,2,128,128]{3,2,1,0:T(8,128)(2,1)} %get-tuple-element.44), channel_id=1, source_target_pairs={{0,8},{8,0},{16,24},{24,16},{32,40},{40,32},{48,56},{56,48},{64,72... | collective-permute-start | bytes 1572872 | tf_op jit(solution)/shard_map/ppermute | solution.py:475
  191.5 4.2 %collective-permute-start.20 = (bf16[8,128,128]{2,1,0:T(8,128)(2,1)S(1)}, bf16[8,128,128]{2,1,0:T(8,128)(2,1)S(1)}, u32[]{:S(2)}, u32[]{:S(2)}) collective-permute-start(bf16[8,128,128]{2,1,0:T(8,128)(2,1)S(1)} %slice_bitcast_fusion), channel_id=1, source_target_pairs={{0,8},{8,0},{16,24},{24,16},{32,40},{40,32},{48,56},{56,48},{64,72... | collective-permute-start | bytes 786440 | tf_op jit(solution)/shard_map/ppermute | solution.py:491
  (11 other events, 96.1 us)

commit v4 on v3

--- a/solution.py
+++ b/solution.py
@@ -127,7 +127,7 @@
 
 
 def pack_kernel(ins, outs, scratch, sems):
-    core_ref, high_ref, q_ref, k_ref, v_ref, w_ref, up_ref = ins
+    core_ref, high_ref, *data = ins
     out_ref, half_ref, keep_ref, core_out_ref, pair_ref, diag_ref = outs
     core, high = core_ref[0], high_ref[0]
     half = half_ref.shape[1]
@@ -138,12 +138,13 @@
         copies.append(pltpu.make_async_copy(src, dst, next(sems)))
         copies[-1].start()
 
-    for a in range(HEADS):
-        cols = pl.ds(a * HS, HS)
-        copy(q_ref.at[0, :, cols], out_ref.at[a, 0])
-        copy(k_ref.at[0, :, cols], out_ref.at[a, 1])
-        copy(v_ref.at[0, :, cols], out_ref.at[a, 2])
+    for i in range(3):
+        ref = data[i].get()
+        for a in range(HEADS):
+            copy(ref.at[:, pl.ds(a * HS, HS)], out_ref.at[a, i])
+    w_ref = data[3].get()
     copy(w_ref.at[:, pl.ds(pl.multiple_of(core * half, half), half)], half_ref)
+    up_ref = data[4].get()
     for ref, x, c in (
         (keep_ref, high, core),
         (core_out_ref, high, 1 - core),
@@ -151,7 +152,7 @@
         (diag_ref, 1 - high, 1 - core),
     ):
         at = pl.multiple_of(x * half + c * quarter, quarter)
-        copy(up_ref.at[0, :, pl.ds(at, quarter)], ref)
+        copy(up_ref.at[:, pl.ds(at, quarter)], ref)
     return copies
 
 
@@ -272,7 +273,7 @@
     up_mine = up_ref[:, pl.ds(pl.multiple_of(core * half, half), half)]
     up_other = up_ref[:, pl.ds(pl.multiple_of((1 - core) * half, half), half)]
     for s in range(1, HEADS):
-        total = dot_nt(up_mine, mine[s - 1].get()[...]) + dot_nt(up_other, other[s - 1].get()[...])
+        total = dot_nt(up_mine, mine[s - 1][...]) + dot_nt(up_other, other[s - 1][...])
         at = jnp.bitwise_xor(row, s)
         out.ref[at] = (total * valid).astype(BF16)
         out.push(at)
@@ -288,7 +289,6 @@
     ctx = jnp.concatenate([ctx_ref[jnp.bitwise_xor(row, s)] for s in range(HEADS)], axis=1)
     step = half // 4
     for side, parts in ((core, mine), (1 - core, other)):
-        parts = [part.get() for part in parts]
         for n in range(4):
             at = pl.ds(pl.multiple_of(side * half + n * step, step), step)
             cols = slice(n * step, (n + 1) * step)
@@ -380,8 +380,8 @@
     packed, own_half, up_keep, up_core, up_pair, up_diag = call(
         pack_kernel,
         [
-            ("S", core_ref), ("S", high_ref), ("R", query_rows), ("R", key_rows),
-            ("R", value_rows), ("R", out_weight), ("R", upstream),
+            ("S", core_ref), ("S", high_ref), ("H", query_rows, 0), ("H", key_rows, 0),
+            ("H", value_rows, 0), ("H", out_weight), ("H", upstream, 0),
         ],
         [("R", (HEADS, 3, BLOCK, HS), BF16), ("R", (HS, half), BF16), part, part, part, part],
     )
@@ -399,17 +399,19 @@
     rows_here = index * BLOCK + jnp.arange(BLOCK, dtype=jnp.int32)
     valid_here = (rows_here < valid_len).astype(F32)[:, None]
 
-    def gather(halves, s):
-        piece = lax.ppermute(halves, "fsdp", [(i, i ^ s) for i in range(8)])
-        return piece, lax.ppermute(piece, "ctx", CORE_SWAP)
-
-    pieces = [gather(own_half, s) for s in (1, 2, 3)]
-    own = after(own, end, valid, valid_here, *[one for one, _ in pieces])
-    own_half = after(own_half, own)
-    pieces += [gather(own_half, s) for s in (4, 5, 6, 7)]
-    mine = [("A", one) for one, _ in pieces]
-    other_half = [("A", one) for _, one in pieces]
-
+    def step(value, s):
+        return lax.ppermute(value, "fsdp", [(i, i ^ s) for i in range(8)])
+
+    own_half = after(own_half, end, valid, valid_here)
+    over = step(own_half, 4)
+    one, three = step(own_half, 1), step(own_half, 3)
+    over_one, over_three = step(over, 1), step(over, 3)
+    two, over_two = step(one, 3), step(over_three, 1)
+    pieces = [one, two, three, over, over_one, over_two, over_three]
+    mine = [("V", piece) for piece in pieces]
+    other_half = [("V", lax.ppermute(piece, "ctx", CORE_SWAP)) for piece in pieces]
+
+    own = after(own, end, valid, valid_here, over, one, three)
     other = lax.ppermute(own, "ctx", CORE_SWAP)
     pairs = 4 * TILE * SPAN * 5 // 2
     rows = ("H", (LEN, HS), BF16)

time: 198 us -> 136 us (0.69)
  Pallas kernels: 75.9 us -> 29.1 us
  waiting for transfers between devices: 45.1 us -> 31.3 us
    pallas_call x8, Pallas kernels: 75.9 us -> 29.1 us  [call(): pl.pallas_call(body, out_shape=[SPACES[o[0]](o[1], o[2]) if o[0] in 'HR'...]
    ppermute x14, waiting for transfers between devices: 21.5 us -> 14.4 us  [the longest x7 13.1 us: step(): return lax.ppermute(value, 'fsdp', [(i, i ^ s) for i in range(8)])]
    ppermute x14, starting transfers between devices: 18.6 us -> 13.2 us  [the longest x7 9.74 us: step(): return lax.ppermute(value, 'fsdp', [(i, i ^ s) for i in range(8)])]
    all_to_all x3, waiting for transfers between devices: 6.65 us -> 2.42 us  [exchange(): lax.all_to_all(operand, 'ctx', split_axis=0, concat_axis=0, tiled=True, a...]
    all_to_all x3, starting transfers between devices: 17.4 us -> 21.5 us  [exchange(): lax.all_to_all(operand, 'ctx', split_axis=0, concat_axis=0, tiled=True, a...]
    all_to_all x1, starting transfers between devices: 4.58 us -> 6.9 us  [shards(): lax.all_to_all(after(terms, grads), ('ctx', 'fsdp'), split_axis=0, concat...]
    ppermute x1, starting transfers between devices: 3.86 us -> 1.63 us  [shards(): other = lax.ppermute(own, 'ctx', CORE_SWAP)]
  transfers between devices with their start and end apart: 25 -> 25, of which waited for: 14 -> 10; matrix products, arithmetic and copies ran while one was open for 1% -> 1% of each run, Pallas kernels for 12% -> 17%
where the time goes in v4:
time: 136 us
  starting transfers between devices  52.9 us (39%)
  waiting for transfers between devices  31.3 us (23%)
  Pallas kernels  29.1 us (21%)
  blocking collectives  18.7 us (14%)
  between operations  1.76 us (1%)
    pallas_call x8, Pallas kernels, call(): pl.pallas_call(body, out_shape=[SPACES[o[0]](o[1], o[2]) if o[0] in 'HR'...  29.1 us
    all_to_all x3, starting transfers between devices, exchange(): lax.all_to_all(operand, 'ctx', split_axis=0, concat_axis=0, tiled=True, a...  21.5 us
    all_to_all x1, blocking collectives, exchange(): lax.all_to_all(operand, 'ctx', split_axis=0, concat_axis=0, tiled=True, a...  18.7 us
    ppermute x7, waiting for transfers between devices, step(): return lax.ppermute(value, 'fsdp', [(i, i ^ s) for i in range(8)])  13.1 us
    ppermute x7, starting transfers between devices, step(): return lax.ppermute(value, 'fsdp', [(i, i ^ s) for i in range(8)])  9.74 us
    all_to_all x1, starting transfers between devices, shards(): lax.all_to_all(after(terms, grads), ('ctx', 'fsdp'), split_axis=0, concat...  6.9 us
    all_to_all x1, waiting for transfers between devices, shards(): lax.all_to_all(after(terms, grads), ('ctx', 'fsdp'), split_axis=0, concat...  4.98 us
    ppermute x1, waiting for transfers between devices, shards(): up_pair = lax.ppermute(after(up_pair, context), 'ctx', PAIR_SWAP)  4.74 us
  transfers between devices with their start and end apart: 25, of which 10 were waited for; matrix products, arithmetic and copies ran while one was open for 1% of the time, Pallas kernels for 17%

profile of v4, /device:TPU:1, one launch (start us, length us, event | category | flops | bytes accessed | tf_op | source)
XLA Modules:
  0.0 135.5 jit_solution(15041001076930433481)
XLA Ops:
  0.6 2.6 %shard_map.110 = (bf16[8,3,128,128]{3,2,1,0:T(8,128)(2,1)}, bf16[128,1024]{1,0:T(8,128)(2,1)}, bf16[128,512]{1,0:T(8,128)(2,1)}, bf16[128,512]{1,0:T(8,128)(2,1)...) custom-call(s32[1]{0:T(128)} %bitcast.refs_0_, s32[1]{0:T(128)} %bitcast.2.refs_1_, bf16[1,128,1024]{2,1,0:T(8,128)(2,1)} %refs_2_.1, ...), custom_call_target="tpu_custom_call" | custom-call | bytes 2000000 | tf_op jit(solution)/shard_map/pallas_call | solution.py:112
  3.3 7.6 %all-to-all-start = ((bf16[8,3,128,128]{3,2,1,0:T(8,128)(2,1)}), bf16[8,3,128,128]{3,2,1,0:T(8,128)(2,1)S(1)}, u32[]{:S(2)}, u32[]{:S(2)}) async-start(bf16[8,3,128,128]{3,2,1,0:T(8,128)(2,1)} %get-tuple-element.31), calls=%async_computation | async-start | bytes 1572864 | tf_op jit(solution)/shard_map/all_to_all | solution.py:359
  14.7 2.2 %collective-permute-start.2 = (bf16[128,1024]{1,0:T(8,128)(2,1)S(1)}, bf16[128,1024]{1,0:T(8,128)(2,1)S(1)}, u32[]{:S(2)}, u32[]{:S(2)}) collective-permute-start(bf16[128,1024]{1,0:T(8,128)(2,1)S(1)} %copy-done.10), channel_id=1, source_target_pairs={{0,3},{1,2},{2,1},{3,0},{4,7},{5,6},{6,5},{7,4},{8,11},{9,10},{10,... | collective-permute-start | bytes 786440 | tf_op jit(solution)/shard_map/ppermute | solution.py:403
  16.9 8.6 %collective-permute-done.refs_7_.refs_8_ = bf16[128,1024]{1,0:T(8,128)(2,1)S(1)} collective-permute-done((bf16[128,1024]{1,0:T(8,128)(2,1)S(1)}, bf16[128,1024]{1,0:T(8,128)(2,1)S(1)}, u32[]{:S(2)}, u32[]{:S(2)}) %collective-permute-start) | collective-permute-done | bytes 262176 | tf_op jit(solution)/shard_map/ppermute | solution.py:403
  27.2 3.8 %collective-permute-start.4 = (bf16[128,1024]{1,0:T(8,128)(2,1)S(1)}, bf16[128,1024]{1,0:T(8,128)(2,1)S(1)}, u32[]{:S(2)}, u32[]{:S(2)}) collective-permute-start(bf16[128,1024]{1,0:T(8,128)(2,1)S(1)} %collective-permute-done.1.refs_4_.refs_5_), channel_id=1, source_target_pairs={{0,3},{1,2},{2,1},{3,0},{4,7},{5,6},{6,5},{7,4},{8,11},{9,10},{10,... | collective-permute-start | bytes 786440 | tf_op jit(solution)/shard_map/ppermute | solution.py:403
  31.0 4.0 %shard_map.111 = (bf16[8,2,128,128]{3,2,1,0:T(8,128)(2,1)}, f32[4,1,256]{2,1,0:T(1,128)}, bf16[8,128,128]{2,1,0:T(8,128)(2,1)}, bf16[2048,128]{1,0:T(8,128)(2,1)}, bf16[2048,128]{1,0:T(8,128)(2,1)}) custom-call(s32[1]{0:T(128)} %bitcast.refs_0_, bf16[8,3,128,128]{3,2,1,0:T(8,128)(2,1)S(1)} %all-to-all-done.refs_1_, ...), custom_call_target="tpu_custom_call" | custom-call | flops 671088640 | bytes 2000000 | tf_op jit(solution)/shard_map/pallas_call | solution.py:112
  35.0 7.3 %all-to-all-start.1 = ((bf16[8,2,128,128]{3,2,1,0:T(8,128)(2,1)}), bf16[8,2,128,128]{3,2,1,0:T(8,128)(2,1)S(1)}, u32[]{:S(2)}, u32[]{:S(2)}) async-start(bf16[8,2,128,128]{3,2,1,0:T(8,128)(2,1)} %get-tuple-element.35.refs_5_), calls=%async_computation.1 | async-start | bytes 1048576 | tf_op jit(solution)/shard_map/all_to_all | solution.py:359
  45.3 4.1 %collective-permute-done.5.refs_8_.refs_9_ = bf16[128,1024]{1,0:T(8,128)(2,1)S(1)} collective-permute-done((bf16[128,1024]{1,0:T(8,128)(2,1)S(1)}, bf16[128,1024]{1,0:T(8,128)(2,1)S(1)}, u32[]{:S(2)}, u32[]{:S(2)}) %collective-permute-start.5) | collective-permute-done | bytes 262176 | tf_op jit(solution)/shard_map/ppermute | solution.py:403
  49.4 2.4 %all-to-all-done.1.refs_2_.refs_4_ = bf16[8,2,128,128]{3,2,1,0:T(8,128)(2,1)S(1)} async-done(((bf16[8,2,128,128]{3,2,1,0:T(8,128)(2,1)}), bf16[8,2,128,128]{3,2,1,0:T(8,128)(2,1)S(1)}, u32[]{:S(2)}, u32[]{:S(2)}) %all-to-all-start.1) | async-done | bytes 524320 | tf_op jit(solution)/shard_map/all_to_all | solution.py:359
  51.8 2.3 %collective-permute-start.19 = (bf16[8,2,128,128]{3,2,1,0:T(8,128)(2,1)S(1)}, bf16[8,2,128,128]{3,2,1,0:T(8,128)(2,1)}, u32[]{:S(2)}, u32[]{:S(2)}) collective-permute-start(bf16[8,2,128,128]{3,2,1,0:T(8,128)(2,1)S(1)} %all-to-all-done.1.refs_2_.refs_4_), channel_id=1, source_target_pairs={{0,8},{8,0},{16,24},{24,16},{32,40},{40,32},{48,56},{56,48},{64,72... | collective-permute-start | bytes 1572872 | tf_op jit(solution)/shard_map/ppermute | solution.py:445
  57.9 4.6 %shard_map.113 = bf16[8,128,128]{2,1,0:T(8,128)(2,1)} custom-call(s32[1]{0:T(128)} %bitcast.refs_0_, s32[1]{0:T(128)} %bitcast.1.refs_1_, f32[128,1]{1,0:T(8,128)S(1)} %fusion.refs_2_, bf16[1,128,2048]{2,1,0:T(8,128)(2,1)} %refs_3_.5, bf16[128,2048]{1,0:T(8,128)(2,1)} %refs_4_.3, bf16[128,1024]{1,0:T(8,128)(2,1)S(1)} %collective-permute-done.1.refs_4_.refs_5_, ...), custom_call_target="tpu_custom_call" | custom-call | flops 536870912 | bytes 2000000 | tf_op jit(solution)/shard_map/pallas_call | solution.py:112
  62.6 6.7 %all-to-all-start.2 = ((bf16[8,128,128]{2,1,0:T(8,128)(2,1)}), bf16[8,128,128]{2,1,0:T(8,128)(2,1)S(1)}, u32[]{:S(2)}, u32[]{:S(2)}) async-start(bf16[8,128,128]{2,1,0:T(8,128)(2,1)} %shard_map.113), calls=%async_computation.2 | async-start | bytes 524288 | tf_op jit(solution)/shard_map/all_to_all | solution.py:359
  69.3 3.0 %collective-permute-start.16 = (bf16[128,512]{1,0:T(8,128)(2,1)}, bf16[128,512]{1,0:T(8,128)(2,1)S(1)}, u32[]{:S(2)}, u32[]{:S(2)}) collective-permute-start(bf16[128,512]{1,0:T(8,128)(2,1)} %get-tuple-element.47), channel_id=1, source_target_pairs={{0,64},{8,72},{16,80},{24,88},{32,96},{40,104},{48,112},{56,120},{... | collective-permute-start | bytes 393224 | tf_op jit(solution)/shard_map/ppermute | solution.py:432
  73.4 4.7 %collective-permute-done.16.refs_1_ = bf16[128,512]{1,0:T(8,128)(2,1)S(1)} collective-permute-done((bf16[128,512]{1,0:T(8,128)(2,1)}, bf16[128,512]{1,0:T(8,128)(2,1)S(1)}, u32[]{:S(2)}, u32[]{:S(2)}) %collective-permute-start.16) | collective-permute-done | bytes 131104 | tf_op jit(solution)/shard_map/ppermute | solution.py:432
  78.2 3.6 %collective-permute-done.18.refs_3_ = bf16[128,512]{1,0:T(8,128)(2,1)S(1)} collective-permute-done((bf16[128,512]{1,0:T(8,128)(2,1)}, bf16[128,512]{1,0:T(8,128)(2,1)S(1)}, u32[]{:S(2)}, u32[]{:S(2)}) %collective-permute-start.18) | collective-permute-done | bytes 131104 | tf_op jit(solution)/shard_map/ppermute | solution.py:433
  81.8 3.4 %shard_map.115 = bf16[32,32,512]{2,1,0:T(8,128)(2,1)} custom-call(bf16[128,512]{1,0:T(8,128)(2,1)} %get-tuple-element.45.refs_0_, bf16[128,512]{1,0:T(8,128)(2,1)S(1)} %collective-permute-done.16.refs_1_, bf16[128,512]{1,0:T(8,128)(2,1)S(1)} %collective-permute-done.17.refs_2_, bf16[128,512]{1,0:T(8,128)(2,1)S(1)} %collective-permute-done.18.refs_3_, ...), custom_call_target="tpu_custom_call" | custom-call | flops 536870912 | bytes 2000000 | tf_op jit(solution)/shard_map/pallas_call | solution.py:112
  85.9 6.9 %all-to-all-start.3 = ((bf16[32,32,512]{2,1,0:T(8,128)(2,1)}), bf16[32,32,512]{2,1,0:T(8,128)(2,1)S(1)}, u32[]{:S(2)}, u32[]{:S(2)}) async-start(bf16[32,32,512]{2,1,0:T(8,128)(2,1)} %shard_map.115), calls=%async_computation.3 | async-start | bytes 2097152 | tf_op jit(solution)/shard_map/all_to_all | solution.py:455
  92.9 6.8 %shard_map.114 = (bf16[8,128,128]{2,1,0:T(8,128)(2,1)}, f32[8,2,128,128]{3,2,1,0:T(8,128)}, bf16[8,2,128,128]{3,2,1,0:T(8,128)(2,1)}) custom-call(s32[1]{0:T(128)} %bitcast.refs_0_, bf16[8,128,128]{2,1,0:T(8,128)(2,1)} %get-tuple-element.36.refs_1_, bf16[2048,128]{1,0:T(8,128)(2,1)} %get-tuple-element.37.refs_2_, bf16[8,128,128]{2,1,0:T(8,128)(2,1)} %copy-done.8, ...), custom_call_target="tpu_custom_call" | custom-call | flops 1677721600 | bytes 2000000 | tf_op jit(solution)/shard_map/pallas_call | solution.py:112
  99.9 4.0 %shard_map.112 = bf16[1,128,2048]{2,1,0:T(8,128)(2,1)} custom-call(s32[1]{0:T(128)} %bitcast.refs_0_, s32[1]{0:T(128)} %bitcast.1.refs_1_, bf16[8,2,128,128]{3,2,1,0:T(8,128)(2,1)S(1)} %all-to-all-done.1.refs_2_.refs_4_, bf16[128,2048]{1,0:T(8,128)(2,1)} %refs_4_.3, bf16[128,1024]{1,0:T(8,128)(2,1)S(1)} %collective-permute-done.1.refs_4_.refs_5_, ...), custom_call_target="tpu_custom_call" | custom-call | flops 536870912 | bytes 2000000 | tf_op jit(solution)/shard_map/pallas_call | solution.py:112
  103.9 5.0 %all-to-all-done.3.refs_3_ = bf16[32,32,512]{2,1,0:T(8,128)(2,1)S(1)} async-done(((bf16[32,32,512]{2,1,0:T(8,128)(2,1)}), bf16[32,32,512]{2,1,0:T(8,128)(2,1)S(1)}, u32[]{:S(2)}, u32[]{:S(2)}) %all-to-all-start.3) | async-done | bytes 1048608 | tf_op jit(solution)/shard_map/all_to_all | solution.py:455
  108.9 2.0 %shard_map.116 = bf16[8,4,128,128]{3,2,1,0:T(8,128)(2,1)S(1)} custom-call(bf16[8,128,128]{2,1,0:T(8,128)(2,1)} %get-tuple-element.42.refs_0_, f32[8,2,128,128]{3,2,1,0:T(8,128)} %get-tuple-element.43.refs_1_, bf16[8,2,128,128]{3,2,1,0:T(8,128)(2,1)} %collective-permute-done.15.refs_2_, bf16[32,32,512]{2,1,0:T(8,128)(2,1)S(1)} %all-to-all-done.3.refs_3_), custom_call_target="tpu_custom_call" | custom-call | bytes 2000000 | tf_op jit(solution)/shard_map/pallas_call | solution.py:112
  110.8 18.7 %all_to_all.25.refs_1_ = bf16[8,4,128,128]{3,2,1,0:T(8,128)(2,1)S(1)} all-to-all(bf16[8,4,128,128]{3,2,1,0:T(8,128)(2,1)S(1)} %shard_map.116), channel_id=1, replica_groups={{0,16,32,48,64,80,96,112},{8,24,40,56,72,88,104,120},{1,17,33,49,65,81,..., dimensions={0} | all-to-all | bytes 2097152 | tf_op jit(solution)/shard_map/all_to_all | solution.py:359
  129.5 3.0 %collective-permute-start.20 = (bf16[8,128,128]{2,1,0:T(8,128)(2,1)S(1)}, bf16[8,128,128]{2,1,0:T(8,128)(2,1)S(1)}, u32[]{:S(2)}, u32[]{:S(2)}) collective-permute-start(bf16[8,128,128]{2,1,0:T(8,128)(2,1)S(1)} %slice_bitcast_fusion), channel_id=1, source_target_pairs={{0,8},{8,0},{16,24},{24,16},{32,40},{40,32},{48,56},{56,48},{64,72... | collective-permute-start | bytes 786440 | tf_op jit(solution)/shard_map/ppermute | solution.py:493
  133.7 1.7 %shard_map.117 = (bf16[1,128,1024]{2,1,0:T(8,128)(2,1)}, bf16[1,128,1024]{2,1,0:T(8,128)(2,1)}, bf16[1,128,1024]{2,1,0:T(8,128)(2,1)}, f32[128,2048]{1,0:T(8,128)}) custom-call(s32[1]{0:T(128)} %bitcast.refs_0_, bf16[8,4,128,128]{3,2,1,0:T(8,128)(2,1)S(1)} %all_to_all.25.refs_1_, bf16[8,128,128]{2,1,0:T(8,128)(2,1)S(1)} %collective-permute-done.20.refs_2_), custom_call_target="tpu_custom_call" | custom-call | bytes 2000000 | tf_op jit(solution)/shard_map/pallas_call | solution.py:112
  (63 shorter events, 14.7 us)
Async XLA Ops:
  3.3 22.3 %all-to-all-start = ((bf16[8,3,128,128]{3,2,1,0:T(8,128)(2,1)}), bf16[8,3,128,128]{3,2,1,0:T(8,128)(2,1)S(1)}, u32[]{:S(2)}, u32[]{:S(2)}) async-start(bf16[8,3,128,128]{3,2,1,0:T(8,128)(2,1)} %get-tuple-element.31), calls=%async_computation | async-start | bytes 1572864 | tf_op jit(solution)/shard_map/all_to_all | solution.py:359
  12.7 12.9 %collective-permute-start = (bf16[128,1024]{1,0:T(8,128)(2,1)S(1)}, bf16[128,1024]{1,0:T(8,128)(2,1)S(1)}, u32[]{:S(2)}, u32[]{:S(2)}) collective-permute-start(bf16[128,1024]{1,0:T(8,128)(2,1)S(1)} %copy-done.10), channel_id=1, source_target_pairs={{0,4},{1,5},{2,6},{3,7},{4,0},{5,1},{6,2},{7,3},{8,12},{9,13},{10,... | collective-permute-start | bytes 786440 | tf_op jit(solution)/shard_map/ppermute | solution.py:403
  13.1 12.5 %collective-permute-start.1 = (bf16[128,1024]{1,0:T(8,128)(2,1)S(1)}, bf16[128,1024]{1,0:T(8,128)(2,1)S(1)}, u32[]{:S(2)}, u32[]{:S(2)}) collective-permute-start(bf16[128,1024]{1,0:T(8,128)(2,1)S(1)} %copy-done.10), channel_id=1, source_target_pairs={{0,1},{1,0},{2,3},{3,2},{4,5},{5,4},{6,7},{7,6},{8,9},{9,8},{10,11... | collective-permute-start | bytes 786440 | tf_op jit(solution)/shard_map/ppermute | solution.py:403
  14.7 10.9 %collective-permute-start.2 = (bf16[128,1024]{1,0:T(8,128)(2,1)S(1)}, bf16[128,1024]{1,0:T(8,128)(2,1)S(1)}, u32[]{:S(2)}, u32[]{:S(2)}) collective-permute-start(bf16[128,1024]{1,0:T(8,128)(2,1)S(1)} %copy-done.10), channel_id=1, source_target_pairs={{0,3},{1,2},{2,1},{3,0},{4,7},{5,6},{6,5},{7,4},{8,11},{9,10},{10,... | collective-permute-start | bytes 786440 | tf_op jit(solution)/shard_map/ppermute | solution.py:403
  25.6 5.4 %collective-permute-start.3 = (bf16[8,3,128,128]{3,2,1,0:T(8,128)(2,1)S(1)}, bf16[8,3,128,128]{3,2,1,0:T(8,128)(2,1)S(1)}, u32[]{:S(2)}, u32[]{:S(2)}) collective-permute-start(bf16[8,3,128,128]{3,2,1,0:T(8,128)(2,1)S(1)} %all-to-all-done.refs_1_), channel_id=1, source_target_pairs={{0,8},{8,0},{16,24},{24,16},{32,40},{40,32},{48,56},{56,48},{64,72... | collective-permute-start | bytes 2359304 | tf_op jit(solution)/shard_map/ppermute | solution.py:415
  27.2 15.9 %collective-permute-start.4 = (bf16[128,1024]{1,0:T(8,128)(2,1)S(1)}, bf16[128,1024]{1,0:T(8,128)(2,1)S(1)}, u32[]{:S(2)}, u32[]{:S(2)}) collective-permute-start(bf16[128,1024]{1,0:T(8,128)(2,1)S(1)} %collective-permute-done.1.refs_4_.refs_5_), channel_id=1, source_target_pairs={{0,3},{1,2},{2,1},{3,0},{4,7},{5,6},{6,5},{7,4},{8,11},{9,10},{10,... | collective-permute-start | bytes 786440 | tf_op jit(solution)/shard_map/ppermute | solution.py:403
  31.0 12.6 %collective-permute-start.6 = (bf16[128,1024]{1,0:T(8,128)(2,1)S(1)}, bf16[128,1024]{1,0:T(8,128)(2,1)S(1)}, u32[]{:S(2)}, u32[]{:S(2)}) collective-permute-start(bf16[128,1024]{1,0:T(8,128)(2,1)S(1)} %collective-permute-done.refs_7_.refs_8_), channel_id=1, source_target_pairs={{0,3},{1,2},{2,1},{3,0},{4,7},{5,6},{6,5},{7,4},{8,11},{9,10},{10,... | collective-permute-start | bytes 786440 | tf_op jit(solution)/shard_map/ppermute | solution.py:403
  35.0 16.8 %all-to-all-start.1 = ((bf16[8,2,128,128]{3,2,1,0:T(8,128)(2,1)}), bf16[8,2,128,128]{3,2,1,0:T(8,128)(2,1)S(1)}, u32[]{:S(2)}, u32[]{:S(2)}) async-start(bf16[8,2,128,128]{3,2,1,0:T(8,128)(2,1)} %get-tuple-element.35.refs_5_), calls=%async_computation.1 | async-start | bytes 1048576 | tf_op jit(solution)/shard_map/all_to_all | solution.py:359
  42.3 7.1 %collective-permute-start.5 = (bf16[128,1024]{1,0:T(8,128)(2,1)S(1)}, bf16[128,1024]{1,0:T(8,128)(2,1)S(1)}, u32[]{:S(2)}, u32[]{:S(2)}) collective-permute-start(bf16[128,1024]{1,0:T(8,128)(2,1)S(1)} %collective-permute-done.refs_7_.refs_8_), channel_id=1, source_target_pairs={{0,1},{1,0},{2,3},{3,2},{4,5},{5,4},{6,7},{7,6},{8,9},{9,8},{10,11... | collective-permute-start | bytes 786440 | tf_op jit(solution)/shard_map/ppermute | solution.py:403
  42.3 11.8 %collective-permute-start.8 = (bf16[128,1024]{1,0:T(8,128)(2,1)S(1)}, bf16[128,1024]{1,0:T(8,128)(2,1)S(1)}, u32[]{:S(2)}, u32[]{:S(2)}) collective-permute-start(bf16[128,1024]{1,0:T(8,128)(2,1)S(1)} %collective-permute-done.1.refs_4_.refs_5_), channel_id=1, source_target_pairs={{0,8},{8,0},{16,24},{24,16},{32,40},{40,32},{48,56},{56,48},{64,72... | collective-permute-start | bytes 786440 | tf_op jit(solution)/shard_map/ppermute | solution.py:412
  43.1 11.1 %collective-permute-start.10 = (bf16[128,1024]{1,0:T(8,128)(2,1)S(1)}, bf16[128,1024]{1,0:T(8,128)(2,1)S(1)}, u32[]{:S(2)}, u32[]{:S(2)}) collective-permute-start(bf16[128,1024]{1,0:T(8,128)(2,1)S(1)} %collective-permute-done.2.refs_6_.refs_7_), channel_id=1, source_target_pairs={{0,8},{8,0},{16,24},{24,16},{32,40},{40,32},{48,56},{56,48},{64,72... | collective-permute-start | bytes 786440 | tf_op jit(solution)/shard_map/ppermute | solution.py:412
  43.2 11.5 %collective-permute-start.11 = (bf16[128,1024]{1,0:T(8,128)(2,1)S(1)}, bf16[128,1024]{1,0:T(8,128)(2,1)S(1)}, u32[]{:S(2)}, u32[]{:S(2)}) collective-permute-start(bf16[128,1024]{1,0:T(8,128)(2,1)S(1)} %collective-permute-done.refs_7_.refs_8_), channel_id=1, source_target_pairs={{0,8},{8,0},{16,24},{24,16},{32,40},{40,32},{48,56},{56,48},{64,72... | collective-permute-start | bytes 786440 | tf_op jit(solution)/shard_map/ppermute | solution.py:412
  43.6 11.4 %collective-permute-start.7 = (bf16[128,1024]{1,0:T(8,128)(2,1)S(1)}, bf16[128,1024]{1,0:T(8,128)(2,1)S(1)}, u32[]{:S(2)}, u32[]{:S(2)}) collective-permute-start(bf16[128,1024]{1,0:T(8,128)(2,1)S(1)} %collective-permute-done.6.refs_10_.refs_11_), channel_id=1, source_target_pairs={{0,1},{1,0},{2,3},{3,2},{4,5},{5,4},{6,7},{7,6},{8,9},{9,8},{10,11... | collective-permute-start | bytes 786440 | tf_op jit(solution)/shard_map/ppermute | solution.py:403
  51.8 30.0 %collective-permute-start.19 = (bf16[8,2,128,128]{3,2,1,0:T(8,128)(2,1)S(1)}, bf16[8,2,128,128]{3,2,1,0:T(8,128)(2,1)}, u32[]{:S(2)}, u32[]{:S(2)}) collective-permute-start(bf16[8,2,128,128]{3,2,1,0:T(8,128)(2,1)S(1)} %all-to-all-done.1.refs_2_.refs_4_), channel_id=1, source_target_pairs={{0,8},{8,0},{16,24},{24,16},{32,40},{40,32},{48,56},{56,48},{64,72... | collective-permute-start | bytes 1572872 | tf_op jit(solution)/shard_map/ppermute | solution.py:445
  54.1 2.8 %collective-permute-start.14 = (bf16[128,1024]{1,0:T(8,128)(2,1)S(1)}, bf16[128,1024]{1,0:T(8,128)(2,1)S(1)}, u32[]{:S(2)}, u32[]{:S(2)}) collective-permute-start(bf16[128,1024]{1,0:T(8,128)(2,1)S(1)} %collective-permute-done.6.refs_10_.refs_11_), channel_id=1, source_target_pairs={{0,8},{8,0},{16,24},{24,16},{32,40},{40,32},{48,56},{56,48},{64,72... | collective-permute-start | bytes 786440 | tf_op jit(solution)/shard_map/ppermute | solution.py:412
  54.2 2.5 %collective-permute-start.9 = (bf16[128,1024]{1,0:T(8,128)(2,1)S(1)}, bf16[128,1024]{1,0:T(8,128)(2,1)}, u32[]{:S(2)}, u32[]{:S(2)}) collective-permute-start(bf16[128,1024]{1,0:T(8,128)(2,1)S(1)} %collective-permute-done.4.refs_5_.refs_6_), channel_id=1, source_target_pairs={{0,8},{8,0},{16,24},{24,16},{32,40},{40,32},{48,56},{56,48},{64,72... | collective-permute-start | bytes 786440 | tf_op jit(solution)/shard_map/ppermute | solution.py:412
  55.0 2.9 %collective-permute-start.13 = (bf16[128,1024]{1,0:T(8,128)(2,1)S(1)}, bf16[128,1024]{1,0:T(8,128)(2,1)}, u32[]{:S(2)}, u32[]{:S(2)}) collective-permute-start(bf16[128,1024]{1,0:T(8,128)(2,1)S(1)} %collective-permute-done.7.refs_9_.refs_10_), channel_id=1, source_target_pairs={{0,8},{8,0},{16,24},{24,16},{32,40},{40,32},{48,56},{56,48},{64,72... | collective-permute-start | bytes 786440 | tf_op jit(solution)/shard_map/ppermute | solution.py:412
  62.6 22.6 %all-to-all-start.2 = ((bf16[8,128,128]{2,1,0:T(8,128)(2,1)}), bf16[8,128,128]{2,1,0:T(8,128)(2,1)S(1)}, u32[]{:S(2)}, u32[]{:S(2)}) async-start(bf16[8,128,128]{2,1,0:T(8,128)(2,1)} %shard_map.113), calls=%async_computation.2 | async-start | bytes 524288 | tf_op jit(solution)/shard_map/all_to_all | solution.py:359
  69.3 8.9 %collective-permute-start.16 = (bf16[128,512]{1,0:T(8,128)(2,1)}, bf16[128,512]{1,0:T(8,128)(2,1)S(1)}, u32[]{:S(2)}, u32[]{:S(2)}) collective-permute-start(bf16[128,512]{1,0:T(8,128)(2,1)} %get-tuple-element.47), channel_id=1, source_target_pairs={{0,64},{8,72},{16,80},{24,88},{32,96},{40,104},{48,112},{56,120},{... | collective-permute-start | bytes 393224 | tf_op jit(solution)/shard_map/ppermute | solution.py:432
  72.2 6.0 %collective-permute-start.17 = (bf16[128,512]{1,0:T(8,128)(2,1)}, bf16[128,512]{1,0:T(8,128)(2,1)S(1)}, u32[]{:S(2)}, u32[]{:S(2)}) collective-permute-start(bf16[128,512]{1,0:T(8,128)(2,1)} %get-tuple-element.49), channel_id=1, source_target_pairs={{0,8},{8,0},{16,24},{24,16},{32,40},{40,32},{48,56},{56,48},{64,72... | collective-permute-start | bytes 393224 | tf_op jit(solution)/shard_map/ppermute | solution.py:434
  73.4 8.4 %collective-permute-start.18 = (bf16[128,512]{1,0:T(8,128)(2,1)}, bf16[128,512]{1,0:T(8,128)(2,1)S(1)}, u32[]{:S(2)}, u32[]{:S(2)}) collective-permute-start(bf16[128,512]{1,0:T(8,128)(2,1)} %get-tuple-element.51), channel_id=1, source_target_pairs={{0,72},{8,64},{16,88},{24,80},{32,104},{40,96},{48,120},{56,112},{... | collective-permute-start | bytes 393224 | tf_op jit(solution)/shard_map/ppermute | solution.py:433
  85.9 22.9 %all-to-all-start.3 = ((bf16[32,32,512]{2,1,0:T(8,128)(2,1)}), bf16[32,32,512]{2,1,0:T(8,128)(2,1)S(1)}, u32[]{:S(2)}, u32[]{:S(2)}) async-start(bf16[32,32,512]{2,1,0:T(8,128)(2,1)} %shard_map.115), calls=%async_computation.3 | async-start | bytes 2097152 | tf_op jit(solution)/shard_map/all_to_all | solution.py:455
  99.7 4.2 %collective-permute-start.15 = (bf16[8,2,128,128]{3,2,1,0:T(8,128)(2,1)}, bf16[8,2,128,128]{3,2,1,0:T(8,128)(2,1)}, u32[]{:S(2)}, u32[]{:S(2)}) collective-permute-start(bf16[8,2,128,128]{3,2,1,0:T(8,128)(2,1)} %get-tuple-element.44), channel_id=1, source_target_pairs={{0,8},{8,0},{16,24},{24,16},{32,40},{40,32},{48,56},{56,48},{64,72... | collective-permute-start | bytes 1572872 | tf_op jit(solution)/shard_map/ppermute | solution.py:477
  129.5 4.2 %collective-permute-start.20 = (bf16[8,128,128]{2,1,0:T(8,128)(2,1)S(1)}, bf16[8,128,128]{2,1,0:T(8,128)(2,1)S(1)}, u32[]{:S(2)}, u32[]{:S(2)}) collective-permute-start(bf16[8,128,128]{2,1,0:T(8,128)(2,1)S(1)} %slice_bitcast_fusion), channel_id=1, source_target_pairs={{0,8},{8,0},{16,24},{24,16},{32,40},{40,32},{48,56},{56,48},{64,72... | collective-permute-start | bytes 786440 | tf_op jit(solution)/shard_map/ppermute | solution.py:493
  (12 other events, 78.1 us)

commit v5 on v4

--- a/solution.py
+++ b/solution.py
@@ -24,11 +24,11 @@
 BF16 = jnp.bfloat16
 
 CORE_SWAP = [(i, i ^ 1) for i in range(16)]
-PAIR_SWAP = [(i, i ^ 8) for i in range(16)]
-DIAG_SWAP = [(i, i ^ 9) for i in range(16)]
+PAIR_SWAP = [(i, i ^ 2) for i in range(16)]
+DIAG_SWAP = [(i, i ^ 3) for i in range(16)]
 SAME_CORE = [[2 * j + c for j in range(CHIPS)] for c in range(2)]
 REDUCE = [
-    [(8 * h + 2 * y + c) * 8 + f for f in range(8) for y in range(4)]
+    [(4 * p + 2 * h + c) * 8 + f for f in range(8) for p in range(4)]
     for h in range(2)
     for c in range(2)
 ]
@@ -210,23 +210,22 @@
             j = 2 * m + t
             block = ctx[t * BLOCK : (t + 1) * BLOCK]
             ctx_out.ref[j, 0] = block
-            ctx_out.ref[j ^ 4, 1] = block
+            ctx_out.ref[j ^ 1, 1] = block
             ctx_out.push(j, 0)
-            ctx_out.push(j ^ 4, 1)
+            ctx_out.push(j ^ 1, 1)
     lse_out.push()
 
 
 def backward_kernel(ins, outs, scratch, sems):
-    core_ref, q_in, k_in, grad_in, v_in, ctx_in, end_in, lse_in = ins
-    dq_out, keep_out, send_out = outs
+    core_ref, grad_ref, q_in, k_in, v_in, ctx_in, end_in, lse_in = ins
+    dq_ref, keep_ref, send_ref = outs
     dk_s, dv_s = scratch
     core = core_ref[0]
     dk_s[...] = jnp.zeros(dk_s.shape, F32)
     dv_s[...] = jnp.zeros(dv_s.shape, F32)
+    q_ref, k_s, v_s, ctx_ref = q_in.get(), k_in.get(), v_in.get(), ctx_in.get()
     end_ref, lse_ref = end_in.get(), lse_in.get()
-    q_ref, k_s = q_in.get(), k_in.get()
-    grad_ref, v_s, ctx_ref = grad_in.get(), v_in.get(), ctx_in.get()
-    for m in range(3, -1, -1):
+    for m in range(4):
         rows = slice(2 * m, 2 * m + 2)
         q = q_ref[rows].reshape(TILE, HS)
         do = grad_ref[rows].reshape(TILE, HS)
@@ -244,58 +243,48 @@
             dk_s[start:stop] += dot_nn(ds, q)
             dq = dq + dot_tn(k_s[start:stop], ds)
         dq_rows = dq.T.astype(BF16)
-        dq_out.ref[2 * m] = dq_rows[:BLOCK]
-        dq_out.ref[2 * m + 1] = dq_rows[BLOCK:]
-        dq_out.push(pl.ds(2 * m, 2))
-        first = 2 * m + 1 if m else 0
-        last = 2 * m + 3 if m < 3 else CHIPS
-        for j in range(first, last):
-            own = pl.multiple_of(2 * BLOCK * j + BLOCK * core, BLOCK)
-            other = pl.multiple_of(2 * BLOCK * j + BLOCK * (1 - core), BLOCK)
-            send_out.ref[j, 0] = dk_s[pl.ds(other, BLOCK)].astype(BF16)
-            send_out.ref[j, 1] = dv_s[pl.ds(other, BLOCK)].astype(BF16)
-            send_out.push(j)
-            keep_out.ref[j, 0] = dk_s[pl.ds(own, BLOCK)]
-            keep_out.ref[j, 1] = dv_s[pl.ds(own, BLOCK)]
-            keep_out.push(j)
+        dq_ref[2 * m] = dq_rows[:BLOCK]
+        dq_ref[2 * m + 1] = dq_rows[BLOCK:]
+    for j in range(CHIPS):
+        own = pl.multiple_of(2 * BLOCK * j + BLOCK * core, BLOCK)
+        other = pl.multiple_of(2 * BLOCK * j + BLOCK * (1 - core), BLOCK)
+        send_ref[j, 0] = dk_s[pl.ds(other, BLOCK)].astype(BF16)
+        send_ref[j, 1] = dv_s[pl.ds(other, BLOCK)].astype(BF16)
+        keep_ref[j, 0] = dk_s[pl.ds(own, BLOCK)]
+        keep_ref[j, 1] = dv_s[pl.ds(own, BLOCK)]
 
 
 def project_kernel(ins, outs, scratch, sems):
-    core_ref, row_ref, valid_ref, up_in, own_in = ins[:5]
-    mine, other = ins[5:12], ins[12:19]
+    core_ref, valid_ref, up_in, mine_in, other_in = ins
     out = outs[0]
-    core, row = core_ref[0], row_ref[0]
+    core = core_ref[0]
     half = up_in.ref.shape[1] // 2
     valid = valid_ref[...]
     up_ref = up_in.get()
-    out.ref[row] = (dot_nt(up_ref[...], own_in.get()[...]) * valid).astype(BF16)
-    out.push(row)
     up_mine = up_ref[:, pl.ds(pl.multiple_of(core * half, half), half)]
     up_other = up_ref[:, pl.ds(pl.multiple_of((1 - core) * half, half), half)]
-    for s in range(1, HEADS):
-        total = dot_nt(up_mine, mine[s - 1][...]) + dot_nt(up_other, other[s - 1][...])
-        at = jnp.bitwise_xor(row, s)
-        out.ref[at] = (total * valid).astype(BF16)
-        out.push(at)
+    mine, other = mine_in.get(), other_in.get()
+    for a in range(HEADS):
+        rows = slice(a * HS, (a + 1) * HS)
+        total = dot_nt(up_mine, mine[rows]) + dot_nt(up_other, other[rows])
+        out.ref[a] = (total * valid).astype(BF16)
+        out.push(a)
 
 
 def attend_kernel(ins, outs, scratch, sems):
-    core_ref, row_ref, ctx_in, own_in = ins[:4]
-    mine, other = ins[4:11], ins[11:18]
+    core_ref, ctx_in, mine_in, other_in = ins
     out = outs[0]
-    core, row = core_ref[0], row_ref[0]
-    ctx_ref, own_ref = ctx_in.get(), own_in.get()
-    half = own_ref.shape[1] // 2
-    ctx = jnp.concatenate([ctx_ref[jnp.bitwise_xor(row, s)] for s in range(HEADS)], axis=1)
+    core = core_ref[0]
+    ctx_ref = ctx_in.get()
+    half = mine_in.ref.shape[1]
+    ctx = jnp.concatenate([ctx_ref[a] for a in range(HEADS)], axis=1)
     step = half // 4
-    for side, parts in ((core, mine), (1 - core, other)):
+    for side, part in ((core, mine_in), (1 - core, other_in)):
+        weight = part.get()
         for n in range(4):
             at = pl.ds(pl.multiple_of(side * half + n * step, step), step)
             cols = slice(n * step, (n + 1) * step)
-            weight = jnp.concatenate(
-                [own_ref[:, at]] + [part[:, cols] for part in parts], axis=0
-            )
-            out.ref[0, :, at] = dot_nn(ctx, weight).astype(BF16)
+            out.ref[0, :, at] = dot_nn(ctx, weight[:, cols]).astype(BF16)
             out.push(0, slice(None), at)
 
 
@@ -314,7 +303,7 @@
 
 
 def join_kernel(ins, outs, scratch, sems):
-    dq_in, keep_in, came_in, terms_ref = ins
+    dq_ref, keep_ref, came_ref, terms_ref = ins
     out_ref = outs[0]
     total = terms_ref[0].astype(F32)
     for s in range(1, terms_ref.shape[0]):
@@ -324,7 +313,6 @@
     for j in range(CHIPS):
         for t in range(4):
             out_ref[j, 3, t * rows : (t + 1) * rows] = weight[:, t * HS : (t + 1) * HS]
-    dq_ref, keep_ref, came_ref = dq_in.get(), keep_in.get(), came_in.get()
     for j in range(CHIPS):
         out_ref[j, 0] = dq_ref[j]
         out_ref[j, 1] = (keep_ref[j, 0] + came_ref[j, 0].astype(F32)).astype(BF16)
@@ -341,15 +329,15 @@
             dst = outs[i].at[0, :, pl.ds(a * HS, HS)]
             copies.append(pltpu.make_async_copy(mine_ref.at[a, i], dst, next(sems)))
             copies[-1].start()
-    for y in range(4):
-        rows = pl.ds(32 * y, 32)
-        for x in range(2):
-            a = 4 * x + y
+    for p in range(4):
+        rows = pl.ds(32 * p, 32)
+        for h in range(2):
+            a = 2 * p + h
             for t in range(4):
                 part = slice(32 * t, 32 * t + 32)
-                at = pl.multiple_of(1024 * x + 512 * core + HS * t, HS)
+                at = pl.multiple_of(1024 * h + 512 * core + HS * t, HS)
                 dw_out.ref[rows, pl.ds(at, HS)] = mine_ref[a, 3, part].astype(F32)
-                at = pl.multiple_of(1024 * x + 512 * (1 - core) + HS * t, HS)
+                at = pl.multiple_of(1024 * h + 512 * (1 - core) + HS * t, HS)
                 dw_out.ref[rows, pl.ds(at, HS)] = other_ref[a, part].astype(F32)
         dw_out.push(rows)
     return copies
@@ -369,8 +357,7 @@
     index = lax.axis_index("ctx").astype(jnp.int32)
     core = index & 1
     core_ref = core.reshape(1)
-    high_ref = (index >> 3).reshape(1)
-    row_ref = lax.axis_index("fsdp").astype(jnp.int32).reshape(1)
+    high_ref = ((index >> 1) & 1).reshape(1)
     valid_len = lengths[0]
     width = out_weight.shape[1]
     half = width // 2
@@ -399,19 +386,9 @@
     rows_here = index * BLOCK + jnp.arange(BLOCK, dtype=jnp.int32)
     valid_here = (rows_here < valid_len).astype(F32)[:, None]
 
-    def step(value, s):
-        return lax.ppermute(value, "fsdp", [(i, i ^ s) for i in range(8)])
-
-    own_half = after(own_half, end, valid, valid_here)
-    over = step(own_half, 4)
-    one, three = step(own_half, 1), step(own_half, 3)
-    over_one, over_three = step(over, 1), step(over, 3)
-    two, over_two = step(one, 3), step(over_three, 1)
-    pieces = [one, two, three, over, over_one, over_two, over_three]
-    mine = [("V", piece) for piece in pieces]
-    other_half = [("V", lax.ppermute(piece, "ctx", CORE_SWAP)) for piece in pieces]
-
-    own = after(own, end, valid, valid_here, over, one, three)
+    weight_mine = lax.all_gather(own_half, "fsdp", axis=0, tiled=True)
+
+    own = after(own, end, valid, valid_here)
     other = lax.ppermute(own, "ctx", CORE_SWAP)
     pairs = 4 * TILE * SPAN * 5 // 2
     rows = ("H", (LEN, HS), BF16)
@@ -432,16 +409,7 @@
     up_pair = lax.ppermute(after(up_pair, context), "ctx", PAIR_SWAP)
     up_diag = lax.ppermute(after(up_diag, context), "ctx", DIAG_SWAP)
     up_core = lax.ppermute(after(up_core, context), "ctx", CORE_SWAP)
-    grads = call(
-        project_kernel,
-        [
-            ("S", core_ref), ("S", row_ref), ("V", valid_here), ("H", upstream, 0),
-            ("H", out_weight), *mine, *other_half,
-        ],
-        [("H", (HEADS, BLOCK, HS), BF16)],
-        flops=2 * 128 * 1024 * 2048,
-    )
-    grads = exchange(after(grads, context_mine))
+    context_mine = after(context_mine, up_pair, up_diag, up_core)
     context_other = lax.ppermute(context_mine, "ctx", CORE_SWAP)
     terms = call(
         weight_kernel,
@@ -452,41 +420,53 @@
         [("H", (32, 32, quarter), BF16)],
         flops=2 * 512 * 1024 * 512,
     )
+    weight_mine = after(weight_mine, terms)
     terms = lax.all_to_all(
-        after(terms, grads),
+        terms,
         ("ctx", "fsdp"),
         split_axis=0,
         concat_axis=0,
         tiled=True,
         axis_index_groups=REDUCE,
     )
+    weight_other = lax.ppermute(weight_mine, "ctx", CORE_SWAP)
+    grads = call(
+        project_kernel,
+        [
+            ("S", core_ref), ("V", valid_here), ("H", upstream, 0), ("H", weight_mine),
+            ("H", weight_other),
+        ],
+        [("H", (HEADS, BLOCK, HS), BF16)],
+        flops=2 * 128 * 1024 * 2048,
+    )
+    grads = exchange(after(grads, terms))
+    attended = call(
+        attend_kernel,
+        [
+            ("S", core_ref), ("A", context_mine, (slice(None), 0)), ("H", weight_mine),
+            ("H", weight_other),
+        ],
+        [("H", (1, BLOCK, width), BF16)],
+        flops=2 * 128 * 1024 * 2048,
+    )
     dq, keep, send = call(
         backward_kernel,
         [
-            ("S", core_ref), ("H", query), ("H", key), ("H", grads), ("H", value),
+            ("S", core_ref), ("V", after(grads, attended)), ("H", query), ("H", key), ("H", value),
             ("H", context, (slice(None), 0)), ("A", end), ("H", lse),
         ],
         [
-            ("H", (CHIPS, BLOCK, HS), BF16),
-            ("H", (CHIPS, 2, BLOCK, HS), F32),
-            ("H", (CHIPS, 2, BLOCK, HS), BF16),
+            ("V", (CHIPS, BLOCK, HS), BF16),
+            ("V", (CHIPS, 2, BLOCK, HS), F32),
+            ("V", (CHIPS, 2, BLOCK, HS), BF16),
         ],
         scratch=(pltpu.VMEM((LEN, HS), F32), pltpu.VMEM((LEN, HS), F32)),
         flops=10 * pairs * HS,
     )
     came = lax.ppermute(send, "ctx", CORE_SWAP)
-    attended = call(
-        attend_kernel,
-        [
-            ("S", core_ref), ("S", row_ref), ("A", context_mine, (slice(None), 0)),
-            ("H", out_weight), *mine, *other_half,
-        ],
-        [("H", (1, BLOCK, width), BF16)],
-        flops=2 * 128 * 1024 * 2048,
-    )
     joined = call(
         join_kernel,
-        [("H", after(dq, attended)), ("H", keep), ("H", came), ("V", terms)],
+        [("V", dq), ("V", keep), ("V", came), ("V", terms)],
         [("V", (CHIPS, 4, BLOCK, HS), BF16)],
     )
     result = exchange(joined)

time: 136 us -> 148 us (1.088)
  waiting for transfers between devices: 31.3 us -> 48.4 us
  starting transfers between devices: 52.9 us -> 38.1 us
  between operations: 1.76 us -> 15 us
  Pallas kernels: 29.1 us -> 26.2 us
    all_to_all x3, waiting for transfers between devices: 2.42 us -> 17.4 us  [exchange(): lax.all_to_all(operand, 'ctx', split_axis=0, concat_axis=0, tiled=True, a...]
    ppermute x14 -> x1, waiting for transfers between devices: 14.4 us -> 0.01 us  [shards(): weight_other = lax.ppermute(weight_mine, 'ctx', CORE_SWAP)]
    ppermute x14 -> x1, starting transfers between devices: 13.2 us -> 0.46 us  [shards(): weight_other = lax.ppermute(weight_mine, 'ctx', CORE_SWAP)]
    all_to_all x1, waiting for transfers between devices: 4.98 us -> 13.5 us  [shards(): lax.all_to_all(terms, ('ctx', 'fsdp'), split_axis=0, concat_axis=0, tiled...]
    all_to_all x3, starting transfers between devices: 21.5 us -> 14.8 us  [exchange(): lax.all_to_all(operand, 'ctx', split_axis=0, concat_axis=0, tiled=True, a...]
    all_to_all x1, starting transfers between devices: 6.9 us -> 11 us  [shards(): lax.all_to_all(terms, ('ctx', 'fsdp'), split_axis=0, concat_axis=0, tiled...]
    ppermute x1, starting transfers between devices: 0.09 us -> 3.14 us  [shards(): came = lax.ppermute(send, 'ctx', CORE_SWAP)]
    pallas_call x8, Pallas kernels: 29.1 us -> 26.2 us  [call(): pl.pallas_call(body, out_shape=[SPACES[o[0]](o[1], o[2]) if o[0] in 'HR'...]
  transfers between devices with their start and end apart: 25 -> 13, of which waited for: 10 -> 10; matrix products, arithmetic and copies ran while one was open for 1% -> 1% of each run, Pallas kernels for 17% -> 10%
where the time goes in v5:
time: 148 us; the launch traced here: 147 us
  waiting for transfers between devices  48.4 us (33%)
  starting transfers between devices  38.1 us (26%)
  Pallas kernels  26.2 us (18%)
  blocking collectives  18.2 us (12%)
  between operations  15 us (10%)
    pallas_call x8, Pallas kernels, call(): pl.pallas_call(body, out_shape=[SPACES[o[0]](o[1], o[2]) if o[0] in 'HR'...  26.2 us
    all_to_all x1, blocking collectives, exchange(): lax.all_to_all(operand, 'ctx', split_axis=0, concat_axis=0, tiled=True, a...  18.2 us
    all_to_all x3, waiting for transfers between devices, exchange(): lax.all_to_all(operand, 'ctx', split_axis=0, concat_axis=0, tiled=True, a...  17.4 us
    all_to_all x3, starting transfers between devices, exchange(): lax.all_to_all(operand, 'ctx', split_axis=0, concat_axis=0, tiled=True, a...  14.8 us
    all_to_all x1, waiting for transfers between devices, shards(): lax.all_to_all(terms, ('ctx', 'fsdp'), split_axis=0, concat_axis=0, tiled...  13.5 us
    all_to_all x1, starting transfers between devices, shards(): lax.all_to_all(terms, ('ctx', 'fsdp'), split_axis=0, concat_axis=0, tiled...  11 us
    ppermute x1, waiting for transfers between devices, shards(): up_pair = lax.ppermute(after(up_pair, context), 'ctx', PAIR_SWAP)  6.37 us
    ppermute x1, waiting for transfers between devices, shards(): up_diag = lax.ppermute(after(up_diag, context), 'ctx', DIAG_SWAP)  5.01 us
  transfers between devices with their start and end apart: 13, of which 10 were waited for; matrix products, arithmetic and copies ran while one was open for 1% of the time, Pallas kernels for 10%

profile of v5, /device:TPU:1, one launch (start us, length us, event | category | flops | bytes accessed | tf_op | source)
XLA Modules:
  0.0 147.0 jit_solution(15208590796591758186)
XLA Ops:
  7.2 2.6 %shard_map.110 = (bf16[8,3,128,128]{3,2,1,0:T(8,128)(2,1)}, bf16[128,1024]{1,0:T(8,128)(2,1)}, bf16[128,512]{1,0:T(8,128)(2,1)}, bf16[128,512]{1,0:T(8,128)(2,1)...) custom-call(s32[1]{0:T(128)} %bitcast.refs_0_, s32[1]{0:T(128)} %bitcast.1.refs_1_, bf16[1,128,1024]{2,1,0:T(8,128)(2,1)} %refs_2_.2, ...), custom_call_target="tpu_custom_call" | custom-call | bytes 2000000 | tf_op jit(solution)/shard_map/pallas_call | solution.py:112
  9.9 7.5 %all-to-all-start = ((bf16[8,3,128,128]{3,2,1,0:T(8,128)(2,1)}), bf16[8,3,128,128]{3,2,1,0:T(8,128)(2,1)S(1)}, u32[]{:S(2)}, u32[]{:S(2)}) async-start(bf16[8,3,128,128]{3,2,1,0:T(8,128)(2,1)} %get-tuple-element.31), calls=%async_computation | async-start | bytes 1572864 | tf_op jit(solution)/shard_map/all_to_all | solution.py:347
  19.2 12.5 %all-to-all-done.refs_1_ = bf16[8,3,128,128]{3,2,1,0:T(8,128)(2,1)S(1)} async-done(((bf16[8,3,128,128]{3,2,1,0:T(8,128)(2,1)}), bf16[8,3,128,128]{3,2,1,0:T(8,128)(2,1)S(1)}, u32[]{:S(2)}, u32[]{:S(2)}) %all-to-all-start) | async-done | bytes 786464 | tf_op jit(solution)/shard_map/all_to_all | solution.py:347
  31.7 2.8 %collective-permute-start = (bf16[8,3,128,128]{3,2,1,0:T(8,128)(2,1)S(1)}, bf16[8,3,128,128]{3,2,1,0:T(8,128)(2,1)S(1)}, u32[]{:S(2)}, u32[]{:S(2)}) collective-permute-start(bf16[8,3,128,128]{3,2,1,0:T(8,128)(2,1)S(1)} %all-to-all-done.refs_1_), channel_id=1, source_target_pairs={{0,8},{8,0},{16,24},{24,16},{32,40},{40,32},{48,56},{56,48},{64,72... | collective-permute-start | bytes 2359304 | tf_op jit(solution)/shard_map/ppermute | solution.py:392
  34.5 1.9 %collective-permute-done.refs_2_ = bf16[8,3,128,128]{3,2,1,0:T(8,128)(2,1)S(1)} collective-permute-done((bf16[8,3,128,128]{3,2,1,0:T(8,128)(2,1)S(1)}, bf16[8,3,128,128]{3,2,1,0:T(8,128)(2,1)S(1)}, u32[]{:S(2)}, u32[]{:S(2)}) %collective-permute-start) | collective-permute-done | bytes 786464 | tf_op jit(solution)/shard_map/ppermute | solution.py:392
  36.4 4.0 %shard_map.111 = (bf16[8,2,128,128]{3,2,1,0:T(8,128)(2,1)}, f32[4,1,256]{2,1,0:T(1,128)}, bf16[8,128,128]{2,1,0:T(8,128)(2,1)}, bf16[2048,128]{1,0:T(8,128)(2,1)}, bf16[2048,128]{1,0:T(8,128)(2,1)}) custom-call(s32[1]{0:T(128)} %bitcast.refs_0_, bf16[8,3,128,128]{3,2,1,0:T(8,128)(2,1)S(1)} %all-to-all-done.refs_1_, ...), custom_call_target="tpu_custom_call" | custom-call | flops 671088640 | bytes 2000000 | tf_op jit(solution)/shard_map/pallas_call | solution.py:112
  40.4 3.7 %all-to-all-start.1 = ((bf16[8,2,128,128]{3,2,1,0:T(8,128)(2,1)}), bf16[8,2,128,128]{3,2,1,0:T(8,128)(2,1)S(1)}, u32[]{:S(2)}, u32[]{:S(2)}) async-start(bf16[8,2,128,128]{3,2,1,0:T(8,128)(2,1)} %get-tuple-element.33.refs_5_), calls=%async_computation.1 | async-start | bytes 1048576 | tf_op jit(solution)/shard_map/all_to_all | solution.py:347
  44.1 1.5 collective-permute-start.1
  46.9 6.4 %collective-permute-done.1.refs_1_ = bf16[128,512]{1,0:T(8,128)(2,1)S(1)} collective-permute-done((bf16[128,512]{1,0:T(8,128)(2,1)S(1)}, bf16[128,512]{1,0:T(8,128)(2,1)S(1)}, u32[]{:S(2)}, u32[]{:S(2)}) %collective-permute-start.1) | collective-permute-done | bytes 131104 | tf_op jit(solution)/shard_map/ppermute | solution.py:409
  53.2 5.0 %collective-permute-done.2.refs_3_ = bf16[128,512]{1,0:T(8,128)(2,1)S(1)} collective-permute-done((bf16[128,512]{1,0:T(8,128)(2,1)S(1)}, bf16[128,512]{1,0:T(8,128)(2,1)S(1)}, u32[]{:S(2)}, u32[]{:S(2)}) %collective-permute-start.2) | collective-permute-done | bytes 131104 | tf_op jit(solution)/shard_map/ppermute | solution.py:410
  60.3 1.5 %collective-permute-done.4.refs_5_ = bf16[8,2,128,128]{3,2,1,0:T(8,128)(2,1)S(1)} collective-permute-done((bf16[8,2,128,128]{3,2,1,0:T(8,128)(2,1)S(1)}, bf16[8,2,128,128]{3,2,1,0:T(8,128)(2,1)S(1)}, u32[]{:S(2)}, u32[]{:S(2)}) %collective-permute-start.4) | collective-permute-done | bytes 524320 | tf_op jit(solution)/shard_map/ppermute | solution.py:413
  61.9 2.7 %shard_map.112 = bf16[32,32,512]{2,1,0:T(8,128)(2,1)} custom-call(bf16[128,512]{1,0:T(8,128)(2,1)} %get-tuple-element.42.refs_0_, bf16[128,512]{1,0:T(8,128)(2,1)S(1)} %collective-permute-done.1.refs_1_, bf16[128,512]{1,0:T(8,128)(2,1)S(1)} %collective-permute-done.3.refs_2_, bf16[128,512]{1,0:T(8,128)(2,1)S(1)} %collective-permute-done.2.refs_3_, ...), custom_call_target="tpu_custom_call" | custom-call | flops 536870912 | bytes 2000000 | tf_op jit(solution)/shard_map/pallas_call | solution.py:112
  65.1 11.0 %all-to-all-start.2 = ((bf16[32,32,512]{2,1,0:T(8,128)(2,1)}), bf16[32,32,512]{2,1,0:T(8,128)(2,1)S(1)}, u32[]{:S(2)}, u32[]{:S(2)}) async-start(bf16[32,32,512]{2,1,0:T(8,128)(2,1)} %shard_map.112), calls=%async_computation.2 | async-start | bytes 2097152 | tf_op jit(solution)/shard_map/all_to_all | solution.py:424
  76.2 4.7 %shard_map.114 = bf16[8,128,128]{2,1,0:T(8,128)(2,1)} custom-call(s32[1]{0:T(128)} %bitcast.refs_0_, f32[128,1]{1,0:T(8,128)S(1)} %fusion.refs_1_, bf16[1,128,2048]{2,1,0:T(8,128)(2,1)} %refs_2_.3, bf16[1024,1024]{1,0:T(8,128)(2,1)} %all-gather.2.cloned.1.call-done.refs_2_.refs_3_, bf16[1024,1024]{1,0:T(8,128)(2,1)} %collective-permute-done.5.refs_3_.refs_4_), custom_call_target="tpu_custom_call" | custom-call | flops 536870912 | bytes 2000000 | tf_op jit(solution)/shard_map/pallas_call | solution.py:112
  80.9 13.5 %all-to-all-done.2.refs_3_ = bf16[32,32,512]{2,1,0:T(8,128)(2,1)S(1)} async-done(((bf16[32,32,512]{2,1,0:T(8,128)(2,1)}), bf16[32,32,512]{2,1,0:T(8,128)(2,1)S(1)}, u32[]{:S(2)}, u32[]{:S(2)}) %all-to-all-start.2) | async-done | bytes 1048608 | tf_op jit(solution)/shard_map/all_to_all | solution.py:424
  94.3 3.6 %all-to-all-start.3 = ((bf16[8,128,128]{2,1,0:T(8,128)(2,1)}), bf16[8,128,128]{2,1,0:T(8,128)(2,1)S(1)}, u32[]{:S(2)}, u32[]{:S(2)}) async-start(bf16[8,128,128]{2,1,0:T(8,128)(2,1)} %shard_map.114), calls=%async_computation.3 | async-start | bytes 524288 | tf_op jit(solution)/shard_map/all_to_all | solution.py:347
  97.9 3.8 %shard_map.113 = bf16[1,128,2048]{2,1,0:T(8,128)(2,1)} custom-call(s32[1]{0:T(128)} %bitcast.refs_0_, bf16[8,2,128,128]{3,2,1,0:T(8,128)(2,1)S(1)} %all-to-all-done.1.refs_4_.refs_1_, bf16[1024,1024]{1,0:T(8,128)(2,1)} %all-gather.2.cloned.1.call-done.refs_2_.refs_3_, bf16[1024,1024]{1,0:T(8,128)(2,1)} %collective-permute-done.5.refs_3_.refs_4_), custom_call_target="tpu_custom_call" | custom-call | flops 536870912 | bytes 2000000 | tf_op jit(solution)/shard_map/pallas_call | solution.py:112
  101.7 3.6 %all-to-all-done.3.refs_1_ = bf16[8,128,128]{2,1,0:T(8,128)(2,1)S(1)} async-done(((bf16[8,128,128]{2,1,0:T(8,128)(2,1)}), bf16[8,128,128]{2,1,0:T(8,128)(2,1)S(1)}, u32[]{:S(2)}, u32[]{:S(2)}) %all-to-all-start.3) | async-done | bytes 262176 | tf_op jit(solution)/shard_map/all_to_all | solution.py:347
  105.3 5.9 %shard_map.115 = (bf16[8,128,128]{2,1,0:T(8,128)(2,1)S(1)}, f32[8,2,128,128]{3,2,1,0:T(8,128)S(1)}, bf16[8,2,128,128]{3,2,1,0:T(8,128)(2,1)S(1)}) custom-call(s32[1]{0:T(128)} %bitcast.refs_0_, bf16[8,128,128]{2,1,0:T(8,128)(2,1)S(1)} %all-to-all-done.3.refs_1_, bf16[8,128,128]{2,1,0:T(8,128)(2,1)} %get-tuple-element.46.refs_2_, ...), custom_call_target="tpu_custom_call" | custom-call | flops 1677721600 | bytes 2000000 | tf_op jit(solution)/shard_map/pallas_call | solution.py:112
  111.3 3.1 %collective-permute-start.6 = (bf16[8,2,128,128]{3,2,1,0:T(8,128)(2,1)S(1)}, bf16[8,2,128,128]{3,2,1,0:T(8,128)(2,1)S(1)}, u32[]{:S(2)}, u32[]{:S(2)}) collective-permute-start(bf16[8,2,128,128]{3,2,1,0:T(8,128)(2,1)S(1)} %get-tuple-element.52), channel_id=1, source_target_pairs={{0,8},{8,0},{16,24},{24,16},{32,40},{40,32},{48,56},{56,48},{64,72... | collective-permute-start | bytes 1572872 | tf_op jit(solution)/shard_map/ppermute | solution.py:466
  114.4 1.5 %collective-permute-done.6.refs_2_ = bf16[8,2,128,128]{3,2,1,0:T(8,128)(2,1)S(1)} collective-permute-done((bf16[8,2,128,128]{3,2,1,0:T(8,128)(2,1)S(1)}, bf16[8,2,128,128]{3,2,1,0:T(8,128)(2,1)S(1)}, u32[]{:S(2)}, u32[]{:S(2)}) %collective-permute-start.6) | collective-permute-done | bytes 524320 | tf_op jit(solution)/shard_map/ppermute | solution.py:466
  116.7 18.2 %all_to_all.25.refs_1_ = bf16[8,4,128,128]{3,2,1,0:T(8,128)(2,1)S(1)} all-to-all(bf16[8,4,128,128]{3,2,1,0:T(8,128)(2,1)S(1)} %shard_map.116), channel_id=1, replica_groups={{0,16,32,48,64,80,96,112},{8,24,40,56,72,88,104,120},{1,17,33,49,65,81,..., dimensions={0} | all-to-all | bytes 2097152 | tf_op jit(solution)/shard_map/all_to_all | solution.py:347
  134.9 2.4 %collective-permute-start.7 = (bf16[8,128,128]{2,1,0:T(8,128)(2,1)S(1)}, bf16[8,128,128]{2,1,0:T(8,128)(2,1)S(1)}, u32[]{:S(2)}, u32[]{:S(2)}) collective-permute-start(bf16[8,128,128]{2,1,0:T(8,128)(2,1)S(1)} %slice_bitcast_fusion), channel_id=1, source_target_pairs={{0,8},{8,0},{16,24},{24,16},{32,40},{40,32},{48,56},{56,48},{64,72... | collective-permute-start | bytes 786440 | tf_op jit(solution)/shard_map/ppermute | solution.py:473
  138.5 1.7 %shard_map.117 = (bf16[1,128,1024]{2,1,0:T(8,128)(2,1)}, bf16[1,128,1024]{2,1,0:T(8,128)(2,1)}, bf16[1,128,1024]{2,1,0:T(8,128)(2,1)}, f32[128,2048]{1,0:T(8,128)}) custom-call(s32[1]{0:T(128)} %bitcast.refs_0_, bf16[8,4,128,128]{3,2,1,0:T(8,128)(2,1)S(1)} %all_to_all.25.refs_1_, bf16[8,128,128]{2,1,0:T(8,128)(2,1)S(1)} %collective-permute-done.7.refs_2_), custom_call_target="tpu_custom_call" | custom-call | bytes 2000000 | tf_op jit(solution)/shard_map/pallas_call | solution.py:112
  (26 shorter events, 6.8 us)
Async XLA Ops:
  7.2 10.3 %copy-start = (s32[1,2048]{1,0:T(1,128)S(1)}, s32[1,2048]{1,0:T(1,128)}, u32[]{:S(2)}) copy-start(s32[1,2048]{1,0:T(1,128)} %param.10) | copy-start | bytes 24580
  7.2 57.5 %all-gather.2.cloned.1.call-start = ((), (), s32[]{:S(2)}) async-start(), calls=%async_computation.5 | async-start | bytes 2359296 | tf_op jit(solution)/shard_map/all_gather | solution.py:389
  9.9 21.8 %all-to-all-start = ((bf16[8,3,128,128]{3,2,1,0:T(8,128)(2,1)}), bf16[8,3,128,128]{3,2,1,0:T(8,128)(2,1)S(1)}, u32[]{:S(2)}, u32[]{:S(2)}) async-start(bf16[8,3,128,128]{3,2,1,0:T(8,128)(2,1)} %get-tuple-element.31), calls=%async_computation | async-start | bytes 1572864 | tf_op jit(solution)/shard_map/all_to_all | solution.py:347
  17.4 26.7 %copy-start.3 = (bf16[128,512]{1,0:T(8,128)(2,1)S(1)}, bf16[128,512]{1,0:T(8,128)(2,1)}, u32[]{:S(2)}) copy-start(bf16[128,512]{1,0:T(8,128)(2,1)} %get-tuple-element.35) | copy-start | bytes 393220
  17.4 28.2 %copy-start.2 = (bf16[128,512]{1,0:T(8,128)(2,1)S(1)}, bf16[128,512]{1,0:T(8,128)(2,1)}, u32[]{:S(2)}) copy-start(bf16[128,512]{1,0:T(8,128)(2,1)} %get-tuple-element.37) | copy-start | bytes 393220
  17.4 29.1 %copy-start.1 = (bf16[128,512]{1,0:T(8,128)(2,1)S(1)}, bf16[128,512]{1,0:T(8,128)(2,1)}, u32[]{:S(2)}) copy-start(bf16[128,512]{1,0:T(8,128)(2,1)} %get-tuple-element.39) | copy-start | bytes 393220
  31.7 4.7 %collective-permute-start = (bf16[8,3,128,128]{3,2,1,0:T(8,128)(2,1)S(1)}, bf16[8,3,128,128]{3,2,1,0:T(8,128)(2,1)S(1)}, u32[]{:S(2)}, u32[]{:S(2)}) collective-permute-start(bf16[8,3,128,128]{3,2,1,0:T(8,128)(2,1)S(1)} %all-to-all-done.refs_1_), channel_id=1, source_target_pairs={{0,8},{8,0},{16,24},{24,16},{32,40},{40,32},{48,56},{56,48},{64,72... | collective-permute-start | bytes 2359304 | tf_op jit(solution)/shard_map/ppermute | solution.py:392
  40.4 19.2 %all-to-all-start.1 = ((bf16[8,2,128,128]{3,2,1,0:T(8,128)(2,1)}), bf16[8,2,128,128]{3,2,1,0:T(8,128)(2,1)S(1)}, u32[]{:S(2)}, u32[]{:S(2)}) async-start(bf16[8,2,128,128]{3,2,1,0:T(8,128)(2,1)} %get-tuple-element.33.refs_5_), calls=%async_computation.1 | async-start | bytes 1048576 | tf_op jit(solution)/shard_map/all_to_all | solution.py:347
  44.1 9.1 %collective-permute-start.1 = (bf16[128,512]{1,0:T(8,128)(2,1)S(1)}, bf16[128,512]{1,0:T(8,128)(2,1)S(1)}, u32[]{:S(2)}, u32[]{:S(2)}) collective-permute-start(bf16[128,512]{1,0:T(8,128)(2,1)S(1)} %copy-done.3), channel_id=1, source_target_pairs={{0,16},{8,24},{16,0},{24,8},{32,48},{40,56},{48,32},{56,40},{64,80... | collective-permute-start | bytes 393224 | tf_op jit(solution)/shard_map/ppermute | solution.py:409
  45.6 12.7 %collective-permute-start.2 = (bf16[128,512]{1,0:T(8,128)(2,1)S(1)}, bf16[128,512]{1,0:T(8,128)(2,1)S(1)}, u32[]{:S(2)}, u32[]{:S(2)}) collective-permute-start(bf16[128,512]{1,0:T(8,128)(2,1)S(1)} %copy-done.2), channel_id=1, source_target_pairs={{0,24},{8,16},{16,8},{24,0},{32,56},{40,48},{48,40},{56,32},{64,88... | collective-permute-start | bytes 393224 | tf_op jit(solution)/shard_map/ppermute | solution.py:410
  46.5 11.8 %collective-permute-start.3 = (bf16[128,512]{1,0:T(8,128)(2,1)S(1)}, bf16[128,512]{1,0:T(8,128)(2,1)S(1)}, u32[]{:S(2)}, u32[]{:S(2)}) collective-permute-start(bf16[128,512]{1,0:T(8,128)(2,1)S(1)} %copy-done.1), channel_id=1, source_target_pairs={{0,8},{8,0},{16,24},{24,16},{32,40},{40,32},{48,56},{56,48},{64,72... | collective-permute-start | bytes 393224 | tf_op jit(solution)/shard_map/ppermute | solution.py:411
  59.6 2.3 %collective-permute-start.4 = (bf16[8,2,128,128]{3,2,1,0:T(8,128)(2,1)S(1)}, bf16[8,2,128,128]{3,2,1,0:T(8,128)(2,1)S(1)}, u32[]{:S(2)}, u32[]{:S(2)}) collective-permute-start(bf16[8,2,128,128]{3,2,1,0:T(8,128)(2,1)S(1)} %all-to-all-done.1.refs_4_.refs_1_), channel_id=1, source_target_pairs={{0,8},{8,0},{16,24},{24,16},{32,40},{40,32},{48,56},{56,48},{64,72... | collective-permute-start | bytes 1572872 | tf_op jit(solution)/shard_map/ppermute | solution.py:413
  64.7 11.5 %collective-permute-start.5 = (bf16[1024,1024]{1,0:T(8,128)(2,1)}, bf16[1024,1024]{1,0:T(8,128)(2,1)}, u32[]{:S(2)}, u32[]{:S(2)}) collective-permute-start(bf16[1024,1024]{1,0:T(8,128)(2,1)} %all-gather.2.cloned.1.call-done.refs_2_.refs_3_), channel_id=1, source_target_pairs={{0,8},{8,0},{16,24},{24,16},{32,40},{40,32},{48,56},{56,48},{64,72... | collective-permute-start | bytes 6291464 | tf_op jit(solution)/shard_map/ppermute | solution.py:432
  65.1 29.2 %all-to-all-start.2 = ((bf16[32,32,512]{2,1,0:T(8,128)(2,1)}), bf16[32,32,512]{2,1,0:T(8,128)(2,1)S(1)}, u32[]{:S(2)}, u32[]{:S(2)}) async-start(bf16[32,32,512]{2,1,0:T(8,128)(2,1)} %shard_map.112), calls=%async_computation.2 | async-start | bytes 2097152 | tf_op jit(solution)/shard_map/all_to_all | solution.py:424
  94.3 11.0 %all-to-all-start.3 = ((bf16[8,128,128]{2,1,0:T(8,128)(2,1)}), bf16[8,128,128]{2,1,0:T(8,128)(2,1)S(1)}, u32[]{:S(2)}, u32[]{:S(2)}) async-start(bf16[8,128,128]{2,1,0:T(8,128)(2,1)} %shard_map.114), calls=%async_computation.3 | async-start | bytes 524288 | tf_op jit(solution)/shard_map/all_to_all | solution.py:347
  111.3 4.7 %collective-permute-start.6 = (bf16[8,2,128,128]{3,2,1,0:T(8,128)(2,1)S(1)}, bf16[8,2,128,128]{3,2,1,0:T(8,128)(2,1)S(1)}, u32[]{:S(2)}, u32[]{:S(2)}) collective-permute-start(bf16[8,2,128,128]{3,2,1,0:T(8,128)(2,1)S(1)} %get-tuple-element.52), channel_id=1, source_target_pairs={{0,8},{8,0},{16,24},{24,16},{32,40},{40,32},{48,56},{56,48},{64,72... | collective-permute-start | bytes 1572872 | tf_op jit(solution)/shard_map/ppermute | solution.py:466
  134.9 3.5 %collective-permute-start.7 = (bf16[8,128,128]{2,1,0:T(8,128)(2,1)S(1)}, bf16[8,128,128]{2,1,0:T(8,128)(2,1)S(1)}, u32[]{:S(2)}, u32[]{:S(2)}) collective-permute-start(bf16[8,128,128]{2,1,0:T(8,128)(2,1)S(1)} %slice_bitcast_fusion), channel_id=1, source_target_pairs={{0,8},{8,0},{16,24},{24,16},{32,40},{40,32},{48,56},{56,48},{64,72... | collective-permute-start | bytes 786440 | tf_op jit(solution)/shard_map/ppermute | solution.py:473
Sparse Core Ops, SparseCore 0:
  10.2 45.4 all-gather.1

commit v6 on v4

--- a/solution.py
+++ b/solution.py
@@ -72,7 +72,7 @@
 SPACES = {"S": pltpu.SMEM, "V": pltpu.VMEM, "H": pltpu.HBM, "A": pl.ANY, "R": pltpu.HBM}
 
 
-def call(kernel, ins, outs, scratch=(), flops=0, mib=14):
+def call(kernel, ins, outs, scratch=(), flops=0, mib=14, aliases=None):
     copied = [
         pltpu.VMEM(jax.eval_shape(lambda x: x[i[2]] if len(i) > 2 else x, i[1]).shape, i[1].dtype)
         for i in ins
@@ -118,6 +118,7 @@
         in_specs=[pl.BlockSpec(memory_space=SPACES[i[0]]) for i in ins],
         out_specs=[pl.BlockSpec(memory_space=SPACES[o[0]]) for o in outs],
         scratch_shapes=[pltpu.SemaphoreType.DMA((SEMS,)), *copied, *scratch],
+        input_output_aliases=aliases or {},
         compiler_params=pltpu.CompilerParams(vmem_limit_bytes=mib * 1024 * 1024),
         cost_estimate=pl.CostEstimate(flops=flops, bytes_accessed=2_000_000, transcendentals=0),
     )(*[
@@ -128,7 +129,7 @@
 
 def pack_kernel(ins, outs, scratch, sems):
     core_ref, high_ref, *data = ins
-    out_ref, half_ref, keep_ref, core_out_ref, pair_ref, diag_ref = outs
+    out_ref, half_ref, up_mine_ref, up_send_ref, pair_ref, diag_ref = outs
     core, high = core_ref[0], high_ref[0]
     half = half_ref.shape[1]
     quarter = half // 2
@@ -138,20 +139,18 @@
         copies.append(pltpu.make_async_copy(src, dst, next(sems)))
         copies[-1].start()
 
+    mine = pl.ds(pl.multiple_of(core * half, half), half)
+    other = pl.ds(pl.multiple_of((1 - core) * half, half), half)
+    copy(data[3].get().at[:, mine], half_ref)
     for i in range(3):
         ref = data[i].get()
         for a in range(HEADS):
             copy(ref.at[:, pl.ds(a * HS, HS)], out_ref.at[a, i])
-    w_ref = data[3].get()
-    copy(w_ref.at[:, pl.ds(pl.multiple_of(core * half, half), half)], half_ref)
     up_ref = data[4].get()
-    for ref, x, c in (
-        (keep_ref, high, core),
-        (core_out_ref, high, 1 - core),
-        (pair_ref, 1 - high, core),
-        (diag_ref, 1 - high, 1 - core),
-    ):
-        at = pl.multiple_of(x * half + c * quarter, quarter)
+    copy(up_ref.at[:, mine], up_mine_ref)
+    copy(up_ref.at[:, other], up_send_ref)
+    for ref, c in ((pair_ref, core), (diag_ref, 1 - core)):
+        at = pl.multiple_of(c * half + (1 - high) * quarter, quarter)
         copy(up_ref.at[:, pl.ds(at, quarter)], ref)
     return copies
 
@@ -261,50 +260,66 @@
 
 
 def project_kernel(ins, outs, scratch, sems):
-    core_ref, row_ref, valid_ref, up_in, own_in = ins[:5]
-    mine, other = ins[5:12], ins[12:19]
-    out = outs[0]
-    core, row = core_ref[0], row_ref[0]
-    half = up_in.ref.shape[1] // 2
-    valid = valid_ref[...]
-    up_ref = up_in.get()
-    out.ref[row] = (dot_nt(up_ref[...], own_in.get()[...]) * valid).astype(BF16)
-    out.push(row)
-    up_mine = up_ref[:, pl.ds(pl.multiple_of(core * half, half), half)]
-    up_other = up_ref[:, pl.ds(pl.multiple_of((1 - core) * half, half), half)]
-    for s in range(1, HEADS):
-        total = dot_nt(up_mine, mine[s - 1][...]) + dot_nt(up_other, other[s - 1][...])
+    row_ref, up_in, up_other_in, *pieces = ins
+    keep_ref, send_ref = outs
+    row = row_ref[0]
+    up = jnp.concatenate([up_in.get()[...], up_other_in.get()[...]], axis=0)
+    for s in range(HEADS):
+        total = dot_nt(up, pieces[s][...])
         at = jnp.bitwise_xor(row, s)
-        out.ref[at] = (total * valid).astype(BF16)
-        out.push(at)
+        keep_ref[at] = total[:BLOCK]
+        send_ref[at] = total[BLOCK:].astype(BF16)
+
+
+def add_kernel(ins, outs, scratch, sems):
+    valid_ref, keep_ref, came_ref = ins
+    outs[0][...] = ((keep_ref[...] + came_ref[...].astype(F32)) * valid_ref[...]).astype(BF16)
 
 
 def attend_kernel(ins, outs, scratch, sems):
-    core_ref, row_ref, ctx_in, own_in = ins[:4]
-    mine, other = ins[4:11], ins[11:18]
-    out = outs[0]
-    core, row = core_ref[0], row_ref[0]
-    ctx_ref, own_ref = ctx_in.get(), own_in.get()
-    half = own_ref.shape[1] // 2
-    ctx = jnp.concatenate([ctx_ref[jnp.bitwise_xor(row, s)] for s in range(HEADS)], axis=1)
-    step = half // 4
-    for side, parts in ((core, mine), (1 - core, other)):
-        for n in range(4):
-            at = pl.ds(pl.multiple_of(side * half + n * step, step), step)
-            cols = slice(n * step, (n + 1) * step)
-            weight = jnp.concatenate(
-                [own_ref[:, at]] + [part[:, cols] for part in parts], axis=0
-            )
-            out.ref[0, :, at] = dot_nn(ctx, weight).astype(BF16)
-            out.push(0, slice(None), at)
+    row_ref, ctx_in, ctx_other_in, *pieces = ins
+    keep, send = outs
+    row = row_ref[0]
+    order = [jnp.bitwise_xor(row, s) for s in range(HEADS)]
+    ctx_ref, ctx_other_ref = ctx_in.get(), ctx_other_in.get()
+    ctx = jnp.concatenate(
+        [
+            jnp.concatenate([ctx_ref[a] for a in order], axis=1),
+            jnp.concatenate([ctx_other_ref[a] for a in order], axis=1),
+        ],
+        axis=0,
+    )
+    pieces = [piece.get() for piece in pieces]
+    for n in range(4):
+        cols = slice(n * TILE, (n + 1) * TILE)
+        weight = jnp.concatenate([piece[:, cols] for piece in pieces], axis=0)
+        total = dot_nn(ctx, weight).astype(BF16)
+        keep.ref[:, cols] = total[:BLOCK]
+        send.ref[:, cols] = total[BLOCK:]
+    send.push()
+    keep.push()
+
+
+def place_kernel(ins, outs, scratch, sems):
+    core_ref, keep_in, came_in = ins
+    core = core_ref[0]
+    half = keep_in.ref.shape[1]
+    copies = []
+    for one, c in ((keep_in, core), (came_in, 1 - core)):
+        at = pl.ds(pl.multiple_of(c * half, half), half)
+        copies.append(pltpu.make_async_copy(one.get(), outs[0].at[0, :, at], next(sems)))
+        copies[-1].start()
+    return copies
 
 
 def weight_kernel(ins, outs, scratch, sems):
     out = outs[0]
-    keep, pair, core, diag, ctx_ref, ctx_other_ref = [one.get() for one in ins]
-    quarter = keep.shape[1]
-    up = jnp.concatenate([keep[...], pair[...]], axis=0)
-    up_other = jnp.concatenate([core[...], diag[...]], axis=0)
+    high_ref = ins[0]
+    mine, other, pair, diag, ctx_ref, ctx_other_ref = [one.get() for one in ins[1:]]
+    quarter = pair.shape[1]
+    at = pl.ds(pl.multiple_of(high_ref[0] * quarter, quarter), quarter)
+    up = jnp.concatenate([mine[:, at], pair[...]], axis=0)
+    up_other = jnp.concatenate([other[:, at], diag[...]], axis=0)
     for a in range(HEADS):
         total = dot_tn(ctx_ref[a].reshape(TILE, HS), up)
         total = total + dot_tn(ctx_other_ref[a].reshape(TILE, HS), up_other)
@@ -314,45 +329,64 @@
 
 
 def join_kernel(ins, outs, scratch, sems):
-    dq_in, keep_in, came_in, terms_ref = ins
-    out_ref = outs[0]
+    dq_in, keep_in, came_in = ins
+    (made,) = scratch
+    copies = []
+    dq_ref, keep_ref, came_ref = dq_in.get(), keep_in.get(), came_in.get()
+    for j in range(CHIPS):
+        made[j, 0] = dq_ref[j]
+        made[j, 1] = (keep_ref[j, 0] + came_ref[j, 0].astype(F32)).astype(BF16)
+        made[j, 2] = (keep_ref[j, 1] + came_ref[j, 1].astype(F32)).astype(BF16)
+        copies.append(
+            pltpu.make_async_copy(made.at[j], outs[0].at[j, pl.ds(0, 3)], next(sems))
+        )
+        copies[-1].start()
+    return copies
+
+
+def total_kernel(ins, outs, scratch, sems):
+    terms_ref = ins[1]
+    (made,) = scratch
     total = terms_ref[0].astype(F32)
     for s in range(1, terms_ref.shape[0]):
         total = total + terms_ref[s].astype(F32)
     weight = total.astype(BF16)
     rows = weight.shape[0]
+    for t in range(4):
+        made[t * rows : (t + 1) * rows] = weight[:, t * HS : (t + 1) * HS]
+    copies = []
     for j in range(CHIPS):
-        for t in range(4):
-            out_ref[j, 3, t * rows : (t + 1) * rows] = weight[:, t * HS : (t + 1) * HS]
-    dq_ref, keep_ref, came_ref = dq_in.get(), keep_in.get(), came_in.get()
-    for j in range(CHIPS):
-        out_ref[j, 0] = dq_ref[j]
-        out_ref[j, 1] = (keep_ref[j, 0] + came_ref[j, 0].astype(F32)).astype(BF16)
-        out_ref[j, 2] = (keep_ref[j, 1] + came_ref[j, 1].astype(F32)).astype(BF16)
+        copies.append(pltpu.make_async_copy(made, outs[0].at[j, 3], next(sems)))
+        copies[-1].start()
+    return copies
 
 
 def unpack_kernel(ins, outs, scratch, sems):
-    core_ref, mine_ref, other_ref = ins
-    dw_out = outs[3]
-    core = core_ref[0]
+    mine_ref = ins[0]
     copies = []
     for a in range(HEADS):
         for i in range(3):
             dst = outs[i].at[0, :, pl.ds(a * HS, HS)]
             copies.append(pltpu.make_async_copy(mine_ref.at[a, i], dst, next(sems)))
             copies[-1].start()
+    return copies
+
+
+def widen_kernel(ins, outs, scratch, sems):
+    core_ref, mine_ref, other_ref = ins
+    out = outs[0]
+    core = core_ref[0]
     for y in range(4):
         rows = pl.ds(32 * y, 32)
         for x in range(2):
             a = 4 * x + y
             for t in range(4):
                 part = slice(32 * t, 32 * t + 32)
-                at = pl.multiple_of(1024 * x + 512 * core + HS * t, HS)
-                dw_out.ref[rows, pl.ds(at, HS)] = mine_ref[a, 3, part].astype(F32)
-                at = pl.multiple_of(1024 * x + 512 * (1 - core) + HS * t, HS)
-                dw_out.ref[rows, pl.ds(at, HS)] = other_ref[a, part].astype(F32)
-        dw_out.push(rows)
-    return copies
+                at = pl.multiple_of(1024 * core + 512 * x + HS * t, HS)
+                out.ref[rows, pl.ds(at, HS)] = mine_ref[a, part].astype(F32)
+                at = pl.multiple_of(1024 * (1 - core) + 512 * x + HS * t, HS)
+                out.ref[rows, pl.ds(at, HS)] = other_ref[a, part].astype(F32)
+        out.push(rows)
 
 
 def exchange(operand):
@@ -376,14 +410,15 @@
     half = width // 2
     quarter = half // 2
 
+    side = ("R", (BLOCK, half), BF16)
     part = ("R", (BLOCK, quarter), BF16)
-    packed, own_half, up_keep, up_core, up_pair, up_diag = call(
+    packed, own_half, up_mine, up_send, up_pair, up_diag = call(
         pack_kernel,
         [
             ("S", core_ref), ("S", high_ref), ("H", query_rows, 0), ("H", key_rows, 0),
             ("H", value_rows, 0), ("H", out_weight), ("H", upstream, 0),
         ],
-        [("R", (HEADS, 3, BLOCK, HS), BF16), ("R", (HS, half), BF16), part, part, part, part],
+        [("R", (HEADS, 3, BLOCK, HS), BF16), ("R", (HS, half), BF16), side, side, part, part],
     )
     own = exchange(packed)
 
@@ -402,16 +437,14 @@
     def step(value, s):
         return lax.ppermute(value, "fsdp", [(i, i ^ s) for i in range(8)])
 
-    own_half = after(own_half, end, valid, valid_here)
     over = step(own_half, 4)
     one, three = step(own_half, 1), step(own_half, 3)
     over_one, over_three = step(over, 1), step(over, 3)
     two, over_two = step(one, 3), step(over_three, 1)
-    pieces = [one, two, three, over, over_one, over_two, over_three]
-    mine = [("V", piece) for piece in pieces]
-    other_half = [("V", lax.ppermute(piece, "ctx", CORE_SWAP)) for piece in pieces]
-
-    own = after(own, end, valid, valid_here, over, one, three)
+    pieces = [own_half, one, two, three, over, over_one, over_two, over_three]
+    up_other = lax.ppermute(up_send, "ctx", CORE_SWAP)
+
+    own = after(own, end, valid, valid_here, one, three, over_one, over_three, up_other)
     other = lax.ppermute(own, "ctx", CORE_SWAP)
     pairs = 4 * TILE * SPAN * 5 // 2
     rows = ("H", (LEN, HS), BF16)
@@ -431,27 +464,29 @@
     context_mine = exchange(context)
     up_pair = lax.ppermute(after(up_pair, context), "ctx", PAIR_SWAP)
     up_diag = lax.ppermute(after(up_diag, context), "ctx", DIAG_SWAP)
-    up_core = lax.ppermute(after(up_core, context), "ctx", CORE_SWAP)
-    grads = call(
+    context_other = lax.ppermute(after(context_mine, up_pair, up_diag), "ctx", CORE_SWAP)
+    grads_keep, grads_send = call(
         project_kernel,
-        [
-            ("S", core_ref), ("S", row_ref), ("V", valid_here), ("H", upstream, 0),
-            ("H", out_weight), *mine, *other_half,
-        ],
-        [("H", (HEADS, BLOCK, HS), BF16)],
-        flops=2 * 128 * 1024 * 2048,
-    )
-    grads = exchange(after(grads, context_mine))
-    context_other = lax.ppermute(context_mine, "ctx", CORE_SWAP)
+        [("S", row_ref), ("A", up_mine), ("A", up_other), *[("V", piece) for piece in pieces]],
+        [("V", (HEADS, BLOCK, HS), F32), ("V", (HEADS, BLOCK, HS), BF16)],
+        flops=2 * 256 * 1024 * 1024,
+    )
+    grads_came = lax.ppermute(grads_send, "ctx", CORE_SWAP)
     terms = call(
         weight_kernel,
         [
-            ("H", up_keep), ("A", up_pair), ("A", up_core), ("A", up_diag),
+            ("S", high_ref), ("A", up_mine), ("A", up_other), ("A", up_pair), ("A", up_diag),
             ("A", context_mine), ("A", context_other),
         ],
         [("H", (32, 32, quarter), BF16)],
         flops=2 * 512 * 1024 * 512,
     )
+    grads = call(
+        add_kernel,
+        [("V", valid_here), ("V", grads_keep), ("V", grads_came)],
+        [("V", (HEADS, BLOCK, HS), BF16)],
+    )
+    grads = exchange(after(grads, context_mine, up_pair, up_diag))
     terms = lax.all_to_all(
         after(terms, grads),
         ("ctx", "fsdp"),
@@ -475,27 +510,44 @@
         flops=10 * pairs * HS,
     )
     came = lax.ppermute(send, "ctx", CORE_SWAP)
+    side = ("H", (BLOCK, half), BF16)
+    attended_keep, attended_send = call(
+        attend_kernel,
+        [
+            ("S", row_ref), ("A", after(context_mine, grads), (slice(None), 0)),
+            ("A", context_other, (slice(None), 0)), *[("A", piece) for piece in pieces],
+        ],
+        [side, side],
+        flops=2 * 256 * 1024 * 1024,
+    )
+    attended_came = lax.ppermute(attended_send, "ctx", CORE_SWAP)
     attended = call(
-        attend_kernel,
-        [
-            ("S", core_ref), ("S", row_ref), ("A", context_mine, (slice(None), 0)),
-            ("H", out_weight), *mine, *other_half,
-        ],
-        [("H", (1, BLOCK, width), BF16)],
-        flops=2 * 128 * 1024 * 2048,
+        place_kernel,
+        [("S", core_ref), ("A", attended_keep), ("A", attended_came)],
+        [("R", (1, BLOCK, width), BF16)],
     )
     joined = call(
         join_kernel,
-        [("H", after(dq, attended)), ("H", keep), ("H", came), ("V", terms)],
-        [("V", (CHIPS, 4, BLOCK, HS), BF16)],
+        [("A", dq), ("A", keep), ("A", came)],
+        [("R", (CHIPS, 4, BLOCK, HS), BF16)],
+        scratch=(pltpu.VMEM((CHIPS, 3, BLOCK, HS), BF16),),
+    )
+    joined = call(
+        total_kernel,
+        [("R", after(joined, attended)), ("V", terms)],
+        [("R", (CHIPS, 4, BLOCK, HS), BF16)],
+        scratch=(pltpu.VMEM((BLOCK, HS), BF16),),
+        aliases={0: 0},
     )
     result = exchange(joined)
-    weight_part = lax.ppermute(result[:, 3], "ctx", CORE_SWAP)
+    weight_mine = result[:, 3]
+    weight_other = lax.ppermute(weight_mine, "ctx", CORE_SWAP)
     grad = ("R", (1, BLOCK, HEADS * HS), BF16)
-    query_grad, key_grad, value_grad, weight_grad = call(
-        unpack_kernel,
-        [("S", core_ref), ("V", result), ("V", weight_part)],
-        [grad, grad, grad, ("H", (HS, width), F32)],
+    query_grad, key_grad, value_grad = call(unpack_kernel, [("V", result)], [grad, grad, grad])
+    weight_grad = call(
+        widen_kernel,
+        [("S", core_ref), ("V", weight_mine), ("V", weight_other)],
+        [("H", (HS, width), F32)],
     )
     return (attended, query_grad, key_grad, value_grad, weight_grad)
 

time: 136 us -> 124 us (0.912)
  starting transfers between devices: 52.9 us -> 43.1 us
  waiting for transfers between devices: 31.3 us -> 27.2 us
    all_to_all x1, waiting for transfers between devices: 4.98 us -> 0.01 us  [shards(): lax.all_to_all(after(terms, grads), ('ctx', 'fsdp'), split_axis=0, concat...]
    ppermute x7, waiting for transfers between devices: 13.1 us -> 8.46 us  [step(): return lax.ppermute(value, 'fsdp', [(i, i ^ s) for i in range(8)])]
    all_to_all x3, starting transfers between devices: 21.5 us -> 17.1 us  [exchange(): lax.all_to_all(operand, 'ctx', split_axis=0, concat_axis=0, tiled=True, a...]
    ppermute x10 -> x5, starting transfers between devices: 10 us -> 6.72 us  [the longest x1 4.03 us: shards(): weight_other = lax.ppermute(weight_mine, 'ctx', CORE_SWAP)]
    all_to_all x3, waiting for transfers between devices: 2.42 us -> 5.28 us  [exchange(): lax.all_to_all(operand, 'ctx', split_axis=0, concat_axis=0, tiled=True, a...]
    all_to_all x1, starting transfers between devices: 6.9 us -> 4.11 us  [shards(): lax.all_to_all(after(terms, grads), ('ctx', 'fsdp'), split_axis=0, concat...]
    ppermute x1, waiting for transfers between devices: 4.74 us -> 7.22 us  [shards(): up_pair = lax.ppermute(after(up_pair, context), 'ctx', PAIR_SWAP)]
    ppermute x7, starting transfers between devices: 9.74 us -> 7.48 us  [step(): return lax.ppermute(value, 'fsdp', [(i, i ^ s) for i in range(8)])]
  transfers between devices with their start and end apart: 25 -> 20, of which waited for: 10 -> 8; matrix products, arithmetic and copies ran while one was open for 1% -> 1% of each run, Pallas kernels for 17% -> 16%
where the time goes in v6:
time: 124 us
  starting transfers between devices  43.1 us (35%)
  Pallas kernels  29.6 us (24%)
  waiting for transfers between devices  27.2 us (22%)
  blocking collectives  18.8 us (15%)
  local copies, waits for them, and re-layouts  2.1 us (2%)
  between operations  1.84 us (1%)
    pallas_call x12, Pallas kernels, call(): pl.pallas_call(body, out_shape=[SPACES[o[0]](o[1], o[2]) if o[0] in 'HR'...  29.6 us
    all_to_all x1, blocking collectives, exchange(): lax.all_to_all(operand, 'ctx', split_axis=0, concat_axis=0, tiled=True, a...  18.8 us
    all_to_all x3, starting transfers between devices, exchange(): lax.all_to_all(operand, 'ctx', split_axis=0, concat_axis=0, tiled=True, a...  17.1 us
    ppermute x7, waiting for transfers between devices, step(): return lax.ppermute(value, 'fsdp', [(i, i ^ s) for i in range(8)])  8.46 us
    ppermute x7, starting transfers between devices, step(): return lax.ppermute(value, 'fsdp', [(i, i ^ s) for i in range(8)])  7.48 us
    ppermute x1, waiting for transfers between devices, shards(): up_pair = lax.ppermute(after(up_pair, context), 'ctx', PAIR_SWAP)  7.22 us
    all_to_all x3, waiting for transfers between devices, exchange(): lax.all_to_all(operand, 'ctx', split_axis=0, concat_axis=0, tiled=True, a...  5.28 us
    all_to_all x1, starting transfers between devices, shards(): lax.all_to_all(after(terms, grads), ('ctx', 'fsdp'), split_axis=0, concat...  4.11 us
  transfers between devices with their start and end apart: 20, of which 8 were waited for; matrix products, arithmetic and copies ran while one was open for 1% of the time, Pallas kernels for 16%

profile of v6, /device:TPU:1, one launch (start us, length us, event | category | flops | bytes accessed | tf_op | source)
XLA Modules:
  0.0 123.6 jit_solution(14895254994151589731)
XLA Ops:
  0.6 2.9 %shard_map.110 = (bf16[8,3,128,128]{3,2,1,0:T(8,128)(2,1)}, bf16[128,1024]{1,0:T(8,128)(2,1)}, bf16[128,1024]{1,0:T(8,128)(2,1)}, bf16[128,1024]{1,0:T(8,128)(2,...) custom-call(s32[1]{0:T(128)} %bitcast.refs_0_, s32[1]{0:T(128)} %bitcast.2.refs_1_.refs_0_, ...), custom_call_target="tpu_custom_call" | custom-call | bytes 2000000 | tf_op jit(solution)/shard_map/pallas_call | solution.py:112
  3.6 2.5 %collective-permute-start = (bf16[128,1024]{1,0:T(8,128)(2,1)}, bf16[128,1024]{1,0:T(8,128)(2,1)S(1)}, u32[]{:S(2)}, u32[]{:S(2)}) collective-permute-start(bf16[128,1024]{1,0:T(8,128)(2,1)} %get-tuple-element.35.refs_3_), channel_id=1, source_target_pairs={{0,1},{1,0},{2,3},{3,2},{4,5},{5,4},{6,7},{7,6},{8,9},{9,8},{10,11... | collective-permute-start | bytes 786440 | tf_op jit(solution)/shard_map/ppermute | solution.py:438
  6.1 2.2 %collective-permute-start.1 = (bf16[128,1024]{1,0:T(8,128)(2,1)}, bf16[128,1024]{1,0:T(8,128)(2,1)S(1)}, u32[]{:S(2)}, u32[]{:S(2)}) collective-permute-start(bf16[128,1024]{1,0:T(8,128)(2,1)} %get-tuple-element.35.refs_3_), channel_id=1, source_target_pairs={{0,3},{1,2},{2,1},{3,0},{4,7},{5,6},{6,5},{7,4},{8,11},{9,10},{10,... | collective-permute-start | bytes 786440 | tf_op jit(solution)/shard_map/ppermute | solution.py:438
  9.6 6.4 %all-to-all-start = ((bf16[8,3,128,128]{3,2,1,0:T(8,128)(2,1)}), bf16[8,3,128,128]{3,2,1,0:T(8,128)(2,1)S(1)}, u32[]{:S(2)}, u32[]{:S(2)}) async-start(bf16[8,3,128,128]{3,2,1,0:T(8,128)(2,1)} %get-tuple-element.34), calls=%async_computation | async-start | bytes 1572864 | tf_op jit(solution)/shard_map/all_to_all | solution.py:393
  16.0 1.9 %collective-permute-start.5 = (bf16[128,1024]{1,0:T(8,128)(2,1)S(1)}, bf16[128,1024]{1,0:T(8,128)(2,1)S(1)}, u32[]{:S(2)}, u32[]{:S(2)}) collective-permute-start(bf16[128,1024]{1,0:T(8,128)(2,1)S(1)} %copy-done.15), channel_id=1, source_target_pairs={{0,8},{8,0},{16,24},{24,16},{32,40},{40,32},{48,56},{56,48},{64,72... | collective-permute-start | bytes 786440 | tf_op jit(solution)/shard_map/ppermute | solution.py:445
  20.7 6.8 %collective-permute-done.3.refs_8_ = bf16[128,1024]{1,0:T(8,128)(2,1)S(1)} collective-permute-done((bf16[128,1024]{1,0:T(8,128)(2,1)S(1)}, bf16[128,1024]{1,0:T(8,128)(2,1)S(1)}, u32[]{:S(2)}, u32[]{:S(2)}) %collective-permute-start.3) | collective-permute-done | bytes 262176 | tf_op jit(solution)/shard_map/ppermute | solution.py:438
  27.5 1.6 %collective-permute-done.4.refs_10_ = bf16[128,1024]{1,0:T(8,128)(2,1)S(1)} collective-permute-done((bf16[128,1024]{1,0:T(8,128)(2,1)S(1)}, bf16[128,1024]{1,0:T(8,128)(2,1)S(1)}, u32[]{:S(2)}, u32[]{:S(2)}) %collective-permute-start.4) | collective-permute-done | bytes 262176 | tf_op jit(solution)/shard_map/ppermute | solution.py:438
  30.5 1.9 %collective-permute-done.6.refs_2_ = bf16[8,3,128,128]{3,2,1,0:T(8,128)(2,1)S(1)} collective-permute-done((bf16[8,3,128,128]{3,2,1,0:T(8,128)(2,1)S(1)}, bf16[8,3,128,128]{3,2,1,0:T(8,128)(2,1)S(1)}, u32[]{:S(2)}, u32[]{:S(2)}) %collective-permute-start.6) | collective-permute-done | bytes 786464 | tf_op jit(solution)/shard_map/ppermute | solution.py:448
  32.4 4.0 %shard_map.111 = (bf16[8,2,128,128]{3,2,1,0:T(8,128)(2,1)}, f32[4,1,256]{2,1,0:T(1,128)}, bf16[8,128,128]{2,1,0:T(8,128)(2,1)}, bf16[2048,128]{1,0:T(8,128)(2,1)}, bf16[2048,128]{1,0:T(8,128)(2,1)}) custom-call(s32[1]{0:T(128)} %bitcast.refs_0_, bf16[8,3,128,128]{3,2,1,0:T(8,128)(2,1)S(1)} %all-to-all-done.refs_1_, ...), custom_call_target="tpu_custom_call" | custom-call | flops 671088640 | bytes 2000000 | tf_op jit(solution)/shard_map/pallas_call | solution.py:112
  36.4 6.8 %all-to-all-start.1 = ((bf16[8,2,128,128]{3,2,1,0:T(8,128)(2,1)}), bf16[8,2,128,128]{3,2,1,0:T(8,128)(2,1)S(1)}, u32[]{:S(2)}, u32[]{:S(2)}) async-start(bf16[8,2,128,128]{3,2,1,0:T(8,128)(2,1)} %get-tuple-element.38.refs_5_), calls=%async_computation.1 | async-start | bytes 1048576 | tf_op jit(solution)/shard_map/all_to_all | solution.py:393
  43.6 3.0 %collective-permute-start.10 = (bf16[128,512]{1,0:T(8,128)(2,1)S(1)}, bf16[128,512]{1,0:T(8,128)(2,1)S(1)}, u32[]{:S(2)}, u32[]{:S(2)}) collective-permute-start(bf16[128,512]{1,0:T(8,128)(2,1)S(1)} %copy-done.17), channel_id=1, source_target_pairs={{0,64},{8,72},{16,80},{24,88},{32,96},{40,104},{48,112},{56,120},{... | collective-permute-start | bytes 393224 | tf_op jit(solution)/shard_map/ppermute | solution.py:465
  47.7 7.2 %collective-permute-done.10.refs_3_ = bf16[128,512]{1,0:T(8,128)(2,1)S(1)} collective-permute-done((bf16[128,512]{1,0:T(8,128)(2,1)S(1)}, bf16[128,512]{1,0:T(8,128)(2,1)S(1)}, u32[]{:S(2)}, u32[]{:S(2)}) %collective-permute-start.10) | collective-permute-done | bytes 131104 | tf_op jit(solution)/shard_map/ppermute | solution.py:465
  55.6 3.0 %collective-permute-done.11.refs_4_ = bf16[128,512]{1,0:T(8,128)(2,1)S(1)} collective-permute-done((bf16[128,512]{1,0:T(8,128)(2,1)S(1)}, bf16[128,512]{1,0:T(8,128)(2,1)S(1)}, u32[]{:S(2)}, u32[]{:S(2)}) %collective-permute-start.11) | collective-permute-done | bytes 131104 | tf_op jit(solution)/shard_map/ppermute | solution.py:466
  59.3 2.7 %shard_map.112 = (f32[8,128,128]{2,1,0:T(8,128)S(1)}, bf16[8,128,128]{2,1,0:T(8,128)(2,1)S(1)}) custom-call(s32[1]{0:T(128)} %bitcast.1.refs_0_, bf16[128,1024]{1,0:T(8,128)(2,1)S(1)} %copy-done.1, bf16[128,1024]{1,0:T(8,128)(2,1)S(1)} %collective-permute-done.5.refs_2_, bf16[128,1024]{1,0:T(8,128)(2,1)S(1)} %copy-done.2, ...), custom_call_target="tpu_custom_call" | custom-call | flops 536870912 | bytes 2000000 | tf_op jit(solution)/shard_map/pallas_call | solution.py:112
  65.1 4.0 %all-to-all-start.2 = ((bf16[8,128,128]{2,1,0:T(8,128)(2,1)}), bf16[8,128,128]{2,1,0:T(8,128)(2,1)S(1)}, u32[]{:S(2)}, u32[]{:S(2)}) async-start(bf16[8,128,128]{2,1,0:T(8,128)(2,1)} %shard_map.113), calls=%async_computation.2 | async-start | bytes 524288 | tf_op jit(solution)/shard_map/all_to_all | solution.py:393
  69.1 2.3 %shard_map.118 = bf16[32,32,512]{2,1,0:T(8,128)(2,1)} custom-call(s32[1]{0:T(128)} %bitcast.2.refs_1_.refs_0_, bf16[128,1024]{1,0:T(8,128)(2,1)S(1)} %copy-done.1, bf16[128,1024]{1,0:T(8,128)(2,1)S(1)} %collective-permute-done.5.refs_2_, bf16[128,512]{1,0:T(8,128)(2,1)S(1)} %copy-done.10, bf16[128,512]{1,0:T(8,128)(2,1)S(1)} %copy-done.12, ...), custom_call_target="tpu_custom_call" | custom-call | flops 536870912 | bytes 2000000 | tf_op jit(solution)/shard_map/pallas_call | solution.py:112
  71.3 5.3 %all-to-all-done.2.refs_3_ = bf16[8,128,128]{2,1,0:T(8,128)(2,1)S(1)} async-done(((bf16[8,128,128]{2,1,0:T(8,128)(2,1)}), bf16[8,128,128]{2,1,0:T(8,128)(2,1)S(1)}, u32[]{:S(2)}, u32[]{:S(2)}) %all-to-all-start.2) | async-done | bytes 262176 | tf_op jit(solution)/shard_map/all_to_all | solution.py:393
  77.3 4.1 %all-to-all-start.3 = ((bf16[32,32,512]{2,1,0:T(8,128)(2,1)}), bf16[32,32,512]{2,1,0:T(8,128)(2,1)S(1)}, u32[]{:S(2)}, u32[]{:S(2)}) async-start(bf16[32,32,512]{2,1,0:T(8,128)(2,1)} %shard_map.118), calls=%async_computation.3 | async-start | bytes 2097152 | tf_op jit(solution)/shard_map/all_to_all | solution.py:490
  81.5 6.8 %shard_map.116 = (bf16[8,128,128]{2,1,0:T(8,128)(2,1)}, f32[8,2,128,128]{3,2,1,0:T(8,128)}, bf16[8,2,128,128]{3,2,1,0:T(8,128)(2,1)}) custom-call(s32[1]{0:T(128)} %bitcast.refs_0_, bf16[8,128,128]{2,1,0:T(8,128)(2,1)} %get-tuple-element.51.refs_1_, bf16[2048,128]{1,0:T(8,128)(2,1)} %get-tuple-element.52.refs_2_, bf16[8,128,128]{2,1,0:T(8,128)(2,1)} %copy-done.13, ...), custom_call_target="tpu_custom_call" | custom-call | flops 1677721600 | bytes 2000000 | tf_op jit(solution)/shard_map/pallas_call | solution.py:112
  88.3 2.2 %collective-permute-start.14 = (bf16[8,2,128,128]{3,2,1,0:T(8,128)(2,1)}, bf16[8,2,128,128]{3,2,1,0:T(8,128)(2,1)S(1)}, u32[]{:S(2)}, u32[]{:S(2)}) collective-permute-start(bf16[8,2,128,128]{3,2,1,0:T(8,128)(2,1)} %get-tuple-element.57), channel_id=1, source_target_pairs={{0,8},{8,0},{16,24},{24,16},{32,40},{40,32},{48,56},{56,48},{64,72... | collective-permute-start | bytes 1572872 | tf_op jit(solution)/shard_map/ppermute | solution.py:512
  90.5 3.0 %shard_map.114 = (bf16[128,1024]{1,0:T(8,128)(2,1)}, bf16[128,1024]{1,0:T(8,128)(2,1)}) custom-call(s32[1]{0:T(128)} %bitcast.1.refs_0_, bf16[8,2,128,128]{3,2,1,0:T(8,128)(2,1)S(1)} %all-to-all-done.1.refs_1_.refs_5_, bf16[8,2,128,128]{3,2,1,0:T(8,128)(2,1)S(1)} %collective-permute-done.12.refs_2_.refs_6_, bf16[128,1024]{1,0:T(8,128)(2,1)S(1)} %copy-done.2, ...), custom_call_target="tpu_custom_call" | custom-call | flops 536870912 | bytes 2000000 | tf_op jit(solution)/shard_map/pallas_call | solution.py:112
  93.7 1.4 %shard_map.117.refs_0_ = bf16[8,4,128,128]{3,2,1,0:T(8,128)(2,1)} custom-call(bf16[8,128,128]{2,1,0:T(8,128)(2,1)S(1)} %copy-done.8, f32[8,2,128,128]{3,2,1,0:T(8,128)S(1)} %copy-done, bf16[8,2,128,128]{3,2,1,0:T(8,128)(2,1)S(1)} %collective-permute-done.14.refs_2_), custom_call_target="tpu_custom_call" | custom-call | bytes 2000000 | tf_op jit(solution)/shard_map/pallas_call | solution.py:112
  97.9 18.8 %all_to_all.25.refs_0_ = bf16[8,4,128,128]{3,2,1,0:T(8,128)(2,1)S(1)} all-to-all(bf16[8,4,128,128]{3,2,1,0:T(8,128)(2,1)} %shard_map.119), channel_id=1, replica_groups={{0,16,32,48,64,80,96,112},{8,24,40,56,72,88,104,120},{1,17,33,49,65,81,..., dimensions={0} | all-to-all | bytes 2097152 | tf_op jit(solution)/shard_map/all_to_all | solution.py:393
  116.7 4.0 %collective-permute-start.15 = (bf16[8,128,128]{2,1,0:T(8,128)(2,1)S(1)}, bf16[8,128,128]{2,1,0:T(8,128)(2,1)S(1)}, u32[]{:S(2)}, u32[]{:S(2)}) collective-permute-start(bf16[8,128,128]{2,1,0:T(8,128)(2,1)S(1)} %slice_bitcast_fusion.refs_1_), channel_id=1, source_target_pairs={{0,8},{8,0},{16,24},{24,16},{32,40},{40,32},{48,56},{56,48},{64,72... | collective-permute-start | bytes 786440 | tf_op jit(solution)/shard_map/ppermute | solution.py:544
  (71 shorter events, 16.9 us)
Async XLA Ops:
  3.6 14.9 %copy-start.14 = (s32[1,2048]{1,0:T(1,128)S(1)}, s32[1,2048]{1,0:T(1,128)}, u32[]{:S(2)}) copy-start(s32[1,2048]{1,0:T(1,128)} %param.10) | copy-start | bytes 24580
  3.6 17.1 %collective-permute-start = (bf16[128,1024]{1,0:T(8,128)(2,1)}, bf16[128,1024]{1,0:T(8,128)(2,1)S(1)}, u32[]{:S(2)}, u32[]{:S(2)}) collective-permute-start(bf16[128,1024]{1,0:T(8,128)(2,1)} %get-tuple-element.35.refs_3_), channel_id=1, source_target_pairs={{0,1},{1,0},{2,3},{3,2},{4,5},{5,4},{6,7},{7,6},{8,9},{9,8},{10,11... | collective-permute-start | bytes 786440 | tf_op jit(solution)/shard_map/ppermute | solution.py:438
  6.1 14.6 %collective-permute-start.1 = (bf16[128,1024]{1,0:T(8,128)(2,1)}, bf16[128,1024]{1,0:T(8,128)(2,1)S(1)}, u32[]{:S(2)}, u32[]{:S(2)}) collective-permute-start(bf16[128,1024]{1,0:T(8,128)(2,1)} %get-tuple-element.35.refs_3_), channel_id=1, source_target_pairs={{0,3},{1,2},{2,1},{3,0},{4,7},{5,6},{6,5},{7,4},{8,11},{9,10},{10,... | collective-permute-start | bytes 786440 | tf_op jit(solution)/shard_map/ppermute | solution.py:438
  8.4 11.1 %collective-permute-start.2 = (bf16[128,1024]{1,0:T(8,128)(2,1)}, bf16[128,1024]{1,0:T(8,128)(2,1)S(1)}, u32[]{:S(2)}, u32[]{:S(2)}) collective-permute-start(bf16[128,1024]{1,0:T(8,128)(2,1)} %get-tuple-element.35.refs_3_), channel_id=1, source_target_pairs={{0,4},{1,5},{2,6},{3,7},{4,0},{5,1},{6,2},{7,3},{8,12},{9,13},{10,... | collective-permute-start | bytes 786440 | tf_op jit(solution)/shard_map/ppermute | solution.py:438
  9.6 19.6 %all-to-all-start = ((bf16[8,3,128,128]{3,2,1,0:T(8,128)(2,1)}), bf16[8,3,128,128]{3,2,1,0:T(8,128)(2,1)S(1)}, u32[]{:S(2)}, u32[]{:S(2)}) async-start(bf16[8,3,128,128]{3,2,1,0:T(8,128)(2,1)} %get-tuple-element.34), calls=%async_computation | async-start | bytes 1572864 | tf_op jit(solution)/shard_map/all_to_all | solution.py:393
  16.0 4.8 %collective-permute-start.5 = (bf16[128,1024]{1,0:T(8,128)(2,1)S(1)}, bf16[128,1024]{1,0:T(8,128)(2,1)S(1)}, u32[]{:S(2)}, u32[]{:S(2)}) collective-permute-start(bf16[128,1024]{1,0:T(8,128)(2,1)S(1)} %copy-done.15), channel_id=1, source_target_pairs={{0,8},{8,0},{16,24},{24,16},{32,40},{40,32},{48,56},{56,48},{64,72... | collective-permute-start | bytes 786440 | tf_op jit(solution)/shard_map/ppermute | solution.py:445
  19.5 8.0 %collective-permute-start.3 = (bf16[128,1024]{1,0:T(8,128)(2,1)S(1)}, bf16[128,1024]{1,0:T(8,128)(2,1)S(1)}, u32[]{:S(2)}, u32[]{:S(2)}) collective-permute-start(bf16[128,1024]{1,0:T(8,128)(2,1)S(1)} %collective-permute-done.2.refs_7_), channel_id=1, source_target_pairs={{0,1},{1,0},{2,3},{3,2},{4,5},{5,4},{6,7},{7,6},{8,9},{9,8},{10,11... | collective-permute-start | bytes 786440 | tf_op jit(solution)/shard_map/ppermute | solution.py:438
  20.4 8.8 %collective-permute-start.4 = (bf16[128,1024]{1,0:T(8,128)(2,1)S(1)}, bf16[128,1024]{1,0:T(8,128)(2,1)S(1)}, u32[]{:S(2)}, u32[]{:S(2)}) collective-permute-start(bf16[128,1024]{1,0:T(8,128)(2,1)S(1)} %collective-permute-done.2.refs_7_), channel_id=1, source_target_pairs={{0,3},{1,2},{2,1},{3,0},{4,7},{5,6},{6,5},{7,4},{8,11},{9,10},{10,... | collective-permute-start | bytes 786440 | tf_op jit(solution)/shard_map/ppermute | solution.py:438
  29.2 30.1 %copy-start.3 = (bf16[128,1024]{1,0:T(8,128)(2,1)}, bf16[128,1024]{1,0:T(8,128)(2,1)S(1)}, u32[]{:S(2)}) copy-start(bf16[128,1024]{1,0:T(8,128)(2,1)S(1)} %collective-permute-done.4.refs_10_) | copy-start | bytes 786436
  29.2 3.2 %collective-permute-start.6 = (bf16[8,3,128,128]{3,2,1,0:T(8,128)(2,1)S(1)}, bf16[8,3,128,128]{3,2,1,0:T(8,128)(2,1)S(1)}, u32[]{:S(2)}, u32[]{:S(2)}) collective-permute-start(bf16[8,3,128,128]{3,2,1,0:T(8,128)(2,1)S(1)} %all-to-all-done.refs_1_), channel_id=1, source_target_pairs={{0,8},{8,0},{16,24},{24,16},{32,40},{40,32},{48,56},{56,48},{64,72... | collective-permute-start | bytes 2359304 | tf_op jit(solution)/shard_map/ppermute | solution.py:448
  36.4 22.8 %copy-start.1 = (bf16[128,1024]{1,0:T(8,128)(2,1)S(1)}, bf16[128,1024]{1,0:T(8,128)(2,1)}, u32[]{:S(2)}) copy-start(bf16[128,1024]{1,0:T(8,128)(2,1)} %get-tuple-element.39.refs_1_) | copy-start | bytes 786436
  36.4 22.8 %copy-start.2 = (bf16[128,1024]{1,0:T(8,128)(2,1)S(1)}, bf16[128,1024]{1,0:T(8,128)(2,1)}, u32[]{:S(2)}) copy-start(bf16[128,1024]{1,0:T(8,128)(2,1)} %get-tuple-element.35.refs_3_) | copy-start | bytes 786436
  36.4 22.8 %all-to-all-start.1 = ((bf16[8,2,128,128]{3,2,1,0:T(8,128)(2,1)}), bf16[8,2,128,128]{3,2,1,0:T(8,128)(2,1)S(1)}, u32[]{:S(2)}, u32[]{:S(2)}) async-start(bf16[8,2,128,128]{3,2,1,0:T(8,128)(2,1)} %get-tuple-element.38.refs_5_), calls=%async_computation.1 | async-start | bytes 1048576 | tf_op jit(solution)/shard_map/all_to_all | solution.py:393
  43.2 16.0 %collective-permute-start.7 = (bf16[128,1024]{1,0:T(8,128)(2,1)S(1)}, bf16[128,1024]{1,0:T(8,128)(2,1)S(1)}, u32[]{:S(2)}, u32[]{:S(2)}) collective-permute-start(bf16[128,1024]{1,0:T(8,128)(2,1)S(1)} %collective-permute-done.refs_4_), channel_id=1, source_target_pairs={{0,3},{1,2},{2,1},{3,0},{4,7},{5,6},{6,5},{7,4},{8,11},{9,10},{10,... | collective-permute-start | bytes 786440 | tf_op jit(solution)/shard_map/ppermute | solution.py:438
  43.6 15.7 %collective-permute-start.8 = (bf16[128,1024]{1,0:T(8,128)(2,1)S(1)}, bf16[128,1024]{1,0:T(8,128)(2,1)}, u32[]{:S(2)}, u32[]{:S(2)}) collective-permute-start(bf16[128,1024]{1,0:T(8,128)(2,1)S(1)} %collective-permute-done.4.refs_10_), channel_id=1, source_target_pairs={{0,1},{1,0},{2,3},{3,2},{4,5},{5,4},{6,7},{7,6},{8,9},{9,8},{10,11... | collective-permute-start | bytes 786440 | tf_op jit(solution)/shard_map/ppermute | solution.py:438
  43.6 11.4 %collective-permute-start.10 = (bf16[128,512]{1,0:T(8,128)(2,1)S(1)}, bf16[128,512]{1,0:T(8,128)(2,1)S(1)}, u32[]{:S(2)}, u32[]{:S(2)}) collective-permute-start(bf16[128,512]{1,0:T(8,128)(2,1)S(1)} %copy-done.17), channel_id=1, source_target_pairs={{0,64},{8,72},{16,80},{24,88},{32,96},{40,104},{48,112},{56,120},{... | collective-permute-start | bytes 393224 | tf_op jit(solution)/shard_map/ppermute | solution.py:465
  46.5 12.1 %collective-permute-start.11 = (bf16[128,512]{1,0:T(8,128)(2,1)S(1)}, bf16[128,512]{1,0:T(8,128)(2,1)S(1)}, u32[]{:S(2)}, u32[]{:S(2)}) collective-permute-start(bf16[128,512]{1,0:T(8,128)(2,1)S(1)} %copy-done.16), channel_id=1, source_target_pairs={{0,72},{8,64},{16,88},{24,80},{32,104},{40,96},{48,120},{56,112},{... | collective-permute-start | bytes 393224 | tf_op jit(solution)/shard_map/ppermute | solution.py:466
  59.2 9.8 %collective-permute-start.12 = (bf16[8,2,128,128]{3,2,1,0:T(8,128)(2,1)S(1)}, bf16[8,2,128,128]{3,2,1,0:T(8,128)(2,1)S(1)}, u32[]{:S(2)}, u32[]{:S(2)}) collective-permute-start(bf16[8,2,128,128]{3,2,1,0:T(8,128)(2,1)S(1)} %all-to-all-done.1.refs_1_.refs_5_), channel_id=1, source_target_pairs={{0,8},{8,0},{16,24},{24,16},{32,40},{40,32},{48,56},{56,48},{64,72... | collective-permute-start | bytes 1572872 | tf_op jit(solution)/shard_map/ppermute | solution.py:467
  62.1 1.8 %collective-permute-start.9 = (bf16[8,128,128]{2,1,0:T(8,128)(2,1)S(1)}, bf16[8,128,128]{2,1,0:T(8,128)(2,1)S(1)}, u32[]{:S(2)}, u32[]{:S(2)}) collective-permute-start(bf16[8,128,128]{2,1,0:T(8,128)(2,1)S(1)} %get-tuple-element.41), channel_id=1, source_target_pairs={{0,8},{8,0},{16,24},{24,16},{32,40},{40,32},{48,56},{56,48},{64,72... | collective-permute-start | bytes 786440 | tf_op jit(solution)/shard_map/ppermute | solution.py:474
  65.1 11.6 %all-to-all-start.2 = ((bf16[8,128,128]{2,1,0:T(8,128)(2,1)}), bf16[8,128,128]{2,1,0:T(8,128)(2,1)S(1)}, u32[]{:S(2)}, u32[]{:S(2)}) async-start(bf16[8,128,128]{2,1,0:T(8,128)(2,1)} %shard_map.113), calls=%async_computation.2 | async-start | bytes 524288 | tf_op jit(solution)/shard_map/all_to_all | solution.py:393
  77.3 19.3 %all-to-all-start.3 = ((bf16[32,32,512]{2,1,0:T(8,128)(2,1)}), bf16[32,32,512]{2,1,0:T(8,128)(2,1)S(1)}, u32[]{:S(2)}, u32[]{:S(2)}) async-start(bf16[32,32,512]{2,1,0:T(8,128)(2,1)} %shard_map.118), calls=%async_computation.3 | async-start | bytes 2097152 | tf_op jit(solution)/shard_map/all_to_all | solution.py:490
  88.3 5.4 %collective-permute-start.14 = (bf16[8,2,128,128]{3,2,1,0:T(8,128)(2,1)}, bf16[8,2,128,128]{3,2,1,0:T(8,128)(2,1)S(1)}, u32[]{:S(2)}, u32[]{:S(2)}) collective-permute-start(bf16[8,2,128,128]{3,2,1,0:T(8,128)(2,1)} %get-tuple-element.57), channel_id=1, source_target_pairs={{0,8},{8,0},{16,24},{24,16},{32,40},{40,32},{48,56},{56,48},{64,72... | collective-permute-start | bytes 1572872 | tf_op jit(solution)/shard_map/ppermute | solution.py:512
  93.5 1.8 %collective-permute-start.13 = (bf16[128,1024]{1,0:T(8,128)(2,1)}, bf16[128,1024]{1,0:T(8,128)(2,1)S(1)}, u32[]{:S(2)}, u32[]{:S(2)}) collective-permute-start(bf16[128,1024]{1,0:T(8,128)(2,1)} %get-tuple-element.50), channel_id=1, source_target_pairs={{0,8},{8,0},{16,24},{24,16},{32,40},{40,32},{48,56},{56,48},{64,72... | collective-permute-start | bytes 786440 | tf_op jit(solution)/shard_map/ppermute | solution.py:523
  116.7 5.3 %collective-permute-start.15 = (bf16[8,128,128]{2,1,0:T(8,128)(2,1)S(1)}, bf16[8,128,128]{2,1,0:T(8,128)(2,1)S(1)}, u32[]{:S(2)}, u32[]{:S(2)}) collective-permute-start(bf16[8,128,128]{2,1,0:T(8,128)(2,1)S(1)} %slice_bitcast_fusion.refs_1_), channel_id=1, source_target_pairs={{0,8},{8,0},{16,24},{24,16},{32,40},{40,32},{48,56},{56,48},{64,72... | collective-permute-start | bytes 786440 | tf_op jit(solution)/shard_map/ppermute | solution.py:544
  (14 other events, 79.0 us)

commit v7 on v6

--- a/solution.py
+++ b/solution.py
@@ -464,7 +464,6 @@
     context_mine = exchange(context)
     up_pair = lax.ppermute(after(up_pair, context), "ctx", PAIR_SWAP)
     up_diag = lax.ppermute(after(up_diag, context), "ctx", DIAG_SWAP)
-    context_other = lax.ppermute(after(context_mine, up_pair, up_diag), "ctx", CORE_SWAP)
     grads_keep, grads_send = call(
         project_kernel,
         [("S", row_ref), ("A", up_mine), ("A", up_other), *[("V", piece) for piece in pieces]],
@@ -472,21 +471,23 @@
         flops=2 * 256 * 1024 * 1024,
     )
     grads_came = lax.ppermute(grads_send, "ctx", CORE_SWAP)
-    terms = call(
-        weight_kernel,
-        [
-            ("S", high_ref), ("A", up_mine), ("A", up_other), ("A", up_pair), ("A", up_diag),
-            ("A", context_mine), ("A", context_other),
-        ],
-        [("H", (32, 32, quarter), BF16)],
-        flops=2 * 512 * 1024 * 512,
-    )
     grads = call(
         add_kernel,
         [("V", valid_here), ("V", grads_keep), ("V", grads_came)],
         [("V", (HEADS, BLOCK, HS), BF16)],
     )
-    grads = exchange(after(grads, context_mine, up_pair, up_diag))
+    context_mine = after(context_mine, grads, up_pair, up_diag)
+    context_other = lax.ppermute(context_mine, "ctx", CORE_SWAP)
+    terms = call(
+        weight_kernel,
+        [
+            ("S", high_ref), ("A", up_mine), ("A", up_other), ("A", up_pair), ("A", up_diag),
+            ("A", context_mine), ("A", context_other),
+        ],
+        [("H", (32, 32, quarter), BF16)],
+        flops=2 * 512 * 1024 * 512,
+    )
+    grads = exchange(after(grads, context_mine))
     terms = lax.all_to_all(
         after(terms, grads),
         ("ctx", "fsdp"),
@@ -510,11 +511,24 @@
         flops=10 * pairs * HS,
     )
     came = lax.ppermute(send, "ctx", CORE_SWAP)
+    joined = call(
+        join_kernel,
+        [("A", dq), ("A", keep), ("A", came)],
+        [("R", (CHIPS, 4, BLOCK, HS), BF16)],
+        scratch=(pltpu.VMEM((CHIPS, 3, BLOCK, HS), BF16),),
+    )
+    joined = call(
+        total_kernel,
+        [("R", joined), ("V", terms)],
+        [("R", (CHIPS, 4, BLOCK, HS), BF16)],
+        scratch=(pltpu.VMEM((BLOCK, HS), BF16),),
+        aliases={0: 0},
+    )
     side = ("H", (BLOCK, half), BF16)
     attended_keep, attended_send = call(
         attend_kernel,
         [
-            ("S", row_ref), ("A", after(context_mine, grads), (slice(None), 0)),
+            ("S", row_ref), ("A", after(context_mine, joined), (slice(None), 0)),
             ("A", context_other, (slice(None), 0)), *[("A", piece) for piece in pieces],
         ],
         [side, side],
@@ -526,20 +540,7 @@
         [("S", core_ref), ("A", attended_keep), ("A", attended_came)],
         [("R", (1, BLOCK, width), BF16)],
     )
-    joined = call(
-        join_kernel,
-        [("A", dq), ("A", keep), ("A", came)],
-        [("R", (CHIPS, 4, BLOCK, HS), BF16)],
-        scratch=(pltpu.VMEM((CHIPS, 3, BLOCK, HS), BF16),),
-    )
-    joined = call(
-        total_kernel,
-        [("R", after(joined, attended)), ("V", terms)],
-        [("R", (CHIPS, 4, BLOCK, HS), BF16)],
-        scratch=(pltpu.VMEM((BLOCK, HS), BF16),),
-        aliases={0: 0},
-    )
-    result = exchange(joined)
+    result = after(exchange(joined), attended)
     weight_mine = result[:, 3]
     weight_other = lax.ppermute(weight_mine, "ctx", CORE_SWAP)
     grad = ("R", (1, BLOCK, HEADS * HS), BF16)

time: 124 us -> 119 us (0.960)
  blocking collectives: 18.8 us -> 0 us
  starting transfers between devices: 43.1 us -> 52.6 us
  local copies, waits for them, and re-layouts: 2.1 us -> 6.75 us
    all_to_all x1 -> x0, blocking collectives: 18.8 us -> none  [exchange(): lax.all_to_all(operand, 'ctx', split_axis=0, concat_axis=0, tiled=True, a...]
    all_to_all x3 -> x4, starting transfers between devices: 17.1 us -> 22.6 us  [exchange(): lax.all_to_all(operand, 'ctx', split_axis=0, concat_axis=0, tiled=True, a...]
    unnamed x36 -> x32, local copies, waits for them, and re-layouts: 2.07 us -> 6.72 us
    ppermute x1, waiting for transfers between devices: 7.22 us -> 4.39 us  [shards(): up_pair = lax.ppermute(after(up_pair, context), 'ctx', PAIR_SWAP)]
    all_to_all x3 -> x4, waiting for transfers between devices: 5.28 us -> 7.55 us  [exchange(): lax.all_to_all(operand, 'ctx', split_axis=0, concat_axis=0, tiled=True, a...]
    ppermute x1, starting transfers between devices: 0.23 us -> 2.17 us  [shards(): attended_came = lax.ppermute(attended_send, 'ctx', CORE_SWAP)]
    ppermute x7, starting transfers between devices: 7.48 us -> 9.41 us  [step(): return lax.ppermute(value, 'fsdp', [(i, i ^ s) for i in range(8)])]
    ppermute x1, waiting for transfers between devices: 0.01 us -> 1.75 us  [shards(): came = lax.ppermute(send, 'ctx', CORE_SWAP)]
  transfers between devices with their start and end apart: 20 -> 21, of which waited for: 8 -> 9; matrix products, arithmetic and copies ran while one was open for 1% -> 1% of each run, Pallas kernels for 16% -> 20%
where the time goes in v7:
time: 119 us; the launch traced here: 118 us
  starting transfers between devices  52.6 us (44%)
  Pallas kernels  28.8 us (24%)
  waiting for transfers between devices  27.1 us (23%)
  local copies, waits for them, and re-layouts  6.75 us (6%)
  between operations  1.77 us (1%)
    pallas_call x12, Pallas kernels, call(): pl.pallas_call(body, out_shape=[SPACES[o[0]](o[1], o[2]) if o[0] in 'HR'...  28.8 us
    all_to_all x4, starting transfers between devices, exchange(): lax.all_to_all(operand, 'ctx', split_axis=0, concat_axis=0, tiled=True, a...  22.6 us
    ppermute x7, starting transfers between devices, step(): return lax.ppermute(value, 'fsdp', [(i, i ^ s) for i in range(8)])  9.41 us
    all_to_all x4, waiting for transfers between devices, exchange(): lax.all_to_all(operand, 'ctx', split_axis=0, concat_axis=0, tiled=True, a...  7.55 us
    ppermute x7, waiting for transfers between devices, step(): return lax.ppermute(value, 'fsdp', [(i, i ^ s) for i in range(8)])  7.38 us
    unnamed x32, local copies, waits for them, and re-layouts  6.72 us
    all_to_all x1, starting transfers between devices, shards(): lax.all_to_all(after(terms, grads), ('ctx', 'fsdp'), split_axis=0, concat...  5.26 us
    ppermute x1, waiting for transfers between devices, shards(): up_pair = lax.ppermute(after(up_pair, context), 'ctx', PAIR_SWAP)  4.39 us
  transfers between devices with their start and end apart: 21, of which 9 were waited for; matrix products, arithmetic and copies ran while one was open for 1% of the time, Pallas kernels for 20%

profile of v7, /device:TPU:1, one launch (start us, length us, event | category | flops | bytes accessed | tf_op | source)
XLA Modules:
  0.0 118.0 jit_solution(17149210016551953932)
XLA Ops:
  0.6 2.9 %shard_map.110 = (bf16[8,3,128,128]{3,2,1,0:T(8,128)(2,1)}, bf16[128,1024]{1,0:T(8,128)(2,1)}, bf16[128,1024]{1,0:T(8,128)(2,1)}, bf16[128,1024]{1,0:T(8,128)(2,...) custom-call(s32[1]{0:T(128)} %bitcast.refs_0_, s32[1]{0:T(128)} %bitcast.2.refs_1_.refs_0_, ...), custom_call_target="tpu_custom_call" | custom-call | bytes 2000000 | tf_op jit(solution)/shard_map/pallas_call | solution.py:112
  3.6 2.1 %collective-permute-start.2 = (bf16[128,1024]{1,0:T(8,128)(2,1)}, bf16[128,1024]{1,0:T(8,128)(2,1)S(1)}, u32[]{:S(2)}, u32[]{:S(2)}) collective-permute-start(bf16[128,1024]{1,0:T(8,128)(2,1)} %get-tuple-element.35.refs_3_), channel_id=1, source_target_pairs={{0,4},{1,5},{2,6},{3,7},{4,0},{5,1},{6,2},{7,3},{8,12},{9,13},{10,... | collective-permute-start | bytes 786440 | tf_op jit(solution)/shard_map/ppermute | solution.py:438
  5.7 3.8 %collective-permute-start.1 = (bf16[128,1024]{1,0:T(8,128)(2,1)}, bf16[128,1024]{1,0:T(8,128)(2,1)S(1)}, u32[]{:S(2)}, u32[]{:S(2)}) collective-permute-start(bf16[128,1024]{1,0:T(8,128)(2,1)} %get-tuple-element.35.refs_3_), channel_id=1, source_target_pairs={{0,3},{1,2},{2,1},{3,0},{4,7},{5,6},{6,5},{7,4},{8,11},{9,10},{10,... | collective-permute-start | bytes 786440 | tf_op jit(solution)/shard_map/ppermute | solution.py:438
  9.5 6.4 %all-to-all-start = ((bf16[8,3,128,128]{3,2,1,0:T(8,128)(2,1)}), bf16[8,3,128,128]{3,2,1,0:T(8,128)(2,1)}, u32[]{:S(2)}, u32[]{:S(2)}) async-start(bf16[8,3,128,128]{3,2,1,0:T(8,128)(2,1)} %get-tuple-element.34), calls=%async_computation | async-start | bytes 1572864 | tf_op jit(solution)/shard_map/all_to_all | solution.py:393
  21.1 7.4 %collective-permute-done.4.refs_10_ = bf16[128,1024]{1,0:T(8,128)(2,1)S(1)} collective-permute-done((bf16[128,1024]{1,0:T(8,128)(2,1)S(1)}, bf16[128,1024]{1,0:T(8,128)(2,1)S(1)}, u32[]{:S(2)}, u32[]{:S(2)}) %collective-permute-start.4) | collective-permute-done | bytes 262176 | tf_op jit(solution)/shard_map/ppermute | solution.py:438
  28.5 1.9 %collective-permute-start.6 = (bf16[8,3,128,128]{3,2,1,0:T(8,128)(2,1)}, bf16[8,3,128,128]{3,2,1,0:T(8,128)(2,1)S(1)}, u32[]{:S(2)}, u32[]{:S(2)}) collective-permute-start(bf16[8,3,128,128]{3,2,1,0:T(8,128)(2,1)} %all-to-all-done.refs_1_), channel_id=1, source_target_pairs={{0,8},{8,0},{16,24},{24,16},{32,40},{40,32},{48,56},{56,48},{64,72... | collective-permute-start | bytes 2359304 | tf_op jit(solution)/shard_map/ppermute | solution.py:448
  32.4 5.1 %shard_map.111 = (bf16[8,2,128,128]{3,2,1,0:T(8,128)(2,1)}, f32[4,1,256]{2,1,0:T(1,128)}, bf16[8,128,128]{2,1,0:T(8,128)(2,1)}, bf16[2048,128]{1,0:T(8,128)(2,1)}, bf16[2048,128]{1,0:T(8,128)(2,1)}) custom-call(s32[1]{0:T(128)} %bitcast.refs_0_, bf16[8,3,128,128]{3,2,1,0:T(8,128)(2,1)} %all-to-all-done.refs_1_, ...), custom_call_target="tpu_custom_call" | custom-call | flops 671088640 | bytes 2000000 | tf_op jit(solution)/shard_map/pallas_call | solution.py:112
  37.6 5.9 %all-to-all-start.1 = ((bf16[8,2,128,128]{3,2,1,0:T(8,128)(2,1)}), bf16[8,2,128,128]{3,2,1,0:T(8,128)(2,1)S(1)}, u32[]{:S(2)}, u32[]{:S(2)}) async-start(bf16[8,2,128,128]{3,2,1,0:T(8,128)(2,1)} %get-tuple-element.38.refs_5_), calls=%async_computation.1 | async-start | bytes 1048576 | tf_op jit(solution)/shard_map/all_to_all | solution.py:393
  43.6 1.7 %shard_map.112 = (f32[8,128,128]{2,1,0:T(8,128)S(1)}, bf16[8,128,128]{2,1,0:T(8,128)(2,1)S(1)}) custom-call(s32[1]{0:T(128)} %bitcast.1.refs_0_, bf16[128,1024]{1,0:T(8,128)(2,1)S(1)} %copy-done.1, bf16[128,1024]{1,0:T(8,128)(2,1)S(1)} %collective-permute-done.5.refs_2_, bf16[128,1024]{1,0:T(8,128)(2,1)S(1)} %copy-done.2, ...), custom_call_target="tpu_custom_call" | custom-call | flops 536870912 | bytes 2000000 | tf_op jit(solution)/shard_map/pallas_call | solution.py:112
  46.1 3.3 %collective-permute-start.10 = (bf16[128,512]{1,0:T(8,128)(2,1)S(1)}, bf16[128,512]{1,0:T(8,128)(2,1)S(1)}, u32[]{:S(2)}, u32[]{:S(2)}) collective-permute-start(bf16[128,512]{1,0:T(8,128)(2,1)S(1)} %copy-done.15), channel_id=1, source_target_pairs={{0,64},{8,72},{16,80},{24,88},{32,96},{40,104},{48,112},{56,120},{... | collective-permute-start | bytes 393224 | tf_op jit(solution)/shard_map/ppermute | solution.py:465
  50.7 4.4 %collective-permute-done.10.refs_3_ = bf16[128,512]{1,0:T(8,128)(2,1)S(1)} collective-permute-done((bf16[128,512]{1,0:T(8,128)(2,1)S(1)}, bf16[128,512]{1,0:T(8,128)(2,1)S(1)}, u32[]{:S(2)}, u32[]{:S(2)}) %collective-permute-start.10) | collective-permute-done | bytes 131104 | tf_op jit(solution)/shard_map/ppermute | solution.py:465
  55.1 3.7 %collective-permute-done.11.refs_4_ = bf16[128,512]{1,0:T(8,128)(2,1)S(1)} collective-permute-done((bf16[128,512]{1,0:T(8,128)(2,1)S(1)}, bf16[128,512]{1,0:T(8,128)(2,1)S(1)}, u32[]{:S(2)}, u32[]{:S(2)}) %collective-permute-start.11) | collective-permute-done | bytes 131104 | tf_op jit(solution)/shard_map/ppermute | solution.py:466
  58.8 4.4 %all-to-all-start.2 = ((bf16[8,128,128]{2,1,0:T(8,128)(2,1)}), bf16[8,128,128]{2,1,0:T(8,128)(2,1)S(1)}, u32[]{:S(2)}, u32[]{:S(2)}) async-start(bf16[8,128,128]{2,1,0:T(8,128)(2,1)} %shard_map.113), calls=%async_computation.2 | async-start | bytes 524288 | tf_op jit(solution)/shard_map/all_to_all | solution.py:393
  63.2 2.3 %shard_map.116 = bf16[32,32,512]{2,1,0:T(8,128)(2,1)} custom-call(s32[1]{0:T(128)} %bitcast.2.refs_1_.refs_0_, bf16[128,1024]{1,0:T(8,128)(2,1)S(1)} %copy-done.1, bf16[128,1024]{1,0:T(8,128)(2,1)S(1)} %collective-permute-done.5.refs_2_, bf16[128,512]{1,0:T(8,128)(2,1)S(1)} %collective-permute-done.10.refs_3_, ...), custom_call_target="tpu_custom_call" | custom-call | flops 536870912 | bytes 2000000 | tf_op jit(solution)/shard_map/pallas_call | solution.py:112
  65.5 5.3 %all-to-all-done.2.refs_3_ = bf16[8,128,128]{2,1,0:T(8,128)(2,1)S(1)} async-done(((bf16[8,128,128]{2,1,0:T(8,128)(2,1)}), bf16[8,128,128]{2,1,0:T(8,128)(2,1)S(1)}, u32[]{:S(2)}, u32[]{:S(2)}) %all-to-all-start.2) | async-done | bytes 262176 | tf_op jit(solution)/shard_map/all_to_all | solution.py:393
  71.5 5.3 %all-to-all-start.3 = ((bf16[32,32,512]{2,1,0:T(8,128)(2,1)}), bf16[32,32,512]{2,1,0:T(8,128)(2,1)S(1)}, u32[]{:S(2)}, u32[]{:S(2)}) async-start(bf16[32,32,512]{2,1,0:T(8,128)(2,1)} %shard_map.116), calls=%async_computation.3 | async-start | bytes 2097152 | tf_op jit(solution)/shard_map/all_to_all | solution.py:491
  76.8 6.8 %shard_map.114 = (bf16[8,128,128]{2,1,0:T(8,128)(2,1)}, f32[8,2,128,128]{3,2,1,0:T(8,128)}, bf16[8,2,128,128]{3,2,1,0:T(8,128)(2,1)}) custom-call(s32[1]{0:T(128)} %bitcast.refs_0_, bf16[8,128,128]{2,1,0:T(8,128)(2,1)} %get-tuple-element.47.refs_1_, bf16[2048,128]{1,0:T(8,128)(2,1)} %get-tuple-element.48.refs_2_, bf16[8,128,128]{2,1,0:T(8,128)(2,1)} %copy-done.11, ...), custom_call_target="tpu_custom_call" | custom-call | flops 1677721600 | bytes 2000000 | tf_op jit(solution)/shard_map/pallas_call | solution.py:112
  83.5 1.6 %collective-permute-start.12 = (bf16[8,2,128,128]{3,2,1,0:T(8,128)(2,1)}, bf16[8,2,128,128]{3,2,1,0:T(8,128)(2,1)S(1)}, u32[]{:S(2)}, u32[]{:S(2)}) collective-permute-start(bf16[8,2,128,128]{3,2,1,0:T(8,128)(2,1)} %get-tuple-element.54), channel_id=1, source_target_pairs={{0,8},{8,0},{16,24},{24,16},{32,40},{40,32},{48,56},{56,48},{64,72... | collective-permute-start | bytes 1572872 | tf_op jit(solution)/shard_map/ppermute | solution.py:513
  85.1 1.7 %collective-permute-done.12.refs_2_ = bf16[8,2,128,128]{3,2,1,0:T(8,128)(2,1)S(1)} collective-permute-done((bf16[8,2,128,128]{3,2,1,0:T(8,128)(2,1)}, bf16[8,2,128,128]{3,2,1,0:T(8,128)(2,1)S(1)}, u32[]{:S(2)}, u32[]{:S(2)}) %collective-permute-start.12) | collective-permute-done | bytes 524320 | tf_op jit(solution)/shard_map/ppermute | solution.py:513
  92.2 6.0 %all-to-all-start.4 = ((bf16[8,4,128,128]{3,2,1,0:T(8,128)(2,1)}), bf16[8,4,128,128]{3,2,1,0:T(8,128)(2,1)S(1)}, u32[]{:S(2)}, u32[]{:S(2)}) async-start(bf16[8,4,128,128]{3,2,1,0:T(8,128)(2,1)} %shard_map.117), calls=%async_computation.4 | async-start | bytes 2097152 | tf_op jit(solution)/shard_map/all_to_all | solution.py:393
  101.1 2.2 %shard_map.118 = (bf16[128,1024]{1,0:T(8,128)(2,1)}, bf16[128,1024]{1,0:T(8,128)(2,1)}) custom-call(s32[1]{0:T(128)} %bitcast.1.refs_0_, bf16[8,2,128,128]{3,2,1,0:T(8,128)(2,1)S(1)} %all-to-all-done.1.refs_5_.refs_1_, bf16[8,2,128,128]{3,2,1,0:T(8,128)(2,1)S(1)} %collective-permute-done.13.refs_6_.refs_2_, bf16[128,1024]{1,0:T(8,128)(2,1)S(1)} %copy-done.2, ...), custom_call_target="tpu_custom_call" | custom-call | flops 536870912 | bytes 2000000 | tf_op jit(solution)/shard_map/pallas_call | solution.py:112
  103.2 2.2 %collective-permute-start.14 = (bf16[128,1024]{1,0:T(8,128)(2,1)}, bf16[128,1024]{1,0:T(8,128)(2,1)S(1)}, u32[]{:S(2)}, u32[]{:S(2)}) collective-permute-start(bf16[128,1024]{1,0:T(8,128)(2,1)} %get-tuple-element.58), channel_id=1, source_target_pairs={{0,8},{8,0},{16,24},{24,16},{32,40},{40,32},{48,56},{56,48},{64,72... | collective-permute-start | bytes 786440 | tf_op jit(solution)/shard_map/ppermute | solution.py:537
  109.0 2.3 %all-to-all-done.4.refs_0_ = bf16[8,4,128,128]{3,2,1,0:T(8,128)(2,1)S(1)} async-done(((bf16[8,4,128,128]{3,2,1,0:T(8,128)(2,1)}), bf16[8,4,128,128]{3,2,1,0:T(8,128)(2,1)S(1)}, u32[]{:S(2)}, u32[]{:S(2)}) %all-to-all-start.4) | async-done | bytes 1048608 | tf_op jit(solution)/shard_map/all_to_all | solution.py:393
  111.3 3.8 %collective-permute-start.15 = (bf16[8,128,128]{2,1,0:T(8,128)(2,1)S(1)}, bf16[8,128,128]{2,1,0:T(8,128)(2,1)S(1)}, u32[]{:S(2)}, u32[]{:S(2)}) collective-permute-start(bf16[8,128,128]{2,1,0:T(8,128)(2,1)S(1)} %slice_bitcast_fusion.refs_1_), channel_id=1, source_target_pairs={{0,8},{8,0},{16,24},{24,16},{32,40},{40,32},{48,56},{56,48},{64,72... | collective-permute-start | bytes 786440 | tf_op jit(solution)/shard_map/ppermute | solution.py:545
  (68 shorter events, 24.0 us)
Async XLA Ops:
  3.6 12.3 %copy-start.13 = (bf16[128,1024]{1,0:T(8,128)(2,1)S(1)}, bf16[128,1024]{1,0:T(8,128)(2,1)}, u32[]{:S(2)}) copy-start(bf16[128,1024]{1,0:T(8,128)(2,1)} %get-tuple-element.36) | copy-start | bytes 786436
  3.6 14.5 %copy-start.12 = (s32[1,2048]{1,0:T(1,128)S(1)}, s32[1,2048]{1,0:T(1,128)}, u32[]{:S(2)}) copy-start(s32[1,2048]{1,0:T(1,128)} %param.10) | copy-start | bytes 24580
  3.6 15.5 %collective-permute-start.2 = (bf16[128,1024]{1,0:T(8,128)(2,1)}, bf16[128,1024]{1,0:T(8,128)(2,1)S(1)}, u32[]{:S(2)}, u32[]{:S(2)}) collective-permute-start(bf16[128,1024]{1,0:T(8,128)(2,1)} %get-tuple-element.35.refs_3_), channel_id=1, source_target_pairs={{0,4},{1,5},{2,6},{3,7},{4,0},{5,1},{6,2},{7,3},{8,12},{9,13},{10,... | collective-permute-start | bytes 786440 | tf_op jit(solution)/shard_map/ppermute | solution.py:438
  5.7 15.4 %collective-permute-start.1 = (bf16[128,1024]{1,0:T(8,128)(2,1)}, bf16[128,1024]{1,0:T(8,128)(2,1)S(1)}, u32[]{:S(2)}, u32[]{:S(2)}) collective-permute-start(bf16[128,1024]{1,0:T(8,128)(2,1)} %get-tuple-element.35.refs_3_), channel_id=1, source_target_pairs={{0,3},{1,2},{2,1},{3,0},{4,7},{5,6},{6,5},{7,4},{8,11},{9,10},{10,... | collective-permute-start | bytes 786440 | tf_op jit(solution)/shard_map/ppermute | solution.py:438
  9.5 11.6 %collective-permute-start = (bf16[128,1024]{1,0:T(8,128)(2,1)}, bf16[128,1024]{1,0:T(8,128)(2,1)S(1)}, u32[]{:S(2)}, u32[]{:S(2)}) collective-permute-start(bf16[128,1024]{1,0:T(8,128)(2,1)} %get-tuple-element.35.refs_3_), channel_id=1, source_target_pairs={{0,1},{1,0},{2,3},{3,2},{4,5},{5,4},{6,7},{7,6},{8,9},{9,8},{10,11... | collective-permute-start | bytes 786440 | tf_op jit(solution)/shard_map/ppermute | solution.py:438
  9.5 19.0 %all-to-all-start = ((bf16[8,3,128,128]{3,2,1,0:T(8,128)(2,1)}), bf16[8,3,128,128]{3,2,1,0:T(8,128)(2,1)}, u32[]{:S(2)}, u32[]{:S(2)}) async-start(bf16[8,3,128,128]{3,2,1,0:T(8,128)(2,1)} %get-tuple-element.34), calls=%async_computation | async-start | bytes 1572864 | tf_op jit(solution)/shard_map/all_to_all | solution.py:393
  15.8 5.2 %collective-permute-start.5 = (bf16[128,1024]{1,0:T(8,128)(2,1)S(1)}, bf16[128,1024]{1,0:T(8,128)(2,1)S(1)}, u32[]{:S(2)}, u32[]{:S(2)}) collective-permute-start(bf16[128,1024]{1,0:T(8,128)(2,1)S(1)} %copy-done.13), channel_id=1, source_target_pairs={{0,8},{8,0},{16,24},{24,16},{32,40},{40,32},{48,56},{56,48},{64,72... | collective-permute-start | bytes 786440 | tf_op jit(solution)/shard_map/ppermute | solution.py:445
  19.1 9.3 %collective-permute-start.4 = (bf16[128,1024]{1,0:T(8,128)(2,1)S(1)}, bf16[128,1024]{1,0:T(8,128)(2,1)S(1)}, u32[]{:S(2)}, u32[]{:S(2)}) collective-permute-start(bf16[128,1024]{1,0:T(8,128)(2,1)S(1)} %collective-permute-done.2.refs_7_), channel_id=1, source_target_pairs={{0,3},{1,2},{2,1},{3,0},{4,7},{5,6},{6,5},{7,4},{8,11},{9,10},{10,... | collective-permute-start | bytes 786440 | tf_op jit(solution)/shard_map/ppermute | solution.py:438
  19.4 9.0 %collective-permute-start.3 = (bf16[128,1024]{1,0:T(8,128)(2,1)S(1)}, bf16[128,1024]{1,0:T(8,128)(2,1)S(1)}, u32[]{:S(2)}, u32[]{:S(2)}) collective-permute-start(bf16[128,1024]{1,0:T(8,128)(2,1)S(1)} %collective-permute-done.2.refs_7_), channel_id=1, source_target_pairs={{0,1},{1,0},{2,3},{3,2},{4,5},{5,4},{6,7},{7,6},{8,9},{9,8},{10,11... | collective-permute-start | bytes 786440 | tf_op jit(solution)/shard_map/ppermute | solution.py:438
  28.4 15.1 %copy-start.3 = (bf16[128,1024]{1,0:T(8,128)(2,1)}, bf16[128,1024]{1,0:T(8,128)(2,1)S(1)}, u32[]{:S(2)}) copy-start(bf16[128,1024]{1,0:T(8,128)(2,1)S(1)} %collective-permute-done.3.refs_8_) | copy-start | bytes 786436
  28.5 4.0 %collective-permute-start.6 = (bf16[8,3,128,128]{3,2,1,0:T(8,128)(2,1)}, bf16[8,3,128,128]{3,2,1,0:T(8,128)(2,1)S(1)}, u32[]{:S(2)}, u32[]{:S(2)}) collective-permute-start(bf16[8,3,128,128]{3,2,1,0:T(8,128)(2,1)} %all-to-all-done.refs_1_), channel_id=1, source_target_pairs={{0,8},{8,0},{16,24},{24,16},{32,40},{40,32},{48,56},{56,48},{64,72... | collective-permute-start | bytes 2359304 | tf_op jit(solution)/shard_map/ppermute | solution.py:448
  30.3 13.2 %collective-permute-start.7 = (bf16[128,1024]{1,0:T(8,128)(2,1)S(1)}, bf16[128,1024]{1,0:T(8,128)(2,1)S(1)}, u32[]{:S(2)}, u32[]{:S(2)}) collective-permute-start(bf16[128,1024]{1,0:T(8,128)(2,1)S(1)} %collective-permute-done.refs_4_), channel_id=1, source_target_pairs={{0,3},{1,2},{2,1},{3,0},{4,7},{5,6},{6,5},{7,4},{8,11},{9,10},{10,... | collective-permute-start | bytes 786440 | tf_op jit(solution)/shard_map/ppermute | solution.py:438
  30.6 12.9 %collective-permute-start.8 = (bf16[128,1024]{1,0:T(8,128)(2,1)S(1)}, bf16[128,1024]{1,0:T(8,128)(2,1)S(1)}, u32[]{:S(2)}, u32[]{:S(2)}) collective-permute-start(bf16[128,1024]{1,0:T(8,128)(2,1)S(1)} %collective-permute-done.4.refs_10_), channel_id=1, source_target_pairs={{0,1},{1,0},{2,3},{3,2},{4,5},{5,4},{6,7},{7,6},{8,9},{9,8},{10,11... | collective-permute-start | bytes 786440 | tf_op jit(solution)/shard_map/ppermute | solution.py:438
  37.6 21.3 %all-to-all-start.1 = ((bf16[8,2,128,128]{3,2,1,0:T(8,128)(2,1)}), bf16[8,2,128,128]{3,2,1,0:T(8,128)(2,1)S(1)}, u32[]{:S(2)}, u32[]{:S(2)}) async-start(bf16[8,2,128,128]{3,2,1,0:T(8,128)(2,1)} %get-tuple-element.38.refs_5_), calls=%async_computation.1 | async-start | bytes 1048576 | tf_op jit(solution)/shard_map/all_to_all | solution.py:393
  45.3 4.2 %collective-permute-start.9 = (bf16[8,128,128]{2,1,0:T(8,128)(2,1)S(1)}, bf16[8,128,128]{2,1,0:T(8,128)(2,1)S(1)}, u32[]{:S(2)}, u32[]{:S(2)}) collective-permute-start(bf16[8,128,128]{2,1,0:T(8,128)(2,1)S(1)} %get-tuple-element.41), channel_id=1, source_target_pairs={{0,8},{8,0},{16,24},{24,16},{32,40},{40,32},{48,56},{56,48},{64,72... | collective-permute-start | bytes 786440 | tf_op jit(solution)/shard_map/ppermute | solution.py:473
  46.1 9.0 %collective-permute-start.10 = (bf16[128,512]{1,0:T(8,128)(2,1)S(1)}, bf16[128,512]{1,0:T(8,128)(2,1)S(1)}, u32[]{:S(2)}, u32[]{:S(2)}) collective-permute-start(bf16[128,512]{1,0:T(8,128)(2,1)S(1)} %copy-done.15), channel_id=1, source_target_pairs={{0,64},{8,72},{16,80},{24,88},{32,96},{40,104},{48,112},{56,120},{... | collective-permute-start | bytes 393224 | tf_op jit(solution)/shard_map/ppermute | solution.py:465
  49.4 9.4 %collective-permute-start.11 = (bf16[128,512]{1,0:T(8,128)(2,1)S(1)}, bf16[128,512]{1,0:T(8,128)(2,1)S(1)}, u32[]{:S(2)}, u32[]{:S(2)}) collective-permute-start(bf16[128,512]{1,0:T(8,128)(2,1)S(1)} %copy-done.14), channel_id=1, source_target_pairs={{0,72},{8,64},{16,88},{24,80},{32,104},{40,96},{48,120},{56,112},{... | collective-permute-start | bytes 393224 | tf_op jit(solution)/shard_map/ppermute | solution.py:466
  58.8 4.4 %collective-permute-start.13 = (bf16[8,2,128,128]{3,2,1,0:T(8,128)(2,1)S(1)}, bf16[8,2,128,128]{3,2,1,0:T(8,128)(2,1)S(1)}, u32[]{:S(2)}, u32[]{:S(2)}) collective-permute-start(bf16[8,2,128,128]{3,2,1,0:T(8,128)(2,1)S(1)} %all-to-all-done.1.refs_5_.refs_1_), channel_id=1, source_target_pairs={{0,8},{8,0},{16,24},{24,16},{32,40},{40,32},{48,56},{56,48},{64,72... | collective-permute-start | bytes 1572872 | tf_op jit(solution)/shard_map/ppermute | solution.py:480
  58.8 11.9 %all-to-all-start.2 = ((bf16[8,128,128]{2,1,0:T(8,128)(2,1)}), bf16[8,128,128]{2,1,0:T(8,128)(2,1)S(1)}, u32[]{:S(2)}, u32[]{:S(2)}) async-start(bf16[8,128,128]{2,1,0:T(8,128)(2,1)} %shard_map.113), calls=%async_computation.2 | async-start | bytes 524288 | tf_op jit(solution)/shard_map/all_to_all | solution.py:393
  71.5 19.4 %all-to-all-start.3 = ((bf16[32,32,512]{2,1,0:T(8,128)(2,1)}), bf16[32,32,512]{2,1,0:T(8,128)(2,1)S(1)}, u32[]{:S(2)}, u32[]{:S(2)}) async-start(bf16[32,32,512]{2,1,0:T(8,128)(2,1)} %shard_map.116), calls=%async_computation.3 | async-start | bytes 2097152 | tf_op jit(solution)/shard_map/all_to_all | solution.py:491
  83.5 3.4 %collective-permute-start.12 = (bf16[8,2,128,128]{3,2,1,0:T(8,128)(2,1)}, bf16[8,2,128,128]{3,2,1,0:T(8,128)(2,1)S(1)}, u32[]{:S(2)}, u32[]{:S(2)}) collective-permute-start(bf16[8,2,128,128]{3,2,1,0:T(8,128)(2,1)} %get-tuple-element.54), channel_id=1, source_target_pairs={{0,8},{8,0},{16,24},{24,16},{32,40},{40,32},{48,56},{56,48},{64,72... | collective-permute-start | bytes 1572872 | tf_op jit(solution)/shard_map/ppermute | solution.py:513
  92.2 19.0 %all-to-all-start.4 = ((bf16[8,4,128,128]{3,2,1,0:T(8,128)(2,1)}), bf16[8,4,128,128]{3,2,1,0:T(8,128)(2,1)S(1)}, u32[]{:S(2)}, u32[]{:S(2)}) async-start(bf16[8,4,128,128]{3,2,1,0:T(8,128)(2,1)} %shard_map.117), calls=%async_computation.4 | async-start | bytes 2097152 | tf_op jit(solution)/shard_map/all_to_all | solution.py:393
  103.2 3.5 %collective-permute-start.14 = (bf16[128,1024]{1,0:T(8,128)(2,1)}, bf16[128,1024]{1,0:T(8,128)(2,1)S(1)}, u32[]{:S(2)}, u32[]{:S(2)}) collective-permute-start(bf16[128,1024]{1,0:T(8,128)(2,1)} %get-tuple-element.58), channel_id=1, source_target_pairs={{0,8},{8,0},{16,24},{24,16},{32,40},{40,32},{48,56},{56,48},{64,72... | collective-permute-start | bytes 786440 | tf_op jit(solution)/shard_map/ppermute | solution.py:537
  111.3 5.1 %collective-permute-start.15 = (bf16[8,128,128]{2,1,0:T(8,128)(2,1)S(1)}, bf16[8,128,128]{2,1,0:T(8,128)(2,1)S(1)}, u32[]{:S(2)}, u32[]{:S(2)}) collective-permute-start(bf16[8,128,128]{2,1,0:T(8,128)(2,1)S(1)} %slice_bitcast_fusion.refs_1_), channel_id=1, source_target_pairs={{0,8},{8,0},{16,24},{24,16},{32,40},{40,32},{48,56},{56,48},{64,72... | collective-permute-start | bytes 786440 | tf_op jit(solution)/shard_map/ppermute | solution.py:545
  (13 other events, 30.7 us)

commit v8 on v7

--- a/solution.py
+++ b/solution.py
@@ -159,7 +159,7 @@
     for j in range(CHIPS):
         own = pl.multiple_of(2 * BLOCK * j + BLOCK * core, BLOCK)
         other = pl.multiple_of(2 * BLOCK * j + BLOCK * (1 - core), BLOCK)
-        dst_ref[pl.ds(own, BLOCK)] = own_ref[j, slot]
+        dst_ref[pl.ds(own, BLOCK)] = own_ref[j]
         dst_ref[pl.ds(other, BLOCK)] = other_ref[j, slot]
 
 
@@ -177,19 +177,20 @@
 
 
 def forward_kernel(ins, outs, scratch, sems):
-    core_ref, own_ref, other_ref, end_ref, valid_ref = ins
+    core_ref, q_in, k_in, v_in, other_ref, end_ref, valid_ref = ins
     ctx_out, lse_out, q_out, k_out, v_out = outs
     (s_s,) = scratch
     core = core_ref[0]
     k_s, v_s = k_out.ref, v_out.ref
-    in_order(core, own_ref, other_ref, 1, k_s)
+    in_order(core, k_in.get(), other_ref, 1, k_s)
     k_out.push()
-    in_order(core, own_ref, other_ref, 2, v_s)
+    q_ref = q_in.get()
+    q_out.ref[...] = q_ref[...]
+    q_out.push()
+    in_order(core, v_in.get(), other_ref, 2, v_s)
     v_out.push()
-    q_out.ref[...] = own_ref[:, 0]
-    q_out.push()
     for m in range(4):
-        q = own_ref[2 * m : 2 * m + 2, 0].reshape(TILE, HS)
+        q = q_ref[2 * m : 2 * m + 2].reshape(TILE, HS)
         end = end_ref[m]
         top = jnp.full((1, TILE), NEG, F32)
         for start, stop in chunks_of(m):
@@ -443,14 +444,21 @@
     two, over_two = step(one, 3), step(over_three, 1)
     pieces = [own_half, one, two, three, over, over_one, over_two, over_three]
     up_other = lax.ppermute(up_send, "ctx", CORE_SWAP)
-
-    own = after(own, end, valid, valid_here, one, three, over_one, over_three, up_other)
+    up_pair = lax.ppermute(after(up_pair, over, one), "ctx", PAIR_SWAP)
+    up_diag = lax.ppermute(after(up_diag, over, one), "ctx", DIAG_SWAP)
+
+    own = after(
+        own, end, valid, valid_here, one, three, over_one, over_three, up_other, up_pair, up_diag
+    )
     other = lax.ppermute(own, "ctx", CORE_SWAP)
     pairs = 4 * TILE * SPAN * 5 // 2
     rows = ("H", (LEN, HS), BF16)
     context, lse, query, key, value = call(
         forward_kernel,
-        [("S", core_ref), ("V", own), ("V", other), ("V", end), ("V", valid)],
+        [
+            ("S", core_ref), ("A", own, (slice(None), 0)), ("A", own, (slice(None), 1)),
+            ("A", own, (slice(None), 2)), ("V", other), ("V", end), ("V", valid),
+        ],
         [
             ("H", (CHIPS, 2, BLOCK, HS), BF16),
             ("H", (4, 1, TILE), F32),
@@ -462,8 +470,6 @@
         flops=4 * pairs * HS,
     )
     context_mine = exchange(context)
-    up_pair = lax.ppermute(after(up_pair, context), "ctx", PAIR_SWAP)
-    up_diag = lax.ppermute(after(up_diag, context), "ctx", DIAG_SWAP)
     grads_keep, grads_send = call(
         project_kernel,
         [("S", row_ref), ("A", up_mine), ("A", up_other), *[("V", piece) for piece in pieces]],
@@ -476,7 +482,7 @@
         [("V", valid_here), ("V", grads_keep), ("V", grads_came)],
         [("V", (HEADS, BLOCK, HS), BF16)],
     )
-    context_mine = after(context_mine, grads, up_pair, up_diag)
+    context_mine = after(context_mine, grads)
     context_other = lax.ppermute(context_mine, "ctx", CORE_SWAP)
     terms = call(
         weight_kernel,

time: 119 us -> 116 us (0.975)
  starting transfers between devices: 52.6 us -> 48.8 us
    ppermute x7, waiting for transfers between devices: 7.38 us -> 0.02 us  [step(): return lax.ppermute(value, 'fsdp', [(i, i ^ s) for i in range(8)])]
    all_to_all x4, waiting for transfers between devices: 7.55 us -> 12.1 us  [exchange(): lax.all_to_all(operand, 'ctx', split_axis=0, concat_axis=0, tiled=True, a...]
    all_to_all x4, starting transfers between devices: 22.6 us -> 19.3 us  [exchange(): lax.all_to_all(operand, 'ctx', split_axis=0, concat_axis=0, tiled=True, a...]
    ppermute x1, starting transfers between devices: 0.01 us -> 2.12 us  [shards(): context_other = lax.ppermute(context_mine, 'ctx', CORE_SWAP)]
    ppermute x1, starting transfers between devices: 1.87 us -> 0.09 us  [shards(): other = lax.ppermute(own, 'ctx', CORE_SWAP)]
    ppermute x2, waiting for transfers between devices: 8.1 us -> 9.4 us  [the longest x1 4.84 us: shards(): up_pair = lax.ppermute(after(up_pair, over, one), 'ctx', PAIR_SWAP)]
    unnamed x32 -> x36, local copies, waits for them, and re-layouts: 6.72 us -> 5.78 us
  transfers between devices with their start and end apart: 21 -> 21, of which waited for: 9 -> 10; matrix products, arithmetic and copies ran while one was open for 1% -> 1% of each run, Pallas kernels for 20% -> 21%
where the time goes in v8:
time: 116 us; the launch traced here: 115 us
  starting transfers between devices  48.8 us (42%)
  Pallas kernels  29.6 us (26%)
  waiting for transfers between devices  27.7 us (24%)
  local copies, waits for them, and re-layouts  5.81 us (5%)
  between operations  1.81 us (2%)
    pallas_call x12, Pallas kernels, call(): pl.pallas_call(body, out_shape=[SPACES[o[0]](o[1], o[2]) if o[0] in 'HR'...  29.6 us
    all_to_all x4, starting transfers between devices, exchange(): lax.all_to_all(operand, 'ctx', split_axis=0, concat_axis=0, tiled=True, a...  19.3 us
    all_to_all x4, waiting for transfers between devices, exchange(): lax.all_to_all(operand, 'ctx', split_axis=0, concat_axis=0, tiled=True, a...  12.1 us
    ppermute x7, starting transfers between devices, step(): return lax.ppermute(value, 'fsdp', [(i, i ^ s) for i in range(8)])  9.43 us
    unnamed x36, local copies, waits for them, and re-layouts  5.78 us
    all_to_all x1, starting transfers between devices, shards(): lax.all_to_all(after(terms, grads), ('ctx', 'fsdp'), split_axis=0, concat...  5.01 us
    ppermute x1, waiting for transfers between devices, shards(): up_pair = lax.ppermute(after(up_pair, over, one), 'ctx', PAIR_SWAP)  4.84 us
    ppermute x1, waiting for transfers between devices, shards(): up_diag = lax.ppermute(after(up_diag, over, one), 'ctx', DIAG_SWAP)  4.56 us
  transfers between devices with their start and end apart: 21, of which 10 were waited for; matrix products, arithmetic and copies ran while one was open for 1% of the time, Pallas kernels for 21%

profile of v8, /device:TPU:1, one launch (start us, length us, event | category | flops | bytes accessed | tf_op | source)
XLA Modules:
  0.0 114.7 jit_solution(3968152270598989777)
XLA Ops:
  0.6 2.9 %shard_map.110 = (bf16[8,3,128,128]{3,2,1,0:T(8,128)(2,1)}, bf16[128,1024]{1,0:T(8,128)(2,1)}, bf16[128,1024]{1,0:T(8,128)(2,1)}, bf16[128,1024]{1,0:T(8,128)(2,...) custom-call(s32[1]{0:T(128)} %bitcast.refs_0_, s32[1]{0:T(128)} %bitcast.2.refs_1_.refs_0_, ...), custom_call_target="tpu_custom_call" | custom-call | bytes 2000000 | tf_op jit(solution)/shard_map/pallas_call | solution.py:112
  3.6 2.1 %collective-permute-start.2 = (bf16[128,1024]{1,0:T(8,128)(2,1)}, bf16[128,1024]{1,0:T(8,128)(2,1)S(1)}, u32[]{:S(2)}, u32[]{:S(2)}) collective-permute-start(bf16[128,1024]{1,0:T(8,128)(2,1)} %get-tuple-element.35.refs_3_), channel_id=1, source_target_pairs={{0,4},{1,5},{2,6},{3,7},{4,0},{5,1},{6,2},{7,3},{8,12},{9,13},{10,... | collective-permute-start | bytes 786440 | tf_op jit(solution)/shard_map/ppermute | solution.py:439
  5.7 3.8 %collective-permute-start.1 = (bf16[128,1024]{1,0:T(8,128)(2,1)}, bf16[128,1024]{1,0:T(8,128)(2,1)S(1)}, u32[]{:S(2)}, u32[]{:S(2)}) collective-permute-start(bf16[128,1024]{1,0:T(8,128)(2,1)} %get-tuple-element.35.refs_3_), channel_id=1, source_target_pairs={{0,3},{1,2},{2,1},{3,0},{4,7},{5,6},{6,5},{7,4},{8,11},{9,10},{10,... | collective-permute-start | bytes 786440 | tf_op jit(solution)/shard_map/ppermute | solution.py:439
  9.5 6.4 %all-to-all-start = ((bf16[8,3,128,128]{3,2,1,0:T(8,128)(2,1)}), bf16[8,3,128,128]{3,2,1,0:T(8,128)(2,1)S(1)}, u32[]{:S(2)}, u32[]{:S(2)}) async-start(bf16[8,3,128,128]{3,2,1,0:T(8,128)(2,1)} %get-tuple-element.34), calls=%async_computation | async-start | bytes 1572864 | tf_op jit(solution)/shard_map/all_to_all | solution.py:394
  19.4 1.6 %collective-permute-start.3 = (bf16[128,1024]{1,0:T(8,128)(2,1)S(1)}, bf16[128,1024]{1,0:T(8,128)(2,1)S(1)}, u32[]{:S(2)}, u32[]{:S(2)}) collective-permute-start(bf16[128,1024]{1,0:T(8,128)(2,1)S(1)} %collective-permute-done.2.refs_7_), channel_id=1, source_target_pairs={{0,1},{1,0},{2,3},{3,2},{4,5},{5,4},{6,7},{7,6},{8,9},{9,8},{10,11... | collective-permute-start | bytes 786440 | tf_op jit(solution)/shard_map/ppermute | solution.py:439
  21.0 3.2 %collective-permute-start.6 = (bf16[128,512]{1,0:T(8,128)(2,1)S(1)}, bf16[128,512]{1,0:T(8,128)(2,1)S(1)}, u32[]{:S(2)}, u32[]{:S(2)}) collective-permute-start(bf16[128,512]{1,0:T(8,128)(2,1)S(1)} %copy-done.17), channel_id=1, source_target_pairs={{0,64},{8,72},{16,80},{24,88},{32,96},{40,104},{48,112},{56,120},{... | collective-permute-start | bytes 393224 | tf_op jit(solution)/shard_map/ppermute | solution.py:447
  24.6 4.8 %collective-permute-done.6.refs_3_ = bf16[128,512]{1,0:T(8,128)(2,1)S(1)} collective-permute-done((bf16[128,512]{1,0:T(8,128)(2,1)S(1)}, bf16[128,512]{1,0:T(8,128)(2,1)S(1)}, u32[]{:S(2)}, u32[]{:S(2)}) %collective-permute-start.6) | collective-permute-done | bytes 131104 | tf_op jit(solution)/shard_map/ppermute | solution.py:447
  29.5 4.6 %collective-permute-done.7.refs_4_ = bf16[128,512]{1,0:T(8,128)(2,1)S(1)} collective-permute-done((bf16[128,512]{1,0:T(8,128)(2,1)S(1)}, bf16[128,512]{1,0:T(8,128)(2,1)S(1)}, u32[]{:S(2)}, u32[]{:S(2)}) %collective-permute-start.7) | collective-permute-done | bytes 131104 | tf_op jit(solution)/shard_map/ppermute | solution.py:448
  36.4 4.1 %shard_map.111 = (bf16[8,2,128,128]{3,2,1,0:T(8,128)(2,1)}, f32[4,1,256]{2,1,0:T(1,128)}, bf16[8,128,128]{2,1,0:T(8,128)(2,1)}, bf16[2048,128]{1,0:T(8,128)(2,1)}, bf16[2048,128]{1,0:T(8,128)(2,1)}) custom-call(s32[1]{0:T(128)} %bitcast.refs_0_, bf16[8,3,128,128]{3,2,1,0:T(8,128)(2,1)S(1)} %all-to-all-done.refs_1_.refs_2_.refs_3_, ...), custom_call_target="tpu_custom_call" | custom-call | flops 671088640 | bytes 2000000 | tf_op jit(solution)/shard_map/pallas_call | solution.py:112
  40.5 4.1 %all-to-all-start.1 = ((bf16[8,2,128,128]{3,2,1,0:T(8,128)(2,1)}), bf16[8,2,128,128]{3,2,1,0:T(8,128)(2,1)S(1)}, u32[]{:S(2)}, u32[]{:S(2)}) async-start(bf16[8,2,128,128]{3,2,1,0:T(8,128)(2,1)} %get-tuple-element.42.refs_5_), calls=%async_computation.1 | async-start | bytes 1048576 | tf_op jit(solution)/shard_map/all_to_all | solution.py:394
  44.7 2.7 %shard_map.112 = (f32[8,128,128]{2,1,0:T(8,128)S(1)}, bf16[8,128,128]{2,1,0:T(8,128)(2,1)S(1)}) custom-call(s32[1]{0:T(128)} %bitcast.1.refs_0_, bf16[128,1024]{1,0:T(8,128)(2,1)S(1)} %copy-done.1, bf16[128,1024]{1,0:T(8,128)(2,1)S(1)} %collective-permute-done.5.refs_2_, bf16[128,1024]{1,0:T(8,128)(2,1)S(1)} %copy-done.2, ...), custom_call_target="tpu_custom_call" | custom-call | flops 536870912 | bytes 2000000 | tf_op jit(solution)/shard_map/pallas_call | solution.py:112
  50.5 3.8 %all-to-all-done.1.refs_5_.refs_1_ = bf16[8,2,128,128]{3,2,1,0:T(8,128)(2,1)S(1)} async-done(((bf16[8,2,128,128]{3,2,1,0:T(8,128)(2,1)}), bf16[8,2,128,128]{3,2,1,0:T(8,128)(2,1)S(1)}, u32[]{:S(2)}, u32[]{:S(2)}) %all-to-all-start.1) | async-done | bytes 524320 | tf_op jit(solution)/shard_map/all_to_all | solution.py:394
  54.4 2.1 %collective-permute-start.13 = (bf16[8,2,128,128]{3,2,1,0:T(8,128)(2,1)S(1)}, bf16[8,2,128,128]{3,2,1,0:T(8,128)(2,1)S(1)}, u32[]{:S(2)}, u32[]{:S(2)}) collective-permute-start(bf16[8,2,128,128]{3,2,1,0:T(8,128)(2,1)S(1)} %all-to-all-done.1.refs_5_.refs_1_), channel_id=1, source_target_pairs={{0,8},{8,0},{16,24},{24,16},{32,40},{40,32},{48,56},{56,48},{64,72... | collective-permute-start | bytes 1572872 | tf_op jit(solution)/shard_map/ppermute | solution.py:486
  56.5 3.4 %all-to-all-start.2 = ((bf16[8,128,128]{2,1,0:T(8,128)(2,1)}), bf16[8,128,128]{2,1,0:T(8,128)(2,1)S(1)}, u32[]{:S(2)}, u32[]{:S(2)}) async-start(bf16[8,128,128]{2,1,0:T(8,128)(2,1)} %shard_map.113), calls=%async_computation.2 | async-start | bytes 524288 | tf_op jit(solution)/shard_map/all_to_all | solution.py:394
  60.0 2.3 %shard_map.116 = bf16[32,32,512]{2,1,0:T(8,128)(2,1)} custom-call(s32[1]{0:T(128)} %bitcast.2.refs_1_.refs_0_, bf16[128,1024]{1,0:T(8,128)(2,1)S(1)} %copy-done.1, bf16[128,1024]{1,0:T(8,128)(2,1)S(1)} %collective-permute-done.5.refs_2_, bf16[128,512]{1,0:T(8,128)(2,1)S(1)} %copy-done.10, bf16[128,512]{1,0:T(8,128)(2,1)S(1)} %copy-done.12, ...), custom_call_target="tpu_custom_call" | custom-call | flops 536870912 | bytes 2000000 | tf_op jit(solution)/shard_map/pallas_call | solution.py:112
  62.2 5.8 %all-to-all-done.2.refs_3_ = bf16[8,128,128]{2,1,0:T(8,128)(2,1)S(1)} async-done(((bf16[8,128,128]{2,1,0:T(8,128)(2,1)}), bf16[8,128,128]{2,1,0:T(8,128)(2,1)S(1)}, u32[]{:S(2)}, u32[]{:S(2)}) %all-to-all-start.2) | async-done | bytes 262176 | tf_op jit(solution)/shard_map/all_to_all | solution.py:394
  68.7 5.0 %all-to-all-start.3 = ((bf16[32,32,512]{2,1,0:T(8,128)(2,1)}), bf16[32,32,512]{2,1,0:T(8,128)(2,1)S(1)}, u32[]{:S(2)}, u32[]{:S(2)}) async-start(bf16[32,32,512]{2,1,0:T(8,128)(2,1)} %shard_map.116), calls=%async_computation.3 | async-start | bytes 2097152 | tf_op jit(solution)/shard_map/all_to_all | solution.py:497
  73.7 6.8 %shard_map.114 = (bf16[8,128,128]{2,1,0:T(8,128)(2,1)}, f32[8,2,128,128]{3,2,1,0:T(8,128)}, bf16[8,2,128,128]{3,2,1,0:T(8,128)(2,1)}) custom-call(s32[1]{0:T(128)} %bitcast.refs_0_, bf16[8,128,128]{2,1,0:T(8,128)(2,1)} %get-tuple-element.47.refs_1_, bf16[2048,128]{1,0:T(8,128)(2,1)} %get-tuple-element.48.refs_2_, bf16[8,128,128]{2,1,0:T(8,128)(2,1)} %copy-done.13, ...), custom_call_target="tpu_custom_call" | custom-call | flops 1677721600 | bytes 2000000 | tf_op jit(solution)/shard_map/pallas_call | solution.py:112
  81.7 1.7 %collective-permute-done.12.refs_2_ = bf16[8,2,128,128]{3,2,1,0:T(8,128)(2,1)S(1)} collective-permute-done((bf16[8,2,128,128]{3,2,1,0:T(8,128)(2,1)}, bf16[8,2,128,128]{3,2,1,0:T(8,128)(2,1)S(1)}, u32[]{:S(2)}, u32[]{:S(2)}) %collective-permute-start.12) | collective-permute-done | bytes 524320 | tf_op jit(solution)/shard_map/ppermute | solution.py:519
  89.5 5.4 %all-to-all-start.4 = ((bf16[8,4,128,128]{3,2,1,0:T(8,128)(2,1)}), bf16[8,4,128,128]{3,2,1,0:T(8,128)(2,1)S(1)}, u32[]{:S(2)}, u32[]{:S(2)}) async-start(bf16[8,4,128,128]{3,2,1,0:T(8,128)(2,1)} %shard_map.117), calls=%async_computation.4 | async-start | bytes 2097152 | tf_op jit(solution)/shard_map/all_to_all | solution.py:394
  96.8 3.0 %shard_map.118 = (bf16[128,1024]{1,0:T(8,128)(2,1)}, bf16[128,1024]{1,0:T(8,128)(2,1)}) custom-call(s32[1]{0:T(128)} %bitcast.1.refs_0_, bf16[8,2,128,128]{3,2,1,0:T(8,128)(2,1)S(1)} %all-to-all-done.1.refs_5_.refs_1_, bf16[8,2,128,128]{3,2,1,0:T(8,128)(2,1)S(1)} %collective-permute-done.13.refs_6_.refs_2_, bf16[128,1024]{1,0:T(8,128)(2,1)S(1)} %copy-done.2, ...), custom_call_target="tpu_custom_call" | custom-call | flops 536870912 | bytes 2000000 | tf_op jit(solution)/shard_map/pallas_call | solution.py:112
  99.8 2.1 %collective-permute-start.14 = (bf16[128,1024]{1,0:T(8,128)(2,1)}, bf16[128,1024]{1,0:T(8,128)(2,1)S(1)}, u32[]{:S(2)}, u32[]{:S(2)}) collective-permute-start(bf16[128,1024]{1,0:T(8,128)(2,1)} %get-tuple-element.58), channel_id=1, source_target_pairs={{0,8},{8,0},{16,24},{24,16},{32,40},{40,32},{48,56},{56,48},{64,72... | collective-permute-start | bytes 786440 | tf_op jit(solution)/shard_map/ppermute | solution.py:543
  105.5 2.4 %all-to-all-done.4.refs_0_ = bf16[8,4,128,128]{3,2,1,0:T(8,128)(2,1)S(1)} async-done(((bf16[8,4,128,128]{3,2,1,0:T(8,128)(2,1)}), bf16[8,4,128,128]{3,2,1,0:T(8,128)(2,1)S(1)}, u32[]{:S(2)}, u32[]{:S(2)}) %all-to-all-start.4) | async-done | bytes 1048608 | tf_op jit(solution)/shard_map/all_to_all | solution.py:394
  108.0 3.8 %collective-permute-start.15 = (bf16[8,128,128]{2,1,0:T(8,128)(2,1)S(1)}, bf16[8,128,128]{2,1,0:T(8,128)(2,1)S(1)}, u32[]{:S(2)}, u32[]{:S(2)}) collective-permute-start(bf16[8,128,128]{2,1,0:T(8,128)(2,1)S(1)} %slice_bitcast_fusion.refs_1_), channel_id=1, source_target_pairs={{0,8},{8,0},{16,24},{24,16},{32,40},{40,32},{48,56},{56,48},{64,72... | collective-permute-start | bytes 786440 | tf_op jit(solution)/shard_map/ppermute | solution.py:551
  (72 shorter events, 24.8 us)
Async XLA Ops:
  3.6 13.9 %copy-start.14 = (s32[1,2048]{1,0:T(1,128)S(1)}, s32[1,2048]{1,0:T(1,128)}, u32[]{:S(2)}) copy-start(s32[1,2048]{1,0:T(1,128)} %param.10) | copy-start | bytes 24580
  3.6 17.4 %copy-start.17 = (bf16[128,512]{1,0:T(8,128)(2,1)S(1)}, bf16[128,512]{1,0:T(8,128)(2,1)}, u32[]{:S(2)}) copy-start(bf16[128,512]{1,0:T(8,128)(2,1)} %get-tuple-element.38) | copy-start | bytes 393220
  3.6 20.7 %copy-start.16 = (bf16[128,512]{1,0:T(8,128)(2,1)S(1)}, bf16[128,512]{1,0:T(8,128)(2,1)}, u32[]{:S(2)}) copy-start(bf16[128,512]{1,0:T(8,128)(2,1)} %get-tuple-element.40) | copy-start | bytes 393220
  3.6 15.5 %collective-permute-start.2 = (bf16[128,1024]{1,0:T(8,128)(2,1)}, bf16[128,1024]{1,0:T(8,128)(2,1)S(1)}, u32[]{:S(2)}, u32[]{:S(2)}) collective-permute-start(bf16[128,1024]{1,0:T(8,128)(2,1)} %get-tuple-element.35.refs_3_), channel_id=1, source_target_pairs={{0,4},{1,5},{2,6},{3,7},{4,0},{5,1},{6,2},{7,3},{8,12},{9,13},{10,... | collective-permute-start | bytes 786440 | tf_op jit(solution)/shard_map/ppermute | solution.py:439
  5.7 18.9 %collective-permute-start.1 = (bf16[128,1024]{1,0:T(8,128)(2,1)}, bf16[128,1024]{1,0:T(8,128)(2,1)S(1)}, u32[]{:S(2)}, u32[]{:S(2)}) collective-permute-start(bf16[128,1024]{1,0:T(8,128)(2,1)} %get-tuple-element.35.refs_3_), channel_id=1, source_target_pairs={{0,3},{1,2},{2,1},{3,0},{4,7},{5,6},{6,5},{7,4},{8,11},{9,10},{10,... | collective-permute-start | bytes 786440 | tf_op jit(solution)/shard_map/ppermute | solution.py:439
  9.5 11.5 %collective-permute-start = (bf16[128,1024]{1,0:T(8,128)(2,1)}, bf16[128,1024]{1,0:T(8,128)(2,1)S(1)}, u32[]{:S(2)}, u32[]{:S(2)}) collective-permute-start(bf16[128,1024]{1,0:T(8,128)(2,1)} %get-tuple-element.35.refs_3_), channel_id=1, source_target_pairs={{0,1},{1,0},{2,3},{3,2},{4,5},{5,4},{6,7},{7,6},{8,9},{9,8},{10,11... | collective-permute-start | bytes 786440 | tf_op jit(solution)/shard_map/ppermute | solution.py:439
  9.5 24.5 %all-to-all-start = ((bf16[8,3,128,128]{3,2,1,0:T(8,128)(2,1)}), bf16[8,3,128,128]{3,2,1,0:T(8,128)(2,1)S(1)}, u32[]{:S(2)}, u32[]{:S(2)}) async-start(bf16[8,3,128,128]{3,2,1,0:T(8,128)(2,1)} %get-tuple-element.34), calls=%async_computation | async-start | bytes 1572864 | tf_op jit(solution)/shard_map/all_to_all | solution.py:394
  15.8 8.4 %collective-permute-start.5 = (bf16[128,1024]{1,0:T(8,128)(2,1)S(1)}, bf16[128,1024]{1,0:T(8,128)(2,1)S(1)}, u32[]{:S(2)}, u32[]{:S(2)}) collective-permute-start(bf16[128,1024]{1,0:T(8,128)(2,1)S(1)} %copy-done.15), channel_id=1, source_target_pairs={{0,8},{8,0},{16,24},{24,16},{32,40},{40,32},{48,56},{56,48},{64,72... | collective-permute-start | bytes 786440 | tf_op jit(solution)/shard_map/ppermute | solution.py:446
  19.1 14.9 %collective-permute-start.4 = (bf16[128,1024]{1,0:T(8,128)(2,1)S(1)}, bf16[128,1024]{1,0:T(8,128)(2,1)S(1)}, u32[]{:S(2)}, u32[]{:S(2)}) collective-permute-start(bf16[128,1024]{1,0:T(8,128)(2,1)S(1)} %collective-permute-done.2.refs_7_), channel_id=1, source_target_pairs={{0,3},{1,2},{2,1},{3,0},{4,7},{5,6},{6,5},{7,4},{8,11},{9,10},{10,... | collective-permute-start | bytes 786440 | tf_op jit(solution)/shard_map/ppermute | solution.py:439
  19.4 14.6 %collective-permute-start.3 = (bf16[128,1024]{1,0:T(8,128)(2,1)S(1)}, bf16[128,1024]{1,0:T(8,128)(2,1)S(1)}, u32[]{:S(2)}, u32[]{:S(2)}) collective-permute-start(bf16[128,1024]{1,0:T(8,128)(2,1)S(1)} %collective-permute-done.2.refs_7_), channel_id=1, source_target_pairs={{0,1},{1,0},{2,3},{3,2},{4,5},{5,4},{6,7},{7,6},{8,9},{9,8},{10,11... | collective-permute-start | bytes 786440 | tf_op jit(solution)/shard_map/ppermute | solution.py:439
  21.0 8.4 %collective-permute-start.6 = (bf16[128,512]{1,0:T(8,128)(2,1)S(1)}, bf16[128,512]{1,0:T(8,128)(2,1)S(1)}, u32[]{:S(2)}, u32[]{:S(2)}) collective-permute-start(bf16[128,512]{1,0:T(8,128)(2,1)S(1)} %copy-done.17), channel_id=1, source_target_pairs={{0,64},{8,72},{16,80},{24,88},{32,96},{40,104},{48,112},{56,120},{... | collective-permute-start | bytes 393224 | tf_op jit(solution)/shard_map/ppermute | solution.py:447
  24.3 9.7 %collective-permute-start.7 = (bf16[128,512]{1,0:T(8,128)(2,1)S(1)}, bf16[128,512]{1,0:T(8,128)(2,1)S(1)}, u32[]{:S(2)}, u32[]{:S(2)}) collective-permute-start(bf16[128,512]{1,0:T(8,128)(2,1)S(1)} %copy-done.16), channel_id=1, source_target_pairs={{0,72},{8,64},{16,88},{24,80},{32,104},{40,96},{48,120},{56,112},{... | collective-permute-start | bytes 393224 | tf_op jit(solution)/shard_map/ppermute | solution.py:448
  34.0 2.4 %collective-permute-start.8 = (bf16[8,3,128,128]{3,2,1,0:T(8,128)(2,1)S(1)}, bf16[8,3,128,128]{3,2,1,0:T(8,128)(2,1)S(1)}, u32[]{:S(2)}, u32[]{:S(2)}) collective-permute-start(bf16[8,3,128,128]{3,2,1,0:T(8,128)(2,1)S(1)} %all-to-all-done.refs_1_.refs_2_.refs_3_), channel_id=1, source_target_pairs={{0,8},{8,0},{16,24},{24,16},{32,40},{40,32},{48,56},{56,48},{64,72... | collective-permute-start | bytes 2359304 | tf_op jit(solution)/shard_map/ppermute | solution.py:453
  34.1 10.5 %collective-permute-start.9 = (bf16[128,1024]{1,0:T(8,128)(2,1)S(1)}, bf16[128,1024]{1,0:T(8,128)(2,1)S(1)}, u32[]{:S(2)}, u32[]{:S(2)}) collective-permute-start(bf16[128,1024]{1,0:T(8,128)(2,1)S(1)} %collective-permute-done.refs_4_), channel_id=1, source_target_pairs={{0,3},{1,2},{2,1},{3,0},{4,7},{5,6},{6,5},{7,4},{8,11},{9,10},{10,... | collective-permute-start | bytes 786440 | tf_op jit(solution)/shard_map/ppermute | solution.py:439
  34.6 10.1 %collective-permute-start.10 = (bf16[128,1024]{1,0:T(8,128)(2,1)S(1)}, bf16[128,1024]{1,0:T(8,128)(2,1)}, u32[]{:S(2)}, u32[]{:S(2)}) collective-permute-start(bf16[128,1024]{1,0:T(8,128)(2,1)S(1)} %collective-permute-done.4.refs_10_), channel_id=1, source_target_pairs={{0,1},{1,0},{2,3},{3,2},{4,5},{5,4},{6,7},{7,6},{8,9},{9,8},{10,11... | collective-permute-start | bytes 786440 | tf_op jit(solution)/shard_map/ppermute | solution.py:439
  40.5 13.9 %all-to-all-start.1 = ((bf16[8,2,128,128]{3,2,1,0:T(8,128)(2,1)}), bf16[8,2,128,128]{3,2,1,0:T(8,128)(2,1)S(1)}, u32[]{:S(2)}, u32[]{:S(2)}) async-start(bf16[8,2,128,128]{3,2,1,0:T(8,128)(2,1)} %get-tuple-element.42.refs_5_), calls=%async_computation.1 | async-start | bytes 1048576 | tf_op jit(solution)/shard_map/all_to_all | solution.py:394
  47.5 1.8 %collective-permute-start.11 = (bf16[8,128,128]{2,1,0:T(8,128)(2,1)S(1)}, bf16[8,128,128]{2,1,0:T(8,128)(2,1)S(1)}, u32[]{:S(2)}, u32[]{:S(2)}) collective-permute-start(bf16[8,128,128]{2,1,0:T(8,128)(2,1)S(1)} %get-tuple-element.45), channel_id=1, source_target_pairs={{0,8},{8,0},{16,24},{24,16},{32,40},{40,32},{48,56},{56,48},{64,72... | collective-permute-start | bytes 786440 | tf_op jit(solution)/shard_map/ppermute | solution.py:479
  54.4 5.5 %collective-permute-start.13 = (bf16[8,2,128,128]{3,2,1,0:T(8,128)(2,1)S(1)}, bf16[8,2,128,128]{3,2,1,0:T(8,128)(2,1)S(1)}, u32[]{:S(2)}, u32[]{:S(2)}) collective-permute-start(bf16[8,2,128,128]{3,2,1,0:T(8,128)(2,1)S(1)} %all-to-all-done.1.refs_5_.refs_1_), channel_id=1, source_target_pairs={{0,8},{8,0},{16,24},{24,16},{32,40},{40,32},{48,56},{56,48},{64,72... | collective-permute-start | bytes 1572872 | tf_op jit(solution)/shard_map/ppermute | solution.py:486
  56.5 11.5 %all-to-all-start.2 = ((bf16[8,128,128]{2,1,0:T(8,128)(2,1)}), bf16[8,128,128]{2,1,0:T(8,128)(2,1)S(1)}, u32[]{:S(2)}, u32[]{:S(2)}) async-start(bf16[8,128,128]{2,1,0:T(8,128)(2,1)} %shard_map.113), calls=%async_computation.2 | async-start | bytes 524288 | tf_op jit(solution)/shard_map/all_to_all | solution.py:394
  68.7 19.5 %all-to-all-start.3 = ((bf16[32,32,512]{2,1,0:T(8,128)(2,1)}), bf16[32,32,512]{2,1,0:T(8,128)(2,1)S(1)}, u32[]{:S(2)}, u32[]{:S(2)}) async-start(bf16[32,32,512]{2,1,0:T(8,128)(2,1)} %shard_map.116), calls=%async_computation.3 | async-start | bytes 2097152 | tf_op jit(solution)/shard_map/all_to_all | solution.py:497
  80.5 2.9 %collective-permute-start.12 = (bf16[8,2,128,128]{3,2,1,0:T(8,128)(2,1)}, bf16[8,2,128,128]{3,2,1,0:T(8,128)(2,1)S(1)}, u32[]{:S(2)}, u32[]{:S(2)}) collective-permute-start(bf16[8,2,128,128]{3,2,1,0:T(8,128)(2,1)} %get-tuple-element.54), channel_id=1, source_target_pairs={{0,8},{8,0},{16,24},{24,16},{32,40},{40,32},{48,56},{56,48},{64,72... | collective-permute-start | bytes 1572872 | tf_op jit(solution)/shard_map/ppermute | solution.py:519
  89.5 18.5 %all-to-all-start.4 = ((bf16[8,4,128,128]{3,2,1,0:T(8,128)(2,1)}), bf16[8,4,128,128]{3,2,1,0:T(8,128)(2,1)S(1)}, u32[]{:S(2)}, u32[]{:S(2)}) async-start(bf16[8,4,128,128]{3,2,1,0:T(8,128)(2,1)} %shard_map.117), calls=%async_computation.4 | async-start | bytes 2097152 | tf_op jit(solution)/shard_map/all_to_all | solution.py:394
  99.8 3.5 %collective-permute-start.14 = (bf16[128,1024]{1,0:T(8,128)(2,1)}, bf16[128,1024]{1,0:T(8,128)(2,1)S(1)}, u32[]{:S(2)}, u32[]{:S(2)}) collective-permute-start(bf16[128,1024]{1,0:T(8,128)(2,1)} %get-tuple-element.58), channel_id=1, source_target_pairs={{0,8},{8,0},{16,24},{24,16},{32,40},{40,32},{48,56},{56,48},{64,72... | collective-permute-start | bytes 786440 | tf_op jit(solution)/shard_map/ppermute | solution.py:543
  108.0 5.1 %collective-permute-start.15 = (bf16[8,128,128]{2,1,0:T(8,128)(2,1)S(1)}, bf16[8,128,128]{2,1,0:T(8,128)(2,1)S(1)}, u32[]{:S(2)}, u32[]{:S(2)}) collective-permute-start(bf16[8,128,128]{2,1,0:T(8,128)(2,1)S(1)} %slice_bitcast_fusion.refs_1_), channel_id=1, source_target_pairs={{0,8},{8,0},{16,24},{24,16},{32,40},{40,32},{48,56},{56,48},{64,72... | collective-permute-start | bytes 786440 | tf_op jit(solution)/shard_map/ppermute | solution.py:551
  (15 other events, 82.3 us)

commit v9 on v8

--- a/solution.py
+++ b/solution.py
@@ -439,17 +439,16 @@
         return lax.ppermute(value, "fsdp", [(i, i ^ s) for i in range(8)])
 
     over = step(own_half, 4)
+    own_half = after(own_half, end)
     one, three = step(own_half, 1), step(own_half, 3)
-    over_one, over_three = step(over, 1), step(over, 3)
+    over_three = step(over, 3)
+    up_other = lax.ppermute(up_send, "ctx", CORE_SWAP)
+    up_pair = lax.ppermute(after(up_pair, over), "ctx", PAIR_SWAP)
+
+    own = after(own, end, valid, valid_here, one, three, over_three, up_other, up_pair)
+    over_one = step(after(over, own), 1)
     two, over_two = step(one, 3), step(over_three, 1)
     pieces = [own_half, one, two, three, over, over_one, over_two, over_three]
-    up_other = lax.ppermute(up_send, "ctx", CORE_SWAP)
-    up_pair = lax.ppermute(after(up_pair, over, one), "ctx", PAIR_SWAP)
-    up_diag = lax.ppermute(after(up_diag, over, one), "ctx", DIAG_SWAP)
-
-    own = after(
-        own, end, valid, valid_here, one, three, over_one, over_three, up_other, up_pair, up_diag
-    )
     other = lax.ppermute(own, "ctx", CORE_SWAP)
     pairs = 4 * TILE * SPAN * 5 // 2
     rows = ("H", (LEN, HS), BF16)
@@ -470,6 +469,7 @@
         flops=4 * pairs * HS,
     )
     context_mine = exchange(context)
+    up_diag = lax.ppermute(after(up_diag, context), "ctx", DIAG_SWAP)
     grads_keep, grads_send = call(
         project_kernel,
         [("S", row_ref), ("A", up_mine), ("A", up_other), *[("V", piece) for piece in pieces]],
@@ -482,7 +482,7 @@
         [("V", valid_here), ("V", grads_keep), ("V", grads_came)],
         [("V", (HEADS, BLOCK, HS), BF16)],
     )
-    context_mine = after(context_mine, grads)
+    context_mine = after(context_mine, grads, up_diag)
     context_other = lax.ppermute(context_mine, "ctx", CORE_SWAP)
     terms = call(
         weight_kernel,

time: 116 us -> 125 us (1.078)
  starting transfers between devices: 48.8 us -> 63.1 us
  waiting for transfers between devices: 27.7 us -> 22.7 us
    ppermute x7, waiting for transfers between devices: 0.02 us -> 7.92 us  [step(): return lax.ppermute(value, 'fsdp', [(i, i ^ s) for i in range(8)])]
    all_to_all x4, starting transfers between devices: 19.3 us -> 25.8 us  [exchange(): lax.all_to_all(operand, 'ctx', split_axis=0, concat_axis=0, tiled=True, a...]
    all_to_all x4, waiting for transfers between devices: 12.1 us -> 5.91 us  [exchange(): lax.all_to_all(operand, 'ctx', split_axis=0, concat_axis=0, tiled=True, a...]
    ppermute x2, waiting for transfers between devices: 9.4 us -> 5.71 us  [the longest x1 3.41 us: shards(): up_diag = lax.ppermute(after(up_diag, context), 'ctx', DIAG_SWAP)]
    ppermute x1, starting transfers between devices: 0.09 us -> 3.09 us  [shards(): other = lax.ppermute(own, 'ctx', CORE_SWAP)]
    ppermute x2, starting transfers between devices: 3.54 us -> 6.49 us  [the longest x1 3.25 us: shards(): up_pair = lax.ppermute(after(up_pair, over), 'ctx', PAIR_SWAP)]
    ppermute x1, starting transfers between devices: 2.12 us -> 0.01 us  [shards(): context_other = lax.ppermute(context_mine, 'ctx', CORE_SWAP)]
    ppermute x1, starting transfers between devices: 3.8 us -> 5.11 us  [shards(): weight_other = lax.ppermute(weight_mine, 'ctx', CORE_SWAP)]
  transfers between devices with their start and end apart: 21 -> 21, of which waited for: 10 -> 8; matrix products, arithmetic and copies ran while one was open for 1% -> 1% of each run, Pallas kernels for 21% -> 19%
where the time goes in v9:
time: 125 us; the launch traced here: 124 us
  starting transfers between devices  63.1 us (50%)
  Pallas kernels  29.6 us (24%)
  waiting for transfers between devices  22.7 us (18%)
  local copies, waits for them, and re-layouts  5.8 us (5%)
  between operations  1.75 us (1%)
    pallas_call x12, Pallas kernels, call(): pl.pallas_call(body, out_shape=[SPACES[o[0]](o[1], o[2]) if o[0] in 'HR'...  29.6 us
    all_to_all x4, starting transfers between devices, exchange(): lax.all_to_all(operand, 'ctx', split_axis=0, concat_axis=0, tiled=True, a...  25.8 us
    ppermute x7, starting transfers between devices, step(): return lax.ppermute(value, 'fsdp', [(i, i ^ s) for i in range(8)])  10.7 us
    ppermute x7, waiting for transfers between devices, step(): return lax.ppermute(value, 'fsdp', [(i, i ^ s) for i in range(8)])  7.92 us
    all_to_all x4, waiting for transfers between devices, exchange(): lax.all_to_all(operand, 'ctx', split_axis=0, concat_axis=0, tiled=True, a...  5.91 us
    unnamed x32, local copies, waits for them, and re-layouts  5.78 us
    ppermute x1, starting transfers between devices, shards(): weight_other = lax.ppermute(weight_mine, 'ctx', CORE_SWAP)  5.11 us
    all_to_all x1, starting transfers between devices, shards(): lax.all_to_all(after(terms, grads), ('ctx', 'fsdp'), split_axis=0, concat...  4.24 us
  transfers between devices with their start and end apart: 21, of which 8 were waited for; matrix products, arithmetic and copies ran while one was open for 1% of the time, Pallas kernels for 19%

profile of v9, /device:TPU:1, one launch (start us, length us, event | category | flops | bytes accessed | tf_op | source)
XLA Modules:
  0.0 123.9 jit_solution(1396526747561278642)
XLA Ops:
  0.6 2.9 %shard_map.110 = (bf16[8,3,128,128]{3,2,1,0:T(8,128)(2,1)}, bf16[128,1024]{1,0:T(8,128)(2,1)}, bf16[128,1024]{1,0:T(8,128)(2,1)}, bf16[128,1024]{1,0:T(8,128)(2,...) custom-call(s32[1]{0:T(128)} %bitcast.refs_0_, s32[1]{0:T(128)} %bitcast.2.refs_1_.refs_0_, ...), custom_call_target="tpu_custom_call" | custom-call | bytes 2000000 | tf_op jit(solution)/shard_map/pallas_call | solution.py:112
  3.6 7.6 %all-to-all-start = ((bf16[8,3,128,128]{3,2,1,0:T(8,128)(2,1)}), bf16[8,3,128,128]{3,2,1,0:T(8,128)(2,1)S(1)}, u32[]{:S(2)}, u32[]{:S(2)}) async-start(bf16[8,3,128,128]{3,2,1,0:T(8,128)(2,1)} %get-tuple-element.36), calls=%async_computation | async-start | bytes 1572864 | tf_op jit(solution)/shard_map/all_to_all | solution.py:394
  13.3 3.8 %collective-permute-start.1 = (bf16[128,1024]{1,0:T(8,128)(2,1)S(1)}, bf16[128,1024]{1,0:T(8,128)(2,1)S(1)}, u32[]{:S(2)}, u32[]{:S(2)}) collective-permute-start(bf16[128,1024]{1,0:T(8,128)(2,1)S(1)} %copy-done.2), channel_id=1, source_target_pairs={{0,3},{1,2},{2,1},{3,0},{4,7},{5,6},{6,5},{7,4},{8,11},{9,10},{10,... | collective-permute-start | bytes 786440 | tf_op jit(solution)/shard_map/ppermute | solution.py:439
  18.6 7.2 %collective-permute-done.2.refs_7_ = bf16[128,1024]{1,0:T(8,128)(2,1)S(1)} collective-permute-done((bf16[128,1024]{1,0:T(8,128)(2,1)S(1)}, bf16[128,1024]{1,0:T(8,128)(2,1)S(1)}, u32[]{:S(2)}, u32[]{:S(2)}) %collective-permute-start.2) | collective-permute-done | bytes 262176 | tf_op jit(solution)/shard_map/ppermute | solution.py:439
  25.9 3.8 %collective-permute-start.3 = (bf16[128,1024]{1,0:T(8,128)(2,1)S(1)}, bf16[128,1024]{1,0:T(8,128)(2,1)S(1)}, u32[]{:S(2)}, u32[]{:S(2)}) collective-permute-start(bf16[128,1024]{1,0:T(8,128)(2,1)S(1)} %collective-permute-done.2.refs_7_), channel_id=1, source_target_pairs={{0,3},{1,2},{2,1},{3,0},{4,7},{5,6},{6,5},{7,4},{8,11},{9,10},{10,... | collective-permute-start | bytes 786440 | tf_op jit(solution)/shard_map/ppermute | solution.py:439
  29.6 3.3 %collective-permute-start.5 = (bf16[128,512]{1,0:T(8,128)(2,1)S(1)}, bf16[128,512]{1,0:T(8,128)(2,1)S(1)}, u32[]{:S(2)}, u32[]{:S(2)}) collective-permute-start(bf16[128,512]{1,0:T(8,128)(2,1)S(1)} %copy-done.15), channel_id=1, source_target_pairs={{0,64},{8,72},{16,80},{24,88},{32,96},{40,104},{48,112},{56,120},{... | collective-permute-start | bytes 393224 | tf_op jit(solution)/shard_map/ppermute | solution.py:446
  32.9 2.3 %collective-permute-done.5.refs_3_ = bf16[128,512]{1,0:T(8,128)(2,1)S(1)} collective-permute-done((bf16[128,512]{1,0:T(8,128)(2,1)S(1)}, bf16[128,512]{1,0:T(8,128)(2,1)S(1)}, u32[]{:S(2)}, u32[]{:S(2)}) %collective-permute-start.5) | collective-permute-done | bytes 131104 | tf_op jit(solution)/shard_map/ppermute | solution.py:446
  35.3 3.1 %collective-permute-start.6 = (bf16[8,3,128,128]{3,2,1,0:T(8,128)(2,1)S(1)}, bf16[8,3,128,128]{3,2,1,0:T(8,128)(2,1)S(1)}, u32[]{:S(2)}, u32[]{:S(2)}) collective-permute-start(bf16[8,3,128,128]{3,2,1,0:T(8,128)(2,1)S(1)} %all-to-all-done.refs_1_.refs_2_.refs_3_), channel_id=1, source_target_pairs={{0,8},{8,0},{16,24},{24,16},{32,40},{40,32},{48,56},{56,48},{64,72... | collective-permute-start | bytes 2359304 | tf_op jit(solution)/shard_map/ppermute | solution.py:452
  41.0 4.1 %shard_map.111 = (bf16[8,2,128,128]{3,2,1,0:T(8,128)(2,1)}, f32[4,1,256]{2,1,0:T(1,128)}, bf16[8,128,128]{2,1,0:T(8,128)(2,1)}, bf16[2048,128]{1,0:T(8,128)(2,1)}, bf16[2048,128]{1,0:T(8,128)(2,1)}) custom-call(s32[1]{0:T(128)} %bitcast.refs_0_, bf16[8,3,128,128]{3,2,1,0:T(8,128)(2,1)S(1)} %all-to-all-done.refs_1_.refs_2_.refs_3_, ...), custom_call_target="tpu_custom_call" | custom-call | flops 671088640 | bytes 2000000 | tf_op jit(solution)/shard_map/pallas_call | solution.py:112
  45.1 7.1 %all-to-all-start.1 = ((bf16[8,2,128,128]{3,2,1,0:T(8,128)(2,1)}), bf16[8,2,128,128]{3,2,1,0:T(8,128)(2,1)S(1)}, u32[]{:S(2)}, u32[]{:S(2)}) async-start(bf16[8,2,128,128]{3,2,1,0:T(8,128)(2,1)} %get-tuple-element.43.refs_5_), calls=%async_computation.1 | async-start | bytes 1048576 | tf_op jit(solution)/shard_map/all_to_all | solution.py:394
  52.9 2.7 %shard_map.112 = (f32[8,128,128]{2,1,0:T(8,128)S(1)}, bf16[8,128,128]{2,1,0:T(8,128)(2,1)S(1)}) custom-call(s32[1]{0:T(128)} %bitcast.1.refs_0_, bf16[128,1024]{1,0:T(8,128)(2,1)S(1)} %copy-done.1, bf16[128,1024]{1,0:T(8,128)(2,1)S(1)} %collective-permute-done.4.refs_2_, bf16[128,1024]{1,0:T(8,128)(2,1)S(1)} %copy-done.2, ...), custom_call_target="tpu_custom_call" | custom-call | flops 536870912 | bytes 2000000 | tf_op jit(solution)/shard_map/pallas_call | solution.py:112
  56.9 3.2 %collective-permute-start.11 = (bf16[128,512]{1,0:T(8,128)(2,1)S(1)}, bf16[128,512]{1,0:T(8,128)(2,1)S(1)}, u32[]{:S(2)}, u32[]{:S(2)}) collective-permute-start(bf16[128,512]{1,0:T(8,128)(2,1)S(1)} %copy-done.14), channel_id=1, source_target_pairs={{0,72},{8,64},{16,88},{24,80},{32,104},{40,96},{48,120},{56,112},{... | collective-permute-start | bytes 393224 | tf_op jit(solution)/shard_map/ppermute | solution.py:472
  61.3 3.4 %collective-permute-done.11.refs_4_ = bf16[128,512]{1,0:T(8,128)(2,1)S(1)} collective-permute-done((bf16[128,512]{1,0:T(8,128)(2,1)S(1)}, bf16[128,512]{1,0:T(8,128)(2,1)S(1)}, u32[]{:S(2)}, u32[]{:S(2)}) %collective-permute-start.11) | collective-permute-done | bytes 131104 | tf_op jit(solution)/shard_map/ppermute | solution.py:472
  64.8 5.9 %all-to-all-start.2 = ((bf16[8,128,128]{2,1,0:T(8,128)(2,1)}), bf16[8,128,128]{2,1,0:T(8,128)(2,1)S(1)}, u32[]{:S(2)}, u32[]{:S(2)}) async-start(bf16[8,128,128]{2,1,0:T(8,128)(2,1)} %shard_map.113), calls=%async_computation.2 | async-start | bytes 524288 | tf_op jit(solution)/shard_map/all_to_all | solution.py:394
  70.7 2.3 %shard_map.116 = bf16[32,32,512]{2,1,0:T(8,128)(2,1)} custom-call(s32[1]{0:T(128)} %bitcast.2.refs_1_.refs_0_, bf16[128,1024]{1,0:T(8,128)(2,1)S(1)} %copy-done.1, bf16[128,1024]{1,0:T(8,128)(2,1)S(1)} %collective-permute-done.4.refs_2_, bf16[128,512]{1,0:T(8,128)(2,1)S(1)} %copy-done.10, bf16[128,512]{1,0:T(8,128)(2,1)S(1)} %collective-permute-done.11.refs_4_, ...), custom_call_target="tpu_custom_call" | custom-call | flops 536870912 | bytes 2000000 | tf_op jit(solution)/shard_map/pallas_call | solution.py:112
  72.9 5.3 %all-to-all-done.2.refs_3_ = bf16[8,128,128]{2,1,0:T(8,128)(2,1)S(1)} async-done(((bf16[8,128,128]{2,1,0:T(8,128)(2,1)}), bf16[8,128,128]{2,1,0:T(8,128)(2,1)S(1)}, u32[]{:S(2)}, u32[]{:S(2)}) %all-to-all-start.2) | async-done | bytes 262176 | tf_op jit(solution)/shard_map/all_to_all | solution.py:394
  78.9 4.2 %all-to-all-start.3 = ((bf16[32,32,512]{2,1,0:T(8,128)(2,1)}), bf16[32,32,512]{2,1,0:T(8,128)(2,1)S(1)}, u32[]{:S(2)}, u32[]{:S(2)}) async-start(bf16[32,32,512]{2,1,0:T(8,128)(2,1)} %shard_map.116), calls=%async_computation.3 | async-start | bytes 2097152 | tf_op jit(solution)/shard_map/all_to_all | solution.py:497
  83.2 6.8 %shard_map.114 = (bf16[8,128,128]{2,1,0:T(8,128)(2,1)}, f32[8,2,128,128]{3,2,1,0:T(8,128)}, bf16[8,2,128,128]{3,2,1,0:T(8,128)(2,1)}) custom-call(s32[1]{0:T(128)} %bitcast.refs_0_, bf16[8,128,128]{2,1,0:T(8,128)(2,1)} %get-tuple-element.51.refs_1_, bf16[2048,128]{1,0:T(8,128)(2,1)} %get-tuple-element.52.refs_2_, bf16[8,128,128]{2,1,0:T(8,128)(2,1)} %copy-done.11, ...), custom_call_target="tpu_custom_call" | custom-call | flops 1677721600 | bytes 2000000 | tf_op jit(solution)/shard_map/pallas_call | solution.py:112
  89.9 2.0 %collective-permute-start.12 = (bf16[8,2,128,128]{3,2,1,0:T(8,128)(2,1)}, bf16[8,2,128,128]{3,2,1,0:T(8,128)(2,1)S(1)}, u32[]{:S(2)}, u32[]{:S(2)}) collective-permute-start(bf16[8,2,128,128]{3,2,1,0:T(8,128)(2,1)} %get-tuple-element.58), channel_id=1, source_target_pairs={{0,8},{8,0},{16,24},{24,16},{32,40},{40,32},{48,56},{56,48},{64,72... | collective-permute-start | bytes 1572872 | tf_op jit(solution)/shard_map/ppermute | solution.py:519
  92.0 1.7 %collective-permute-done.12.refs_2_ = bf16[8,2,128,128]{3,2,1,0:T(8,128)(2,1)S(1)} collective-permute-done((bf16[8,2,128,128]{3,2,1,0:T(8,128)(2,1)}, bf16[8,2,128,128]{3,2,1,0:T(8,128)(2,1)S(1)}, u32[]{:S(2)}, u32[]{:S(2)}) %collective-permute-start.12) | collective-permute-done | bytes 524320 | tf_op jit(solution)/shard_map/ppermute | solution.py:519
  98.6 5.3 %all-to-all-start.4 = ((bf16[8,4,128,128]{3,2,1,0:T(8,128)(2,1)}), bf16[8,4,128,128]{3,2,1,0:T(8,128)(2,1)S(1)}, u32[]{:S(2)}, u32[]{:S(2)}) async-start(bf16[8,4,128,128]{3,2,1,0:T(8,128)(2,1)} %shard_map.117), calls=%async_computation.4 | async-start | bytes 2097152 | tf_op jit(solution)/shard_map/all_to_all | solution.py:394
  105.8 3.0 %shard_map.118 = (bf16[128,1024]{1,0:T(8,128)(2,1)}, bf16[128,1024]{1,0:T(8,128)(2,1)}) custom-call(s32[1]{0:T(128)} %bitcast.1.refs_0_, bf16[8,2,128,128]{3,2,1,0:T(8,128)(2,1)S(1)} %all-to-all-done.1.refs_5_.refs_1_, bf16[8,2,128,128]{3,2,1,0:T(8,128)(2,1)S(1)} %collective-permute-done.13.refs_6_.refs_2_, bf16[128,1024]{1,0:T(8,128)(2,1)S(1)} %copy-done.2, ...), custom_call_target="tpu_custom_call" | custom-call | flops 536870912 | bytes 2000000 | tf_op jit(solution)/shard_map/pallas_call | solution.py:112
  108.8 2.9 %collective-permute-start.14 = (bf16[128,1024]{1,0:T(8,128)(2,1)}, bf16[128,1024]{1,0:T(8,128)(2,1)S(1)}, u32[]{:S(2)}, u32[]{:S(2)}) collective-permute-start(bf16[128,1024]{1,0:T(8,128)(2,1)} %get-tuple-element.62), channel_id=1, source_target_pairs={{0,8},{8,0},{16,24},{24,16},{32,40},{40,32},{48,56},{56,48},{64,72... | collective-permute-start | bytes 786440 | tf_op jit(solution)/shard_map/ppermute | solution.py:543
  115.9 5.1 %collective-permute-start.15 = (bf16[8,128,128]{2,1,0:T(8,128)(2,1)S(1)}, bf16[8,128,128]{2,1,0:T(8,128)(2,1)S(1)}, u32[]{:S(2)}, u32[]{:S(2)}) collective-permute-start(bf16[8,128,128]{2,1,0:T(8,128)(2,1)S(1)} %slice_bitcast_fusion.refs_1_), channel_id=1, source_target_pairs={{0,8},{8,0},{16,24},{24,16},{32,40},{40,32},{48,56},{56,48},{64,72... | collective-permute-start | bytes 786440 | tf_op jit(solution)/shard_map/ppermute | solution.py:551
  (68 shorter events, 23.2 us)
Async XLA Ops:
  3.6 13.6 %copy-start.13 = (bf16[128,1024]{1,0:T(8,128)(2,1)S(1)}, bf16[128,1024]{1,0:T(8,128)(2,1)}, u32[]{:S(2)}) copy-start(bf16[128,1024]{1,0:T(8,128)(2,1)} %get-tuple-element.39) | copy-start | bytes 786436
  3.6 26.1 %copy-start.15 = (bf16[128,512]{1,0:T(8,128)(2,1)S(1)}, bf16[128,512]{1,0:T(8,128)(2,1)}, u32[]{:S(2)}) copy-start(bf16[128,512]{1,0:T(8,128)(2,1)} %get-tuple-element.41) | copy-start | bytes 393220
  3.6 31.7 %all-to-all-start = ((bf16[8,3,128,128]{3,2,1,0:T(8,128)(2,1)}), bf16[8,3,128,128]{3,2,1,0:T(8,128)(2,1)S(1)}, u32[]{:S(2)}, u32[]{:S(2)}) async-start(bf16[8,3,128,128]{3,2,1,0:T(8,128)(2,1)} %get-tuple-element.36), calls=%async_computation | async-start | bytes 1572864 | tf_op jit(solution)/shard_map/all_to_all | solution.py:394
  11.2 14.6 %collective-permute-start.2 = (bf16[128,1024]{1,0:T(8,128)(2,1)S(1)}, bf16[128,1024]{1,0:T(8,128)(2,1)S(1)}, u32[]{:S(2)}, u32[]{:S(2)}) collective-permute-start(bf16[128,1024]{1,0:T(8,128)(2,1)S(1)} %copy-done.2), channel_id=1, source_target_pairs={{0,4},{1,5},{2,6},{3,7},{4,0},{5,1},{6,2},{7,3},{8,12},{9,13},{10,... | collective-permute-start | bytes 786440 | tf_op jit(solution)/shard_map/ppermute | solution.py:439
  13.3 19.6 %collective-permute-start.1 = (bf16[128,1024]{1,0:T(8,128)(2,1)S(1)}, bf16[128,1024]{1,0:T(8,128)(2,1)S(1)}, u32[]{:S(2)}, u32[]{:S(2)}) collective-permute-start(bf16[128,1024]{1,0:T(8,128)(2,1)S(1)} %copy-done.2), channel_id=1, source_target_pairs={{0,3},{1,2},{2,1},{3,0},{4,7},{5,6},{6,5},{7,4},{8,11},{9,10},{10,... | collective-permute-start | bytes 786440 | tf_op jit(solution)/shard_map/ppermute | solution.py:439
  17.1 15.8 %collective-permute-start = (bf16[128,1024]{1,0:T(8,128)(2,1)S(1)}, bf16[128,1024]{1,0:T(8,128)(2,1)S(1)}, u32[]{:S(2)}, u32[]{:S(2)}) collective-permute-start(bf16[128,1024]{1,0:T(8,128)(2,1)S(1)} %copy-done.2), channel_id=1, source_target_pairs={{0,1},{1,0},{2,3},{3,2},{4,5},{5,4},{6,7},{7,6},{8,9},{9,8},{10,11... | collective-permute-start | bytes 786440 | tf_op jit(solution)/shard_map/ppermute | solution.py:439
  17.1 15.8 %collective-permute-start.4 = (bf16[128,1024]{1,0:T(8,128)(2,1)S(1)}, bf16[128,1024]{1,0:T(8,128)(2,1)S(1)}, u32[]{:S(2)}, u32[]{:S(2)}) collective-permute-start(bf16[128,1024]{1,0:T(8,128)(2,1)S(1)} %copy-done.13), channel_id=1, source_target_pairs={{0,8},{8,0},{16,24},{24,16},{32,40},{40,32},{48,56},{56,48},{64,72... | collective-permute-start | bytes 786440 | tf_op jit(solution)/shard_map/ppermute | solution.py:445
  25.9 9.4 %collective-permute-start.3 = (bf16[128,1024]{1,0:T(8,128)(2,1)S(1)}, bf16[128,1024]{1,0:T(8,128)(2,1)S(1)}, u32[]{:S(2)}, u32[]{:S(2)}) collective-permute-start(bf16[128,1024]{1,0:T(8,128)(2,1)S(1)} %collective-permute-done.2.refs_7_), channel_id=1, source_target_pairs={{0,3},{1,2},{2,1},{3,0},{4,7},{5,6},{6,5},{7,4},{8,11},{9,10},{10,... | collective-permute-start | bytes 786440 | tf_op jit(solution)/shard_map/ppermute | solution.py:439
  29.6 5.6 %collective-permute-start.5 = (bf16[128,512]{1,0:T(8,128)(2,1)S(1)}, bf16[128,512]{1,0:T(8,128)(2,1)S(1)}, u32[]{:S(2)}, u32[]{:S(2)}) collective-permute-start(bf16[128,512]{1,0:T(8,128)(2,1)S(1)} %copy-done.15), channel_id=1, source_target_pairs={{0,64},{8,72},{16,80},{24,88},{32,96},{40,104},{48,112},{56,120},{... | collective-permute-start | bytes 393224 | tf_op jit(solution)/shard_map/ppermute | solution.py:446
  35.3 5.8 %collective-permute-start.6 = (bf16[8,3,128,128]{3,2,1,0:T(8,128)(2,1)S(1)}, bf16[8,3,128,128]{3,2,1,0:T(8,128)(2,1)S(1)}, u32[]{:S(2)}, u32[]{:S(2)}) collective-permute-start(bf16[8,3,128,128]{3,2,1,0:T(8,128)(2,1)S(1)} %all-to-all-done.refs_1_.refs_2_.refs_3_), channel_id=1, source_target_pairs={{0,8},{8,0},{16,24},{24,16},{32,40},{40,32},{48,56},{56,48},{64,72... | collective-permute-start | bytes 2359304 | tf_op jit(solution)/shard_map/ppermute | solution.py:452
  38.3 13.9 %collective-permute-start.7 = (bf16[128,1024]{1,0:T(8,128)(2,1)S(1)}, bf16[128,1024]{1,0:T(8,128)(2,1)S(1)}, u32[]{:S(2)}, u32[]{:S(2)}) collective-permute-start(bf16[128,1024]{1,0:T(8,128)(2,1)S(1)} %collective-permute-done.refs_4_), channel_id=1, source_target_pairs={{0,3},{1,2},{2,1},{3,0},{4,7},{5,6},{6,5},{7,4},{8,11},{9,10},{10,... | collective-permute-start | bytes 786440 | tf_op jit(solution)/shard_map/ppermute | solution.py:439
  39.6 12.7 %collective-permute-start.9 = (bf16[128,1024]{1,0:T(8,128)(2,1)S(1)}, bf16[128,1024]{1,0:T(8,128)(2,1)S(1)}, u32[]{:S(2)}, u32[]{:S(2)}) collective-permute-start(bf16[128,1024]{1,0:T(8,128)(2,1)S(1)} %collective-permute-done.3.refs_10_), channel_id=1, source_target_pairs={{0,1},{1,0},{2,3},{3,2},{4,5},{5,4},{6,7},{7,6},{8,9},{9,8},{10,11... | collective-permute-start | bytes 786440 | tf_op jit(solution)/shard_map/ppermute | solution.py:439
  39.6 13.3 %collective-permute-start.8 = (bf16[128,1024]{1,0:T(8,128)(2,1)S(1)}, bf16[128,1024]{1,0:T(8,128)(2,1)}, u32[]{:S(2)}, u32[]{:S(2)}) collective-permute-start(bf16[128,1024]{1,0:T(8,128)(2,1)S(1)} %collective-permute-done.2.refs_7_), channel_id=1, source_target_pairs={{0,1},{1,0},{2,3},{3,2},{4,5},{5,4},{6,7},{7,6},{8,9},{9,8},{10,11... | collective-permute-start | bytes 786440 | tf_op jit(solution)/shard_map/ppermute | solution.py:439
  45.1 19.6 %all-to-all-start.1 = ((bf16[8,2,128,128]{3,2,1,0:T(8,128)(2,1)}), bf16[8,2,128,128]{3,2,1,0:T(8,128)(2,1)S(1)}, u32[]{:S(2)}, u32[]{:S(2)}) async-start(bf16[8,2,128,128]{3,2,1,0:T(8,128)(2,1)} %get-tuple-element.43.refs_5_), calls=%async_computation.1 | async-start | bytes 1048576 | tf_op jit(solution)/shard_map/all_to_all | solution.py:394
  55.7 15.0 %copy-start.10 = (bf16[128,512]{1,0:T(8,128)(2,1)S(1)}, bf16[128,512]{1,0:T(8,128)(2,1)}, u32[]{:S(2)}) copy-start(bf16[128,512]{1,0:T(8,128)(2,1)} %copy-done.9) | copy-start | bytes 393220
  55.7 4.4 %collective-permute-start.10 = (bf16[8,128,128]{2,1,0:T(8,128)(2,1)S(1)}, bf16[8,128,128]{2,1,0:T(8,128)(2,1)S(1)}, u32[]{:S(2)}, u32[]{:S(2)}) collective-permute-start(bf16[8,128,128]{2,1,0:T(8,128)(2,1)S(1)} %get-tuple-element.47), channel_id=1, source_target_pairs={{0,8},{8,0},{16,24},{24,16},{32,40},{40,32},{48,56},{56,48},{64,72... | collective-permute-start | bytes 786440 | tf_op jit(solution)/shard_map/ppermute | solution.py:479
  56.9 7.9 %collective-permute-start.11 = (bf16[128,512]{1,0:T(8,128)(2,1)S(1)}, bf16[128,512]{1,0:T(8,128)(2,1)S(1)}, u32[]{:S(2)}, u32[]{:S(2)}) collective-permute-start(bf16[128,512]{1,0:T(8,128)(2,1)S(1)} %copy-done.14), channel_id=1, source_target_pairs={{0,72},{8,64},{16,88},{24,80},{32,104},{40,96},{48,120},{56,112},{... | collective-permute-start | bytes 393224 | tf_op jit(solution)/shard_map/ppermute | solution.py:472
  64.8 5.9 %collective-permute-start.13 = (bf16[8,2,128,128]{3,2,1,0:T(8,128)(2,1)S(1)}, bf16[8,2,128,128]{3,2,1,0:T(8,128)(2,1)S(1)}, u32[]{:S(2)}, u32[]{:S(2)}) collective-permute-start(bf16[8,2,128,128]{3,2,1,0:T(8,128)(2,1)S(1)} %all-to-all-done.1.refs_5_.refs_1_), channel_id=1, source_target_pairs={{0,8},{8,0},{16,24},{24,16},{32,40},{40,32},{48,56},{56,48},{64,72... | collective-permute-start | bytes 1572872 | tf_op jit(solution)/shard_map/ppermute | solution.py:486
  64.8 13.5 %all-to-all-start.2 = ((bf16[8,128,128]{2,1,0:T(8,128)(2,1)}), bf16[8,128,128]{2,1,0:T(8,128)(2,1)S(1)}, u32[]{:S(2)}, u32[]{:S(2)}) async-start(bf16[8,128,128]{2,1,0:T(8,128)(2,1)} %shard_map.113), calls=%async_computation.2 | async-start | bytes 524288 | tf_op jit(solution)/shard_map/all_to_all | solution.py:394
  78.9 18.4 %all-to-all-start.3 = ((bf16[32,32,512]{2,1,0:T(8,128)(2,1)}), bf16[32,32,512]{2,1,0:T(8,128)(2,1)S(1)}, u32[]{:S(2)}, u32[]{:S(2)}) async-start(bf16[32,32,512]{2,1,0:T(8,128)(2,1)} %shard_map.116), calls=%async_computation.3 | async-start | bytes 2097152 | tf_op jit(solution)/shard_map/all_to_all | solution.py:497
  89.9 3.8 %collective-permute-start.12 = (bf16[8,2,128,128]{3,2,1,0:T(8,128)(2,1)}, bf16[8,2,128,128]{3,2,1,0:T(8,128)(2,1)S(1)}, u32[]{:S(2)}, u32[]{:S(2)}) collective-permute-start(bf16[8,2,128,128]{3,2,1,0:T(8,128)(2,1)} %get-tuple-element.58), channel_id=1, source_target_pairs={{0,8},{8,0},{16,24},{24,16},{32,40},{40,32},{48,56},{56,48},{64,72... | collective-permute-start | bytes 1572872 | tf_op jit(solution)/shard_map/ppermute | solution.py:519
  98.6 17.3 %all-to-all-start.4 = ((bf16[8,4,128,128]{3,2,1,0:T(8,128)(2,1)}), bf16[8,4,128,128]{3,2,1,0:T(8,128)(2,1)S(1)}, u32[]{:S(2)}, u32[]{:S(2)}) async-start(bf16[8,4,128,128]{3,2,1,0:T(8,128)(2,1)} %shard_map.117), calls=%async_computation.4 | async-start | bytes 2097152 | tf_op jit(solution)/shard_map/all_to_all | solution.py:394
  108.8 4.3 %collective-permute-start.14 = (bf16[128,1024]{1,0:T(8,128)(2,1)}, bf16[128,1024]{1,0:T(8,128)(2,1)S(1)}, u32[]{:S(2)}, u32[]{:S(2)}) collective-permute-start(bf16[128,1024]{1,0:T(8,128)(2,1)} %get-tuple-element.62), channel_id=1, source_target_pairs={{0,8},{8,0},{16,24},{24,16},{32,40},{40,32},{48,56},{56,48},{64,72... | collective-permute-start | bytes 786440 | tf_op jit(solution)/shard_map/ppermute | solution.py:543
  115.9 6.4 %collective-permute-start.15 = (bf16[8,128,128]{2,1,0:T(8,128)(2,1)S(1)}, bf16[8,128,128]{2,1,0:T(8,128)(2,1)S(1)}, u32[]{:S(2)}, u32[]{:S(2)}) collective-permute-start(bf16[8,128,128]{2,1,0:T(8,128)(2,1)S(1)} %slice_bitcast_fusion.refs_1_), channel_id=1, source_target_pairs={{0,8},{8,0},{16,24},{24,16},{32,40},{40,32},{48,56},{56,48},{64,72... | collective-permute-start | bytes 786440 | tf_op jit(solution)/shard_map/ppermute | solution.py:551
  (13 other events, 49.9 us)

commit v10 on v8

--- a/solution.py
+++ b/solution.py
@@ -25,7 +25,6 @@
 
 CORE_SWAP = [(i, i ^ 1) for i in range(16)]
 PAIR_SWAP = [(i, i ^ 8) for i in range(16)]
-DIAG_SWAP = [(i, i ^ 9) for i in range(16)]
 SAME_CORE = [[2 * j + c for j in range(CHIPS)] for c in range(2)]
 REDUCE = [
     [(8 * h + 2 * y + c) * 8 + f for f in range(8) for y in range(4)]
@@ -128,11 +127,10 @@
 
 
 def pack_kernel(ins, outs, scratch, sems):
-    core_ref, high_ref, *data = ins
-    out_ref, half_ref, up_mine_ref, up_send_ref, pair_ref, diag_ref = outs
-    core, high = core_ref[0], high_ref[0]
+    core_ref, *data = ins
+    out_ref, half_ref, up_mine_ref, up_send_ref = outs
+    core = core_ref[0]
     half = half_ref.shape[1]
-    quarter = half // 2
     copies = []
 
     def copy(src, dst):
@@ -149,9 +147,20 @@
     up_ref = data[4].get()
     copy(up_ref.at[:, mine], up_mine_ref)
     copy(up_ref.at[:, other], up_send_ref)
-    for ref, c in ((pair_ref, core), (diag_ref, 1 - core)):
-        at = pl.multiple_of(c * half + (1 - high) * quarter, quarter)
-        copy(up_ref.at[:, pl.ds(at, quarter)], ref)
+    return copies
+
+
+def quarter_kernel(ins, outs, scratch, sems):
+    high_ref, mine_in, other_in = ins
+    out = outs[0]
+    quarter = out.shape[1]
+    at = pl.ds(pl.multiple_of((1 - high_ref[0]) * quarter, quarter), quarter)
+    copies = []
+    for n, one in enumerate((mine_in, other_in)):
+        copies.append(
+            pltpu.make_async_copy(one.get().at[:, at], out.at[pl.ds(n * BLOCK, BLOCK)], next(sems))
+        )
+        copies[-1].start()
     return copies
 
 
@@ -316,11 +325,11 @@
 def weight_kernel(ins, outs, scratch, sems):
     out = outs[0]
     high_ref = ins[0]
-    mine, other, pair, diag, ctx_ref, ctx_other_ref = [one.get() for one in ins[1:]]
+    mine, other, pair, ctx_ref, ctx_other_ref = [one.get() for one in ins[1:]]
     quarter = pair.shape[1]
     at = pl.ds(pl.multiple_of(high_ref[0] * quarter, quarter), quarter)
-    up = jnp.concatenate([mine[:, at], pair[...]], axis=0)
-    up_other = jnp.concatenate([other[:, at], diag[...]], axis=0)
+    up = jnp.concatenate([mine[:, at], pair[:BLOCK]], axis=0)
+    up_other = jnp.concatenate([other[:, at], pair[BLOCK:]], axis=0)
     for a in range(HEADS):
         total = dot_tn(ctx_ref[a].reshape(TILE, HS), up)
         total = total + dot_tn(ctx_other_ref[a].reshape(TILE, HS), up_other)
@@ -412,14 +421,13 @@
     quarter = half // 2
 
     side = ("R", (BLOCK, half), BF16)
-    part = ("R", (BLOCK, quarter), BF16)
-    packed, own_half, up_mine, up_send, up_pair, up_diag = call(
+    packed, own_half, up_mine, up_send = call(
         pack_kernel,
         [
-            ("S", core_ref), ("S", high_ref), ("H", query_rows, 0), ("H", key_rows, 0),
+            ("S", core_ref), ("H", query_rows, 0), ("H", key_rows, 0),
             ("H", value_rows, 0), ("H", out_weight), ("H", upstream, 0),
         ],
-        [("R", (HEADS, 3, BLOCK, HS), BF16), ("R", (HS, half), BF16), side, side, part, part],
+        [("R", (HEADS, 3, BLOCK, HS), BF16), side, side, side],
     )
     own = exchange(packed)
 
@@ -444,11 +452,15 @@
     two, over_two = step(one, 3), step(over_three, 1)
     pieces = [own_half, one, two, three, over, over_one, over_two, over_three]
     up_other = lax.ppermute(up_send, "ctx", CORE_SWAP)
-    up_pair = lax.ppermute(after(up_pair, over, one), "ctx", PAIR_SWAP)
-    up_diag = lax.ppermute(after(up_diag, over, one), "ctx", DIAG_SWAP)
+    up_pair = call(
+        quarter_kernel,
+        [("S", high_ref), ("A", up_mine), ("A", up_other)],
+        [("R", (2 * BLOCK, quarter), BF16)],
+    )
+    up_pair = lax.ppermute(after(up_pair, over), "ctx", PAIR_SWAP)
 
     own = after(
-        own, end, valid, valid_here, one, three, over_one, over_three, up_other, up_pair, up_diag
+        own, end, valid, valid_here, one, three, over_one, over_three, up_other, up_pair
     )
     other = lax.ppermute(own, "ctx", CORE_SWAP)
     pairs = 4 * TILE * SPAN * 5 // 2
@@ -487,7 +499,7 @@
     terms = call(
         weight_kernel,
         [
-            ("S", high_ref), ("A", up_mine), ("A", up_other), ("A", up_pair), ("A", up_diag),
+            ("S", high_ref), ("A", up_mine), ("A", up_other), ("A", up_pair),
             ("A", context_mine), ("A", context_other),
         ],
         [("H", (32, 32, quarter), BF16)],

time: 116 us -> 117 us (level)
  starting transfers between devices: 48.8 us -> 51 us
  waiting for transfers between devices: 27.7 us -> 26 us
    ppermute x2 -> x1, waiting for transfers between devices: 9.4 us -> 6.89 us  [shards(): up_pair = lax.ppermute(after(up_pair, over), 'ctx', PAIR_SWAP)]
    ppermute x1, starting transfers between devices: 0.09 us -> 2.52 us  [shards(): other = lax.ppermute(own, 'ctx', CORE_SWAP)]
    pallas_call x12 -> x13, Pallas kernels: 29.6 us -> 30.5 us  [call(): pl.pallas_call(body, out_shape=[SPACES[o[0]](o[1], o[2]) if o[0] in 'HR'...]
    ppermute x2 -> x1, starting transfers between devices: 3.54 us -> 3.24 us  [shards(): up_pair = lax.ppermute(after(up_pair, over), 'ctx', PAIR_SWAP)]
    unnamed x36 -> x28, local copies, waits for them, and re-layouts: 5.78 us -> 5.51 us
  transfers between devices with their start and end apart: 21 -> 20, of which waited for: 10 -> 9; matrix products, arithmetic and copies ran while one was open for 1% -> 1% of each run, Pallas kernels for 21% -> 22%
where the time goes in v10:
time: 117 us; the launch traced here: 116 us
  starting transfers between devices  51 us (44%)
  Pallas kernels  30.5 us (26%)
  waiting for transfers between devices  26 us (22%)
  local copies, waits for them, and re-layouts  5.54 us (5%)
  between operations  1.8 us (2%)
    pallas_call x13, Pallas kernels, call(): pl.pallas_call(body, out_shape=[SPACES[o[0]](o[1], o[2]) if o[0] in 'HR'...  30.5 us
    all_to_all x4, starting transfers between devices, exchange(): lax.all_to_all(operand, 'ctx', split_axis=0, concat_axis=0, tiled=True, a...  19.6 us
    all_to_all x4, waiting for transfers between devices, exchange(): lax.all_to_all(operand, 'ctx', split_axis=0, concat_axis=0, tiled=True, a...  13.1 us
    ppermute x7, starting transfers between devices, step(): return lax.ppermute(value, 'fsdp', [(i, i ^ s) for i in range(8)])  9.09 us
    ppermute x1, waiting for transfers between devices, shards(): up_pair = lax.ppermute(after(up_pair, over), 'ctx', PAIR_SWAP)  6.89 us
    unnamed x28, local copies, waits for them, and re-layouts  5.51 us
    all_to_all x1, starting transfers between devices, shards(): lax.all_to_all(after(terms, grads), ('ctx', 'fsdp'), split_axis=0, concat...  5.03 us
    ppermute x1, starting transfers between devices, shards(): weight_other = lax.ppermute(weight_mine, 'ctx', CORE_SWAP)  3.8 us
  transfers between devices with their start and end apart: 20, of which 9 were waited for; matrix products, arithmetic and copies ran while one was open for 1% of the time, Pallas kernels for 22%

profile of v10, /device:TPU:1, one launch (start us, length us, event | category | flops | bytes accessed | tf_op | source)
XLA Modules:
  0.0 115.9 jit_solution(17755624901338830740)
XLA Ops:
  0.6 2.8 %shard_map.110 = (bf16[8,3,128,128]{3,2,1,0:T(8,128)(2,1)}, bf16[128,1024]{1,0:T(8,128)(2,1)}, bf16[128,1024]{1,0:T(8,128)(2,1)}, bf16[128,1024]{1,0:T(8,128)(2,1)}) custom-call(s32[1]{0:T(128)} %bitcast.refs_0_, bf16[1,128,1024]{2,1,0:T(8,128)(2,1)} %refs_1_.1, bf16[1,128,1024]{2,1,0:T(8,128)(2,1)} %refs_2_.1, bf16[1,128,1024]{2,1,0:T(8,128)(2,1)} %refs_3_.1, ...), custom_call_target="tpu_custom_call" | custom-call | bytes 2000000 | tf_op jit(solution)/shard_map/pallas_call | solution.py:111
  3.5 2.1 %collective-permute-start.2 = (bf16[128,1024]{1,0:T(8,128)(2,1)}, bf16[128,1024]{1,0:T(8,128)(2,1)S(1)}, u32[]{:S(2)}, u32[]{:S(2)}) collective-permute-start(bf16[128,1024]{1,0:T(8,128)(2,1)} %get-tuple-element.32.refs_3_), channel_id=1, source_target_pairs={{0,4},{1,5},{2,6},{3,7},{4,0},{5,1},{6,2},{7,3},{8,12},{9,13},{10,... | collective-permute-start | bytes 786440 | tf_op jit(solution)/shard_map/ppermute | solution.py:447
  5.6 3.8 %collective-permute-start.1 = (bf16[128,1024]{1,0:T(8,128)(2,1)}, bf16[128,1024]{1,0:T(8,128)(2,1)S(1)}, u32[]{:S(2)}, u32[]{:S(2)}) collective-permute-start(bf16[128,1024]{1,0:T(8,128)(2,1)} %get-tuple-element.32.refs_3_), channel_id=1, source_target_pairs={{0,3},{1,2},{2,1},{3,0},{4,7},{5,6},{6,5},{7,4},{8,11},{9,10},{10,... | collective-permute-start | bytes 786440 | tf_op jit(solution)/shard_map/ppermute | solution.py:447
  9.4 6.4 %all-to-all-start = ((bf16[8,3,128,128]{3,2,1,0:T(8,128)(2,1)}), bf16[8,3,128,128]{3,2,1,0:T(8,128)(2,1)S(1)}, u32[]{:S(2)}, u32[]{:S(2)}) async-start(bf16[8,3,128,128]{3,2,1,0:T(8,128)(2,1)} %get-tuple-element.31), calls=%async_computation | async-start | bytes 1572864 | tf_op jit(solution)/shard_map/all_to_all | solution.py:403
  15.8 1.6 %collective-permute-start.5 = (bf16[128,1024]{1,0:T(8,128)(2,1)S(1)}, bf16[128,1024]{1,0:T(8,128)(2,1)S(1)}, u32[]{:S(2)}, u32[]{:S(2)}) collective-permute-start(bf16[128,1024]{1,0:T(8,128)(2,1)S(1)} %copy-done.13), channel_id=1, source_target_pairs={{0,8},{8,0},{16,24},{24,16},{32,40},{40,32},{48,56},{56,48},{64,72... | collective-permute-start | bytes 786440 | tf_op jit(solution)/shard_map/ppermute | solution.py:454
  20.3 3.2 %collective-permute-start.6 = (bf16[256,512]{1,0:T(8,128)(2,1)}, bf16[256,512]{1,0:T(8,128)(2,1)S(1)}, u32[]{:S(2)}, u32[]{:S(2)}) collective-permute-start(bf16[256,512]{1,0:T(8,128)(2,1)} %shard_map.111), channel_id=1, source_target_pairs={{0,64},{8,72},{16,80},{24,88},{32,96},{40,104},{48,112},{56,120},{... | collective-permute-start | bytes 786440 | tf_op jit(solution)/shard_map/ppermute | solution.py:460
  25.3 6.9 %collective-permute-done.6.refs_3_ = bf16[256,512]{1,0:T(8,128)(2,1)S(1)} collective-permute-done((bf16[256,512]{1,0:T(8,128)(2,1)}, bf16[256,512]{1,0:T(8,128)(2,1)S(1)}, u32[]{:S(2)}, u32[]{:S(2)}) %collective-permute-start.6) | collective-permute-done | bytes 262176 | tf_op jit(solution)/shard_map/ppermute | solution.py:460
  32.9 2.5 %collective-permute-start.7 = (bf16[8,3,128,128]{3,2,1,0:T(8,128)(2,1)S(1)}, bf16[8,3,128,128]{3,2,1,0:T(8,128)(2,1)S(1)}, u32[]{:S(2)}, u32[]{:S(2)}) collective-permute-start(bf16[8,3,128,128]{3,2,1,0:T(8,128)(2,1)S(1)} %all-to-all-done.refs_1_.refs_2_.refs_3_), channel_id=1, source_target_pairs={{0,8},{8,0},{16,24},{24,16},{32,40},{40,32},{48,56},{56,48},{64,72... | collective-permute-start | bytes 2359304 | tf_op jit(solution)/shard_map/ppermute | solution.py:465
  37.3 4.1 %shard_map.112 = (bf16[8,2,128,128]{3,2,1,0:T(8,128)(2,1)}, f32[4,1,256]{2,1,0:T(1,128)}, bf16[8,128,128]{2,1,0:T(8,128)(2,1)}, bf16[2048,128]{1,0:T(8,128)(2,1)}, bf16[2048,128]{1,0:T(8,128)(2,1)}) custom-call(s32[1]{0:T(128)} %bitcast.refs_0_, bf16[8,3,128,128]{3,2,1,0:T(8,128)(2,1)S(1)} %all-to-all-done.refs_1_.refs_2_.refs_3_, ...), custom_call_target="tpu_custom_call" | custom-call | flops 671088640 | bytes 2000000 | tf_op jit(solution)/shard_map/pallas_call | solution.py:111
  41.4 4.1 %all-to-all-start.1 = ((bf16[8,2,128,128]{3,2,1,0:T(8,128)(2,1)}), bf16[8,2,128,128]{3,2,1,0:T(8,128)(2,1)S(1)}, u32[]{:S(2)}, u32[]{:S(2)}) async-start(bf16[8,2,128,128]{3,2,1,0:T(8,128)(2,1)} %get-tuple-element.37.refs_5_), calls=%async_computation.1 | async-start | bytes 1048576 | tf_op jit(solution)/shard_map/all_to_all | solution.py:403
  45.6 2.8 %shard_map.113 = (f32[8,128,128]{2,1,0:T(8,128)S(1)}, bf16[8,128,128]{2,1,0:T(8,128)(2,1)S(1)}) custom-call(s32[1]{0:T(128)} %bitcast.1.refs_0_, bf16[128,1024]{1,0:T(8,128)(2,1)S(1)} %copy-done, bf16[128,1024]{1,0:T(8,128)(2,1)S(1)} %collective-permute-done.5.refs_2_, bf16[128,1024]{1,0:T(8,128)(2,1)S(1)} %copy-done.2, ...), custom_call_target="tpu_custom_call" | custom-call | flops 536870912 | bytes 2000000 | tf_op jit(solution)/shard_map/pallas_call | solution.py:111
  51.5 3.7 %all-to-all-done.1.refs_4_.refs_1_ = bf16[8,2,128,128]{3,2,1,0:T(8,128)(2,1)S(1)} async-done(((bf16[8,2,128,128]{3,2,1,0:T(8,128)(2,1)}), bf16[8,2,128,128]{3,2,1,0:T(8,128)(2,1)S(1)}, u32[]{:S(2)}, u32[]{:S(2)}) %all-to-all-start.1) | async-done | bytes 524320 | tf_op jit(solution)/shard_map/all_to_all | solution.py:403
  55.2 2.2 %collective-permute-start.12 = (bf16[8,2,128,128]{3,2,1,0:T(8,128)(2,1)S(1)}, bf16[8,2,128,128]{3,2,1,0:T(8,128)(2,1)S(1)}, u32[]{:S(2)}, u32[]{:S(2)}) collective-permute-start(bf16[8,2,128,128]{3,2,1,0:T(8,128)(2,1)S(1)} %all-to-all-done.1.refs_4_.refs_1_), channel_id=1, source_target_pairs={{0,8},{8,0},{16,24},{24,16},{32,40},{40,32},{48,56},{56,48},{64,72... | collective-permute-start | bytes 1572872 | tf_op jit(solution)/shard_map/ppermute | solution.py:498
  57.4 3.4 %all-to-all-start.2 = ((bf16[8,128,128]{2,1,0:T(8,128)(2,1)}), bf16[8,128,128]{2,1,0:T(8,128)(2,1)S(1)}, u32[]{:S(2)}, u32[]{:S(2)}) async-start(bf16[8,128,128]{2,1,0:T(8,128)(2,1)} %shard_map.114), calls=%async_computation.2 | async-start | bytes 524288 | tf_op jit(solution)/shard_map/all_to_all | solution.py:403
  60.8 2.0 %shard_map.117 = bf16[32,32,512]{2,1,0:T(8,128)(2,1)} custom-call(s32[1]{0:T(128)} %bitcast.8.refs_0_, bf16[128,1024]{1,0:T(8,128)(2,1)S(1)} %copy-done, bf16[128,1024]{1,0:T(8,128)(2,1)S(1)} %collective-permute-done.5.refs_2_, bf16[256,512]{1,0:T(8,128)(2,1)S(1)} %copy-done.8, bf16[8,2,128,128]{3,2,1,0:T(8,128)(2,1)S(1)} %all-to-all-done.1.refs_4_.refs_1_, ...), custom_call_target="tpu_custom_call" | custom-call | flops 536870912 | bytes 2000000 | tf_op jit(solution)/shard_map/pallas_call | solution.py:111
  62.8 6.1 %all-to-all-done.2.refs_3_ = bf16[8,128,128]{2,1,0:T(8,128)(2,1)S(1)} async-done(((bf16[8,128,128]{2,1,0:T(8,128)(2,1)}), bf16[8,128,128]{2,1,0:T(8,128)(2,1)S(1)}, u32[]{:S(2)}, u32[]{:S(2)}) %all-to-all-start.2) | async-done | bytes 262176 | tf_op jit(solution)/shard_map/all_to_all | solution.py:403
  69.6 5.0 %all-to-all-start.3 = ((bf16[32,32,512]{2,1,0:T(8,128)(2,1)}), bf16[32,32,512]{2,1,0:T(8,128)(2,1)S(1)}, u32[]{:S(2)}, u32[]{:S(2)}) async-start(bf16[32,32,512]{2,1,0:T(8,128)(2,1)} %shard_map.117), calls=%async_computation.3 | async-start | bytes 2097152 | tf_op jit(solution)/shard_map/all_to_all | solution.py:509
  74.7 6.8 %shard_map.115 = (bf16[8,128,128]{2,1,0:T(8,128)(2,1)}, f32[8,2,128,128]{3,2,1,0:T(8,128)}, bf16[8,2,128,128]{3,2,1,0:T(8,128)(2,1)}) custom-call(s32[1]{0:T(128)} %bitcast.refs_0_, bf16[8,128,128]{2,1,0:T(8,128)(2,1)} %get-tuple-element.41.refs_1_, bf16[2048,128]{1,0:T(8,128)(2,1)} %get-tuple-element.42.refs_2_, bf16[8,128,128]{2,1,0:T(8,128)(2,1)} %copy-done.11, ...), custom_call_target="tpu_custom_call" | custom-call | flops 1677721600 | bytes 2000000 | tf_op jit(solution)/shard_map/pallas_call | solution.py:111
  82.6 1.7 %collective-permute-done.11.refs_2_ = bf16[8,2,128,128]{3,2,1,0:T(8,128)(2,1)S(1)} collective-permute-done((bf16[8,2,128,128]{3,2,1,0:T(8,128)(2,1)}, bf16[8,2,128,128]{3,2,1,0:T(8,128)(2,1)S(1)}, u32[]{:S(2)}, u32[]{:S(2)}) %collective-permute-start.11) | collective-permute-done | bytes 524320 | tf_op jit(solution)/shard_map/ppermute | solution.py:531
  90.5 5.6 %all-to-all-start.4 = ((bf16[8,4,128,128]{3,2,1,0:T(8,128)(2,1)}), bf16[8,4,128,128]{3,2,1,0:T(8,128)(2,1)S(1)}, u32[]{:S(2)}, u32[]{:S(2)}) async-start(bf16[8,4,128,128]{3,2,1,0:T(8,128)(2,1)} %shard_map.118), calls=%async_computation.4 | async-start | bytes 2097152 | tf_op jit(solution)/shard_map/all_to_all | solution.py:403
  97.1 3.0 %shard_map.119 = (bf16[128,1024]{1,0:T(8,128)(2,1)}, bf16[128,1024]{1,0:T(8,128)(2,1)}) custom-call(s32[1]{0:T(128)} %bitcast.1.refs_0_, bf16[8,2,128,128]{3,2,1,0:T(8,128)(2,1)S(1)} %all-to-all-done.1.refs_4_.refs_1_, bf16[8,2,128,128]{3,2,1,0:T(8,128)(2,1)S(1)} %collective-permute-done.12.refs_5_.refs_2_, bf16[128,1024]{1,0:T(8,128)(2,1)S(1)} %copy-done.2, ...), custom_call_target="tpu_custom_call" | custom-call | flops 536870912 | bytes 2000000 | tf_op jit(solution)/shard_map/pallas_call | solution.py:111
  100.1 2.1 %collective-permute-start.13 = (bf16[128,1024]{1,0:T(8,128)(2,1)}, bf16[128,1024]{1,0:T(8,128)(2,1)S(1)}, u32[]{:S(2)}, u32[]{:S(2)}) collective-permute-start(bf16[128,1024]{1,0:T(8,128)(2,1)} %get-tuple-element.52), channel_id=1, source_target_pairs={{0,8},{8,0},{16,24},{24,16},{32,40},{40,32},{48,56},{56,48},{64,72... | collective-permute-start | bytes 786440 | tf_op jit(solution)/shard_map/ppermute | solution.py:555
  105.8 3.4 %all-to-all-done.4.refs_0_ = bf16[8,4,128,128]{3,2,1,0:T(8,128)(2,1)S(1)} async-done(((bf16[8,4,128,128]{3,2,1,0:T(8,128)(2,1)}), bf16[8,4,128,128]{3,2,1,0:T(8,128)(2,1)S(1)}, u32[]{:S(2)}, u32[]{:S(2)}) %all-to-all-start.4) | async-done | bytes 1048608 | tf_op jit(solution)/shard_map/all_to_all | solution.py:403
  109.2 3.8 %collective-permute-start.14 = (bf16[8,128,128]{2,1,0:T(8,128)(2,1)S(1)}, bf16[8,128,128]{2,1,0:T(8,128)(2,1)S(1)}, u32[]{:S(2)}, u32[]{:S(2)}) collective-permute-start(bf16[8,128,128]{2,1,0:T(8,128)(2,1)S(1)} %slice_bitcast_fusion.refs_1_), channel_id=1, source_target_pairs={{0,8},{8,0},{16,24},{24,16},{32,40},{40,32},{48,56},{56,48},{64,72... | collective-permute-start | bytes 786440 | tf_op jit(solution)/shard_map/ppermute | solution.py:563
  (63 shorter events, 24.9 us)
Async XLA Ops:
  3.5 14.5 %copy-start.12 = (s32[1,2048]{1,0:T(1,128)S(1)}, s32[1,2048]{1,0:T(1,128)}, u32[]{:S(2)}) copy-start(s32[1,2048]{1,0:T(1,128)} %param.10) | copy-start | bytes 24580
  3.5 15.6 %copy-start = (bf16[128,1024]{1,0:T(8,128)(2,1)S(1)}, bf16[128,1024]{1,0:T(8,128)(2,1)}, u32[]{:S(2)}) copy-start(bf16[128,1024]{1,0:T(8,128)(2,1)} %get-tuple-element.34.refs_1_) | copy-start | bytes 786436
  3.5 16.7 %collective-permute-start.2 = (bf16[128,1024]{1,0:T(8,128)(2,1)}, bf16[128,1024]{1,0:T(8,128)(2,1)S(1)}, u32[]{:S(2)}, u32[]{:S(2)}) collective-permute-start(bf16[128,1024]{1,0:T(8,128)(2,1)} %get-tuple-element.32.refs_3_), channel_id=1, source_target_pairs={{0,4},{1,5},{2,6},{3,7},{4,0},{5,1},{6,2},{7,3},{8,12},{9,13},{10,... | collective-permute-start | bytes 786440 | tf_op jit(solution)/shard_map/ppermute | solution.py:447
  5.6 19.6 %collective-permute-start.1 = (bf16[128,1024]{1,0:T(8,128)(2,1)}, bf16[128,1024]{1,0:T(8,128)(2,1)S(1)}, u32[]{:S(2)}, u32[]{:S(2)}) collective-permute-start(bf16[128,1024]{1,0:T(8,128)(2,1)} %get-tuple-element.32.refs_3_), channel_id=1, source_target_pairs={{0,3},{1,2},{2,1},{3,0},{4,7},{5,6},{6,5},{7,4},{8,11},{9,10},{10,... | collective-permute-start | bytes 786440 | tf_op jit(solution)/shard_map/ppermute | solution.py:447
  9.4 15.9 %collective-permute-start = (bf16[128,1024]{1,0:T(8,128)(2,1)}, bf16[128,1024]{1,0:T(8,128)(2,1)S(1)}, u32[]{:S(2)}, u32[]{:S(2)}) collective-permute-start(bf16[128,1024]{1,0:T(8,128)(2,1)} %get-tuple-element.32.refs_3_), channel_id=1, source_target_pairs={{0,1},{1,0},{2,3},{3,2},{4,5},{5,4},{6,7},{7,6},{8,9},{9,8},{10,11... | collective-permute-start | bytes 786440 | tf_op jit(solution)/shard_map/ppermute | solution.py:447
  9.4 23.5 %all-to-all-start = ((bf16[8,3,128,128]{3,2,1,0:T(8,128)(2,1)}), bf16[8,3,128,128]{3,2,1,0:T(8,128)(2,1)S(1)}, u32[]{:S(2)}, u32[]{:S(2)}) async-start(bf16[8,3,128,128]{3,2,1,0:T(8,128)(2,1)} %get-tuple-element.31), calls=%async_computation | async-start | bytes 1572864 | tf_op jit(solution)/shard_map/all_to_all | solution.py:403
  15.8 3.3 %collective-permute-start.5 = (bf16[128,1024]{1,0:T(8,128)(2,1)S(1)}, bf16[128,1024]{1,0:T(8,128)(2,1)S(1)}, u32[]{:S(2)}, u32[]{:S(2)}) collective-permute-start(bf16[128,1024]{1,0:T(8,128)(2,1)S(1)} %copy-done.13), channel_id=1, source_target_pairs={{0,8},{8,0},{16,24},{24,16},{32,40},{40,32},{48,56},{56,48},{64,72... | collective-permute-start | bytes 786440 | tf_op jit(solution)/shard_map/ppermute | solution.py:454
  20.3 11.9 %collective-permute-start.6 = (bf16[256,512]{1,0:T(8,128)(2,1)}, bf16[256,512]{1,0:T(8,128)(2,1)S(1)}, u32[]{:S(2)}, u32[]{:S(2)}) collective-permute-start(bf16[256,512]{1,0:T(8,128)(2,1)} %shard_map.111), channel_id=1, source_target_pairs={{0,64},{8,72},{16,80},{24,88},{32,96},{40,104},{48,112},{56,120},{... | collective-permute-start | bytes 786440 | tf_op jit(solution)/shard_map/ppermute | solution.py:460
  23.5 9.4 %collective-permute-start.4 = (bf16[128,1024]{1,0:T(8,128)(2,1)S(1)}, bf16[128,1024]{1,0:T(8,128)(2,1)S(1)}, u32[]{:S(2)}, u32[]{:S(2)}) collective-permute-start(bf16[128,1024]{1,0:T(8,128)(2,1)S(1)} %collective-permute-done.2.refs_7_), channel_id=1, source_target_pairs={{0,3},{1,2},{2,1},{3,0},{4,7},{5,6},{6,5},{7,4},{8,11},{9,10},{10,... | collective-permute-start | bytes 786440 | tf_op jit(solution)/shard_map/ppermute | solution.py:447
  23.7 9.1 %collective-permute-start.3 = (bf16[128,1024]{1,0:T(8,128)(2,1)S(1)}, bf16[128,1024]{1,0:T(8,128)(2,1)S(1)}, u32[]{:S(2)}, u32[]{:S(2)}) collective-permute-start(bf16[128,1024]{1,0:T(8,128)(2,1)S(1)} %collective-permute-done.2.refs_7_), channel_id=1, source_target_pairs={{0,1},{1,0},{2,3},{3,2},{4,5},{5,4},{6,7},{7,6},{8,9},{9,8},{10,11... | collective-permute-start | bytes 786440 | tf_op jit(solution)/shard_map/ppermute | solution.py:447
  32.9 12.7 %copy-start.3 = (bf16[128,1024]{1,0:T(8,128)(2,1)}, bf16[128,1024]{1,0:T(8,128)(2,1)S(1)}, u32[]{:S(2)}) copy-start(bf16[128,1024]{1,0:T(8,128)(2,1)S(1)} %collective-permute-done.4.refs_10_) | copy-start | bytes 786436
  32.9 12.7 %copy-start.5 = (bf16[128,1024]{1,0:T(8,128)(2,1)}, bf16[128,1024]{1,0:T(8,128)(2,1)S(1)}, u32[]{:S(2)}) copy-start(bf16[128,1024]{1,0:T(8,128)(2,1)S(1)} %collective-permute-done.3.refs_8_) | copy-start | bytes 786436
  32.9 4.4 %collective-permute-start.7 = (bf16[8,3,128,128]{3,2,1,0:T(8,128)(2,1)S(1)}, bf16[8,3,128,128]{3,2,1,0:T(8,128)(2,1)S(1)}, u32[]{:S(2)}, u32[]{:S(2)}) collective-permute-start(bf16[8,3,128,128]{3,2,1,0:T(8,128)(2,1)S(1)} %all-to-all-done.refs_1_.refs_2_.refs_3_), channel_id=1, source_target_pairs={{0,8},{8,0},{16,24},{24,16},{32,40},{40,32},{48,56},{56,48},{64,72... | collective-permute-start | bytes 2359304 | tf_op jit(solution)/shard_map/ppermute | solution.py:465
  35.4 10.1 %collective-permute-start.8 = (bf16[128,1024]{1,0:T(8,128)(2,1)S(1)}, bf16[128,1024]{1,0:T(8,128)(2,1)}, u32[]{:S(2)}, u32[]{:S(2)}) collective-permute-start(bf16[128,1024]{1,0:T(8,128)(2,1)S(1)} %collective-permute-done.refs_4_), channel_id=1, source_target_pairs={{0,3},{1,2},{2,1},{3,0},{4,7},{5,6},{6,5},{7,4},{8,11},{9,10},{10,... | collective-permute-start | bytes 786440 | tf_op jit(solution)/shard_map/ppermute | solution.py:447
  35.6 10.0 %collective-permute-start.9 = (bf16[128,1024]{1,0:T(8,128)(2,1)S(1)}, bf16[128,1024]{1,0:T(8,128)(2,1)}, u32[]{:S(2)}, u32[]{:S(2)}) collective-permute-start(bf16[128,1024]{1,0:T(8,128)(2,1)S(1)} %collective-permute-done.4.refs_10_), channel_id=1, source_target_pairs={{0,1},{1,0},{2,3},{3,2},{4,5},{5,4},{6,7},{7,6},{8,9},{9,8},{10,11... | collective-permute-start | bytes 786440 | tf_op jit(solution)/shard_map/ppermute | solution.py:447
  41.4 13.8 %all-to-all-start.1 = ((bf16[8,2,128,128]{3,2,1,0:T(8,128)(2,1)}), bf16[8,2,128,128]{3,2,1,0:T(8,128)(2,1)S(1)}, u32[]{:S(2)}, u32[]{:S(2)}) async-start(bf16[8,2,128,128]{3,2,1,0:T(8,128)(2,1)} %get-tuple-element.37.refs_5_), calls=%async_computation.1 | async-start | bytes 1048576 | tf_op jit(solution)/shard_map/all_to_all | solution.py:403
  48.4 1.9 %collective-permute-start.10 = (bf16[8,128,128]{2,1,0:T(8,128)(2,1)S(1)}, bf16[8,128,128]{2,1,0:T(8,128)(2,1)S(1)}, u32[]{:S(2)}, u32[]{:S(2)}) collective-permute-start(bf16[8,128,128]{2,1,0:T(8,128)(2,1)S(1)} %get-tuple-element.39), channel_id=1, source_target_pairs={{0,8},{8,0},{16,24},{24,16},{32,40},{40,32},{48,56},{56,48},{64,72... | collective-permute-start | bytes 786440 | tf_op jit(solution)/shard_map/ppermute | solution.py:491
  55.2 5.6 %collective-permute-start.12 = (bf16[8,2,128,128]{3,2,1,0:T(8,128)(2,1)S(1)}, bf16[8,2,128,128]{3,2,1,0:T(8,128)(2,1)S(1)}, u32[]{:S(2)}, u32[]{:S(2)}) collective-permute-start(bf16[8,2,128,128]{3,2,1,0:T(8,128)(2,1)S(1)} %all-to-all-done.1.refs_4_.refs_1_), channel_id=1, source_target_pairs={{0,8},{8,0},{16,24},{24,16},{32,40},{40,32},{48,56},{56,48},{64,72... | collective-permute-start | bytes 1572872 | tf_op jit(solution)/shard_map/ppermute | solution.py:498
  57.4 11.5 %all-to-all-start.2 = ((bf16[8,128,128]{2,1,0:T(8,128)(2,1)}), bf16[8,128,128]{2,1,0:T(8,128)(2,1)S(1)}, u32[]{:S(2)}, u32[]{:S(2)}) async-start(bf16[8,128,128]{2,1,0:T(8,128)(2,1)} %shard_map.114), calls=%async_computation.2 | async-start | bytes 524288 | tf_op jit(solution)/shard_map/all_to_all | solution.py:403
  69.6 19.5 %all-to-all-start.3 = ((bf16[32,32,512]{2,1,0:T(8,128)(2,1)}), bf16[32,32,512]{2,1,0:T(8,128)(2,1)S(1)}, u32[]{:S(2)}, u32[]{:S(2)}) async-start(bf16[32,32,512]{2,1,0:T(8,128)(2,1)} %shard_map.117), calls=%async_computation.3 | async-start | bytes 2097152 | tf_op jit(solution)/shard_map/all_to_all | solution.py:509
  81.4 2.9 %collective-permute-start.11 = (bf16[8,2,128,128]{3,2,1,0:T(8,128)(2,1)}, bf16[8,2,128,128]{3,2,1,0:T(8,128)(2,1)S(1)}, u32[]{:S(2)}, u32[]{:S(2)}) collective-permute-start(bf16[8,2,128,128]{3,2,1,0:T(8,128)(2,1)} %get-tuple-element.48), channel_id=1, source_target_pairs={{0,8},{8,0},{16,24},{24,16},{32,40},{40,32},{48,56},{56,48},{64,72... | collective-permute-start | bytes 1572872 | tf_op jit(solution)/shard_map/ppermute | solution.py:531
  90.5 18.7 %all-to-all-start.4 = ((bf16[8,4,128,128]{3,2,1,0:T(8,128)(2,1)}), bf16[8,4,128,128]{3,2,1,0:T(8,128)(2,1)S(1)}, u32[]{:S(2)}, u32[]{:S(2)}) async-start(bf16[8,4,128,128]{3,2,1,0:T(8,128)(2,1)} %shard_map.118), calls=%async_computation.4 | async-start | bytes 2097152 | tf_op jit(solution)/shard_map/all_to_all | solution.py:403
  100.1 3.5 %collective-permute-start.13 = (bf16[128,1024]{1,0:T(8,128)(2,1)}, bf16[128,1024]{1,0:T(8,128)(2,1)S(1)}, u32[]{:S(2)}, u32[]{:S(2)}) collective-permute-start(bf16[128,1024]{1,0:T(8,128)(2,1)} %get-tuple-element.52), channel_id=1, source_target_pairs={{0,8},{8,0},{16,24},{24,16},{32,40},{40,32},{48,56},{56,48},{64,72... | collective-permute-start | bytes 786440 | tf_op jit(solution)/shard_map/ppermute | solution.py:555
  109.2 5.1 %collective-permute-start.14 = (bf16[8,128,128]{2,1,0:T(8,128)(2,1)S(1)}, bf16[8,128,128]{2,1,0:T(8,128)(2,1)S(1)}, u32[]{:S(2)}, u32[]{:S(2)}) collective-permute-start(bf16[8,128,128]{2,1,0:T(8,128)(2,1)S(1)} %slice_bitcast_fusion.refs_1_), channel_id=1, source_target_pairs={{0,8},{8,0},{16,24},{24,16},{32,40},{40,32},{48,56},{56,48},{64,72... | collective-permute-start | bytes 786440 | tf_op jit(solution)/shard_map/ppermute | solution.py:563
  (10 other events, 40.1 us)

commit v11 on v10

--- a/solution.py
+++ b/solution.py
@@ -457,11 +457,12 @@
         [("S", high_ref), ("A", up_mine), ("A", up_other)],
         [("R", (2 * BLOCK, quarter), BF16)],
     )
-    up_pair = lax.ppermute(after(up_pair, over), "ctx", PAIR_SWAP)
 
     own = after(
         own, end, valid, valid_here, one, three, over_one, over_three, up_other, up_pair
     )
+    up_pair = lax.ppermute(after(up_pair, own), "ctx", PAIR_SWAP)
+    pieces[6] = after(pieces[6], up_pair)
     other = lax.ppermute(own, "ctx", CORE_SWAP)
     pairs = 4 * TILE * SPAN * 5 // 2
     rows = ("H", (LEN, HS), BF16)

time: 117 us -> 113 us (0.966)
  waiting for transfers between devices: 26 us -> 22.4 us
    ppermute x1, waiting for transfers between devices: 6.89 us -> 0.01 us  [shards(): up_pair = lax.ppermute(after(up_pair, own), 'ctx', PAIR_SWAP)]
    ppermute x7, waiting for transfers between devices: 0.02 us -> 6.08 us  [step(): return lax.ppermute(value, 'fsdp', [(i, i ^ s) for i in range(8)])]
    ppermute x7, starting transfers between devices: 9.09 us -> 11.4 us  [step(): return lax.ppermute(value, 'fsdp', [(i, i ^ s) for i in range(8)])]
    all_to_all x4, waiting for transfers between devices: 13.1 us -> 10.9 us  [exchange(): lax.all_to_all(operand, 'ctx', split_axis=0, concat_axis=0, tiled=True, a...]
    ppermute x1, starting transfers between devices: 3.24 us -> 1.11 us  [shards(): up_pair = lax.ppermute(after(up_pair, own), 'ctx', PAIR_SWAP)]
    ppermute x1, starting transfers between devices: 2.22 us -> 3.4 us  [shards(): context_other = lax.ppermute(context_mine, 'ctx', CORE_SWAP)]
    unnamed x28 -> x24, local copies, waits for them, and re-layouts: 5.51 us -> 4.81 us
  transfers between devices with their start and end apart: 20 -> 20, of which waited for: 9 -> 8; matrix products, arithmetic and copies ran while one was open for 1% -> 1% of each run, Pallas kernels for 22% -> 23%
where the time goes in v11:
time: 113 us; the launch traced here: 112 us
  starting transfers between devices  51.1 us (45%)
  Pallas kernels  31.3 us (28%)
  waiting for transfers between devices  22.4 us (20%)
  local copies, waits for them, and re-layouts  4.84 us (4%)
  between operations  1.78 us (2%)
    pallas_call x13, Pallas kernels, call(): pl.pallas_call(body, out_shape=[SPACES[o[0]](o[1], o[2]) if o[0] in 'HR'...  31.3 us
    all_to_all x4, starting transfers between devices, exchange(): lax.all_to_all(operand, 'ctx', split_axis=0, concat_axis=0, tiled=True, a...  19.3 us
    ppermute x7, starting transfers between devices, step(): return lax.ppermute(value, 'fsdp', [(i, i ^ s) for i in range(8)])  11.4 us
    all_to_all x4, waiting for transfers between devices, exchange(): lax.all_to_all(operand, 'ctx', split_axis=0, concat_axis=0, tiled=True, a...  10.9 us
    ppermute x7, waiting for transfers between devices, step(): return lax.ppermute(value, 'fsdp', [(i, i ^ s) for i in range(8)])  6.08 us
    unnamed x24, local copies, waits for them, and re-layouts  4.81 us
    all_to_all x1, starting transfers between devices, shards(): lax.all_to_all(after(terms, grads), ('ctx', 'fsdp'), split_axis=0, concat...  4.11 us
    ppermute x1, starting transfers between devices, shards(): weight_other = lax.ppermute(weight_mine, 'ctx', CORE_SWAP)  3.8 us
  transfers between devices with their start and end apart: 20, of which 8 were waited for; matrix products, arithmetic and copies ran while one was open for 1% of the time, Pallas kernels for 23%

profile of v11, /device:TPU:1, one launch (start us, length us, event | category | flops | bytes accessed | tf_op | source)
XLA Modules:
  0.0 112.5 jit_solution(5496683006898370540)
XLA Ops:
  0.6 2.8 %shard_map.110 = (bf16[8,3,128,128]{3,2,1,0:T(8,128)(2,1)}, bf16[128,1024]{1,0:T(8,128)(2,1)}, bf16[128,1024]{1,0:T(8,128)(2,1)}, bf16[128,1024]{1,0:T(8,128)(2,1)}) custom-call(s32[1]{0:T(128)} %bitcast.refs_0_, bf16[1,128,1024]{2,1,0:T(8,128)(2,1)} %refs_1_.1, bf16[1,128,1024]{2,1,0:T(8,128)(2,1)} %refs_2_.1, bf16[1,128,1024]{2,1,0:T(8,128)(2,1)} %refs_3_.1, ...), custom_call_target="tpu_custom_call" | custom-call | bytes 2000000 | tf_op jit(solution)/shard_map/pallas_call | solution.py:111
  3.5 2.1 %collective-permute-start.2 = (bf16[128,1024]{1,0:T(8,128)(2,1)}, bf16[128,1024]{1,0:T(8,128)(2,1)S(1)}, u32[]{:S(2)}, u32[]{:S(2)}) collective-permute-start(bf16[128,1024]{1,0:T(8,128)(2,1)} %get-tuple-element.33.refs_3_), channel_id=1, source_target_pairs={{0,4},{1,5},{2,6},{3,7},{4,0},{5,1},{6,2},{7,3},{8,12},{9,13},{10,... | collective-permute-start | bytes 786440 | tf_op jit(solution)/shard_map/ppermute | solution.py:447
  5.6 3.8 %collective-permute-start.1 = (bf16[128,1024]{1,0:T(8,128)(2,1)}, bf16[128,1024]{1,0:T(8,128)(2,1)S(1)}, u32[]{:S(2)}, u32[]{:S(2)}) collective-permute-start(bf16[128,1024]{1,0:T(8,128)(2,1)} %get-tuple-element.33.refs_3_), channel_id=1, source_target_pairs={{0,3},{1,2},{2,1},{3,0},{4,7},{5,6},{6,5},{7,4},{8,11},{9,10},{10,... | collective-permute-start | bytes 786440 | tf_op jit(solution)/shard_map/ppermute | solution.py:447
  9.4 6.4 %all-to-all-start = ((bf16[8,3,128,128]{3,2,1,0:T(8,128)(2,1)}), bf16[8,3,128,128]{3,2,1,0:T(8,128)(2,1)S(1)}, u32[]{:S(2)}, u32[]{:S(2)}) async-start(bf16[8,3,128,128]{3,2,1,0:T(8,128)(2,1)} %get-tuple-element.32), calls=%async_computation | async-start | bytes 1572864 | tf_op jit(solution)/shard_map/all_to_all | solution.py:403
  22.2 6.1 %collective-permute-done.4.refs_10_ = bf16[128,1024]{1,0:T(8,128)(2,1)S(1)} collective-permute-done((bf16[128,1024]{1,0:T(8,128)(2,1)S(1)}, bf16[128,1024]{1,0:T(8,128)(2,1)S(1)}, u32[]{:S(2)}, u32[]{:S(2)}) %collective-permute-start.4) | collective-permute-done | bytes 262176 | tf_op jit(solution)/shard_map/ppermute | solution.py:447
  28.3 1.9 %collective-permute-start.6 = (bf16[8,3,128,128]{3,2,1,0:T(8,128)(2,1)S(1)}, bf16[8,3,128,128]{3,2,1,0:T(8,128)(2,1)S(1)}, u32[]{:S(2)}, u32[]{:S(2)}) collective-permute-start(bf16[8,3,128,128]{3,2,1,0:T(8,128)(2,1)S(1)} %all-to-all-done.refs_1_.refs_2_.refs_3_), channel_id=1, source_target_pairs={{0,8},{8,0},{16,24},{24,16},{32,40},{40,32},{48,56},{56,48},{64,72... | collective-permute-start | bytes 2359304 | tf_op jit(solution)/shard_map/ppermute | solution.py:466
  30.2 1.6 %collective-permute-start.8 = (bf16[128,1024]{1,0:T(8,128)(2,1)S(1)}, bf16[128,1024]{1,0:T(8,128)(2,1)}, u32[]{:S(2)}, u32[]{:S(2)}) collective-permute-start(bf16[128,1024]{1,0:T(8,128)(2,1)S(1)} %collective-permute-done.4.refs_10_), channel_id=1, source_target_pairs={{0,1},{1,0},{2,3},{3,2},{4,5},{5,4},{6,7},{7,6},{8,9},{9,8},{10,11... | collective-permute-start | bytes 786440 | tf_op jit(solution)/shard_map/ppermute | solution.py:447
  32.9 2.0 %collective-permute-start.7 = (bf16[128,1024]{1,0:T(8,128)(2,1)S(1)}, bf16[128,1024]{1,0:T(8,128)(2,1)}, u32[]{:S(2)}, u32[]{:S(2)}) collective-permute-start(bf16[128,1024]{1,0:T(8,128)(2,1)S(1)} %collective-permute-done.refs_4_), channel_id=1, source_target_pairs={{0,3},{1,2},{2,1},{3,0},{4,7},{5,6},{6,5},{7,4},{8,11},{9,10},{10,... | collective-permute-start | bytes 786440 | tf_op jit(solution)/shard_map/ppermute | solution.py:447
  34.9 4.1 %shard_map.112 = (bf16[8,2,128,128]{3,2,1,0:T(8,128)(2,1)}, f32[4,1,256]{2,1,0:T(1,128)}, bf16[8,128,128]{2,1,0:T(8,128)(2,1)}, bf16[2048,128]{1,0:T(8,128)(2,1)}, bf16[2048,128]{1,0:T(8,128)(2,1)}) custom-call(s32[1]{0:T(128)} %bitcast.refs_0_, bf16[8,3,128,128]{3,2,1,0:T(8,128)(2,1)S(1)} %all-to-all-done.refs_1_.refs_2_.refs_3_, ...), custom_call_target="tpu_custom_call" | custom-call | flops 671088640 | bytes 2000000 | tf_op jit(solution)/shard_map/pallas_call | solution.py:111
  38.9 4.1 %all-to-all-start.1 = ((bf16[8,2,128,128]{3,2,1,0:T(8,128)(2,1)}), bf16[8,2,128,128]{3,2,1,0:T(8,128)(2,1)S(1)}, u32[]{:S(2)}, u32[]{:S(2)}) async-start(bf16[8,2,128,128]{3,2,1,0:T(8,128)(2,1)} %get-tuple-element.37.refs_5_), calls=%async_computation.1 | async-start | bytes 1048576 | tf_op jit(solution)/shard_map/all_to_all | solution.py:403
  43.1 2.8 %shard_map.113 = (f32[8,128,128]{2,1,0:T(8,128)S(1)}, bf16[8,128,128]{2,1,0:T(8,128)(2,1)S(1)}) custom-call(s32[1]{0:T(128)} %bitcast.1.refs_0_, bf16[128,1024]{1,0:T(8,128)(2,1)S(1)} %copy-done, bf16[128,1024]{1,0:T(8,128)(2,1)S(1)} %collective-permute-done.5.refs_2_, bf16[128,1024]{1,0:T(8,128)(2,1)S(1)} %copy-done.2, ...), custom_call_target="tpu_custom_call" | custom-call | flops 536870912 | bytes 2000000 | tf_op jit(solution)/shard_map/pallas_call | solution.py:111
  49.5 2.2 %all-to-all-done.1.refs_4_.refs_1_ = bf16[8,2,128,128]{3,2,1,0:T(8,128)(2,1)S(1)} async-done(((bf16[8,2,128,128]{3,2,1,0:T(8,128)(2,1)}), bf16[8,2,128,128]{3,2,1,0:T(8,128)(2,1)S(1)}, u32[]{:S(2)}, u32[]{:S(2)}) %all-to-all-start.1) | async-done | bytes 524320 | tf_op jit(solution)/shard_map/all_to_all | solution.py:403
  51.8 3.4 %collective-permute-start.12 = (bf16[8,2,128,128]{3,2,1,0:T(8,128)(2,1)S(1)}, bf16[8,2,128,128]{3,2,1,0:T(8,128)(2,1)S(1)}, u32[]{:S(2)}, u32[]{:S(2)}) collective-permute-start(bf16[8,2,128,128]{3,2,1,0:T(8,128)(2,1)S(1)} %all-to-all-done.1.refs_4_.refs_1_), channel_id=1, source_target_pairs={{0,8},{8,0},{16,24},{24,16},{32,40},{40,32},{48,56},{56,48},{64,72... | collective-permute-start | bytes 1572872 | tf_op jit(solution)/shard_map/ppermute | solution.py:499
  55.2 3.4 %all-to-all-start.2 = ((bf16[8,128,128]{2,1,0:T(8,128)(2,1)}), bf16[8,128,128]{2,1,0:T(8,128)(2,1)S(1)}, u32[]{:S(2)}, u32[]{:S(2)}) async-start(bf16[8,128,128]{2,1,0:T(8,128)(2,1)} %shard_map.114), calls=%async_computation.2 | async-start | bytes 524288 | tf_op jit(solution)/shard_map/all_to_all | solution.py:403
  58.6 2.8 %shard_map.117 = bf16[32,32,512]{2,1,0:T(8,128)(2,1)} custom-call(s32[1]{0:T(128)} %bitcast.8.refs_0_, bf16[128,1024]{1,0:T(8,128)(2,1)S(1)} %copy-done, bf16[128,1024]{1,0:T(8,128)(2,1)S(1)} %collective-permute-done.5.refs_2_, bf16[256,512]{1,0:T(8,128)(2,1)} %collective-permute-done.9.refs_3_, bf16[8,2,128,128]{3,2,1,0:T(8,128)(2,1)S(1)} %all-to-all-done.1.refs_4_.refs_1_, ...), custom_call_target="tpu_custom_call" | custom-call | flops 536870912 | bytes 2000000 | tf_op jit(solution)/shard_map/pallas_call | solution.py:111
  61.4 5.4 %all-to-all-done.2.refs_3_ = bf16[8,128,128]{2,1,0:T(8,128)(2,1)S(1)} async-done(((bf16[8,128,128]{2,1,0:T(8,128)(2,1)}), bf16[8,128,128]{2,1,0:T(8,128)(2,1)S(1)}, u32[]{:S(2)}, u32[]{:S(2)}) %all-to-all-start.2) | async-done | bytes 262176 | tf_op jit(solution)/shard_map/all_to_all | solution.py:403
  67.5 4.1 %all-to-all-start.3 = ((bf16[32,32,512]{2,1,0:T(8,128)(2,1)}), bf16[32,32,512]{2,1,0:T(8,128)(2,1)S(1)}, u32[]{:S(2)}, u32[]{:S(2)}) async-start(bf16[32,32,512]{2,1,0:T(8,128)(2,1)} %shard_map.117), calls=%async_computation.3 | async-start | bytes 2097152 | tf_op jit(solution)/shard_map/all_to_all | solution.py:510
  71.6 6.8 %shard_map.115 = (bf16[8,128,128]{2,1,0:T(8,128)(2,1)}, f32[8,2,128,128]{3,2,1,0:T(8,128)}, bf16[8,2,128,128]{3,2,1,0:T(8,128)(2,1)}) custom-call(s32[1]{0:T(128)} %bitcast.refs_0_, bf16[8,128,128]{2,1,0:T(8,128)(2,1)} %get-tuple-element.43.refs_1_, bf16[2048,128]{1,0:T(8,128)(2,1)} %get-tuple-element.44.refs_2_, bf16[8,128,128]{2,1,0:T(8,128)(2,1)} %copy-done.9, ...), custom_call_target="tpu_custom_call" | custom-call | flops 1677721600 | bytes 2000000 | tf_op jit(solution)/shard_map/pallas_call | solution.py:111
  79.6 1.7 %collective-permute-done.11.refs_2_ = bf16[8,2,128,128]{3,2,1,0:T(8,128)(2,1)S(1)} collective-permute-done((bf16[8,2,128,128]{3,2,1,0:T(8,128)(2,1)}, bf16[8,2,128,128]{3,2,1,0:T(8,128)(2,1)S(1)}, u32[]{:S(2)}, u32[]{:S(2)}) %collective-permute-start.11) | collective-permute-done | bytes 524320 | tf_op jit(solution)/shard_map/ppermute | solution.py:532
  87.3 5.4 %all-to-all-start.4 = ((bf16[8,4,128,128]{3,2,1,0:T(8,128)(2,1)}), bf16[8,4,128,128]{3,2,1,0:T(8,128)(2,1)S(1)}, u32[]{:S(2)}, u32[]{:S(2)}) async-start(bf16[8,4,128,128]{3,2,1,0:T(8,128)(2,1)} %shard_map.118), calls=%async_computation.4 | async-start | bytes 2097152 | tf_op jit(solution)/shard_map/all_to_all | solution.py:403
  93.7 3.0 %shard_map.119 = (bf16[128,1024]{1,0:T(8,128)(2,1)}, bf16[128,1024]{1,0:T(8,128)(2,1)}) custom-call(s32[1]{0:T(128)} %bitcast.1.refs_0_, bf16[8,2,128,128]{3,2,1,0:T(8,128)(2,1)S(1)} %all-to-all-done.1.refs_4_.refs_1_, bf16[8,2,128,128]{3,2,1,0:T(8,128)(2,1)S(1)} %collective-permute-done.12.refs_5_.refs_2_, bf16[128,1024]{1,0:T(8,128)(2,1)S(1)} %copy-done.2, ...), custom_call_target="tpu_custom_call" | custom-call | flops 536870912 | bytes 2000000 | tf_op jit(solution)/shard_map/pallas_call | solution.py:111
  96.7 2.1 %collective-permute-start.13 = (bf16[128,1024]{1,0:T(8,128)(2,1)}, bf16[128,1024]{1,0:T(8,128)(2,1)S(1)}, u32[]{:S(2)}, u32[]{:S(2)}) collective-permute-start(bf16[128,1024]{1,0:T(8,128)(2,1)} %get-tuple-element.54), channel_id=1, source_target_pairs={{0,8},{8,0},{16,24},{24,16},{32,40},{40,32},{48,56},{56,48},{64,72... | collective-permute-start | bytes 786440 | tf_op jit(solution)/shard_map/ppermute | solution.py:556
  102.4 3.4 %all-to-all-done.4.refs_0_ = bf16[8,4,128,128]{3,2,1,0:T(8,128)(2,1)S(1)} async-done(((bf16[8,4,128,128]{3,2,1,0:T(8,128)(2,1)}), bf16[8,4,128,128]{3,2,1,0:T(8,128)(2,1)S(1)}, u32[]{:S(2)}, u32[]{:S(2)}) %all-to-all-start.4) | async-done | bytes 1048608 | tf_op jit(solution)/shard_map/all_to_all | solution.py:403
  105.8 3.8 %collective-permute-start.14 = (bf16[8,128,128]{2,1,0:T(8,128)(2,1)S(1)}, bf16[8,128,128]{2,1,0:T(8,128)(2,1)S(1)}, u32[]{:S(2)}, u32[]{:S(2)}) collective-permute-start(bf16[8,128,128]{2,1,0:T(8,128)(2,1)S(1)} %slice_bitcast_fusion.refs_1_), channel_id=1, source_target_pairs={{0,8},{8,0},{16,24},{24,16},{32,40},{40,32},{48,56},{56,48},{64,72... | collective-permute-start | bytes 786440 | tf_op jit(solution)/shard_map/ppermute | solution.py:564
  (59 shorter events, 25.7 us)
Async XLA Ops:
  3.5 14.5 %copy-start.10 = (s32[1,2048]{1,0:T(1,128)S(1)}, s32[1,2048]{1,0:T(1,128)}, u32[]{:S(2)}) copy-start(s32[1,2048]{1,0:T(1,128)} %param.10) | copy-start | bytes 24580
  3.5 17.5 %copy-start = (bf16[128,1024]{1,0:T(8,128)(2,1)S(1)}, bf16[128,1024]{1,0:T(8,128)(2,1)}, u32[]{:S(2)}) copy-start(bf16[128,1024]{1,0:T(8,128)(2,1)} %get-tuple-element.35.refs_1_) | copy-start | bytes 786436
  3.5 15.5 %collective-permute-start.2 = (bf16[128,1024]{1,0:T(8,128)(2,1)}, bf16[128,1024]{1,0:T(8,128)(2,1)S(1)}, u32[]{:S(2)}, u32[]{:S(2)}) collective-permute-start(bf16[128,1024]{1,0:T(8,128)(2,1)} %get-tuple-element.33.refs_3_), channel_id=1, source_target_pairs={{0,4},{1,5},{2,6},{3,7},{4,0},{5,1},{6,2},{7,3},{8,12},{9,13},{10,... | collective-permute-start | bytes 786440 | tf_op jit(solution)/shard_map/ppermute | solution.py:447
  5.6 16.6 %collective-permute-start.1 = (bf16[128,1024]{1,0:T(8,128)(2,1)}, bf16[128,1024]{1,0:T(8,128)(2,1)S(1)}, u32[]{:S(2)}, u32[]{:S(2)}) collective-permute-start(bf16[128,1024]{1,0:T(8,128)(2,1)} %get-tuple-element.33.refs_3_), channel_id=1, source_target_pairs={{0,3},{1,2},{2,1},{3,0},{4,7},{5,6},{6,5},{7,4},{8,11},{9,10},{10,... | collective-permute-start | bytes 786440 | tf_op jit(solution)/shard_map/ppermute | solution.py:447
  9.4 12.8 %collective-permute-start = (bf16[128,1024]{1,0:T(8,128)(2,1)}, bf16[128,1024]{1,0:T(8,128)(2,1)S(1)}, u32[]{:S(2)}, u32[]{:S(2)}) collective-permute-start(bf16[128,1024]{1,0:T(8,128)(2,1)} %get-tuple-element.33.refs_3_), channel_id=1, source_target_pairs={{0,1},{1,0},{2,3},{3,2},{4,5},{5,4},{6,7},{7,6},{8,9},{9,8},{10,11... | collective-permute-start | bytes 786440 | tf_op jit(solution)/shard_map/ppermute | solution.py:447
  9.4 18.9 %all-to-all-start = ((bf16[8,3,128,128]{3,2,1,0:T(8,128)(2,1)}), bf16[8,3,128,128]{3,2,1,0:T(8,128)(2,1)S(1)}, u32[]{:S(2)}, u32[]{:S(2)}) async-start(bf16[8,3,128,128]{3,2,1,0:T(8,128)(2,1)} %get-tuple-element.32), calls=%async_computation | async-start | bytes 1572864 | tf_op jit(solution)/shard_map/all_to_all | solution.py:403
  15.8 5.2 %collective-permute-start.5 = (bf16[128,1024]{1,0:T(8,128)(2,1)S(1)}, bf16[128,1024]{1,0:T(8,128)(2,1)S(1)}, u32[]{:S(2)}, u32[]{:S(2)}) collective-permute-start(bf16[128,1024]{1,0:T(8,128)(2,1)S(1)} %copy-done.11), channel_id=1, source_target_pairs={{0,8},{8,0},{16,24},{24,16},{32,40},{40,32},{48,56},{56,48},{64,72... | collective-permute-start | bytes 786440 | tf_op jit(solution)/shard_map/ppermute | solution.py:454
  19.1 9.2 %collective-permute-start.4 = (bf16[128,1024]{1,0:T(8,128)(2,1)S(1)}, bf16[128,1024]{1,0:T(8,128)(2,1)S(1)}, u32[]{:S(2)}, u32[]{:S(2)}) collective-permute-start(bf16[128,1024]{1,0:T(8,128)(2,1)S(1)} %collective-permute-done.2.refs_7_), channel_id=1, source_target_pairs={{0,3},{1,2},{2,1},{3,0},{4,7},{5,6},{6,5},{7,4},{8,11},{9,10},{10,... | collective-permute-start | bytes 786440 | tf_op jit(solution)/shard_map/ppermute | solution.py:447
  19.4 8.9 %collective-permute-start.3 = (bf16[128,1024]{1,0:T(8,128)(2,1)S(1)}, bf16[128,1024]{1,0:T(8,128)(2,1)S(1)}, u32[]{:S(2)}, u32[]{:S(2)}) collective-permute-start(bf16[128,1024]{1,0:T(8,128)(2,1)S(1)} %collective-permute-done.2.refs_7_), channel_id=1, source_target_pairs={{0,1},{1,0},{2,3},{3,2},{4,5},{5,4},{6,7},{7,6},{8,9},{9,8},{10,11... | collective-permute-start | bytes 786440 | tf_op jit(solution)/shard_map/ppermute | solution.py:447
  28.3 14.8 %copy-start.3 = (bf16[128,1024]{1,0:T(8,128)(2,1)}, bf16[128,1024]{1,0:T(8,128)(2,1)S(1)}, u32[]{:S(2)}) copy-start(bf16[128,1024]{1,0:T(8,128)(2,1)S(1)} %collective-permute-done.4.refs_10_) | copy-start | bytes 786436
  28.3 14.8 %copy-start.5 = (bf16[128,1024]{1,0:T(8,128)(2,1)}, bf16[128,1024]{1,0:T(8,128)(2,1)S(1)}, u32[]{:S(2)}) copy-start(bf16[128,1024]{1,0:T(8,128)(2,1)S(1)} %collective-permute-done.3.refs_8_) | copy-start | bytes 786436
  28.3 6.6 %collective-permute-start.6 = (bf16[8,3,128,128]{3,2,1,0:T(8,128)(2,1)S(1)}, bf16[8,3,128,128]{3,2,1,0:T(8,128)(2,1)S(1)}, u32[]{:S(2)}, u32[]{:S(2)}) collective-permute-start(bf16[8,3,128,128]{3,2,1,0:T(8,128)(2,1)S(1)} %all-to-all-done.refs_1_.refs_2_.refs_3_), channel_id=1, source_target_pairs={{0,8},{8,0},{16,24},{24,16},{32,40},{40,32},{48,56},{56,48},{64,72... | collective-permute-start | bytes 2359304 | tf_op jit(solution)/shard_map/ppermute | solution.py:466
  30.2 12.9 %collective-permute-start.8 = (bf16[128,1024]{1,0:T(8,128)(2,1)S(1)}, bf16[128,1024]{1,0:T(8,128)(2,1)}, u32[]{:S(2)}, u32[]{:S(2)}) collective-permute-start(bf16[128,1024]{1,0:T(8,128)(2,1)S(1)} %collective-permute-done.4.refs_10_), channel_id=1, source_target_pairs={{0,1},{1,0},{2,3},{3,2},{4,5},{5,4},{6,7},{7,6},{8,9},{9,8},{10,11... | collective-permute-start | bytes 786440 | tf_op jit(solution)/shard_map/ppermute | solution.py:447
  31.8 11.3 %collective-permute-start.9 = (bf16[256,512]{1,0:T(8,128)(2,1)}, bf16[256,512]{1,0:T(8,128)(2,1)}, u32[]{:S(2)}, u32[]{:S(2)}) collective-permute-start(bf16[256,512]{1,0:T(8,128)(2,1)} %shard_map.111), channel_id=1, source_target_pairs={{0,64},{8,72},{16,80},{24,88},{32,96},{40,104},{48,112},{56,120},{... | collective-permute-start | bytes 786440 | tf_op jit(solution)/shard_map/ppermute | solution.py:464
  32.9 10.2 %collective-permute-start.7 = (bf16[128,1024]{1,0:T(8,128)(2,1)S(1)}, bf16[128,1024]{1,0:T(8,128)(2,1)}, u32[]{:S(2)}, u32[]{:S(2)}) collective-permute-start(bf16[128,1024]{1,0:T(8,128)(2,1)S(1)} %collective-permute-done.refs_4_), channel_id=1, source_target_pairs={{0,3},{1,2},{2,1},{3,0},{4,7},{5,6},{6,5},{7,4},{8,11},{9,10},{10,... | collective-permute-start | bytes 786440 | tf_op jit(solution)/shard_map/ppermute | solution.py:447
  38.9 12.8 %all-to-all-start.1 = ((bf16[8,2,128,128]{3,2,1,0:T(8,128)(2,1)}), bf16[8,2,128,128]{3,2,1,0:T(8,128)(2,1)S(1)}, u32[]{:S(2)}, u32[]{:S(2)}) async-start(bf16[8,2,128,128]{3,2,1,0:T(8,128)(2,1)} %get-tuple-element.37.refs_5_), calls=%async_computation.1 | async-start | bytes 1048576 | tf_op jit(solution)/shard_map/all_to_all | solution.py:403
  45.9 2.4 %collective-permute-start.10 = (bf16[8,128,128]{2,1,0:T(8,128)(2,1)S(1)}, bf16[8,128,128]{2,1,0:T(8,128)(2,1)S(1)}, u32[]{:S(2)}, u32[]{:S(2)}) collective-permute-start(bf16[8,128,128]{2,1,0:T(8,128)(2,1)S(1)} %get-tuple-element.41), channel_id=1, source_target_pairs={{0,8},{8,0},{16,24},{24,16},{32,40},{40,32},{48,56},{56,48},{64,72... | collective-permute-start | bytes 786440 | tf_op jit(solution)/shard_map/ppermute | solution.py:492
  51.8 6.8 %collective-permute-start.12 = (bf16[8,2,128,128]{3,2,1,0:T(8,128)(2,1)S(1)}, bf16[8,2,128,128]{3,2,1,0:T(8,128)(2,1)S(1)}, u32[]{:S(2)}, u32[]{:S(2)}) collective-permute-start(bf16[8,2,128,128]{3,2,1,0:T(8,128)(2,1)S(1)} %all-to-all-done.1.refs_4_.refs_1_), channel_id=1, source_target_pairs={{0,8},{8,0},{16,24},{24,16},{32,40},{40,32},{48,56},{56,48},{64,72... | collective-permute-start | bytes 1572872 | tf_op jit(solution)/shard_map/ppermute | solution.py:499
  55.2 11.6 %all-to-all-start.2 = ((bf16[8,128,128]{2,1,0:T(8,128)(2,1)}), bf16[8,128,128]{2,1,0:T(8,128)(2,1)S(1)}, u32[]{:S(2)}, u32[]{:S(2)}) async-start(bf16[8,128,128]{2,1,0:T(8,128)(2,1)} %shard_map.114), calls=%async_computation.2 | async-start | bytes 524288 | tf_op jit(solution)/shard_map/all_to_all | solution.py:403
  67.5 18.6 %all-to-all-start.3 = ((bf16[32,32,512]{2,1,0:T(8,128)(2,1)}), bf16[32,32,512]{2,1,0:T(8,128)(2,1)S(1)}, u32[]{:S(2)}, u32[]{:S(2)}) async-start(bf16[32,32,512]{2,1,0:T(8,128)(2,1)} %shard_map.117), calls=%async_computation.3 | async-start | bytes 2097152 | tf_op jit(solution)/shard_map/all_to_all | solution.py:510
  78.4 3.0 %collective-permute-start.11 = (bf16[8,2,128,128]{3,2,1,0:T(8,128)(2,1)}, bf16[8,2,128,128]{3,2,1,0:T(8,128)(2,1)S(1)}, u32[]{:S(2)}, u32[]{:S(2)}) collective-permute-start(bf16[8,2,128,128]{3,2,1,0:T(8,128)(2,1)} %get-tuple-element.50), channel_id=1, source_target_pairs={{0,8},{8,0},{16,24},{24,16},{32,40},{40,32},{48,56},{56,48},{64,72... | collective-permute-start | bytes 1572872 | tf_op jit(solution)/shard_map/ppermute | solution.py:532
  87.3 18.5 %all-to-all-start.4 = ((bf16[8,4,128,128]{3,2,1,0:T(8,128)(2,1)}), bf16[8,4,128,128]{3,2,1,0:T(8,128)(2,1)S(1)}, u32[]{:S(2)}, u32[]{:S(2)}) async-start(bf16[8,4,128,128]{3,2,1,0:T(8,128)(2,1)} %shard_map.118), calls=%async_computation.4 | async-start | bytes 2097152 | tf_op jit(solution)/shard_map/all_to_all | solution.py:403
  96.7 3.5 %collective-permute-start.13 = (bf16[128,1024]{1,0:T(8,128)(2,1)}, bf16[128,1024]{1,0:T(8,128)(2,1)S(1)}, u32[]{:S(2)}, u32[]{:S(2)}) collective-permute-start(bf16[128,1024]{1,0:T(8,128)(2,1)} %get-tuple-element.54), channel_id=1, source_target_pairs={{0,8},{8,0},{16,24},{24,16},{32,40},{40,32},{48,56},{56,48},{64,72... | collective-permute-start | bytes 786440 | tf_op jit(solution)/shard_map/ppermute | solution.py:556
  105.8 5.1 %collective-permute-start.14 = (bf16[8,128,128]{2,1,0:T(8,128)(2,1)S(1)}, bf16[8,128,128]{2,1,0:T(8,128)(2,1)S(1)}, u32[]{:S(2)}, u32[]{:S(2)}) collective-permute-start(bf16[8,128,128]{2,1,0:T(8,128)(2,1)S(1)} %slice_bitcast_fusion.refs_1_), channel_id=1, source_target_pairs={{0,8},{8,0},{16,24},{24,16},{32,40},{40,32},{48,56},{56,48},{64,72... | collective-permute-start | bytes 786440 | tf_op jit(solution)/shard_map/ppermute | solution.py:564
  (8 other events, 26.6 us)

commit v12 on v11

--- a/solution.py
+++ b/solution.py
@@ -431,7 +431,12 @@
     )
     own = exchange(packed)
 
-    session_ids = session[0]
+    def step(value, s):
+        return lax.ppermute(value, "fsdp", [(i, i ^ s) for i in range(8)])
+
+    over = step(own_half, 4)
+
+    session_ids = after(session[0], over)
     positions = jnp.arange(LEN, dtype=jnp.int32).reshape(CHIPS, 2, BLOCK)
     own_sessions = lax.dynamic_index_in_dim(session_ids.reshape(CHIPS, 2, BLOCK), core, 1, False)
     own_positions = lax.dynamic_index_in_dim(positions, core, 1, False)
@@ -443,15 +448,11 @@
     rows_here = index * BLOCK + jnp.arange(BLOCK, dtype=jnp.int32)
     valid_here = (rows_here < valid_len).astype(F32)[:, None]
 
-    def step(value, s):
-        return lax.ppermute(value, "fsdp", [(i, i ^ s) for i in range(8)])
-
-    over = step(own_half, 4)
     one, three = step(own_half, 1), step(own_half, 3)
     over_one, over_three = step(over, 1), step(over, 3)
     two, over_two = step(one, 3), step(over_three, 1)
     pieces = [own_half, one, two, three, over, over_one, over_two, over_three]
-    up_other = lax.ppermute(up_send, "ctx", CORE_SWAP)
+    up_other = lax.ppermute(after(up_send, over), "ctx", CORE_SWAP)
     up_pair = call(
         quarter_kernel,
         [("S", high_ref), ("A", up_mine), ("A", up_other)],

time: 113 us -> 113 us (level)
    ppermute x1, starting transfers between devices: 1.86 us -> 3.01 us  [shards(): other = lax.ppermute(own, 'ctx', CORE_SWAP)]
where the time goes in v12:
time: 113 us; the launch traced here: 112 us
  starting transfers between devices  52 us (46%)
  Pallas kernels  31.3 us (28%)
  waiting for transfers between devices  21.6 us (19%)
  local copies, waits for them, and re-layouts  4.83 us (4%)
  between operations  1.78 us (2%)
    pallas_call x13, Pallas kernels, call(): pl.pallas_call(body, out_shape=[SPACES[o[0]](o[1], o[2]) if o[0] in 'HR'...  31.3 us
    all_to_all x4, starting transfers between devices, exchange(): lax.all_to_all(operand, 'ctx', split_axis=0, concat_axis=0, tiled=True, a...  19.5 us
    all_to_all x4, waiting for transfers between devices, exchange(): lax.all_to_all(operand, 'ctx', split_axis=0, concat_axis=0, tiled=True, a...  11 us
    ppermute x7, starting transfers between devices, step(): return lax.ppermute(value, 'fsdp', [(i, i ^ s) for i in range(8)])  10.3 us
    ppermute x7, waiting for transfers between devices, step(): return lax.ppermute(value, 'fsdp', [(i, i ^ s) for i in range(8)])  5.1 us
    unnamed x24, local copies, waits for them, and re-layouts  4.81 us
    all_to_all x1, starting transfers between devices, shards(): lax.all_to_all(after(terms, grads), ('ctx', 'fsdp'), split_axis=0, concat...  4.76 us
    ppermute x1, starting transfers between devices, shards(): weight_other = lax.ppermute(weight_mine, 'ctx', CORE_SWAP)  3.8 us
  transfers between devices with their start and end apart: 20, of which 8 were waited for; matrix products, arithmetic and copies ran while one was open for 1% of the time, Pallas kernels for 23%

profile of v12, /device:TPU:1, one launch (start us, length us, event | category | flops | bytes accessed | tf_op | source)
XLA Modules:
  0.0 112.5 jit_solution(6623716462180319617)
XLA Ops:
  0.6 2.8 %shard_map.110 = (bf16[8,3,128,128]{3,2,1,0:T(8,128)(2,1)}, bf16[128,1024]{1,0:T(8,128)(2,1)}, bf16[128,1024]{1,0:T(8,128)(2,1)}, bf16[128,1024]{1,0:T(8,128)(2,1)}) custom-call(s32[1]{0:T(128)} %bitcast.refs_0_, bf16[1,128,1024]{2,1,0:T(8,128)(2,1)} %refs_1_.1, bf16[1,128,1024]{2,1,0:T(8,128)(2,1)} %refs_2_.1, bf16[1,128,1024]{2,1,0:T(8,128)(2,1)} %refs_3_.1, ...), custom_call_target="tpu_custom_call" | custom-call | bytes 2000000 | tf_op jit(solution)/shard_map/pallas_call | solution.py:111
  3.5 2.1 %collective-permute-start = (bf16[128,1024]{1,0:T(8,128)(2,1)}, bf16[128,1024]{1,0:T(8,128)(2,1)S(1)}, u32[]{:S(2)}, u32[]{:S(2)}) collective-permute-start(bf16[128,1024]{1,0:T(8,128)(2,1)} %get-tuple-element.35.refs_3_), channel_id=1, source_target_pairs={{0,4},{1,5},{2,6},{3,7},{4,0},{5,1},{6,2},{7,3},{8,12},{9,13},{10,... | collective-permute-start | bytes 786440 | tf_op jit(solution)/shard_map/ppermute | solution.py:435
  5.6 3.8 %collective-permute-start.2 = (bf16[128,1024]{1,0:T(8,128)(2,1)}, bf16[128,1024]{1,0:T(8,128)(2,1)S(1)}, u32[]{:S(2)}, u32[]{:S(2)}) collective-permute-start(bf16[128,1024]{1,0:T(8,128)(2,1)} %get-tuple-element.35.refs_3_), channel_id=1, source_target_pairs={{0,3},{1,2},{2,1},{3,0},{4,7},{5,6},{6,5},{7,4},{8,11},{9,10},{10,... | collective-permute-start | bytes 786440 | tf_op jit(solution)/shard_map/ppermute | solution.py:435
  9.4 6.4 %all-to-all-start = ((bf16[8,3,128,128]{3,2,1,0:T(8,128)(2,1)}), bf16[8,3,128,128]{3,2,1,0:T(8,128)(2,1)S(1)}, u32[]{:S(2)}, u32[]{:S(2)}) async-start(bf16[8,3,128,128]{3,2,1,0:T(8,128)(2,1)} %get-tuple-element.34), calls=%async_computation | async-start | bytes 1572864 | tf_op jit(solution)/shard_map/all_to_all | solution.py:403
  16.5 1.6 %collective-permute-start.5 = (bf16[128,1024]{1,0:T(8,128)(2,1)S(1)}, bf16[128,1024]{1,0:T(8,128)(2,1)S(1)}, u32[]{:S(2)}, u32[]{:S(2)}) collective-permute-start(bf16[128,1024]{1,0:T(8,128)(2,1)S(1)} %copy-done.11), channel_id=1, source_target_pairs={{0,8},{8,0},{16,24},{24,16},{32,40},{40,32},{48,56},{56,48},{64,72... | collective-permute-start | bytes 786440 | tf_op jit(solution)/shard_map/ppermute | solution.py:455
  22.1 5.1 %collective-permute-done.4.refs_10_ = bf16[128,1024]{1,0:T(8,128)(2,1)S(1)} collective-permute-done((bf16[128,1024]{1,0:T(8,128)(2,1)S(1)}, bf16[128,1024]{1,0:T(8,128)(2,1)S(1)}, u32[]{:S(2)}, u32[]{:S(2)}) %collective-permute-start.4) | collective-permute-done | bytes 262176 | tf_op jit(solution)/shard_map/ppermute | solution.py:435
  27.2 3.0 %collective-permute-start.6 = (bf16[8,3,128,128]{3,2,1,0:T(8,128)(2,1)S(1)}, bf16[8,3,128,128]{3,2,1,0:T(8,128)(2,1)S(1)}, u32[]{:S(2)}, u32[]{:S(2)}) collective-permute-start(bf16[8,3,128,128]{3,2,1,0:T(8,128)(2,1)S(1)} %all-to-all-done.refs_1_.refs_2_.refs_3_), channel_id=1, source_target_pairs={{0,8},{8,0},{16,24},{24,16},{32,40},{40,32},{48,56},{56,48},{64,72... | collective-permute-start | bytes 2359304 | tf_op jit(solution)/shard_map/ppermute | solution.py:467
  30.2 1.6 %collective-permute-start.8 = (bf16[128,1024]{1,0:T(8,128)(2,1)S(1)}, bf16[128,1024]{1,0:T(8,128)(2,1)}, u32[]{:S(2)}, u32[]{:S(2)}) collective-permute-start(bf16[128,1024]{1,0:T(8,128)(2,1)S(1)} %collective-permute-done.4.refs_10_), channel_id=1, source_target_pairs={{0,1},{1,0},{2,3},{3,2},{4,5},{5,4},{6,7},{7,6},{8,9},{9,8},{10,11... | collective-permute-start | bytes 786440 | tf_op jit(solution)/shard_map/ppermute | solution.py:435
  33.9 4.1 %shard_map.112 = (bf16[8,2,128,128]{3,2,1,0:T(8,128)(2,1)}, f32[4,1,256]{2,1,0:T(1,128)}, bf16[8,128,128]{2,1,0:T(8,128)(2,1)}, bf16[2048,128]{1,0:T(8,128)(2,1)}, bf16[2048,128]{1,0:T(8,128)(2,1)}) custom-call(s32[1]{0:T(128)} %bitcast.refs_0_, bf16[8,3,128,128]{3,2,1,0:T(8,128)(2,1)S(1)} %all-to-all-done.refs_1_.refs_2_.refs_3_, ...), custom_call_target="tpu_custom_call" | custom-call | flops 671088640 | bytes 2000000 | tf_op jit(solution)/shard_map/pallas_call | solution.py:111
  38.0 4.1 %all-to-all-start.1 = ((bf16[8,2,128,128]{3,2,1,0:T(8,128)(2,1)}), bf16[8,2,128,128]{3,2,1,0:T(8,128)(2,1)S(1)}, u32[]{:S(2)}, u32[]{:S(2)}) async-start(bf16[8,2,128,128]{3,2,1,0:T(8,128)(2,1)} %get-tuple-element.41.refs_5_), calls=%async_computation.1 | async-start | bytes 1048576 | tf_op jit(solution)/shard_map/all_to_all | solution.py:403
  42.1 2.8 %shard_map.113 = (f32[8,128,128]{2,1,0:T(8,128)S(1)}, bf16[8,128,128]{2,1,0:T(8,128)(2,1)S(1)}) custom-call(s32[1]{0:T(128)} %bitcast.1.refs_0_, bf16[128,1024]{1,0:T(8,128)(2,1)S(1)} %copy-done, bf16[128,1024]{1,0:T(8,128)(2,1)S(1)} %collective-permute-done.5.refs_2_, bf16[128,1024]{1,0:T(8,128)(2,1)S(1)} %copy-done.2, ...), custom_call_target="tpu_custom_call" | custom-call | flops 536870912 | bytes 2000000 | tf_op jit(solution)/shard_map/pallas_call | solution.py:111
  48.6 2.2 %all-to-all-done.1.refs_4_.refs_1_ = bf16[8,2,128,128]{3,2,1,0:T(8,128)(2,1)S(1)} async-done(((bf16[8,2,128,128]{3,2,1,0:T(8,128)(2,1)}), bf16[8,2,128,128]{3,2,1,0:T(8,128)(2,1)S(1)}, u32[]{:S(2)}, u32[]{:S(2)}) %all-to-all-start.1) | async-done | bytes 524320 | tf_op jit(solution)/shard_map/all_to_all | solution.py:403
  50.8 3.4 %collective-permute-start.12 = (bf16[8,2,128,128]{3,2,1,0:T(8,128)(2,1)S(1)}, bf16[8,2,128,128]{3,2,1,0:T(8,128)(2,1)S(1)}, u32[]{:S(2)}, u32[]{:S(2)}) collective-permute-start(bf16[8,2,128,128]{3,2,1,0:T(8,128)(2,1)S(1)} %all-to-all-done.1.refs_4_.refs_1_), channel_id=1, source_target_pairs={{0,8},{8,0},{16,24},{24,16},{32,40},{40,32},{48,56},{56,48},{64,72... | collective-permute-start | bytes 1572872 | tf_op jit(solution)/shard_map/ppermute | solution.py:500
  54.2 3.4 %all-to-all-start.2 = ((bf16[8,128,128]{2,1,0:T(8,128)(2,1)}), bf16[8,128,128]{2,1,0:T(8,128)(2,1)S(1)}, u32[]{:S(2)}, u32[]{:S(2)}) async-start(bf16[8,128,128]{2,1,0:T(8,128)(2,1)} %shard_map.114), calls=%async_computation.2 | async-start | bytes 524288 | tf_op jit(solution)/shard_map/all_to_all | solution.py:403
  57.6 2.8 %shard_map.117 = bf16[32,32,512]{2,1,0:T(8,128)(2,1)} custom-call(s32[1]{0:T(128)} %bitcast.8.refs_0_, bf16[128,1024]{1,0:T(8,128)(2,1)S(1)} %copy-done, bf16[128,1024]{1,0:T(8,128)(2,1)S(1)} %collective-permute-done.5.refs_2_, bf16[256,512]{1,0:T(8,128)(2,1)} %collective-permute-done.9.refs_3_, bf16[8,2,128,128]{3,2,1,0:T(8,128)(2,1)S(1)} %all-to-all-done.1.refs_4_.refs_1_, ...), custom_call_target="tpu_custom_call" | custom-call | flops 536870912 | bytes 2000000 | tf_op jit(solution)/shard_map/pallas_call | solution.py:111
  60.5 5.4 %all-to-all-done.2.refs_3_ = bf16[8,128,128]{2,1,0:T(8,128)(2,1)S(1)} async-done(((bf16[8,128,128]{2,1,0:T(8,128)(2,1)}), bf16[8,128,128]{2,1,0:T(8,128)(2,1)S(1)}, u32[]{:S(2)}, u32[]{:S(2)}) %all-to-all-start.2) | async-done | bytes 262176 | tf_op jit(solution)/shard_map/all_to_all | solution.py:403
  66.5 4.8 %all-to-all-start.3 = ((bf16[32,32,512]{2,1,0:T(8,128)(2,1)}), bf16[32,32,512]{2,1,0:T(8,128)(2,1)S(1)}, u32[]{:S(2)}, u32[]{:S(2)}) async-start(bf16[32,32,512]{2,1,0:T(8,128)(2,1)} %shard_map.117), calls=%async_computation.3 | async-start | bytes 2097152 | tf_op jit(solution)/shard_map/all_to_all | solution.py:511
  71.3 6.8 %shard_map.115 = (bf16[8,128,128]{2,1,0:T(8,128)(2,1)}, f32[8,2,128,128]{3,2,1,0:T(8,128)}, bf16[8,2,128,128]{3,2,1,0:T(8,128)(2,1)}) custom-call(s32[1]{0:T(128)} %bitcast.refs_0_, bf16[8,128,128]{2,1,0:T(8,128)(2,1)} %get-tuple-element.47.refs_1_, bf16[2048,128]{1,0:T(8,128)(2,1)} %get-tuple-element.48.refs_2_, bf16[8,128,128]{2,1,0:T(8,128)(2,1)} %copy-done.9, ...), custom_call_target="tpu_custom_call" | custom-call | flops 1677721600 | bytes 2000000 | tf_op jit(solution)/shard_map/pallas_call | solution.py:111
  79.2 1.7 %collective-permute-done.11.refs_2_ = bf16[8,2,128,128]{3,2,1,0:T(8,128)(2,1)S(1)} collective-permute-done((bf16[8,2,128,128]{3,2,1,0:T(8,128)(2,1)}, bf16[8,2,128,128]{3,2,1,0:T(8,128)(2,1)S(1)}, u32[]{:S(2)}, u32[]{:S(2)}) %collective-permute-start.11) | collective-permute-done | bytes 524320 | tf_op jit(solution)/shard_map/ppermute | solution.py:533
  87.1 5.6 %all-to-all-start.4 = ((bf16[8,4,128,128]{3,2,1,0:T(8,128)(2,1)}), bf16[8,4,128,128]{3,2,1,0:T(8,128)(2,1)S(1)}, u32[]{:S(2)}, u32[]{:S(2)}) async-start(bf16[8,4,128,128]{3,2,1,0:T(8,128)(2,1)} %shard_map.118), calls=%async_computation.4 | async-start | bytes 2097152 | tf_op jit(solution)/shard_map/all_to_all | solution.py:403
  93.7 3.0 %shard_map.119 = (bf16[128,1024]{1,0:T(8,128)(2,1)}, bf16[128,1024]{1,0:T(8,128)(2,1)}) custom-call(s32[1]{0:T(128)} %bitcast.1.refs_0_, bf16[8,2,128,128]{3,2,1,0:T(8,128)(2,1)S(1)} %all-to-all-done.1.refs_4_.refs_1_, bf16[8,2,128,128]{3,2,1,0:T(8,128)(2,1)S(1)} %collective-permute-done.12.refs_5_.refs_2_, bf16[128,1024]{1,0:T(8,128)(2,1)S(1)} %copy-done.2, ...), custom_call_target="tpu_custom_call" | custom-call | flops 536870912 | bytes 2000000 | tf_op jit(solution)/shard_map/pallas_call | solution.py:111
  96.7 2.1 %collective-permute-start.13 = (bf16[128,1024]{1,0:T(8,128)(2,1)}, bf16[128,1024]{1,0:T(8,128)(2,1)S(1)}, u32[]{:S(2)}, u32[]{:S(2)}) collective-permute-start(bf16[128,1024]{1,0:T(8,128)(2,1)} %get-tuple-element.58), channel_id=1, source_target_pairs={{0,8},{8,0},{16,24},{24,16},{32,40},{40,32},{48,56},{56,48},{64,72... | collective-permute-start | bytes 786440 | tf_op jit(solution)/shard_map/ppermute | solution.py:557
  102.4 3.4 %all-to-all-done.4.refs_0_ = bf16[8,4,128,128]{3,2,1,0:T(8,128)(2,1)S(1)} async-done(((bf16[8,4,128,128]{3,2,1,0:T(8,128)(2,1)}), bf16[8,4,128,128]{3,2,1,0:T(8,128)(2,1)S(1)}, u32[]{:S(2)}, u32[]{:S(2)}) %all-to-all-start.4) | async-done | bytes 1048608 | tf_op jit(solution)/shard_map/all_to_all | solution.py:403
  105.8 3.8 %collective-permute-start.14 = (bf16[8,128,128]{2,1,0:T(8,128)(2,1)S(1)}, bf16[8,128,128]{2,1,0:T(8,128)(2,1)S(1)}, u32[]{:S(2)}, u32[]{:S(2)}) collective-permute-start(bf16[8,128,128]{2,1,0:T(8,128)(2,1)S(1)} %slice_bitcast_fusion.refs_1_), channel_id=1, source_target_pairs={{0,8},{8,0},{16,24},{24,16},{32,40},{40,32},{48,56},{56,48},{64,72... | collective-permute-start | bytes 786440 | tf_op jit(solution)/shard_map/ppermute | solution.py:565
  (59 shorter events, 25.0 us)
Async XLA Ops:
  3.5 16.3 %copy-start.10 = (s32[1,2048]{1,0:T(1,128)S(1)}, s32[1,2048]{1,0:T(1,128)}, u32[]{:S(2)}) copy-start(s32[1,2048]{1,0:T(1,128)} %param.10) | copy-start | bytes 24580
  3.5 17.3 %copy-start = (bf16[128,1024]{1,0:T(8,128)(2,1)S(1)}, bf16[128,1024]{1,0:T(8,128)(2,1)}, u32[]{:S(2)}) copy-start(bf16[128,1024]{1,0:T(8,128)(2,1)} %get-tuple-element.39.refs_1_) | copy-start | bytes 786436
  3.5 12.9 %collective-permute-start = (bf16[128,1024]{1,0:T(8,128)(2,1)}, bf16[128,1024]{1,0:T(8,128)(2,1)S(1)}, u32[]{:S(2)}, u32[]{:S(2)}) collective-permute-start(bf16[128,1024]{1,0:T(8,128)(2,1)} %get-tuple-element.35.refs_3_), channel_id=1, source_target_pairs={{0,4},{1,5},{2,6},{3,7},{4,0},{5,1},{6,2},{7,3},{8,12},{9,13},{10,... | collective-permute-start | bytes 786440 | tf_op jit(solution)/shard_map/ppermute | solution.py:435
  5.6 16.4 %collective-permute-start.2 = (bf16[128,1024]{1,0:T(8,128)(2,1)}, bf16[128,1024]{1,0:T(8,128)(2,1)S(1)}, u32[]{:S(2)}, u32[]{:S(2)}) collective-permute-start(bf16[128,1024]{1,0:T(8,128)(2,1)} %get-tuple-element.35.refs_3_), channel_id=1, source_target_pairs={{0,3},{1,2},{2,1},{3,0},{4,7},{5,6},{6,5},{7,4},{8,11},{9,10},{10,... | collective-permute-start | bytes 786440 | tf_op jit(solution)/shard_map/ppermute | solution.py:435
  9.4 12.7 %collective-permute-start.1 = (bf16[128,1024]{1,0:T(8,128)(2,1)}, bf16[128,1024]{1,0:T(8,128)(2,1)S(1)}, u32[]{:S(2)}, u32[]{:S(2)}) collective-permute-start(bf16[128,1024]{1,0:T(8,128)(2,1)} %get-tuple-element.35.refs_3_), channel_id=1, source_target_pairs={{0,1},{1,0},{2,3},{3,2},{4,5},{5,4},{6,7},{7,6},{8,9},{9,8},{10,11... | collective-permute-start | bytes 786440 | tf_op jit(solution)/shard_map/ppermute | solution.py:435
  9.4 17.7 %all-to-all-start = ((bf16[8,3,128,128]{3,2,1,0:T(8,128)(2,1)}), bf16[8,3,128,128]{3,2,1,0:T(8,128)(2,1)S(1)}, u32[]{:S(2)}, u32[]{:S(2)}) async-start(bf16[8,3,128,128]{3,2,1,0:T(8,128)(2,1)} %get-tuple-element.34), calls=%async_computation | async-start | bytes 1572864 | tf_op jit(solution)/shard_map/all_to_all | solution.py:403
  16.5 4.4 %collective-permute-start.5 = (bf16[128,1024]{1,0:T(8,128)(2,1)S(1)}, bf16[128,1024]{1,0:T(8,128)(2,1)S(1)}, u32[]{:S(2)}, u32[]{:S(2)}) collective-permute-start(bf16[128,1024]{1,0:T(8,128)(2,1)S(1)} %copy-done.11), channel_id=1, source_target_pairs={{0,8},{8,0},{16,24},{24,16},{32,40},{40,32},{48,56},{56,48},{64,72... | collective-permute-start | bytes 786440 | tf_op jit(solution)/shard_map/ppermute | solution.py:455
  18.1 9.1 %collective-permute-start.4 = (bf16[128,1024]{1,0:T(8,128)(2,1)S(1)}, bf16[128,1024]{1,0:T(8,128)(2,1)S(1)}, u32[]{:S(2)}, u32[]{:S(2)}) collective-permute-start(bf16[128,1024]{1,0:T(8,128)(2,1)S(1)} %collective-permute-done.refs_7_), channel_id=1, source_target_pairs={{0,3},{1,2},{2,1},{3,0},{4,7},{5,6},{6,5},{7,4},{8,11},{9,10},{10,... | collective-permute-start | bytes 786440 | tf_op jit(solution)/shard_map/ppermute | solution.py:435
  18.3 8.8 %collective-permute-start.3 = (bf16[128,1024]{1,0:T(8,128)(2,1)S(1)}, bf16[128,1024]{1,0:T(8,128)(2,1)S(1)}, u32[]{:S(2)}, u32[]{:S(2)}) collective-permute-start(bf16[128,1024]{1,0:T(8,128)(2,1)S(1)} %collective-permute-done.refs_7_), channel_id=1, source_target_pairs={{0,1},{1,0},{2,3},{3,2},{4,5},{5,4},{6,7},{7,6},{8,9},{9,8},{10,11... | collective-permute-start | bytes 786440 | tf_op jit(solution)/shard_map/ppermute | solution.py:435
  27.1 15.0 %copy-start.3 = (bf16[128,1024]{1,0:T(8,128)(2,1)}, bf16[128,1024]{1,0:T(8,128)(2,1)S(1)}, u32[]{:S(2)}) copy-start(bf16[128,1024]{1,0:T(8,128)(2,1)S(1)} %collective-permute-done.4.refs_10_) | copy-start | bytes 786436
  27.1 15.0 %copy-start.5 = (bf16[128,1024]{1,0:T(8,128)(2,1)}, bf16[128,1024]{1,0:T(8,128)(2,1)S(1)}, u32[]{:S(2)}) copy-start(bf16[128,1024]{1,0:T(8,128)(2,1)S(1)} %collective-permute-done.3.refs_8_) | copy-start | bytes 786436
  27.2 6.7 %collective-permute-start.6 = (bf16[8,3,128,128]{3,2,1,0:T(8,128)(2,1)S(1)}, bf16[8,3,128,128]{3,2,1,0:T(8,128)(2,1)S(1)}, u32[]{:S(2)}, u32[]{:S(2)}) collective-permute-start(bf16[8,3,128,128]{3,2,1,0:T(8,128)(2,1)S(1)} %all-to-all-done.refs_1_.refs_2_.refs_3_), channel_id=1, source_target_pairs={{0,8},{8,0},{16,24},{24,16},{32,40},{40,32},{48,56},{56,48},{64,72... | collective-permute-start | bytes 2359304 | tf_op jit(solution)/shard_map/ppermute | solution.py:467
  30.2 11.9 %collective-permute-start.8 = (bf16[128,1024]{1,0:T(8,128)(2,1)S(1)}, bf16[128,1024]{1,0:T(8,128)(2,1)}, u32[]{:S(2)}, u32[]{:S(2)}) collective-permute-start(bf16[128,1024]{1,0:T(8,128)(2,1)S(1)} %collective-permute-done.4.refs_10_), channel_id=1, source_target_pairs={{0,1},{1,0},{2,3},{3,2},{4,5},{5,4},{6,7},{7,6},{8,9},{9,8},{10,11... | collective-permute-start | bytes 786440 | tf_op jit(solution)/shard_map/ppermute | solution.py:435
  31.8 10.3 %collective-permute-start.9 = (bf16[256,512]{1,0:T(8,128)(2,1)}, bf16[256,512]{1,0:T(8,128)(2,1)}, u32[]{:S(2)}, u32[]{:S(2)}) collective-permute-start(bf16[256,512]{1,0:T(8,128)(2,1)} %shard_map.111), channel_id=1, source_target_pairs={{0,64},{8,72},{16,80},{24,88},{32,96},{40,104},{48,112},{56,120},{... | collective-permute-start | bytes 786440 | tf_op jit(solution)/shard_map/ppermute | solution.py:465
  32.9 9.2 %collective-permute-start.7 = (bf16[128,1024]{1,0:T(8,128)(2,1)S(1)}, bf16[128,1024]{1,0:T(8,128)(2,1)}, u32[]{:S(2)}, u32[]{:S(2)}) collective-permute-start(bf16[128,1024]{1,0:T(8,128)(2,1)S(1)} %collective-permute-done.1.refs_4_), channel_id=1, source_target_pairs={{0,3},{1,2},{2,1},{3,0},{4,7},{5,6},{6,5},{7,4},{8,11},{9,10},{10,... | collective-permute-start | bytes 786440 | tf_op jit(solution)/shard_map/ppermute | solution.py:435
  38.0 12.8 %all-to-all-start.1 = ((bf16[8,2,128,128]{3,2,1,0:T(8,128)(2,1)}), bf16[8,2,128,128]{3,2,1,0:T(8,128)(2,1)S(1)}, u32[]{:S(2)}, u32[]{:S(2)}) async-start(bf16[8,2,128,128]{3,2,1,0:T(8,128)(2,1)} %get-tuple-element.41.refs_5_), calls=%async_computation.1 | async-start | bytes 1048576 | tf_op jit(solution)/shard_map/all_to_all | solution.py:403
  44.9 2.4 %collective-permute-start.10 = (bf16[8,128,128]{2,1,0:T(8,128)(2,1)S(1)}, bf16[8,128,128]{2,1,0:T(8,128)(2,1)S(1)}, u32[]{:S(2)}, u32[]{:S(2)}) collective-permute-start(bf16[8,128,128]{2,1,0:T(8,128)(2,1)S(1)} %get-tuple-element.45), channel_id=1, source_target_pairs={{0,8},{8,0},{16,24},{24,16},{32,40},{40,32},{48,56},{56,48},{64,72... | collective-permute-start | bytes 786440 | tf_op jit(solution)/shard_map/ppermute | solution.py:493
  50.8 6.8 %collective-permute-start.12 = (bf16[8,2,128,128]{3,2,1,0:T(8,128)(2,1)S(1)}, bf16[8,2,128,128]{3,2,1,0:T(8,128)(2,1)S(1)}, u32[]{:S(2)}, u32[]{:S(2)}) collective-permute-start(bf16[8,2,128,128]{3,2,1,0:T(8,128)(2,1)S(1)} %all-to-all-done.1.refs_4_.refs_1_), channel_id=1, source_target_pairs={{0,8},{8,0},{16,24},{24,16},{32,40},{40,32},{48,56},{56,48},{64,72... | collective-permute-start | bytes 1572872 | tf_op jit(solution)/shard_map/ppermute | solution.py:500
  54.2 11.6 %all-to-all-start.2 = ((bf16[8,128,128]{2,1,0:T(8,128)(2,1)}), bf16[8,128,128]{2,1,0:T(8,128)(2,1)S(1)}, u32[]{:S(2)}, u32[]{:S(2)}) async-start(bf16[8,128,128]{2,1,0:T(8,128)(2,1)} %shard_map.114), calls=%async_computation.2 | async-start | bytes 524288 | tf_op jit(solution)/shard_map/all_to_all | solution.py:403
  66.5 19.3 %all-to-all-start.3 = ((bf16[32,32,512]{2,1,0:T(8,128)(2,1)}), bf16[32,32,512]{2,1,0:T(8,128)(2,1)S(1)}, u32[]{:S(2)}, u32[]{:S(2)}) async-start(bf16[32,32,512]{2,1,0:T(8,128)(2,1)} %shard_map.117), calls=%async_computation.3 | async-start | bytes 2097152 | tf_op jit(solution)/shard_map/all_to_all | solution.py:511
  78.0 2.9 %collective-permute-start.11 = (bf16[8,2,128,128]{3,2,1,0:T(8,128)(2,1)}, bf16[8,2,128,128]{3,2,1,0:T(8,128)(2,1)S(1)}, u32[]{:S(2)}, u32[]{:S(2)}) collective-permute-start(bf16[8,2,128,128]{3,2,1,0:T(8,128)(2,1)} %get-tuple-element.54), channel_id=1, source_target_pairs={{0,8},{8,0},{16,24},{24,16},{32,40},{40,32},{48,56},{56,48},{64,72... | collective-permute-start | bytes 1572872 | tf_op jit(solution)/shard_map/ppermute | solution.py:533
  87.1 18.7 %all-to-all-start.4 = ((bf16[8,4,128,128]{3,2,1,0:T(8,128)(2,1)}), bf16[8,4,128,128]{3,2,1,0:T(8,128)(2,1)S(1)}, u32[]{:S(2)}, u32[]{:S(2)}) async-start(bf16[8,4,128,128]{3,2,1,0:T(8,128)(2,1)} %shard_map.118), calls=%async_computation.4 | async-start | bytes 2097152 | tf_op jit(solution)/shard_map/all_to_all | solution.py:403
  96.7 3.5 %collective-permute-start.13 = (bf16[128,1024]{1,0:T(8,128)(2,1)}, bf16[128,1024]{1,0:T(8,128)(2,1)S(1)}, u32[]{:S(2)}, u32[]{:S(2)}) collective-permute-start(bf16[128,1024]{1,0:T(8,128)(2,1)} %get-tuple-element.58), channel_id=1, source_target_pairs={{0,8},{8,0},{16,24},{24,16},{32,40},{40,32},{48,56},{56,48},{64,72... | collective-permute-start | bytes 786440 | tf_op jit(solution)/shard_map/ppermute | solution.py:557
  105.8 5.1 %collective-permute-start.14 = (bf16[8,128,128]{2,1,0:T(8,128)(2,1)S(1)}, bf16[8,128,128]{2,1,0:T(8,128)(2,1)S(1)}, u32[]{:S(2)}, u32[]{:S(2)}) collective-permute-start(bf16[8,128,128]{2,1,0:T(8,128)(2,1)S(1)} %slice_bitcast_fusion.refs_1_), channel_id=1, source_target_pairs={{0,8},{8,0},{16,24},{24,16},{32,40},{40,32},{48,56},{56,48},{64,72... | collective-permute-start | bytes 786440 | tf_op jit(solution)/shard_map/ppermute | solution.py:565
  (8 other events, 27.6 us)

commit v13 on v12

--- a/solution.py
+++ b/solution.py
@@ -128,7 +128,7 @@
 
 def pack_kernel(ins, outs, scratch, sems):
     core_ref, *data = ins
-    out_ref, half_ref, up_mine_ref, up_send_ref = outs
+    out_ref, half_ref, again_ref, up_mine_ref, up_send_ref = outs
     core = core_ref[0]
     half = half_ref.shape[1]
     copies = []
@@ -140,6 +140,7 @@
     mine = pl.ds(pl.multiple_of(core * half, half), half)
     other = pl.ds(pl.multiple_of((1 - core) * half, half), half)
     copy(data[3].get().at[:, mine], half_ref)
+    copy(data[3].get().at[:, mine], again_ref)
     for i in range(3):
         ref = data[i].get()
         for a in range(HEADS):
@@ -421,13 +422,13 @@
     quarter = half // 2
 
     side = ("R", (BLOCK, half), BF16)
-    packed, own_half, up_mine, up_send = call(
+    packed, own_half, again_half, up_mine, up_send = call(
         pack_kernel,
         [
             ("S", core_ref), ("H", query_rows, 0), ("H", key_rows, 0),
             ("H", value_rows, 0), ("H", out_weight), ("H", upstream, 0),
         ],
-        [("R", (HEADS, 3, BLOCK, HS), BF16), side, side, side],
+        [("R", (HEADS, 3, BLOCK, HS), BF16), side, side, side, side],
     )
     own = exchange(packed)
 
@@ -448,7 +449,8 @@
     rows_here = index * BLOCK + jnp.arange(BLOCK, dtype=jnp.int32)
     valid_here = (rows_here < valid_len).astype(F32)[:, None]
 
-    one, three = step(own_half, 1), step(own_half, 3)
+    again_half = after(again_half, over)
+    one, three = step(again_half, 1), step(again_half, 3)
     over_one, over_three = step(over, 1), step(over, 3)
     two, over_two = step(one, 3), step(over_three, 1)
     pieces = [own_half, one, two, three, over, over_one, over_two, over_three]

time: 113 us -> 115 us (1.018)
  waiting for transfers between devices: 21.6 us -> 24.1 us
    ppermute x1, starting transfers between devices: 1.08 us -> 2.97 us  [shards(): up_pair = lax.ppermute(after(up_pair, own), 'ctx', PAIR_SWAP)]
    ppermute x7, waiting for transfers between devices: 5.1 us -> 6.39 us  [step(): return lax.ppermute(value, 'fsdp', [(i, i ^ s) for i in range(8)])]
    ppermute x7, starting transfers between devices: 10.3 us -> 9.02 us  [step(): return lax.ppermute(value, 'fsdp', [(i, i ^ s) for i in range(8)])]
    all_to_all x4, waiting for transfers between devices: 11 us -> 12.2 us  [exchange(): lax.all_to_all(operand, 'ctx', split_axis=0, concat_axis=0, tiled=True, a...]
    unnamed x24 -> x26, local copies, waits for them, and re-layouts: 4.81 us -> 4.81 us
  transfers between devices with their start and end apart: 20 -> 20, of which waited for: 8 -> 10; matrix products, arithmetic and copies ran while one was open for 1% -> 1% of each run, Pallas kernels for 23% -> 23%
where the time goes in v13:
time: 115 us; the launch traced here: 114 us
  starting transfers between devices  50.9 us (44%)
  Pallas kernels  31.4 us (27%)
  waiting for transfers between devices  24.1 us (21%)
  local copies, waits for them, and re-layouts  4.84 us (4%)
  between operations  1.78 us (2%)
    pallas_call x13, Pallas kernels, call(): pl.pallas_call(body, out_shape=[SPACES[o[0]](o[1], o[2]) if o[0] in 'HR'...  31.4 us
    all_to_all x4, starting transfers between devices, exchange(): lax.all_to_all(operand, 'ctx', split_axis=0, concat_axis=0, tiled=True, a...  19.9 us
    all_to_all x4, waiting for transfers between devices, exchange(): lax.all_to_all(operand, 'ctx', split_axis=0, concat_axis=0, tiled=True, a...  12.2 us
    ppermute x7, starting transfers between devices, step(): return lax.ppermute(value, 'fsdp', [(i, i ^ s) for i in range(8)])  9.02 us
    ppermute x7, waiting for transfers between devices, step(): return lax.ppermute(value, 'fsdp', [(i, i ^ s) for i in range(8)])  6.39 us
    all_to_all x1, starting transfers between devices, shards(): lax.all_to_all(after(terms, grads), ('ctx', 'fsdp'), split_axis=0, concat...  4.85 us
    unnamed x26, local copies, waits for them, and re-layouts  4.81 us
    ppermute x1, starting transfers between devices, shards(): weight_other = lax.ppermute(weight_mine, 'ctx', CORE_SWAP)  3.8 us
  transfers between devices with their start and end apart: 20, of which 10 were waited for; matrix products, arithmetic and copies ran while one was open for 1% of the time, Pallas kernels for 23%

profile of v13, /device:TPU:1, one launch (start us, length us, event | category | flops | bytes accessed | tf_op | source)
XLA Modules:
  0.0 114.0 jit_solution(8538324604775575548)
XLA Ops:
  0.6 2.9 %shard_map.110 = (bf16[8,3,128,128]{3,2,1,0:T(8,128)(2,1)}, bf16[128,1024]{1,0:T(8,128)(2,1)}, bf16[128,1024]{1,0:T(8,128)(2,1)}, bf16[128,1024]{1,0:T(8,128)(2,1)}, bf16[128,1024]{1,0:T(8,128)(2,1)}) custom-call(s32[1]{0:T(128)} %bitcast.refs_0_, bf16[1,128,1024]{2,1,0:T(8,128)(2,1)} %refs_1_.1, bf16[1,128,1024]{2,1,0:T(8,128)(2,1)} %refs_2_.1, ...), custom_call_target="tpu_custom_call" | custom-call | bytes 2000000 | tf_op jit(solution)/shard_map/pallas_call | solution.py:111
  3.6 2.1 %collective-permute-start = (bf16[128,1024]{1,0:T(8,128)(2,1)}, bf16[128,1024]{1,0:T(8,128)(2,1)S(1)}, u32[]{:S(2)}, u32[]{:S(2)}) collective-permute-start(bf16[128,1024]{1,0:T(8,128)(2,1)} %get-tuple-element.37.refs_3_), channel_id=1, source_target_pairs={{0,4},{1,5},{2,6},{3,7},{4,0},{5,1},{6,2},{7,3},{8,12},{9,13},{10,... | collective-permute-start | bytes 786440 | tf_op jit(solution)/shard_map/ppermute | solution.py:436
  5.7 6.4 %all-to-all-start = ((bf16[8,3,128,128]{3,2,1,0:T(8,128)(2,1)}), bf16[8,3,128,128]{3,2,1,0:T(8,128)(2,1)S(1)}, u32[]{:S(2)}, u32[]{:S(2)}) async-start(bf16[8,3,128,128]{3,2,1,0:T(8,128)(2,1)} %get-tuple-element.36), calls=%async_computation | async-start | bytes 1572864 | tf_op jit(solution)/shard_map/all_to_all | solution.py:404
  12.8 3.8 %collective-permute-start.2 = (bf16[128,1024]{1,0:T(8,128)(2,1)S(1)}, bf16[128,1024]{1,0:T(8,128)(2,1)S(1)}, u32[]{:S(2)}, u32[]{:S(2)}) collective-permute-start(bf16[128,1024]{1,0:T(8,128)(2,1)S(1)} %copy-done.11), channel_id=1, source_target_pairs={{0,3},{1,2},{2,1},{3,0},{4,7},{5,6},{6,5},{7,4},{8,11},{9,10},{10,... | collective-permute-start | bytes 786440 | tf_op jit(solution)/shard_map/ppermute | solution.py:436
  18.4 1.5 %collective-permute-start.3 = (bf16[128,1024]{1,0:T(8,128)(2,1)S(1)}, bf16[128,1024]{1,0:T(8,128)(2,1)S(1)}, u32[]{:S(2)}, u32[]{:S(2)}) collective-permute-start(bf16[128,1024]{1,0:T(8,128)(2,1)S(1)} %collective-permute-done.refs_7_), channel_id=1, source_target_pairs={{0,1},{1,0},{2,3},{3,2},{4,5},{5,4},{6,7},{7,6},{8,9},{9,8},{10,11... | collective-permute-start | bytes 786440 | tf_op jit(solution)/shard_map/ppermute | solution.py:436
  22.9 4.9 %collective-permute-done.4.refs_10_ = bf16[128,1024]{1,0:T(8,128)(2,1)S(1)} collective-permute-done((bf16[128,1024]{1,0:T(8,128)(2,1)S(1)}, bf16[128,1024]{1,0:T(8,128)(2,1)S(1)}, u32[]{:S(2)}, u32[]{:S(2)}) %collective-permute-start.4) | collective-permute-done | bytes 262176 | tf_op jit(solution)/shard_map/ppermute | solution.py:436
  28.5 2.4 %collective-permute-start.6 = (bf16[8,3,128,128]{3,2,1,0:T(8,128)(2,1)S(1)}, bf16[8,3,128,128]{3,2,1,0:T(8,128)(2,1)S(1)}, u32[]{:S(2)}, u32[]{:S(2)}) collective-permute-start(bf16[8,3,128,128]{3,2,1,0:T(8,128)(2,1)S(1)} %all-to-all-done.refs_1_.refs_2_.refs_3_), channel_id=1, source_target_pairs={{0,8},{8,0},{16,24},{24,16},{32,40},{40,32},{48,56},{56,48},{64,72... | collective-permute-start | bytes 2359304 | tf_op jit(solution)/shard_map/ppermute | solution.py:469
  31.0 3.0 %collective-permute-start.9 = (bf16[256,512]{1,0:T(8,128)(2,1)}, bf16[256,512]{1,0:T(8,128)(2,1)}, u32[]{:S(2)}, u32[]{:S(2)}) collective-permute-start(bf16[256,512]{1,0:T(8,128)(2,1)} %shard_map.111), channel_id=1, source_target_pairs={{0,64},{8,72},{16,80},{24,88},{32,96},{40,104},{48,112},{56,120},{... | collective-permute-start | bytes 786440 | tf_op jit(solution)/shard_map/ppermute | solution.py:467
  35.3 4.1 %shard_map.112 = (bf16[8,2,128,128]{3,2,1,0:T(8,128)(2,1)}, f32[4,1,256]{2,1,0:T(1,128)}, bf16[8,128,128]{2,1,0:T(8,128)(2,1)}, bf16[2048,128]{1,0:T(8,128)(2,1)}, bf16[2048,128]{1,0:T(8,128)(2,1)}) custom-call(s32[1]{0:T(128)} %bitcast.refs_0_, bf16[8,3,128,128]{3,2,1,0:T(8,128)(2,1)S(1)} %all-to-all-done.refs_1_.refs_2_.refs_3_, ...), custom_call_target="tpu_custom_call" | custom-call | flops 671088640 | bytes 2000000 | tf_op jit(solution)/shard_map/pallas_call | solution.py:111
  39.3 4.4 %all-to-all-start.1 = ((bf16[8,2,128,128]{3,2,1,0:T(8,128)(2,1)}), bf16[8,2,128,128]{3,2,1,0:T(8,128)(2,1)S(1)}, u32[]{:S(2)}, u32[]{:S(2)}) async-start(bf16[8,2,128,128]{3,2,1,0:T(8,128)(2,1)} %get-tuple-element.45.refs_5_), calls=%async_computation.1 | async-start | bytes 1048576 | tf_op jit(solution)/shard_map/all_to_all | solution.py:404
  43.8 2.8 %shard_map.113 = (f32[8,128,128]{2,1,0:T(8,128)S(1)}, bf16[8,128,128]{2,1,0:T(8,128)(2,1)S(1)}) custom-call(s32[1]{0:T(128)} %bitcast.1.refs_0_, bf16[128,1024]{1,0:T(8,128)(2,1)S(1)} %copy-done, bf16[128,1024]{1,0:T(8,128)(2,1)S(1)} %collective-permute-done.5.refs_2_, bf16[128,1024]{1,0:T(8,128)(2,1)S(1)} %copy-done.2, ...), custom_call_target="tpu_custom_call" | custom-call | flops 536870912 | bytes 2000000 | tf_op jit(solution)/shard_map/pallas_call | solution.py:111
  49.8 3.5 %all-to-all-done.1.refs_4_.refs_1_ = bf16[8,2,128,128]{3,2,1,0:T(8,128)(2,1)S(1)} async-done(((bf16[8,2,128,128]{3,2,1,0:T(8,128)(2,1)}), bf16[8,2,128,128]{3,2,1,0:T(8,128)(2,1)S(1)}, u32[]{:S(2)}, u32[]{:S(2)}) %all-to-all-start.1) | async-done | bytes 524320 | tf_op jit(solution)/shard_map/all_to_all | solution.py:404
  53.3 2.3 %collective-permute-start.12 = (bf16[8,2,128,128]{3,2,1,0:T(8,128)(2,1)S(1)}, bf16[8,2,128,128]{3,2,1,0:T(8,128)(2,1)S(1)}, u32[]{:S(2)}, u32[]{:S(2)}) collective-permute-start(bf16[8,2,128,128]{3,2,1,0:T(8,128)(2,1)S(1)} %all-to-all-done.1.refs_4_.refs_1_), channel_id=1, source_target_pairs={{0,8},{8,0},{16,24},{24,16},{32,40},{40,32},{48,56},{56,48},{64,72... | collective-permute-start | bytes 1572872 | tf_op jit(solution)/shard_map/ppermute | solution.py:502
  55.6 3.4 %all-to-all-start.2 = ((bf16[8,128,128]{2,1,0:T(8,128)(2,1)}), bf16[8,128,128]{2,1,0:T(8,128)(2,1)S(1)}, u32[]{:S(2)}, u32[]{:S(2)}) async-start(bf16[8,128,128]{2,1,0:T(8,128)(2,1)} %shard_map.114), calls=%async_computation.2 | async-start | bytes 524288 | tf_op jit(solution)/shard_map/all_to_all | solution.py:404
  59.0 2.8 %shard_map.117 = bf16[32,32,512]{2,1,0:T(8,128)(2,1)} custom-call(s32[1]{0:T(128)} %bitcast.8.refs_0_, bf16[128,1024]{1,0:T(8,128)(2,1)S(1)} %copy-done, bf16[128,1024]{1,0:T(8,128)(2,1)S(1)} %collective-permute-done.5.refs_2_, bf16[256,512]{1,0:T(8,128)(2,1)} %collective-permute-done.9.refs_3_, bf16[8,2,128,128]{3,2,1,0:T(8,128)(2,1)S(1)} %all-to-all-done.1.refs_4_.refs_1_, ...), custom_call_target="tpu_custom_call" | custom-call | flops 536870912 | bytes 2000000 | tf_op jit(solution)/shard_map/pallas_call | solution.py:111
  61.9 5.3 %all-to-all-done.2.refs_3_ = bf16[8,128,128]{2,1,0:T(8,128)(2,1)S(1)} async-done(((bf16[8,128,128]{2,1,0:T(8,128)(2,1)}), bf16[8,128,128]{2,1,0:T(8,128)(2,1)S(1)}, u32[]{:S(2)}, u32[]{:S(2)}) %all-to-all-start.2) | async-done | bytes 262176 | tf_op jit(solution)/shard_map/all_to_all | solution.py:404
  67.8 4.8 %all-to-all-start.3 = ((bf16[32,32,512]{2,1,0:T(8,128)(2,1)}), bf16[32,32,512]{2,1,0:T(8,128)(2,1)S(1)}, u32[]{:S(2)}, u32[]{:S(2)}) async-start(bf16[32,32,512]{2,1,0:T(8,128)(2,1)} %shard_map.117), calls=%async_computation.3 | async-start | bytes 2097152 | tf_op jit(solution)/shard_map/all_to_all | solution.py:513
  72.7 6.8 %shard_map.115 = (bf16[8,128,128]{2,1,0:T(8,128)(2,1)}, f32[8,2,128,128]{3,2,1,0:T(8,128)}, bf16[8,2,128,128]{3,2,1,0:T(8,128)(2,1)}) custom-call(s32[1]{0:T(128)} %bitcast.refs_0_, bf16[8,128,128]{2,1,0:T(8,128)(2,1)} %get-tuple-element.51.refs_1_, bf16[2048,128]{1,0:T(8,128)(2,1)} %get-tuple-element.52.refs_2_, bf16[8,128,128]{2,1,0:T(8,128)(2,1)} %copy-done.9, ...), custom_call_target="tpu_custom_call" | custom-call | flops 1677721600 | bytes 2000000 | tf_op jit(solution)/shard_map/pallas_call | solution.py:111
  80.6 1.7 %collective-permute-done.11.refs_2_ = bf16[8,2,128,128]{3,2,1,0:T(8,128)(2,1)S(1)} collective-permute-done((bf16[8,2,128,128]{3,2,1,0:T(8,128)(2,1)}, bf16[8,2,128,128]{3,2,1,0:T(8,128)(2,1)S(1)}, u32[]{:S(2)}, u32[]{:S(2)}) %collective-permute-start.11) | collective-permute-done | bytes 524320 | tf_op jit(solution)/shard_map/ppermute | solution.py:535
  88.5 5.7 %all-to-all-start.4 = ((bf16[8,4,128,128]{3,2,1,0:T(8,128)(2,1)}), bf16[8,4,128,128]{3,2,1,0:T(8,128)(2,1)S(1)}, u32[]{:S(2)}, u32[]{:S(2)}) async-start(bf16[8,4,128,128]{3,2,1,0:T(8,128)(2,1)} %shard_map.118), calls=%async_computation.4 | async-start | bytes 2097152 | tf_op jit(solution)/shard_map/all_to_all | solution.py:404
  95.2 3.0 %shard_map.119 = (bf16[128,1024]{1,0:T(8,128)(2,1)}, bf16[128,1024]{1,0:T(8,128)(2,1)}) custom-call(s32[1]{0:T(128)} %bitcast.1.refs_0_, bf16[8,2,128,128]{3,2,1,0:T(8,128)(2,1)S(1)} %all-to-all-done.1.refs_4_.refs_1_, bf16[8,2,128,128]{3,2,1,0:T(8,128)(2,1)S(1)} %collective-permute-done.12.refs_5_.refs_2_, bf16[128,1024]{1,0:T(8,128)(2,1)S(1)} %copy-done.2, ...), custom_call_target="tpu_custom_call" | custom-call | flops 536870912 | bytes 2000000 | tf_op jit(solution)/shard_map/pallas_call | solution.py:111
  98.2 2.1 %collective-permute-start.13 = (bf16[128,1024]{1,0:T(8,128)(2,1)}, bf16[128,1024]{1,0:T(8,128)(2,1)S(1)}, u32[]{:S(2)}, u32[]{:S(2)}) collective-permute-start(bf16[128,1024]{1,0:T(8,128)(2,1)} %get-tuple-element.62), channel_id=1, source_target_pairs={{0,8},{8,0},{16,24},{24,16},{32,40},{40,32},{48,56},{56,48},{64,72... | collective-permute-start | bytes 786440 | tf_op jit(solution)/shard_map/ppermute | solution.py:559
  103.9 3.4 %all-to-all-done.4.refs_0_ = bf16[8,4,128,128]{3,2,1,0:T(8,128)(2,1)S(1)} async-done(((bf16[8,4,128,128]{3,2,1,0:T(8,128)(2,1)}), bf16[8,4,128,128]{3,2,1,0:T(8,128)(2,1)S(1)}, u32[]{:S(2)}, u32[]{:S(2)}) %all-to-all-start.4) | async-done | bytes 1048608 | tf_op jit(solution)/shard_map/all_to_all | solution.py:404
  107.3 3.8 %collective-permute-start.14 = (bf16[8,128,128]{2,1,0:T(8,128)(2,1)S(1)}, bf16[8,128,128]{2,1,0:T(8,128)(2,1)S(1)}, u32[]{:S(2)}, u32[]{:S(2)}) collective-permute-start(bf16[8,128,128]{2,1,0:T(8,128)(2,1)S(1)} %slice_bitcast_fusion.refs_1_), channel_id=1, source_target_pairs={{0,8},{8,0},{16,24},{24,16},{32,40},{40,32},{48,56},{56,48},{64,72... | collective-permute-start | bytes 786440 | tf_op jit(solution)/shard_map/ppermute | solution.py:567
  (61 shorter events, 25.2 us)
Async XLA Ops:
  3.6 16.3 %copy-start.10 = (s32[1,2048]{1,0:T(1,128)S(1)}, s32[1,2048]{1,0:T(1,128)}, u32[]{:S(2)}) copy-start(s32[1,2048]{1,0:T(1,128)} %param.10) | copy-start | bytes 24580
  3.6 17.3 %copy-start = (bf16[128,1024]{1,0:T(8,128)(2,1)S(1)}, bf16[128,1024]{1,0:T(8,128)(2,1)}, u32[]{:S(2)}) copy-start(bf16[128,1024]{1,0:T(8,128)(2,1)} %get-tuple-element.43.refs_1_) | copy-start | bytes 786436
  3.6 9.2 %collective-permute-start = (bf16[128,1024]{1,0:T(8,128)(2,1)}, bf16[128,1024]{1,0:T(8,128)(2,1)S(1)}, u32[]{:S(2)}, u32[]{:S(2)}) collective-permute-start(bf16[128,1024]{1,0:T(8,128)(2,1)} %get-tuple-element.37.refs_3_), channel_id=1, source_target_pairs={{0,4},{1,5},{2,6},{3,7},{4,0},{5,1},{6,2},{7,3},{8,12},{9,13},{10,... | collective-permute-start | bytes 786440 | tf_op jit(solution)/shard_map/ppermute | solution.py:436
  5.7 22.8 %all-to-all-start = ((bf16[8,3,128,128]{3,2,1,0:T(8,128)(2,1)}), bf16[8,3,128,128]{3,2,1,0:T(8,128)(2,1)S(1)}, u32[]{:S(2)}, u32[]{:S(2)}) async-start(bf16[8,3,128,128]{3,2,1,0:T(8,128)(2,1)} %get-tuple-element.36), calls=%async_computation | async-start | bytes 1572864 | tf_op jit(solution)/shard_map/all_to_all | solution.py:404
  12.8 9.3 %collective-permute-start.2 = (bf16[128,1024]{1,0:T(8,128)(2,1)S(1)}, bf16[128,1024]{1,0:T(8,128)(2,1)S(1)}, u32[]{:S(2)}, u32[]{:S(2)}) collective-permute-start(bf16[128,1024]{1,0:T(8,128)(2,1)S(1)} %copy-done.11), channel_id=1, source_target_pairs={{0,3},{1,2},{2,1},{3,0},{4,7},{5,6},{6,5},{7,4},{8,11},{9,10},{10,... | collective-permute-start | bytes 786440 | tf_op jit(solution)/shard_map/ppermute | solution.py:436
  16.6 6.3 %collective-permute-start.1 = (bf16[128,1024]{1,0:T(8,128)(2,1)S(1)}, bf16[128,1024]{1,0:T(8,128)(2,1)S(1)}, u32[]{:S(2)}, u32[]{:S(2)}) collective-permute-start(bf16[128,1024]{1,0:T(8,128)(2,1)S(1)} %copy-done.11), channel_id=1, source_target_pairs={{0,1},{1,0},{2,3},{3,2},{4,5},{5,4},{6,7},{7,6},{8,9},{9,8},{10,11... | collective-permute-start | bytes 786440 | tf_op jit(solution)/shard_map/ppermute | solution.py:436
  16.6 4.3 %collective-permute-start.5 = (bf16[128,1024]{1,0:T(8,128)(2,1)S(1)}, bf16[128,1024]{1,0:T(8,128)(2,1)S(1)}, u32[]{:S(2)}, u32[]{:S(2)}) collective-permute-start(bf16[128,1024]{1,0:T(8,128)(2,1)S(1)} %copy-done.12), channel_id=1, source_target_pairs={{0,8},{8,0},{16,24},{24,16},{32,40},{40,32},{48,56},{56,48},{64,72... | collective-permute-start | bytes 786440 | tf_op jit(solution)/shard_map/ppermute | solution.py:457
  18.2 9.6 %collective-permute-start.4 = (bf16[128,1024]{1,0:T(8,128)(2,1)S(1)}, bf16[128,1024]{1,0:T(8,128)(2,1)S(1)}, u32[]{:S(2)}, u32[]{:S(2)}) collective-permute-start(bf16[128,1024]{1,0:T(8,128)(2,1)S(1)} %collective-permute-done.refs_7_), channel_id=1, source_target_pairs={{0,3},{1,2},{2,1},{3,0},{4,7},{5,6},{6,5},{7,4},{8,11},{9,10},{10,... | collective-permute-start | bytes 786440 | tf_op jit(solution)/shard_map/ppermute | solution.py:436
  18.4 10.1 %collective-permute-start.3 = (bf16[128,1024]{1,0:T(8,128)(2,1)S(1)}, bf16[128,1024]{1,0:T(8,128)(2,1)S(1)}, u32[]{:S(2)}, u32[]{:S(2)}) collective-permute-start(bf16[128,1024]{1,0:T(8,128)(2,1)S(1)} %collective-permute-done.refs_7_), channel_id=1, source_target_pairs={{0,1},{1,0},{2,3},{3,2},{4,5},{5,4},{6,7},{7,6},{8,9},{9,8},{10,11... | collective-permute-start | bytes 786440 | tf_op jit(solution)/shard_map/ppermute | solution.py:436
  27.8 16.0 %copy-start.3 = (bf16[128,1024]{1,0:T(8,128)(2,1)}, bf16[128,1024]{1,0:T(8,128)(2,1)S(1)}, u32[]{:S(2)}) copy-start(bf16[128,1024]{1,0:T(8,128)(2,1)S(1)} %collective-permute-done.4.refs_10_) | copy-start | bytes 786436
  28.5 15.3 %copy-start.5 = (bf16[128,1024]{1,0:T(8,128)(2,1)}, bf16[128,1024]{1,0:T(8,128)(2,1)S(1)}, u32[]{:S(2)}) copy-start(bf16[128,1024]{1,0:T(8,128)(2,1)S(1)} %collective-permute-done.3.refs_8_) | copy-start | bytes 786436
  28.5 6.7 %collective-permute-start.6 = (bf16[8,3,128,128]{3,2,1,0:T(8,128)(2,1)S(1)}, bf16[8,3,128,128]{3,2,1,0:T(8,128)(2,1)S(1)}, u32[]{:S(2)}, u32[]{:S(2)}) collective-permute-start(bf16[8,3,128,128]{3,2,1,0:T(8,128)(2,1)S(1)} %all-to-all-done.refs_1_.refs_2_.refs_3_), channel_id=1, source_target_pairs={{0,8},{8,0},{16,24},{24,16},{32,40},{40,32},{48,56},{56,48},{64,72... | collective-permute-start | bytes 2359304 | tf_op jit(solution)/shard_map/ppermute | solution.py:469
  31.0 12.8 %collective-permute-start.8 = (bf16[128,1024]{1,0:T(8,128)(2,1)S(1)}, bf16[128,1024]{1,0:T(8,128)(2,1)}, u32[]{:S(2)}, u32[]{:S(2)}) collective-permute-start(bf16[128,1024]{1,0:T(8,128)(2,1)S(1)} %collective-permute-done.4.refs_10_), channel_id=1, source_target_pairs={{0,1},{1,0},{2,3},{3,2},{4,5},{5,4},{6,7},{7,6},{8,9},{9,8},{10,11... | collective-permute-start | bytes 786440 | tf_op jit(solution)/shard_map/ppermute | solution.py:436
  31.0 12.8 %collective-permute-start.9 = (bf16[256,512]{1,0:T(8,128)(2,1)}, bf16[256,512]{1,0:T(8,128)(2,1)}, u32[]{:S(2)}, u32[]{:S(2)}) collective-permute-start(bf16[256,512]{1,0:T(8,128)(2,1)} %shard_map.111), channel_id=1, source_target_pairs={{0,64},{8,72},{16,80},{24,88},{32,96},{40,104},{48,112},{56,120},{... | collective-permute-start | bytes 786440 | tf_op jit(solution)/shard_map/ppermute | solution.py:467
  34.0 9.8 %collective-permute-start.7 = (bf16[128,1024]{1,0:T(8,128)(2,1)S(1)}, bf16[128,1024]{1,0:T(8,128)(2,1)}, u32[]{:S(2)}, u32[]{:S(2)}) collective-permute-start(bf16[128,1024]{1,0:T(8,128)(2,1)S(1)} %collective-permute-done.1.refs_4_), channel_id=1, source_target_pairs={{0,3},{1,2},{2,1},{3,0},{4,7},{5,6},{6,5},{7,4},{8,11},{9,10},{10,... | collective-permute-start | bytes 786440 | tf_op jit(solution)/shard_map/ppermute | solution.py:436
  39.3 14.0 %all-to-all-start.1 = ((bf16[8,2,128,128]{3,2,1,0:T(8,128)(2,1)}), bf16[8,2,128,128]{3,2,1,0:T(8,128)(2,1)S(1)}, u32[]{:S(2)}, u32[]{:S(2)}) async-start(bf16[8,2,128,128]{3,2,1,0:T(8,128)(2,1)} %get-tuple-element.45.refs_5_), calls=%async_computation.1 | async-start | bytes 1048576 | tf_op jit(solution)/shard_map/all_to_all | solution.py:404
  46.6 1.9 %collective-permute-start.10 = (bf16[8,128,128]{2,1,0:T(8,128)(2,1)S(1)}, bf16[8,128,128]{2,1,0:T(8,128)(2,1)S(1)}, u32[]{:S(2)}, u32[]{:S(2)}) collective-permute-start(bf16[8,128,128]{2,1,0:T(8,128)(2,1)S(1)} %get-tuple-element.49), channel_id=1, source_target_pairs={{0,8},{8,0},{16,24},{24,16},{32,40},{40,32},{48,56},{56,48},{64,72... | collective-permute-start | bytes 786440 | tf_op jit(solution)/shard_map/ppermute | solution.py:495
  53.3 5.7 %collective-permute-start.12 = (bf16[8,2,128,128]{3,2,1,0:T(8,128)(2,1)S(1)}, bf16[8,2,128,128]{3,2,1,0:T(8,128)(2,1)S(1)}, u32[]{:S(2)}, u32[]{:S(2)}) collective-permute-start(bf16[8,2,128,128]{3,2,1,0:T(8,128)(2,1)S(1)} %all-to-all-done.1.refs_4_.refs_1_), channel_id=1, source_target_pairs={{0,8},{8,0},{16,24},{24,16},{32,40},{40,32},{48,56},{56,48},{64,72... | collective-permute-start | bytes 1572872 | tf_op jit(solution)/shard_map/ppermute | solution.py:502
  55.6 11.5 %all-to-all-start.2 = ((bf16[8,128,128]{2,1,0:T(8,128)(2,1)}), bf16[8,128,128]{2,1,0:T(8,128)(2,1)S(1)}, u32[]{:S(2)}, u32[]{:S(2)}) async-start(bf16[8,128,128]{2,1,0:T(8,128)(2,1)} %shard_map.114), calls=%async_computation.2 | async-start | bytes 524288 | tf_op jit(solution)/shard_map/all_to_all | solution.py:404
  67.8 19.4 %all-to-all-start.3 = ((bf16[32,32,512]{2,1,0:T(8,128)(2,1)}), bf16[32,32,512]{2,1,0:T(8,128)(2,1)S(1)}, u32[]{:S(2)}, u32[]{:S(2)}) async-start(bf16[32,32,512]{2,1,0:T(8,128)(2,1)} %shard_map.117), calls=%async_computation.3 | async-start | bytes 2097152 | tf_op jit(solution)/shard_map/all_to_all | solution.py:513
  79.5 2.9 %collective-permute-start.11 = (bf16[8,2,128,128]{3,2,1,0:T(8,128)(2,1)}, bf16[8,2,128,128]{3,2,1,0:T(8,128)(2,1)S(1)}, u32[]{:S(2)}, u32[]{:S(2)}) collective-permute-start(bf16[8,2,128,128]{3,2,1,0:T(8,128)(2,1)} %get-tuple-element.58), channel_id=1, source_target_pairs={{0,8},{8,0},{16,24},{24,16},{32,40},{40,32},{48,56},{56,48},{64,72... | collective-permute-start | bytes 1572872 | tf_op jit(solution)/shard_map/ppermute | solution.py:535
  88.5 18.8 %all-to-all-start.4 = ((bf16[8,4,128,128]{3,2,1,0:T(8,128)(2,1)}), bf16[8,4,128,128]{3,2,1,0:T(8,128)(2,1)S(1)}, u32[]{:S(2)}, u32[]{:S(2)}) async-start(bf16[8,4,128,128]{3,2,1,0:T(8,128)(2,1)} %shard_map.118), calls=%async_computation.4 | async-start | bytes 2097152 | tf_op jit(solution)/shard_map/all_to_all | solution.py:404
  98.2 3.5 %collective-permute-start.13 = (bf16[128,1024]{1,0:T(8,128)(2,1)}, bf16[128,1024]{1,0:T(8,128)(2,1)S(1)}, u32[]{:S(2)}, u32[]{:S(2)}) collective-permute-start(bf16[128,1024]{1,0:T(8,128)(2,1)} %get-tuple-element.62), channel_id=1, source_target_pairs={{0,8},{8,0},{16,24},{24,16},{32,40},{40,32},{48,56},{56,48},{64,72... | collective-permute-start | bytes 786440 | tf_op jit(solution)/shard_map/ppermute | solution.py:559
  107.3 5.1 %collective-permute-start.14 = (bf16[8,128,128]{2,1,0:T(8,128)(2,1)S(1)}, bf16[8,128,128]{2,1,0:T(8,128)(2,1)S(1)}, u32[]{:S(2)}, u32[]{:S(2)}) collective-permute-start(bf16[8,128,128]{2,1,0:T(8,128)(2,1)S(1)} %slice_bitcast_fusion.refs_1_), channel_id=1, source_target_pairs={{0,8},{8,0},{16,24},{24,16},{32,40},{40,32},{48,56},{56,48},{64,72... | collective-permute-start | bytes 786440 | tf_op jit(solution)/shard_map/ppermute | solution.py:567
  (9 other events, 37.3 us)

commit v14 on v12

--- a/solution.py
+++ b/solution.py
@@ -371,32 +371,34 @@
     return copies
 
 
+def widen(ref, core, wide, out, sems):
+    for y in range(4):
+        for x in range(2):
+            for t in range(4):
+                wide[32 * y : 32 * y + 32, 512 * x + HS * t : 512 * x + HS * (t + 1)] = ref[
+                    4 * x + y, 32 * t : 32 * t + 32
+                ].astype(F32)
+    half = wide.shape[1]
+    at = pl.ds(pl.multiple_of(core * half, half), half)
+    copy = pltpu.make_async_copy(wide, out.at[:, at], next(sems))
+    copy.start()
+    return copy
+
+
 def unpack_kernel(ins, outs, scratch, sems):
-    mine_ref = ins[0]
+    core_ref, mine_ref = ins
     copies = []
     for a in range(HEADS):
         for i in range(3):
             dst = outs[i].at[0, :, pl.ds(a * HS, HS)]
             copies.append(pltpu.make_async_copy(mine_ref.at[a, i], dst, next(sems)))
             copies[-1].start()
+    copies.append(widen(mine_ref.at[:, 3], core_ref[0], scratch[0], outs[3], sems))
     return copies
 
 
 def widen_kernel(ins, outs, scratch, sems):
-    core_ref, mine_ref, other_ref = ins
-    out = outs[0]
-    core = core_ref[0]
-    for y in range(4):
-        rows = pl.ds(32 * y, 32)
-        for x in range(2):
-            a = 4 * x + y
-            for t in range(4):
-                part = slice(32 * t, 32 * t + 32)
-                at = pl.multiple_of(1024 * core + 512 * x + HS * t, HS)
-                out.ref[rows, pl.ds(at, HS)] = mine_ref[a, part].astype(F32)
-                at = pl.multiple_of(1024 * (1 - core) + 512 * x + HS * t, HS)
-                out.ref[rows, pl.ds(at, HS)] = other_ref[a, part].astype(F32)
-        out.push(rows)
+    return [widen(ins[1], 1 - ins[0][0], scratch[0], outs[0], sems)]
 
 
 def exchange(operand):
@@ -561,14 +563,19 @@
         [("R", (1, BLOCK, width), BF16)],
     )
     result = after(exchange(joined), attended)
-    weight_mine = result[:, 3]
-    weight_other = lax.ppermute(weight_mine, "ctx", CORE_SWAP)
+    weight_other = lax.ppermute(result[:, 3], "ctx", CORE_SWAP)
     grad = ("R", (1, BLOCK, HEADS * HS), BF16)
-    query_grad, key_grad, value_grad = call(unpack_kernel, [("V", result)], [grad, grad, grad])
+    whole = ("R", (HS, width), F32)
+    wide = (pltpu.VMEM((HS, half), F32),)
+    query_grad, key_grad, value_grad, weight_grad = call(
+        unpack_kernel, [("S", core_ref), ("V", result)], [grad, grad, grad, whole], scratch=wide
+    )
     weight_grad = call(
         widen_kernel,
-        [("S", core_ref), ("V", weight_mine), ("V", weight_other)],
-        [("H", (HS, width), F32)],
+        [("S", core_ref), ("V", weight_other), ("R", weight_grad)],
+        [whole],
+        scratch=wide,
+        aliases={2: 0},
     )
     return (attended, query_grad, key_grad, value_grad, weight_grad)
 

time: 113 us -> 113 us (level)
  no operation moved by 1% of the time
where the time goes in v14:
time: 113 us
  starting transfers between devices  52 us (46%)
  Pallas kernels  31.4 us (28%)
  waiting for transfers between devices  21.6 us (19%)
  local copies, waits for them, and re-layouts  4.83 us (4%)
  between operations  1.78 us (2%)
    pallas_call x13, Pallas kernels, call(): pl.pallas_call(body, out_shape=[SPACES[o[0]](o[1], o[2]) if o[0] in 'HR'...  31.4 us
    all_to_all x4, starting transfers between devices, exchange(): lax.all_to_all(operand, 'ctx', split_axis=0, concat_axis=0, tiled=True, a...  19.5 us
    all_to_all x4, waiting for transfers between devices, exchange(): lax.all_to_all(operand, 'ctx', split_axis=0, concat_axis=0, tiled=True, a...  11 us
    ppermute x7, starting transfers between devices, step(): return lax.ppermute(value, 'fsdp', [(i, i ^ s) for i in range(8)])  10.3 us
    ppermute x7, waiting for transfers between devices, step(): return lax.ppermute(value, 'fsdp', [(i, i ^ s) for i in range(8)])  5.1 us
    unnamed x24, local copies, waits for them, and re-layouts  4.81 us
    all_to_all x1, starting transfers between devices, shards(): lax.all_to_all(after(terms, grads), ('ctx', 'fsdp'), split_axis=0, concat...  4.76 us
    ppermute x1, starting transfers between devices, shards(): weight_other = lax.ppermute(result[:, 3], 'ctx', CORE_SWAP)  3.8 us
  transfers between devices with their start and end apart: 20, of which 8 were waited for; matrix products, arithmetic and copies ran while one was open for 1% of the time, Pallas kernels for 23%

profile of v14, /device:TPU:1, one launch (start us, length us, event | category | flops | bytes accessed | tf_op | source)
XLA Modules:
  0.0 112.5 jit_solution(4637407971465223518)
XLA Ops:
  0.6 2.8 %shard_map.110 = (bf16[8,3,128,128]{3,2,1,0:T(8,128)(2,1)}, bf16[128,1024]{1,0:T(8,128)(2,1)}, bf16[128,1024]{1,0:T(8,128)(2,1)}, bf16[128,1024]{1,0:T(8,128)(2,1)}) custom-call(s32[1]{0:T(128)} %bitcast.refs_0_, bf16[1,128,1024]{2,1,0:T(8,128)(2,1)} %refs_1_.1, bf16[1,128,1024]{2,1,0:T(8,128)(2,1)} %refs_2_.1, bf16[1,128,1024]{2,1,0:T(8,128)(2,1)} %refs_3_.1, ...), custom_call_target="tpu_custom_call" | custom-call | bytes 2000000 | tf_op jit(solution)/shard_map/pallas_call | solution.py:111
  3.5 2.1 %collective-permute-start = (bf16[128,1024]{1,0:T(8,128)(2,1)}, bf16[128,1024]{1,0:T(8,128)(2,1)S(1)}, u32[]{:S(2)}, u32[]{:S(2)}) collective-permute-start(bf16[128,1024]{1,0:T(8,128)(2,1)} %get-tuple-element.36.refs_3_), channel_id=1, source_target_pairs={{0,4},{1,5},{2,6},{3,7},{4,0},{5,1},{6,2},{7,3},{8,12},{9,13},{10,... | collective-permute-start | bytes 786440 | tf_op jit(solution)/shard_map/ppermute | solution.py:437
  5.6 3.8 %collective-permute-start.2 = (bf16[128,1024]{1,0:T(8,128)(2,1)}, bf16[128,1024]{1,0:T(8,128)(2,1)S(1)}, u32[]{:S(2)}, u32[]{:S(2)}) collective-permute-start(bf16[128,1024]{1,0:T(8,128)(2,1)} %get-tuple-element.36.refs_3_), channel_id=1, source_target_pairs={{0,3},{1,2},{2,1},{3,0},{4,7},{5,6},{6,5},{7,4},{8,11},{9,10},{10,... | collective-permute-start | bytes 786440 | tf_op jit(solution)/shard_map/ppermute | solution.py:437
  9.4 6.4 %all-to-all-start = ((bf16[8,3,128,128]{3,2,1,0:T(8,128)(2,1)}), bf16[8,3,128,128]{3,2,1,0:T(8,128)(2,1)S(1)}, u32[]{:S(2)}, u32[]{:S(2)}) async-start(bf16[8,3,128,128]{3,2,1,0:T(8,128)(2,1)} %get-tuple-element.35), calls=%async_computation | async-start | bytes 1572864 | tf_op jit(solution)/shard_map/all_to_all | solution.py:405
  16.5 1.6 %collective-permute-start.5 = (bf16[128,1024]{1,0:T(8,128)(2,1)S(1)}, bf16[128,1024]{1,0:T(8,128)(2,1)S(1)}, u32[]{:S(2)}, u32[]{:S(2)}) collective-permute-start(bf16[128,1024]{1,0:T(8,128)(2,1)S(1)} %copy-done.11), channel_id=1, source_target_pairs={{0,8},{8,0},{16,24},{24,16},{32,40},{40,32},{48,56},{56,48},{64,72... | collective-permute-start | bytes 786440 | tf_op jit(solution)/shard_map/ppermute | solution.py:457
  22.1 5.1 %collective-permute-done.4.refs_10_ = bf16[128,1024]{1,0:T(8,128)(2,1)S(1)} collective-permute-done((bf16[128,1024]{1,0:T(8,128)(2,1)S(1)}, bf16[128,1024]{1,0:T(8,128)(2,1)S(1)}, u32[]{:S(2)}, u32[]{:S(2)}) %collective-permute-start.4) | collective-permute-done | bytes 262176 | tf_op jit(solution)/shard_map/ppermute | solution.py:437
  27.2 3.0 %collective-permute-start.6 = (bf16[8,3,128,128]{3,2,1,0:T(8,128)(2,1)S(1)}, bf16[8,3,128,128]{3,2,1,0:T(8,128)(2,1)S(1)}, u32[]{:S(2)}, u32[]{:S(2)}) collective-permute-start(bf16[8,3,128,128]{3,2,1,0:T(8,128)(2,1)S(1)} %all-to-all-done.refs_1_.refs_2_.refs_3_), channel_id=1, source_target_pairs={{0,8},{8,0},{16,24},{24,16},{32,40},{40,32},{48,56},{56,48},{64,72... | collective-permute-start | bytes 2359304 | tf_op jit(solution)/shard_map/ppermute | solution.py:469
  30.2 1.6 %collective-permute-start.8 = (bf16[128,1024]{1,0:T(8,128)(2,1)S(1)}, bf16[128,1024]{1,0:T(8,128)(2,1)}, u32[]{:S(2)}, u32[]{:S(2)}) collective-permute-start(bf16[128,1024]{1,0:T(8,128)(2,1)S(1)} %collective-permute-done.4.refs_10_), channel_id=1, source_target_pairs={{0,1},{1,0},{2,3},{3,2},{4,5},{5,4},{6,7},{7,6},{8,9},{9,8},{10,11... | collective-permute-start | bytes 786440 | tf_op jit(solution)/shard_map/ppermute | solution.py:437
  33.9 4.1 %shard_map.112 = (bf16[8,2,128,128]{3,2,1,0:T(8,128)(2,1)}, f32[4,1,256]{2,1,0:T(1,128)}, bf16[8,128,128]{2,1,0:T(8,128)(2,1)}, bf16[2048,128]{1,0:T(8,128)(2,1)}, bf16[2048,128]{1,0:T(8,128)(2,1)}) custom-call(s32[1]{0:T(128)} %bitcast.refs_0_, bf16[8,3,128,128]{3,2,1,0:T(8,128)(2,1)S(1)} %all-to-all-done.refs_1_.refs_2_.refs_3_, ...), custom_call_target="tpu_custom_call" | custom-call | flops 671088640 | bytes 2000000 | tf_op jit(solution)/shard_map/pallas_call | solution.py:111
  38.0 4.1 %all-to-all-start.1 = ((bf16[8,2,128,128]{3,2,1,0:T(8,128)(2,1)}), bf16[8,2,128,128]{3,2,1,0:T(8,128)(2,1)S(1)}, u32[]{:S(2)}, u32[]{:S(2)}) async-start(bf16[8,2,128,128]{3,2,1,0:T(8,128)(2,1)} %get-tuple-element.42.refs_5_), calls=%async_computation.1 | async-start | bytes 1048576 | tf_op jit(solution)/shard_map/all_to_all | solution.py:405
  42.1 2.8 %shard_map.113 = (f32[8,128,128]{2,1,0:T(8,128)S(1)}, bf16[8,128,128]{2,1,0:T(8,128)(2,1)S(1)}) custom-call(s32[1]{0:T(128)} %bitcast.1.refs_0_, bf16[128,1024]{1,0:T(8,128)(2,1)S(1)} %copy-done, bf16[128,1024]{1,0:T(8,128)(2,1)S(1)} %collective-permute-done.5.refs_2_, bf16[128,1024]{1,0:T(8,128)(2,1)S(1)} %copy-done.2, ...), custom_call_target="tpu_custom_call" | custom-call | flops 536870912 | bytes 2000000 | tf_op jit(solution)/shard_map/pallas_call | solution.py:111
  48.6 2.2 %all-to-all-done.1.refs_4_.refs_1_ = bf16[8,2,128,128]{3,2,1,0:T(8,128)(2,1)S(1)} async-done(((bf16[8,2,128,128]{3,2,1,0:T(8,128)(2,1)}), bf16[8,2,128,128]{3,2,1,0:T(8,128)(2,1)S(1)}, u32[]{:S(2)}, u32[]{:S(2)}) %all-to-all-start.1) | async-done | bytes 524320 | tf_op jit(solution)/shard_map/all_to_all | solution.py:405
  50.8 3.4 %collective-permute-start.12 = (bf16[8,2,128,128]{3,2,1,0:T(8,128)(2,1)S(1)}, bf16[8,2,128,128]{3,2,1,0:T(8,128)(2,1)S(1)}, u32[]{:S(2)}, u32[]{:S(2)}) collective-permute-start(bf16[8,2,128,128]{3,2,1,0:T(8,128)(2,1)S(1)} %all-to-all-done.1.refs_4_.refs_1_), channel_id=1, source_target_pairs={{0,8},{8,0},{16,24},{24,16},{32,40},{40,32},{48,56},{56,48},{64,72... | collective-permute-start | bytes 1572872 | tf_op jit(solution)/shard_map/ppermute | solution.py:502
  54.2 3.4 %all-to-all-start.2 = ((bf16[8,128,128]{2,1,0:T(8,128)(2,1)}), bf16[8,128,128]{2,1,0:T(8,128)(2,1)S(1)}, u32[]{:S(2)}, u32[]{:S(2)}) async-start(bf16[8,128,128]{2,1,0:T(8,128)(2,1)} %shard_map.114), calls=%async_computation.2 | async-start | bytes 524288 | tf_op jit(solution)/shard_map/all_to_all | solution.py:405
  57.6 2.8 %shard_map.117 = bf16[32,32,512]{2,1,0:T(8,128)(2,1)} custom-call(s32[1]{0:T(128)} %bitcast.8.refs_0_, bf16[128,1024]{1,0:T(8,128)(2,1)S(1)} %copy-done, bf16[128,1024]{1,0:T(8,128)(2,1)S(1)} %collective-permute-done.5.refs_2_, bf16[256,512]{1,0:T(8,128)(2,1)} %collective-permute-done.9.refs_3_, bf16[8,2,128,128]{3,2,1,0:T(8,128)(2,1)S(1)} %all-to-all-done.1.refs_4_.refs_1_, ...), custom_call_target="tpu_custom_call" | custom-call | flops 536870912 | bytes 2000000 | tf_op jit(solution)/shard_map/pallas_call | solution.py:111
  60.5 5.4 %all-to-all-done.2.refs_3_ = bf16[8,128,128]{2,1,0:T(8,128)(2,1)S(1)} async-done(((bf16[8,128,128]{2,1,0:T(8,128)(2,1)}), bf16[8,128,128]{2,1,0:T(8,128)(2,1)S(1)}, u32[]{:S(2)}, u32[]{:S(2)}) %all-to-all-start.2) | async-done | bytes 262176 | tf_op jit(solution)/shard_map/all_to_all | solution.py:405
  66.5 4.8 %all-to-all-start.3 = ((bf16[32,32,512]{2,1,0:T(8,128)(2,1)}), bf16[32,32,512]{2,1,0:T(8,128)(2,1)S(1)}, u32[]{:S(2)}, u32[]{:S(2)}) async-start(bf16[32,32,512]{2,1,0:T(8,128)(2,1)} %shard_map.117), calls=%async_computation.3 | async-start | bytes 2097152 | tf_op jit(solution)/shard_map/all_to_all | solution.py:513
  71.3 6.8 %shard_map.115 = (bf16[8,128,128]{2,1,0:T(8,128)(2,1)}, f32[8,2,128,128]{3,2,1,0:T(8,128)}, bf16[8,2,128,128]{3,2,1,0:T(8,128)(2,1)}) custom-call(s32[1]{0:T(128)} %bitcast.refs_0_, bf16[8,128,128]{2,1,0:T(8,128)(2,1)} %get-tuple-element.48.refs_1_, bf16[2048,128]{1,0:T(8,128)(2,1)} %get-tuple-element.49.refs_2_, bf16[8,128,128]{2,1,0:T(8,128)(2,1)} %copy-done.9, ...), custom_call_target="tpu_custom_call" | custom-call | flops 1677721600 | bytes 2000000 | tf_op jit(solution)/shard_map/pallas_call | solution.py:111
  79.2 1.7 %collective-permute-done.11.refs_2_ = bf16[8,2,128,128]{3,2,1,0:T(8,128)(2,1)S(1)} collective-permute-done((bf16[8,2,128,128]{3,2,1,0:T(8,128)(2,1)}, bf16[8,2,128,128]{3,2,1,0:T(8,128)(2,1)S(1)}, u32[]{:S(2)}, u32[]{:S(2)}) %collective-permute-start.11) | collective-permute-done | bytes 524320 | tf_op jit(solution)/shard_map/ppermute | solution.py:535
  87.1 5.6 %all-to-all-start.4 = ((bf16[8,4,128,128]{3,2,1,0:T(8,128)(2,1)}), bf16[8,4,128,128]{3,2,1,0:T(8,128)(2,1)S(1)}, u32[]{:S(2)}, u32[]{:S(2)}) async-start(bf16[8,4,128,128]{3,2,1,0:T(8,128)(2,1)} %shard_map.118), calls=%async_computation.4 | async-start | bytes 2097152 | tf_op jit(solution)/shard_map/all_to_all | solution.py:405
  93.7 3.0 %shard_map.119 = (bf16[128,1024]{1,0:T(8,128)(2,1)}, bf16[128,1024]{1,0:T(8,128)(2,1)}) custom-call(s32[1]{0:T(128)} %bitcast.1.refs_0_, bf16[8,2,128,128]{3,2,1,0:T(8,128)(2,1)S(1)} %all-to-all-done.1.refs_4_.refs_1_, bf16[8,2,128,128]{3,2,1,0:T(8,128)(2,1)S(1)} %collective-permute-done.12.refs_5_.refs_2_, bf16[128,1024]{1,0:T(8,128)(2,1)S(1)} %copy-done.2, ...), custom_call_target="tpu_custom_call" | custom-call | flops 536870912 | bytes 2000000 | tf_op jit(solution)/shard_map/pallas_call | solution.py:111
  96.7 2.1 %collective-permute-start.13 = (bf16[128,1024]{1,0:T(8,128)(2,1)}, bf16[128,1024]{1,0:T(8,128)(2,1)S(1)}, u32[]{:S(2)}, u32[]{:S(2)}) collective-permute-start(bf16[128,1024]{1,0:T(8,128)(2,1)} %get-tuple-element.59), channel_id=1, source_target_pairs={{0,8},{8,0},{16,24},{24,16},{32,40},{40,32},{48,56},{56,48},{64,72... | collective-permute-start | bytes 786440 | tf_op jit(solution)/shard_map/ppermute | solution.py:559
  102.4 3.4 %all-to-all-done.4.refs_1_ = bf16[8,4,128,128]{3,2,1,0:T(8,128)(2,1)S(1)} async-done(((bf16[8,4,128,128]{3,2,1,0:T(8,128)(2,1)}), bf16[8,4,128,128]{3,2,1,0:T(8,128)(2,1)S(1)}, u32[]{:S(2)}, u32[]{:S(2)}) %all-to-all-start.4) | async-done | bytes 1048608 | tf_op jit(solution)/shard_map/all_to_all | solution.py:405
  105.8 3.8 %collective-permute-start.14 = (bf16[8,128,128]{2,1,0:T(8,128)(2,1)S(1)}, bf16[8,128,128]{2,1,0:T(8,128)(2,1)S(1)}, u32[]{:S(2)}, u32[]{:S(2)}) collective-permute-start(bf16[8,128,128]{2,1,0:T(8,128)(2,1)S(1)} %slice_bitcast_fusion), channel_id=1, source_target_pairs={{0,8},{8,0},{16,24},{24,16},{32,40},{40,32},{48,56},{56,48},{64,72... | collective-permute-start | bytes 786440 | tf_op jit(solution)/shard_map/ppermute | solution.py:566
  (59 shorter events, 25.0 us)
Async XLA Ops:
  3.5 16.3 %copy-start.10 = (s32[1,2048]{1,0:T(1,128)S(1)}, s32[1,2048]{1,0:T(1,128)}, u32[]{:S(2)}) copy-start(s32[1,2048]{1,0:T(1,128)} %param.10) | copy-start | bytes 24580
  3.5 17.3 %copy-start = (bf16[128,1024]{1,0:T(8,128)(2,1)S(1)}, bf16[128,1024]{1,0:T(8,128)(2,1)}, u32[]{:S(2)}) copy-start(bf16[128,1024]{1,0:T(8,128)(2,1)} %get-tuple-element.40.refs_1_) | copy-start | bytes 786436
  3.5 12.9 %collective-permute-start = (bf16[128,1024]{1,0:T(8,128)(2,1)}, bf16[128,1024]{1,0:T(8,128)(2,1)S(1)}, u32[]{:S(2)}, u32[]{:S(2)}) collective-permute-start(bf16[128,1024]{1,0:T(8,128)(2,1)} %get-tuple-element.36.refs_3_), channel_id=1, source_target_pairs={{0,4},{1,5},{2,6},{3,7},{4,0},{5,1},{6,2},{7,3},{8,12},{9,13},{10,... | collective-permute-start | bytes 786440 | tf_op jit(solution)/shard_map/ppermute | solution.py:437
  5.6 16.4 %collective-permute-start.2 = (bf16[128,1024]{1,0:T(8,128)(2,1)}, bf16[128,1024]{1,0:T(8,128)(2,1)S(1)}, u32[]{:S(2)}, u32[]{:S(2)}) collective-permute-start(bf16[128,1024]{1,0:T(8,128)(2,1)} %get-tuple-element.36.refs_3_), channel_id=1, source_target_pairs={{0,3},{1,2},{2,1},{3,0},{4,7},{5,6},{6,5},{7,4},{8,11},{9,10},{10,... | collective-permute-start | bytes 786440 | tf_op jit(solution)/shard_map/ppermute | solution.py:437
  9.4 12.7 %collective-permute-start.1 = (bf16[128,1024]{1,0:T(8,128)(2,1)}, bf16[128,1024]{1,0:T(8,128)(2,1)S(1)}, u32[]{:S(2)}, u32[]{:S(2)}) collective-permute-start(bf16[128,1024]{1,0:T(8,128)(2,1)} %get-tuple-element.36.refs_3_), channel_id=1, source_target_pairs={{0,1},{1,0},{2,3},{3,2},{4,5},{5,4},{6,7},{7,6},{8,9},{9,8},{10,11... | collective-permute-start | bytes 786440 | tf_op jit(solution)/shard_map/ppermute | solution.py:437
  9.4 17.7 %all-to-all-start = ((bf16[8,3,128,128]{3,2,1,0:T(8,128)(2,1)}), bf16[8,3,128,128]{3,2,1,0:T(8,128)(2,1)S(1)}, u32[]{:S(2)}, u32[]{:S(2)}) async-start(bf16[8,3,128,128]{3,2,1,0:T(8,128)(2,1)} %get-tuple-element.35), calls=%async_computation | async-start | bytes 1572864 | tf_op jit(solution)/shard_map/all_to_all | solution.py:405
  16.5 4.4 %collective-permute-start.5 = (bf16[128,1024]{1,0:T(8,128)(2,1)S(1)}, bf16[128,1024]{1,0:T(8,128)(2,1)S(1)}, u32[]{:S(2)}, u32[]{:S(2)}) collective-permute-start(bf16[128,1024]{1,0:T(8,128)(2,1)S(1)} %copy-done.11), channel_id=1, source_target_pairs={{0,8},{8,0},{16,24},{24,16},{32,40},{40,32},{48,56},{56,48},{64,72... | collective-permute-start | bytes 786440 | tf_op jit(solution)/shard_map/ppermute | solution.py:457
  18.1 9.1 %collective-permute-start.4 = (bf16[128,1024]{1,0:T(8,128)(2,1)S(1)}, bf16[128,1024]{1,0:T(8,128)(2,1)S(1)}, u32[]{:S(2)}, u32[]{:S(2)}) collective-permute-start(bf16[128,1024]{1,0:T(8,128)(2,1)S(1)} %collective-permute-done.refs_7_), channel_id=1, source_target_pairs={{0,3},{1,2},{2,1},{3,0},{4,7},{5,6},{6,5},{7,4},{8,11},{9,10},{10,... | collective-permute-start | bytes 786440 | tf_op jit(solution)/shard_map/ppermute | solution.py:437
  18.3 8.8 %collective-permute-start.3 = (bf16[128,1024]{1,0:T(8,128)(2,1)S(1)}, bf16[128,1024]{1,0:T(8,128)(2,1)S(1)}, u32[]{:S(2)}, u32[]{:S(2)}) collective-permute-start(bf16[128,1024]{1,0:T(8,128)(2,1)S(1)} %collective-permute-done.refs_7_), channel_id=1, source_target_pairs={{0,1},{1,0},{2,3},{3,2},{4,5},{5,4},{6,7},{7,6},{8,9},{9,8},{10,11... | collective-permute-start | bytes 786440 | tf_op jit(solution)/shard_map/ppermute | solution.py:437
  27.1 15.0 %copy-start.3 = (bf16[128,1024]{1,0:T(8,128)(2,1)}, bf16[128,1024]{1,0:T(8,128)(2,1)S(1)}, u32[]{:S(2)}) copy-start(bf16[128,1024]{1,0:T(8,128)(2,1)S(1)} %collective-permute-done.4.refs_10_) | copy-start | bytes 786436
  27.1 15.0 %copy-start.5 = (bf16[128,1024]{1,0:T(8,128)(2,1)}, bf16[128,1024]{1,0:T(8,128)(2,1)S(1)}, u32[]{:S(2)}) copy-start(bf16[128,1024]{1,0:T(8,128)(2,1)S(1)} %collective-permute-done.3.refs_8_) | copy-start | bytes 786436
  27.2 6.7 %collective-permute-start.6 = (bf16[8,3,128,128]{3,2,1,0:T(8,128)(2,1)S(1)}, bf16[8,3,128,128]{3,2,1,0:T(8,128)(2,1)S(1)}, u32[]{:S(2)}, u32[]{:S(2)}) collective-permute-start(bf16[8,3,128,128]{3,2,1,0:T(8,128)(2,1)S(1)} %all-to-all-done.refs_1_.refs_2_.refs_3_), channel_id=1, source_target_pairs={{0,8},{8,0},{16,24},{24,16},{32,40},{40,32},{48,56},{56,48},{64,72... | collective-permute-start | bytes 2359304 | tf_op jit(solution)/shard_map/ppermute | solution.py:469
  30.2 11.9 %collective-permute-start.8 = (bf16[128,1024]{1,0:T(8,128)(2,1)S(1)}, bf16[128,1024]{1,0:T(8,128)(2,1)}, u32[]{:S(2)}, u32[]{:S(2)}) collective-permute-start(bf16[128,1024]{1,0:T(8,128)(2,1)S(1)} %collective-permute-done.4.refs_10_), channel_id=1, source_target_pairs={{0,1},{1,0},{2,3},{3,2},{4,5},{5,4},{6,7},{7,6},{8,9},{9,8},{10,11... | collective-permute-start | bytes 786440 | tf_op jit(solution)/shard_map/ppermute | solution.py:437
  31.8 10.3 %collective-permute-start.9 = (bf16[256,512]{1,0:T(8,128)(2,1)}, bf16[256,512]{1,0:T(8,128)(2,1)}, u32[]{:S(2)}, u32[]{:S(2)}) collective-permute-start(bf16[256,512]{1,0:T(8,128)(2,1)} %shard_map.111), channel_id=1, source_target_pairs={{0,64},{8,72},{16,80},{24,88},{32,96},{40,104},{48,112},{56,120},{... | collective-permute-start | bytes 786440 | tf_op jit(solution)/shard_map/ppermute | solution.py:467
  32.9 9.2 %collective-permute-start.7 = (bf16[128,1024]{1,0:T(8,128)(2,1)S(1)}, bf16[128,1024]{1,0:T(8,128)(2,1)}, u32[]{:S(2)}, u32[]{:S(2)}) collective-permute-start(bf16[128,1024]{1,0:T(8,128)(2,1)S(1)} %collective-permute-done.1.refs_4_), channel_id=1, source_target_pairs={{0,3},{1,2},{2,1},{3,0},{4,7},{5,6},{6,5},{7,4},{8,11},{9,10},{10,... | collective-permute-start | bytes 786440 | tf_op jit(solution)/shard_map/ppermute | solution.py:437
  38.0 12.8 %all-to-all-start.1 = ((bf16[8,2,128,128]{3,2,1,0:T(8,128)(2,1)}), bf16[8,2,128,128]{3,2,1,0:T(8,128)(2,1)S(1)}, u32[]{:S(2)}, u32[]{:S(2)}) async-start(bf16[8,2,128,128]{3,2,1,0:T(8,128)(2,1)} %get-tuple-element.42.refs_5_), calls=%async_computation.1 | async-start | bytes 1048576 | tf_op jit(solution)/shard_map/all_to_all | solution.py:405
  44.9 2.4 %collective-permute-start.10 = (bf16[8,128,128]{2,1,0:T(8,128)(2,1)S(1)}, bf16[8,128,128]{2,1,0:T(8,128)(2,1)S(1)}, u32[]{:S(2)}, u32[]{:S(2)}) collective-permute-start(bf16[8,128,128]{2,1,0:T(8,128)(2,1)S(1)} %get-tuple-element.46), channel_id=1, source_target_pairs={{0,8},{8,0},{16,24},{24,16},{32,40},{40,32},{48,56},{56,48},{64,72... | collective-permute-start | bytes 786440 | tf_op jit(solution)/shard_map/ppermute | solution.py:495
  50.8 6.8 %collective-permute-start.12 = (bf16[8,2,128,128]{3,2,1,0:T(8,128)(2,1)S(1)}, bf16[8,2,128,128]{3,2,1,0:T(8,128)(2,1)S(1)}, u32[]{:S(2)}, u32[]{:S(2)}) collective-permute-start(bf16[8,2,128,128]{3,2,1,0:T(8,128)(2,1)S(1)} %all-to-all-done.1.refs_4_.refs_1_), channel_id=1, source_target_pairs={{0,8},{8,0},{16,24},{24,16},{32,40},{40,32},{48,56},{56,48},{64,72... | collective-permute-start | bytes 1572872 | tf_op jit(solution)/shard_map/ppermute | solution.py:502
  54.2 11.6 %all-to-all-start.2 = ((bf16[8,128,128]{2,1,0:T(8,128)(2,1)}), bf16[8,128,128]{2,1,0:T(8,128)(2,1)S(1)}, u32[]{:S(2)}, u32[]{:S(2)}) async-start(bf16[8,128,128]{2,1,0:T(8,128)(2,1)} %shard_map.114), calls=%async_computation.2 | async-start | bytes 524288 | tf_op jit(solution)/shard_map/all_to_all | solution.py:405
  66.5 19.3 %all-to-all-start.3 = ((bf16[32,32,512]{2,1,0:T(8,128)(2,1)}), bf16[32,32,512]{2,1,0:T(8,128)(2,1)S(1)}, u32[]{:S(2)}, u32[]{:S(2)}) async-start(bf16[32,32,512]{2,1,0:T(8,128)(2,1)} %shard_map.117), calls=%async_computation.3 | async-start | bytes 2097152 | tf_op jit(solution)/shard_map/all_to_all | solution.py:513
  78.0 2.9 %collective-permute-start.11 = (bf16[8,2,128,128]{3,2,1,0:T(8,128)(2,1)}, bf16[8,2,128,128]{3,2,1,0:T(8,128)(2,1)S(1)}, u32[]{:S(2)}, u32[]{:S(2)}) collective-permute-start(bf16[8,2,128,128]{3,2,1,0:T(8,128)(2,1)} %get-tuple-element.55), channel_id=1, source_target_pairs={{0,8},{8,0},{16,24},{24,16},{32,40},{40,32},{48,56},{56,48},{64,72... | collective-permute-start | bytes 1572872 | tf_op jit(solution)/shard_map/ppermute | solution.py:535
  87.1 18.7 %all-to-all-start.4 = ((bf16[8,4,128,128]{3,2,1,0:T(8,128)(2,1)}), bf16[8,4,128,128]{3,2,1,0:T(8,128)(2,1)S(1)}, u32[]{:S(2)}, u32[]{:S(2)}) async-start(bf16[8,4,128,128]{3,2,1,0:T(8,128)(2,1)} %shard_map.118), calls=%async_computation.4 | async-start | bytes 2097152 | tf_op jit(solution)/shard_map/all_to_all | solution.py:405
  96.7 3.5 %collective-permute-start.13 = (bf16[128,1024]{1,0:T(8,128)(2,1)}, bf16[128,1024]{1,0:T(8,128)(2,1)S(1)}, u32[]{:S(2)}, u32[]{:S(2)}) collective-permute-start(bf16[128,1024]{1,0:T(8,128)(2,1)} %get-tuple-element.59), channel_id=1, source_target_pairs={{0,8},{8,0},{16,24},{24,16},{32,40},{40,32},{48,56},{56,48},{64,72... | collective-permute-start | bytes 786440 | tf_op jit(solution)/shard_map/ppermute | solution.py:559
  105.8 5.3 %collective-permute-start.14 = (bf16[8,128,128]{2,1,0:T(8,128)(2,1)S(1)}, bf16[8,128,128]{2,1,0:T(8,128)(2,1)S(1)}, u32[]{:S(2)}, u32[]{:S(2)}) collective-permute-start(bf16[8,128,128]{2,1,0:T(8,128)(2,1)S(1)} %slice_bitcast_fusion), channel_id=1, source_target_pairs={{0,8},{8,0},{16,24},{24,16},{32,40},{40,32},{48,56},{56,48},{64,72... | collective-permute-start | bytes 786440 | tf_op jit(solution)/shard_map/ppermute | solution.py:566
  (8 other events, 27.6 us)

commit v15 on v12

--- a/solution.py
+++ b/solution.py
@@ -139,11 +139,14 @@
 
     mine = pl.ds(pl.multiple_of(core * half, half), half)
     other = pl.ds(pl.multiple_of((1 - core) * half, half), half)
-    copy(data[3].get().at[:, mine], half_ref)
+    load = pltpu.make_async_copy(data[3].at[:, mine], scratch[0], next(sems))
+    load.start()
     for i in range(3):
         ref = data[i].get()
         for a in range(HEADS):
             copy(ref.at[:, pl.ds(a * HS, HS)], out_ref.at[a, i])
+    load.wait()
+    copy(scratch[0], half_ref)
     up_ref = data[4].get()
     copy(up_ref.at[:, mine], up_mine_ref)
     copy(up_ref.at[:, other], up_send_ref)
@@ -425,9 +428,10 @@
         pack_kernel,
         [
             ("S", core_ref), ("H", query_rows, 0), ("H", key_rows, 0),
-            ("H", value_rows, 0), ("H", out_weight), ("H", upstream, 0),
+            ("H", value_rows, 0), ("R", out_weight), ("H", upstream, 0),
         ],
         [("R", (HEADS, 3, BLOCK, HS), BF16), side, side, side],
+        scratch=(pltpu.VMEM((HS, half), BF16),),
     )
     own = exchange(packed)
 

time: 113 us -> 113 us (level)
  no operation moved by 1% of the time
where the time goes in v15:
time: 113 us; the launch traced here: 112 us
  starting transfers between devices  52 us (46%)
  Pallas kernels  31.1 us (28%)
  waiting for transfers between devices  21.6 us (19%)
  local copies, waits for them, and re-layouts  4.83 us (4%)
  between operations  1.78 us (2%)
    pallas_call x13, Pallas kernels, call(): pl.pallas_call(body, out_shape=[SPACES[o[0]](o[1], o[2]) if o[0] in 'HR'...  31.1 us
    all_to_all x4, starting transfers between devices, exchange(): lax.all_to_all(operand, 'ctx', split_axis=0, concat_axis=0, tiled=True, a...  19.5 us
    all_to_all x4, waiting for transfers between devices, exchange(): lax.all_to_all(operand, 'ctx', split_axis=0, concat_axis=0, tiled=True, a...  10.9 us
    ppermute x7, starting transfers between devices, step(): return lax.ppermute(value, 'fsdp', [(i, i ^ s) for i in range(8)])  10.3 us
    ppermute x7, waiting for transfers between devices, step(): return lax.ppermute(value, 'fsdp', [(i, i ^ s) for i in range(8)])  5.1 us
    unnamed x24, local copies, waits for them, and re-layouts  4.81 us
    all_to_all x1, starting transfers between devices, shards(): lax.all_to_all(after(terms, grads), ('ctx', 'fsdp'), split_axis=0, concat...  4.75 us
    ppermute x1, starting transfers between devices, shards(): weight_other = lax.ppermute(weight_mine, 'ctx', CORE_SWAP)  3.8 us
  transfers between devices with their start and end apart: 20, of which 8 were waited for; matrix products, arithmetic and copies ran while one was open for 1% of the time, Pallas kernels for 23%

profile of v15, /device:TPU:1, one launch (start us, length us, event | category | flops | bytes accessed | tf_op | source)
XLA Modules:
  0.0 112.3 jit_solution(1173408426178072396)
XLA Ops:
  0.6 2.6 %shard_map.110 = (bf16[8,3,128,128]{3,2,1,0:T(8,128)(2,1)}, bf16[128,1024]{1,0:T(8,128)(2,1)}, bf16[128,1024]{1,0:T(8,128)(2,1)}, bf16[128,1024]{1,0:T(8,128)(2,1)}) custom-call(s32[1]{0:T(128)} %bitcast.refs_0_, bf16[1,128,1024]{2,1,0:T(8,128)(2,1)} %refs_1_.1, bf16[1,128,1024]{2,1,0:T(8,128)(2,1)} %refs_2_.1, bf16[1,128,1024]{2,1,0:T(8,128)(2,1)} %refs_3_.1, ...), custom_call_target="tpu_custom_call" | custom-call | bytes 2000000 | tf_op jit(solution)/shard_map/pallas_call | solution.py:111
  3.3 2.1 %collective-permute-start = (bf16[128,1024]{1,0:T(8,128)(2,1)}, bf16[128,1024]{1,0:T(8,128)(2,1)S(1)}, u32[]{:S(2)}, u32[]{:S(2)}) collective-permute-start(bf16[128,1024]{1,0:T(8,128)(2,1)} %get-tuple-element.35.refs_3_), channel_id=1, source_target_pairs={{0,4},{1,5},{2,6},{3,7},{4,0},{5,1},{6,2},{7,3},{8,12},{9,13},{10,... | collective-permute-start | bytes 786440 | tf_op jit(solution)/shard_map/ppermute | solution.py:439
  5.5 3.8 %collective-permute-start.2 = (bf16[128,1024]{1,0:T(8,128)(2,1)}, bf16[128,1024]{1,0:T(8,128)(2,1)S(1)}, u32[]{:S(2)}, u32[]{:S(2)}) collective-permute-start(bf16[128,1024]{1,0:T(8,128)(2,1)} %get-tuple-element.35.refs_3_), channel_id=1, source_target_pairs={{0,3},{1,2},{2,1},{3,0},{4,7},{5,6},{6,5},{7,4},{8,11},{9,10},{10,... | collective-permute-start | bytes 786440 | tf_op jit(solution)/shard_map/ppermute | solution.py:439
  9.2 6.4 %all-to-all-start = ((bf16[8,3,128,128]{3,2,1,0:T(8,128)(2,1)}), bf16[8,3,128,128]{3,2,1,0:T(8,128)(2,1)S(1)}, u32[]{:S(2)}, u32[]{:S(2)}) async-start(bf16[8,3,128,128]{3,2,1,0:T(8,128)(2,1)} %get-tuple-element.34), calls=%async_computation | async-start | bytes 1572864 | tf_op jit(solution)/shard_map/all_to_all | solution.py:406
  16.3 1.6 %collective-permute-start.5 = (bf16[128,1024]{1,0:T(8,128)(2,1)S(1)}, bf16[128,1024]{1,0:T(8,128)(2,1)S(1)}, u32[]{:S(2)}, u32[]{:S(2)}) collective-permute-start(bf16[128,1024]{1,0:T(8,128)(2,1)S(1)} %copy-done.11), channel_id=1, source_target_pairs={{0,8},{8,0},{16,24},{24,16},{32,40},{40,32},{48,56},{56,48},{64,72... | collective-permute-start | bytes 786440 | tf_op jit(solution)/shard_map/ppermute | solution.py:459
  21.9 5.1 %collective-permute-done.4.refs_10_ = bf16[128,1024]{1,0:T(8,128)(2,1)S(1)} collective-permute-done((bf16[128,1024]{1,0:T(8,128)(2,1)S(1)}, bf16[128,1024]{1,0:T(8,128)(2,1)S(1)}, u32[]{:S(2)}, u32[]{:S(2)}) %collective-permute-start.4) | collective-permute-done | bytes 262176 | tf_op jit(solution)/shard_map/ppermute | solution.py:439
  27.0 3.0 %collective-permute-start.6 = (bf16[8,3,128,128]{3,2,1,0:T(8,128)(2,1)S(1)}, bf16[8,3,128,128]{3,2,1,0:T(8,128)(2,1)S(1)}, u32[]{:S(2)}, u32[]{:S(2)}) collective-permute-start(bf16[8,3,128,128]{3,2,1,0:T(8,128)(2,1)S(1)} %all-to-all-done.refs_1_.refs_2_.refs_3_), channel_id=1, source_target_pairs={{0,8},{8,0},{16,24},{24,16},{32,40},{40,32},{48,56},{56,48},{64,72... | collective-permute-start | bytes 2359304 | tf_op jit(solution)/shard_map/ppermute | solution.py:471
  30.0 1.6 %collective-permute-start.8 = (bf16[128,1024]{1,0:T(8,128)(2,1)S(1)}, bf16[128,1024]{1,0:T(8,128)(2,1)}, u32[]{:S(2)}, u32[]{:S(2)}) collective-permute-start(bf16[128,1024]{1,0:T(8,128)(2,1)S(1)} %collective-permute-done.4.refs_10_), channel_id=1, source_target_pairs={{0,1},{1,0},{2,3},{3,2},{4,5},{5,4},{6,7},{7,6},{8,9},{9,8},{10,11... | collective-permute-start | bytes 786440 | tf_op jit(solution)/shard_map/ppermute | solution.py:439
  33.7 4.1 %shard_map.112 = (bf16[8,2,128,128]{3,2,1,0:T(8,128)(2,1)}, f32[4,1,256]{2,1,0:T(1,128)}, bf16[8,128,128]{2,1,0:T(8,128)(2,1)}, bf16[2048,128]{1,0:T(8,128)(2,1)}, bf16[2048,128]{1,0:T(8,128)(2,1)}) custom-call(s32[1]{0:T(128)} %bitcast.refs_0_, bf16[8,3,128,128]{3,2,1,0:T(8,128)(2,1)S(1)} %all-to-all-done.refs_1_.refs_2_.refs_3_, ...), custom_call_target="tpu_custom_call" | custom-call | flops 671088640 | bytes 2000000 | tf_op jit(solution)/shard_map/pallas_call | solution.py:111
  37.8 4.1 %all-to-all-start.1 = ((bf16[8,2,128,128]{3,2,1,0:T(8,128)(2,1)}), bf16[8,2,128,128]{3,2,1,0:T(8,128)(2,1)S(1)}, u32[]{:S(2)}, u32[]{:S(2)}) async-start(bf16[8,2,128,128]{3,2,1,0:T(8,128)(2,1)} %get-tuple-element.41.refs_5_), calls=%async_computation.1 | async-start | bytes 1048576 | tf_op jit(solution)/shard_map/all_to_all | solution.py:406
  41.9 2.8 %shard_map.113 = (f32[8,128,128]{2,1,0:T(8,128)S(1)}, bf16[8,128,128]{2,1,0:T(8,128)(2,1)S(1)}) custom-call(s32[1]{0:T(128)} %bitcast.1.refs_0_, bf16[128,1024]{1,0:T(8,128)(2,1)S(1)} %copy-done, bf16[128,1024]{1,0:T(8,128)(2,1)S(1)} %collective-permute-done.5.refs_2_, bf16[128,1024]{1,0:T(8,128)(2,1)S(1)} %copy-done.2, ...), custom_call_target="tpu_custom_call" | custom-call | flops 536870912 | bytes 2000000 | tf_op jit(solution)/shard_map/pallas_call | solution.py:111
  48.4 2.2 %all-to-all-done.1.refs_4_.refs_1_ = bf16[8,2,128,128]{3,2,1,0:T(8,128)(2,1)S(1)} async-done(((bf16[8,2,128,128]{3,2,1,0:T(8,128)(2,1)}), bf16[8,2,128,128]{3,2,1,0:T(8,128)(2,1)S(1)}, u32[]{:S(2)}, u32[]{:S(2)}) %all-to-all-start.1) | async-done | bytes 524320 | tf_op jit(solution)/shard_map/all_to_all | solution.py:406
  50.6 3.4 %collective-permute-start.12 = (bf16[8,2,128,128]{3,2,1,0:T(8,128)(2,1)S(1)}, bf16[8,2,128,128]{3,2,1,0:T(8,128)(2,1)S(1)}, u32[]{:S(2)}, u32[]{:S(2)}) collective-permute-start(bf16[8,2,128,128]{3,2,1,0:T(8,128)(2,1)S(1)} %all-to-all-done.1.refs_4_.refs_1_), channel_id=1, source_target_pairs={{0,8},{8,0},{16,24},{24,16},{32,40},{40,32},{48,56},{56,48},{64,72... | collective-permute-start | bytes 1572872 | tf_op jit(solution)/shard_map/ppermute | solution.py:504
  54.0 3.4 %all-to-all-start.2 = ((bf16[8,128,128]{2,1,0:T(8,128)(2,1)}), bf16[8,128,128]{2,1,0:T(8,128)(2,1)S(1)}, u32[]{:S(2)}, u32[]{:S(2)}) async-start(bf16[8,128,128]{2,1,0:T(8,128)(2,1)} %shard_map.114), calls=%async_computation.2 | async-start | bytes 524288 | tf_op jit(solution)/shard_map/all_to_all | solution.py:406
  57.4 2.8 %shard_map.117 = bf16[32,32,512]{2,1,0:T(8,128)(2,1)} custom-call(s32[1]{0:T(128)} %bitcast.8.refs_0_, bf16[128,1024]{1,0:T(8,128)(2,1)S(1)} %copy-done, bf16[128,1024]{1,0:T(8,128)(2,1)S(1)} %collective-permute-done.5.refs_2_, bf16[256,512]{1,0:T(8,128)(2,1)} %collective-permute-done.9.refs_3_, bf16[8,2,128,128]{3,2,1,0:T(8,128)(2,1)S(1)} %all-to-all-done.1.refs_4_.refs_1_, ...), custom_call_target="tpu_custom_call" | custom-call | flops 536870912 | bytes 2000000 | tf_op jit(solution)/shard_map/pallas_call | solution.py:111
  60.3 5.4 %all-to-all-done.2.refs_3_ = bf16[8,128,128]{2,1,0:T(8,128)(2,1)S(1)} async-done(((bf16[8,128,128]{2,1,0:T(8,128)(2,1)}), bf16[8,128,128]{2,1,0:T(8,128)(2,1)S(1)}, u32[]{:S(2)}, u32[]{:S(2)}) %all-to-all-start.2) | async-done | bytes 262176 | tf_op jit(solution)/shard_map/all_to_all | solution.py:406
  66.3 4.8 %all-to-all-start.3 = ((bf16[32,32,512]{2,1,0:T(8,128)(2,1)}), bf16[32,32,512]{2,1,0:T(8,128)(2,1)S(1)}, u32[]{:S(2)}, u32[]{:S(2)}) async-start(bf16[32,32,512]{2,1,0:T(8,128)(2,1)} %shard_map.117), calls=%async_computation.3 | async-start | bytes 2097152 | tf_op jit(solution)/shard_map/all_to_all | solution.py:515
  71.1 6.8 %shard_map.115 = (bf16[8,128,128]{2,1,0:T(8,128)(2,1)}, f32[8,2,128,128]{3,2,1,0:T(8,128)}, bf16[8,2,128,128]{3,2,1,0:T(8,128)(2,1)}) custom-call(s32[1]{0:T(128)} %bitcast.refs_0_, bf16[8,128,128]{2,1,0:T(8,128)(2,1)} %get-tuple-element.47.refs_1_, bf16[2048,128]{1,0:T(8,128)(2,1)} %get-tuple-element.48.refs_2_, bf16[8,128,128]{2,1,0:T(8,128)(2,1)} %copy-done.9, ...), custom_call_target="tpu_custom_call" | custom-call | flops 1677721600 | bytes 2000000 | tf_op jit(solution)/shard_map/pallas_call | solution.py:111
  79.0 1.7 %collective-permute-done.11.refs_2_ = bf16[8,2,128,128]{3,2,1,0:T(8,128)(2,1)S(1)} collective-permute-done((bf16[8,2,128,128]{3,2,1,0:T(8,128)(2,1)}, bf16[8,2,128,128]{3,2,1,0:T(8,128)(2,1)S(1)}, u32[]{:S(2)}, u32[]{:S(2)}) %collective-permute-start.11) | collective-permute-done | bytes 524320 | tf_op jit(solution)/shard_map/ppermute | solution.py:537
  86.9 5.6 %all-to-all-start.4 = ((bf16[8,4,128,128]{3,2,1,0:T(8,128)(2,1)}), bf16[8,4,128,128]{3,2,1,0:T(8,128)(2,1)S(1)}, u32[]{:S(2)}, u32[]{:S(2)}) async-start(bf16[8,4,128,128]{3,2,1,0:T(8,128)(2,1)} %shard_map.118), calls=%async_computation.4 | async-start | bytes 2097152 | tf_op jit(solution)/shard_map/all_to_all | solution.py:406
  93.5 3.0 %shard_map.119 = (bf16[128,1024]{1,0:T(8,128)(2,1)}, bf16[128,1024]{1,0:T(8,128)(2,1)}) custom-call(s32[1]{0:T(128)} %bitcast.1.refs_0_, bf16[8,2,128,128]{3,2,1,0:T(8,128)(2,1)S(1)} %all-to-all-done.1.refs_4_.refs_1_, bf16[8,2,128,128]{3,2,1,0:T(8,128)(2,1)S(1)} %collective-permute-done.12.refs_5_.refs_2_, bf16[128,1024]{1,0:T(8,128)(2,1)S(1)} %copy-done.2, ...), custom_call_target="tpu_custom_call" | custom-call | flops 536870912 | bytes 2000000 | tf_op jit(solution)/shard_map/pallas_call | solution.py:111
  96.5 2.1 %collective-permute-start.13 = (bf16[128,1024]{1,0:T(8,128)(2,1)}, bf16[128,1024]{1,0:T(8,128)(2,1)S(1)}, u32[]{:S(2)}, u32[]{:S(2)}) collective-permute-start(bf16[128,1024]{1,0:T(8,128)(2,1)} %get-tuple-element.58), channel_id=1, source_target_pairs={{0,8},{8,0},{16,24},{24,16},{32,40},{40,32},{48,56},{56,48},{64,72... | collective-permute-start | bytes 786440 | tf_op jit(solution)/shard_map/ppermute | solution.py:561
  102.2 3.4 %all-to-all-done.4.refs_0_ = bf16[8,4,128,128]{3,2,1,0:T(8,128)(2,1)S(1)} async-done(((bf16[8,4,128,128]{3,2,1,0:T(8,128)(2,1)}), bf16[8,4,128,128]{3,2,1,0:T(8,128)(2,1)S(1)}, u32[]{:S(2)}, u32[]{:S(2)}) %all-to-all-start.4) | async-done | bytes 1048608 | tf_op jit(solution)/shard_map/all_to_all | solution.py:406
  105.6 3.8 %collective-permute-start.14 = (bf16[8,128,128]{2,1,0:T(8,128)(2,1)S(1)}, bf16[8,128,128]{2,1,0:T(8,128)(2,1)S(1)}, u32[]{:S(2)}, u32[]{:S(2)}) collective-permute-start(bf16[8,128,128]{2,1,0:T(8,128)(2,1)S(1)} %slice_bitcast_fusion.refs_1_), channel_id=1, source_target_pairs={{0,8},{8,0},{16,24},{24,16},{32,40},{40,32},{48,56},{56,48},{64,72... | collective-permute-start | bytes 786440 | tf_op jit(solution)/shard_map/ppermute | solution.py:569
  (59 shorter events, 25.0 us)
Async XLA Ops:
  3.3 16.3 %copy-start.10 = (s32[1,2048]{1,0:T(1,128)S(1)}, s32[1,2048]{1,0:T(1,128)}, u32[]{:S(2)}) copy-start(s32[1,2048]{1,0:T(1,128)} %param.10) | copy-start | bytes 24580
  3.3 17.3 %copy-start = (bf16[128,1024]{1,0:T(8,128)(2,1)S(1)}, bf16[128,1024]{1,0:T(8,128)(2,1)}, u32[]{:S(2)}) copy-start(bf16[128,1024]{1,0:T(8,128)(2,1)} %get-tuple-element.39.refs_1_) | copy-start | bytes 786436
  3.3 12.9 %collective-permute-start = (bf16[128,1024]{1,0:T(8,128)(2,1)}, bf16[128,1024]{1,0:T(8,128)(2,1)S(1)}, u32[]{:S(2)}, u32[]{:S(2)}) collective-permute-start(bf16[128,1024]{1,0:T(8,128)(2,1)} %get-tuple-element.35.refs_3_), channel_id=1, source_target_pairs={{0,4},{1,5},{2,6},{3,7},{4,0},{5,1},{6,2},{7,3},{8,12},{9,13},{10,... | collective-permute-start | bytes 786440 | tf_op jit(solution)/shard_map/ppermute | solution.py:439
  5.5 16.4 %collective-permute-start.2 = (bf16[128,1024]{1,0:T(8,128)(2,1)}, bf16[128,1024]{1,0:T(8,128)(2,1)S(1)}, u32[]{:S(2)}, u32[]{:S(2)}) collective-permute-start(bf16[128,1024]{1,0:T(8,128)(2,1)} %get-tuple-element.35.refs_3_), channel_id=1, source_target_pairs={{0,3},{1,2},{2,1},{3,0},{4,7},{5,6},{6,5},{7,4},{8,11},{9,10},{10,... | collective-permute-start | bytes 786440 | tf_op jit(solution)/shard_map/ppermute | solution.py:439
  9.2 12.7 %collective-permute-start.1 = (bf16[128,1024]{1,0:T(8,128)(2,1)}, bf16[128,1024]{1,0:T(8,128)(2,1)S(1)}, u32[]{:S(2)}, u32[]{:S(2)}) collective-permute-start(bf16[128,1024]{1,0:T(8,128)(2,1)} %get-tuple-element.35.refs_3_), channel_id=1, source_target_pairs={{0,1},{1,0},{2,3},{3,2},{4,5},{5,4},{6,7},{7,6},{8,9},{9,8},{10,11... | collective-permute-start | bytes 786440 | tf_op jit(solution)/shard_map/ppermute | solution.py:439
  9.2 17.7 %all-to-all-start = ((bf16[8,3,128,128]{3,2,1,0:T(8,128)(2,1)}), bf16[8,3,128,128]{3,2,1,0:T(8,128)(2,1)S(1)}, u32[]{:S(2)}, u32[]{:S(2)}) async-start(bf16[8,3,128,128]{3,2,1,0:T(8,128)(2,1)} %get-tuple-element.34), calls=%async_computation | async-start | bytes 1572864 | tf_op jit(solution)/shard_map/all_to_all | solution.py:406
  16.3 4.4 %collective-permute-start.5 = (bf16[128,1024]{1,0:T(8,128)(2,1)S(1)}, bf16[128,1024]{1,0:T(8,128)(2,1)S(1)}, u32[]{:S(2)}, u32[]{:S(2)}) collective-permute-start(bf16[128,1024]{1,0:T(8,128)(2,1)S(1)} %copy-done.11), channel_id=1, source_target_pairs={{0,8},{8,0},{16,24},{24,16},{32,40},{40,32},{48,56},{56,48},{64,72... | collective-permute-start | bytes 786440 | tf_op jit(solution)/shard_map/ppermute | solution.py:459
  17.9 9.1 %collective-permute-start.4 = (bf16[128,1024]{1,0:T(8,128)(2,1)S(1)}, bf16[128,1024]{1,0:T(8,128)(2,1)S(1)}, u32[]{:S(2)}, u32[]{:S(2)}) collective-permute-start(bf16[128,1024]{1,0:T(8,128)(2,1)S(1)} %collective-permute-done.refs_7_), channel_id=1, source_target_pairs={{0,3},{1,2},{2,1},{3,0},{4,7},{5,6},{6,5},{7,4},{8,11},{9,10},{10,... | collective-permute-start | bytes 786440 | tf_op jit(solution)/shard_map/ppermute | solution.py:439
  18.1 8.8 %collective-permute-start.3 = (bf16[128,1024]{1,0:T(8,128)(2,1)S(1)}, bf16[128,1024]{1,0:T(8,128)(2,1)S(1)}, u32[]{:S(2)}, u32[]{:S(2)}) collective-permute-start(bf16[128,1024]{1,0:T(8,128)(2,1)S(1)} %collective-permute-done.refs_7_), channel_id=1, source_target_pairs={{0,1},{1,0},{2,3},{3,2},{4,5},{5,4},{6,7},{7,6},{8,9},{9,8},{10,11... | collective-permute-start | bytes 786440 | tf_op jit(solution)/shard_map/ppermute | solution.py:439
  26.9 15.0 %copy-start.3 = (bf16[128,1024]{1,0:T(8,128)(2,1)}, bf16[128,1024]{1,0:T(8,128)(2,1)S(1)}, u32[]{:S(2)}) copy-start(bf16[128,1024]{1,0:T(8,128)(2,1)S(1)} %collective-permute-done.4.refs_10_) | copy-start | bytes 786436
  27.0 15.0 %copy-start.5 = (bf16[128,1024]{1,0:T(8,128)(2,1)}, bf16[128,1024]{1,0:T(8,128)(2,1)S(1)}, u32[]{:S(2)}) copy-start(bf16[128,1024]{1,0:T(8,128)(2,1)S(1)} %collective-permute-done.3.refs_8_) | copy-start | bytes 786436
  27.0 6.7 %collective-permute-start.6 = (bf16[8,3,128,128]{3,2,1,0:T(8,128)(2,1)S(1)}, bf16[8,3,128,128]{3,2,1,0:T(8,128)(2,1)S(1)}, u32[]{:S(2)}, u32[]{:S(2)}) collective-permute-start(bf16[8,3,128,128]{3,2,1,0:T(8,128)(2,1)S(1)} %all-to-all-done.refs_1_.refs_2_.refs_3_), channel_id=1, source_target_pairs={{0,8},{8,0},{16,24},{24,16},{32,40},{40,32},{48,56},{56,48},{64,72... | collective-permute-start | bytes 2359304 | tf_op jit(solution)/shard_map/ppermute | solution.py:471
  30.0 11.9 %collective-permute-start.8 = (bf16[128,1024]{1,0:T(8,128)(2,1)S(1)}, bf16[128,1024]{1,0:T(8,128)(2,1)}, u32[]{:S(2)}, u32[]{:S(2)}) collective-permute-start(bf16[128,1024]{1,0:T(8,128)(2,1)S(1)} %collective-permute-done.4.refs_10_), channel_id=1, source_target_pairs={{0,1},{1,0},{2,3},{3,2},{4,5},{5,4},{6,7},{7,6},{8,9},{9,8},{10,11... | collective-permute-start | bytes 786440 | tf_op jit(solution)/shard_map/ppermute | solution.py:439
  31.6 10.3 %collective-permute-start.9 = (bf16[256,512]{1,0:T(8,128)(2,1)}, bf16[256,512]{1,0:T(8,128)(2,1)}, u32[]{:S(2)}, u32[]{:S(2)}) collective-permute-start(bf16[256,512]{1,0:T(8,128)(2,1)} %shard_map.111), channel_id=1, source_target_pairs={{0,64},{8,72},{16,80},{24,88},{32,96},{40,104},{48,112},{56,120},{... | collective-permute-start | bytes 786440 | tf_op jit(solution)/shard_map/ppermute | solution.py:469
  32.7 9.2 %collective-permute-start.7 = (bf16[128,1024]{1,0:T(8,128)(2,1)S(1)}, bf16[128,1024]{1,0:T(8,128)(2,1)}, u32[]{:S(2)}, u32[]{:S(2)}) collective-permute-start(bf16[128,1024]{1,0:T(8,128)(2,1)S(1)} %collective-permute-done.1.refs_4_), channel_id=1, source_target_pairs={{0,3},{1,2},{2,1},{3,0},{4,7},{5,6},{6,5},{7,4},{8,11},{9,10},{10,... | collective-permute-start | bytes 786440 | tf_op jit(solution)/shard_map/ppermute | solution.py:439
  37.8 12.8 %all-to-all-start.1 = ((bf16[8,2,128,128]{3,2,1,0:T(8,128)(2,1)}), bf16[8,2,128,128]{3,2,1,0:T(8,128)(2,1)S(1)}, u32[]{:S(2)}, u32[]{:S(2)}) async-start(bf16[8,2,128,128]{3,2,1,0:T(8,128)(2,1)} %get-tuple-element.41.refs_5_), calls=%async_computation.1 | async-start | bytes 1048576 | tf_op jit(solution)/shard_map/all_to_all | solution.py:406
  44.7 2.4 %collective-permute-start.10 = (bf16[8,128,128]{2,1,0:T(8,128)(2,1)S(1)}, bf16[8,128,128]{2,1,0:T(8,128)(2,1)S(1)}, u32[]{:S(2)}, u32[]{:S(2)}) collective-permute-start(bf16[8,128,128]{2,1,0:T(8,128)(2,1)S(1)} %get-tuple-element.45), channel_id=1, source_target_pairs={{0,8},{8,0},{16,24},{24,16},{32,40},{40,32},{48,56},{56,48},{64,72... | collective-permute-start | bytes 786440 | tf_op jit(solution)/shard_map/ppermute | solution.py:497
  50.6 6.8 %collective-permute-start.12 = (bf16[8,2,128,128]{3,2,1,0:T(8,128)(2,1)S(1)}, bf16[8,2,128,128]{3,2,1,0:T(8,128)(2,1)S(1)}, u32[]{:S(2)}, u32[]{:S(2)}) collective-permute-start(bf16[8,2,128,128]{3,2,1,0:T(8,128)(2,1)S(1)} %all-to-all-done.1.refs_4_.refs_1_), channel_id=1, source_target_pairs={{0,8},{8,0},{16,24},{24,16},{32,40},{40,32},{48,56},{56,48},{64,72... | collective-permute-start | bytes 1572872 | tf_op jit(solution)/shard_map/ppermute | solution.py:504
  54.0 11.6 %all-to-all-start.2 = ((bf16[8,128,128]{2,1,0:T(8,128)(2,1)}), bf16[8,128,128]{2,1,0:T(8,128)(2,1)S(1)}, u32[]{:S(2)}, u32[]{:S(2)}) async-start(bf16[8,128,128]{2,1,0:T(8,128)(2,1)} %shard_map.114), calls=%async_computation.2 | async-start | bytes 524288 | tf_op jit(solution)/shard_map/all_to_all | solution.py:406
  66.3 19.3 %all-to-all-start.3 = ((bf16[32,32,512]{2,1,0:T(8,128)(2,1)}), bf16[32,32,512]{2,1,0:T(8,128)(2,1)S(1)}, u32[]{:S(2)}, u32[]{:S(2)}) async-start(bf16[32,32,512]{2,1,0:T(8,128)(2,1)} %shard_map.117), calls=%async_computation.3 | async-start | bytes 2097152 | tf_op jit(solution)/shard_map/all_to_all | solution.py:515
  77.8 2.9 %collective-permute-start.11 = (bf16[8,2,128,128]{3,2,1,0:T(8,128)(2,1)}, bf16[8,2,128,128]{3,2,1,0:T(8,128)(2,1)S(1)}, u32[]{:S(2)}, u32[]{:S(2)}) collective-permute-start(bf16[8,2,128,128]{3,2,1,0:T(8,128)(2,1)} %get-tuple-element.54), channel_id=1, source_target_pairs={{0,8},{8,0},{16,24},{24,16},{32,40},{40,32},{48,56},{56,48},{64,72... | collective-permute-start | bytes 1572872 | tf_op jit(solution)/shard_map/ppermute | solution.py:537
  86.9 18.7 %all-to-all-start.4 = ((bf16[8,4,128,128]{3,2,1,0:T(8,128)(2,1)}), bf16[8,4,128,128]{3,2,1,0:T(8,128)(2,1)S(1)}, u32[]{:S(2)}, u32[]{:S(2)}) async-start(bf16[8,4,128,128]{3,2,1,0:T(8,128)(2,1)} %shard_map.118), calls=%async_computation.4 | async-start | bytes 2097152 | tf_op jit(solution)/shard_map/all_to_all | solution.py:406
  96.5 3.5 %collective-permute-start.13 = (bf16[128,1024]{1,0:T(8,128)(2,1)}, bf16[128,1024]{1,0:T(8,128)(2,1)S(1)}, u32[]{:S(2)}, u32[]{:S(2)}) collective-permute-start(bf16[128,1024]{1,0:T(8,128)(2,1)} %get-tuple-element.58), channel_id=1, source_target_pairs={{0,8},{8,0},{16,24},{24,16},{32,40},{40,32},{48,56},{56,48},{64,72... | collective-permute-start | bytes 786440 | tf_op jit(solution)/shard_map/ppermute | solution.py:561
  105.6 5.1 %collective-permute-start.14 = (bf16[8,128,128]{2,1,0:T(8,128)(2,1)S(1)}, bf16[8,128,128]{2,1,0:T(8,128)(2,1)S(1)}, u32[]{:S(2)}, u32[]{:S(2)}) collective-permute-start(bf16[8,128,128]{2,1,0:T(8,128)(2,1)S(1)} %slice_bitcast_fusion.refs_1_), channel_id=1, source_target_pairs={{0,8},{8,0},{16,24},{24,16},{32,40},{40,32},{48,56},{56,48},{64,72... | collective-permute-start | bytes 786440 | tf_op jit(solution)/shard_map/ppermute | solution.py:569
  (8 other events, 27.6 us)
